TPU v7x, 256 devices: a whole 4x4x8 slice. The times are simulated.
256 devices in a mesh: head: 8 (over z_lo, core), depth: 32 (over x, y, z_hi).
Axes of the slice: x: 4, y: 4, z: 8 (z_hi: 2, z_lo: 4; z = z_hi * 4 + z_lo), core: 2. Of those that a mesh axis runs over, the one named last changes fastest.
Arguments:
- tokens: bfloat16 [128, 1280, 768], P('depth', 'head'), may hold values from -6 to 6
- ln_gain: float32 [768], replicated, may hold values from 0.1 to 1.9
- w_qkv: bfloat16 [768, 3, 512], replicated, may hold values from -0.21875 to 0.21875
- w_out: bfloat16 [512, 768], replicated, may hold values from -2.390625 to 2.390625
Outputs:
- mixed: float32 [128, 1280, 768], P('depth', 'head')
All inputs are finite; a program needn't handle non-finite values.
Results may differ from a plain program's by a relative error of at most 0.0095.
Values may be sent and summed in bfloat16 or wider, within the bound.
No kernel may reach another device: no remote copies, remote signals or barrier semaphores. Data moves between devices by JAX's collectives and lax.ppermute only.
A program may use at most 64 MiB of HBM per device.

v0:
```python
import math

import jax
import jax.numpy as jnp
from jax import lax
from jax.sharding import PartitionSpec as P

HEAD_DIM = 64


def soft_weights(logits):
    expo = jnp.exp(logits)
    return (expo / jnp.sum(expo, axis=-1, keepdims=True)).astype(jnp.bfloat16)


def shards(tokens, ln_gain, w_qkv, w_out):
    x = tokens.astype(jnp.float32)
    mean = jnp.mean(x, axis=-1, keepdims=True)
    var = jnp.mean((x - mean) ** 2, axis=-1, keepdims=True)
    normed = ((x - mean) / jnp.sqrt(var + 1e-05) * ln_gain).astype(jnp.bfloat16)
    qkv = jnp.einsum("rld,dcf->rlcf", normed, w_qkv, preferred_element_type=jnp.float32).astype(
        jnp.bfloat16
    )
    mine = lax.all_to_all(qkv, "head", split_axis=3, concat_axis=1, tiled=True)
    seqs, length = (mine.shape[0], mine.shape[1])
    heads_here = mine.shape[3] // HEAD_DIM
    shape = (seqs, length, heads_here, HEAD_DIM)
    query = mine[:, :, 0].reshape(shape)
    keys = mine[:, :, 1].reshape(shape)
    values = mine[:, :, 2].reshape(shape)
    depth_size = lax.axis_size("depth")
    factor = 1.0 / math.sqrt(HEAD_DIM * seqs * depth_size)
    term = jnp.einsum("rihe,rjhe->ihj", query, keys, preferred_element_type=jnp.float32) * factor
    logits = lax.psum(term, "depth")
    probs = soft_weights(logits)
    context = jnp.einsum(
        "ihj,rjhe->rihe", probs, values, preferred_element_type=jnp.float32
    ).astype(jnp.bfloat16)
    context = context.reshape(seqs, length, heads_here * HEAD_DIM)
    returned = lax.all_to_all(context, "head", split_axis=1, concat_axis=2, tiled=True)
    mixed = jnp.einsum("rlf,fd->rld", returned, w_out, preferred_element_type=jnp.float32)
    return mixed


def solution(mesh):
    in_specs = (P("depth", "head", None), P(), P(), P())
    out_specs = P("depth", "head", None)
    return jax.shard_map(shards, mesh=mesh, in_specs=in_specs, out_specs=out_specs, check_vma=False)
```

profile of v0, /device:TPU:6, one launch (start us, length us, event | category | flops | bytes accessed | tf_op | source)
XLA Modules:
  0.0 771.1 jit_solution(3011407343537525544)
XLA Ops:
  6.5 0.0 copy-start
  6.5 0.0 copy-start.2
  6.5 0.0 copy-start.3
  6.5 0.0 all-reduce.2.cloned.1.call-start
  6.5 1.6 convert_reduce_fusion
  8.1 1.6 fusion.14
  9.8 0.0 copy-done
  9.8 0.0 copy-done.2
  9.8 0.0 copy-done.3
  9.8 3.1 fusion.17
  12.9 5.7 copy.17
  18.6 77.4 %all_to_all.36 = bf16[4,160,3,512]{1,0,2,3:T(4,128)(2,1)S(1)} all-to-all(bf16[4,160,3,512]{1,0,2,3:T(4,128)(2,1)} %copy.17), channel_id=1, replica_groups=mesh['head'=8,'depth'=32] {'head'}, dimensions={3} | all-to-all | bytes 3932160 | tf_op jit(solution)/shard_map/all_to_all | solution.py:24
  96.0 3.4 copy.30
  99.5 6.2 all_to_all.29
  105.7 5.1 fusion.1
  110.7 0.0 all-reduce.2.cloned.1.call-update
  110.8 596.0 %all-reduce.2.cloned.1.call-done = f32[1280,1,1280]{0,2,1:T(8,128)} async-done(((f32[1280,1,1280]{0,2,1:T(8,128)}), f32[1280,1,1280]{0,2,1:T(8,128)}) %all-reduce.2.cloned.1.call-update) | async-done | bytes 6553616 | tf_op jit(solution)/shard_map/psum | solution.py:34
  706.8 0.0 copy-start.1
  706.8 4.0 exponential_reduce_fusion
  710.8 0.7 copy-done.1
  711.5 2.2 fusion.7
  713.8 2.1 copy.21
  715.9 3.1 reshape.48
  719.0 32.9 %all_to_all.37 = bf16[8,2,20480]{2,1,0:T(2,128)(2,1)} all-to-all(bf16[8,2,20480]{2,1,0:T(2,128)(2,1)S(1)} %reshape.48), channel_id=1, replica_groups=mesh['head'=8,'depth'=32] {'head'}, dimensions={0} | all-to-all | bytes 1310720 | tf_op jit(solution)/shard_map/all_to_all | solution.py:40
  751.9 4.0 reshape.49
  755.9 3.2 copy.31
  759.1 2.0 all_to_all.33
  761.2 3.1 fusion.25
  (2 shorter events, 0.0 us)
Async XLA Ops:
  6.5 3.3 copy-start
  6.5 3.3 copy-start.2
  6.5 3.3 copy-start.3
  6.5 700.2 %all-reduce.2.cloned.1.call-start = ((), (), s32[]{:S(2)}) async-start(), calls=%async_computation.2 | async-start | bytes 13107200 | tf_op jit(solution)/shard_map/psum | solution.py:34
  706.8 4.7 copy-start.1
Sparse Core Ops, SparseCore 0:
  110.9 595.8 all-reduce.1
where the time goes:
time: 786 us; the launch traced here: 771 us
  waiting for transfers between devices  596 us (76%)
  blocking collectives  110 us (14%)
  local copies, waits for them, and re-layouts  30.5 us (4%)
  matrix products  13.5 us (2%)
  between operations  13.5 us (2%)
    psum x1, waiting for transfers between devices, shards(): logits = lax.psum(term, 'depth')  596 us
    all_to_all x1, blocking collectives, shards(): mine = lax.all_to_all(qkv, 'head', split_axis=3, concat_axis=1, tiled=True)  77.4 us
    all_to_all x1, blocking collectives, shards(): lax.all_to_all(context, 'head', split_axis=1, concat_axis=2, tiled=True)  32.9 us
  transfers between devices with their start and end apart: 1, of which 1 were waited for; matrix products, arithmetic and copies ran while one was open for 0% of the time, Pallas kernels for 0%

commit v1 on v0

v1 whole, which is shorter than its diff:
```python
import functools
import math

import jax
import jax.numpy as jnp
from jax import lax
from jax.experimental import pallas as pl
from jax.experimental.pallas import tpu as pltpu
from jax.sharding import Mesh
from jax.sharding import PartitionSpec as P

HEAD_DIM = 64
Z, CORE, X, Y, W = 4, 2, 4, 4, 2
RING = Z * W
PLANE = X * Y
BF = jnp.bfloat16
F32 = jnp.float32
VMEM = pl.BlockSpec(memory_space=pltpu.VMEM)
SMEM = pl.BlockSpec(memory_space=pltpu.SMEM)
PARAMS = pltpu.CompilerParams(vmem_limit_bytes=48 * 1024 * 1024)


def place(index):
    return (index % W) * Z + index // W


def index_of(position):
    return (position % Z) * W + position // Z


def head_at(position):
    pos = lax.rem(position, RING)
    return lax.rem(pos, Z) * W + lax.div(pos, Z)


def project_kernel(pos_ref, x_ref, gain_ref, w_ref, *refs):
    outs, (normed, mine) = refs[:-2], refs[-2:]
    seqs, length, width = x_ref.shape
    inner = w_ref.shape[2]
    heads = inner // HEAD_DIM
    for r in range(seqs):
        x = x_ref[r].astype(F32)
        mean = jnp.mean(x, axis=-1, keepdims=True)
        off = x - mean
        var = jnp.mean(off * off, axis=-1, keepdims=True)
        normed[r * length : (r + 1) * length] = (off / jnp.sqrt(var + 1e-05) * gain_ref[...]).astype(BF)
    pos = pos_ref[0]
    for c in range(3):
        y = jnp.dot(normed[...], w_ref[c], preferred_element_type=F32)
        for h in range(heads):
            mine[h] = jnp.concatenate(
                [y[r * length : (r + 1) * length, h * HEAD_DIM : (h + 1) * HEAD_DIM] for r in range(seqs)], axis=1
            ).astype(BF)
        for s in range(RING):
            outs[c * RING + s][...] = mine[head_at(pos + s)]


def gather_kernel(pos_ref, *refs):
    parts, out = refs[:-1], refs[-1]
    pos = pos_ref[0]
    for s in range(RING):
        src = lax.rem(pos + RING - s, RING)
        out[lax.div(src, Z), lax.rem(src, Z)] = parts[s][...]


def logits_kernel(pos_ref, *refs):
    q_parts, (k_ref, k_far, out_ref, q) = refs[:RING], refs[RING:]
    pos = pos_ref[0]
    for s in range(RING):
        src = lax.rem(pos + RING - s, RING)
        q[lax.div(src, Z), lax.rem(src, Z)] = q_parts[s][...]
    half = k_ref.shape[1] * k_ref.shape[2]
    for side, keys in enumerate((k_ref, k_far)):
        total = None
        for w in range(W):
            a = q[w].reshape(half, -1)
            b = keys[w].reshape(half, -1)
            term = lax.dot_general(a, b, (((1,), (1,)), ((), ())), preferred_element_type=F32)
            total = term if total is None else total + term
        out_ref[:, side * half : (side + 1) * half] = total.astype(BF)


def probs_kernel(scale, x_ref, out_ref):
    logits = x_ref[0].astype(F32)
    for i in range(1, x_ref.shape[0]):
        logits = logits + x_ref[i].astype(F32)
    expo = jnp.exp(logits * scale)
    probs = (expo / jnp.sum(expo, axis=-1, keepdims=True)).astype(BF)
    for i in range(out_ref.shape[0]):
        out_ref[i] = probs


def context_kernel(pos_ref, p_ref, v_ref, v_far, *refs):
    outs, mine = refs[:-1], refs[-1]
    half = v_ref.shape[1] * v_ref.shape[2]
    length = v_ref.shape[2]
    for w in range(W):
        a = jnp.dot(p_ref[:, :half], v_ref[w].reshape(half, -1), preferred_element_type=F32)
        a = a + jnp.dot(p_ref[:, half:], v_far[w].reshape(half, -1), preferred_element_type=F32)
        a = a.astype(BF)
        for z in range(Z):
            mine[w * Z + z] = a[z * length : (z + 1) * length]
    pos = pos_ref[0]
    for s in range(RING):
        outs[s][...] = mine[lax.rem(pos + s, RING)]


def mix_kernel(pos_ref, w_ref, *refs):
    parts, (out_ref, rows) = refs[:-2], refs[-2:]
    pos = pos_ref[0]
    for s in range(RING):
        h = head_at(pos + RING - s)
        rows[s * HEAD_DIM : (s + 1) * HEAD_DIM] = w_ref[pl.ds(pl.multiple_of(h * HEAD_DIM, HEAD_DIM), HEAD_DIM)]
    for r in range(out_ref.shape[0]):
        lhs = jnp.concatenate([part[:, r * HEAD_DIM : (r + 1) * HEAD_DIM] for part in parts], axis=1)
        out_ref[r] = jnp.dot(lhs, rows[...], preferred_element_type=F32)


def call(kernel, out_shape, operands, scratch=(), flops=0):
    moved = sum(math.prod(o.shape) * o.dtype.itemsize for o in operands)
    return pl.pallas_call(
        kernel,
        out_shape=out_shape,
        in_specs=[SMEM if o.dtype == jnp.int32 else VMEM for o in operands],
        out_specs=jax.tree.map(lambda _: VMEM, out_shape),
        scratch_shapes=list(scratch),
        compiler_params=PARAMS,
        cost_estimate=pl.CostEstimate(flops=flops, bytes_accessed=2 * moved, transcendentals=0),
    )(*operands)


def along_ring(parts):
    got = [parts[0]] + [None] * (RING - 1)
    for s in (4, 3, 5, 2, 6, 1, 7):
        pairs = [(i, index_of((place(i) + s) % RING)) for i in range(RING)]
        got[s] = lax.ppermute(parts[s], ("z", "w"), pairs)
    return got


def other_core(a):
    return lax.ppermute(a, "c", [(0, 1), (1, 0)])


def shards(tokens, ln_gain, w_qkv, w_out):
    seqs, length, width = tokens.shape
    inner = w_qkv.shape[2]
    lanes = seqs * HEAD_DIM
    pos = (lax.axis_index("w") * Z + lax.axis_index("z")).astype(jnp.int32).reshape(1)
    block = jax.ShapeDtypeStruct((length, lanes), BF)
    whole = jax.ShapeDtypeStruct((W, Z, length, lanes), BF)
    half = Z * length
    full = CORE * half
    scale = 1.0 / math.sqrt(HEAD_DIM * seqs * W * PLANE)

    outs = call(
        project_kernel,
        [block] * (3 * RING),
        [pos, tokens, ln_gain.reshape(1, width), jnp.transpose(w_qkv, (1, 0, 2))],
        [pltpu.VMEM((seqs * length, width), BF), pltpu.VMEM((RING, length, lanes), BF)],
        flops=2 * seqs * length * width * 3 * inner,
    )
    query, keys, values = outs[:RING], outs[RING : 2 * RING], outs[2 * RING :]
    keys = along_ring(keys)
    query = along_ring(query)
    values = along_ring(values)
    keys = call(gather_kernel, whole, [pos, *keys])
    keys_far = other_core(keys)
    term = call(
        logits_kernel,
        jax.ShapeDtypeStruct((half, full), BF),
        [pos, *query, keys, keys_far],
        [pltpu.VMEM(whole.shape, BF)],
        flops=2 * half * full * W * lanes,
    )
    chunk = (PLANE, half // PLANE, full)
    terms = lax.all_to_all(term.reshape(chunk), ("x", "y"), 0, 0, tiled=True)
    probs = call(functools.partial(probs_kernel, scale), jax.ShapeDtypeStruct(chunk, BF), [terms])
    probs = lax.all_to_all(probs, ("x", "y"), 0, 0, tiled=True).reshape(half, full)
    values = call(gather_kernel, whole, [pos, *values])
    values_far = other_core(values)
    context = call(
        context_kernel,
        [block] * RING,
        [pos, probs, values, values_far],
        [pltpu.VMEM((RING, length, lanes), BF)],
        flops=2 * half * full * W * lanes,
    )
    context = along_ring(context)
    return call(
        mix_kernel,
        jax.ShapeDtypeStruct((seqs, length, width), F32),
        [pos, w_out, *context],
        [pltpu.VMEM(w_out.shape, BF)],
        flops=2 * seqs * length * inner * width,
    )


def solution(mesh):
    cut = Mesh(mesh.devices.reshape(Z, CORE, X, Y, W), ("z", "c", "x", "y", "w"))
    split = P(("x", "y", "w"), ("z", "c"), None)
    return jax.shard_map(shards, mesh=cut, in_specs=(split, P(), P(), P()), out_specs=split, check_vma=False)
```

time: 786 us -> 149 us (0.19); the launches traced: 771 us -> 149 us
  waiting for transfers between devices: 596 us -> 41.3 us
  blocking collectives: 110 us -> 28.4 us
  starting transfers between devices: 0.01 us -> 64.8 us
  local copies, waits for them, and re-layouts: 30.5 us -> 5.51 us
  matrix products: 13.5 us -> 0 us
  between operations: 13.5 us -> 0.1 us
  Pallas kernels: 0 us -> 8.55 us
    psum x1 -> x0, waiting for transfers between devices: 596 us -> none  [shards(): logits = lax.psum(term, 'depth')]
    all_to_all x2 -> x1, blocking collectives: 110 us -> 28.4 us  [shards(): terms = lax.all_to_all(term.reshape(chunk), ('x', 'y'), 0, 0, tiled=True)]
    ppermute x0 -> x30, starting transfers between devices: none -> 59.1 us  [the longest x28 58.9 us: along_ring(): got[s] = lax.ppermute(parts[s], ('z', 'w'), pairs)]
    ppermute x0 -> x30, waiting for transfers between devices: none -> 41.3 us  [the longest x28 39.2 us: along_ring(): got[s] = lax.ppermute(parts[s], ('z', 'w'), pairs)]
    all_to_all x4 -> x0, local copies, waits for them, and re-layouts: 15 us -> none  [the longest x2 9.68 us: shards(): mine = lax.all_to_all(qkv, 'head', split_axis=3, concat_axis=1, tiled=True)]
    dot_general x4 -> x0, matrix products: 13.5 us -> none  [the longest x1 5.05 us: shards(): jnp.einsum('rihe,rjhe->ihj', query, keys, preferred_element_type=jnp.floa...]
    pallas_call x0 -> x7, Pallas kernels: none -> 8.55 us  [call(): pl.pallas_call(kernel, out_shape=out_shape, in_specs=[SMEM if o.dtype ==...]
  transfers between devices with their start and end apart: 1 -> 31, of which waited for: 1 -> 18; matrix products, arithmetic and copies ran while one was open for 0% -> 0% of each run, Pallas kernels for 0% -> 0%
where the time goes in v1:
time: 149 us
  starting transfers between devices  64.8 us (43%)
  waiting for transfers between devices  41.3 us (28%)
  blocking collectives  28.4 us (19%)
  Pallas kernels  8.55 us (6%)
  local copies, waits for them, and re-layouts  5.51 us (4%)
    ppermute x28, starting transfers between devices, along_ring(): got[s] = lax.ppermute(parts[s], ('z', 'w'), pairs)  58.9 us
    ppermute x28, waiting for transfers between devices, along_ring(): got[s] = lax.ppermute(parts[s], ('z', 'w'), pairs)  39.2 us
    all_to_all x1, blocking collectives, shards(): terms = lax.all_to_all(term.reshape(chunk), ('x', 'y'), 0, 0, tiled=True)  28.4 us
    pallas_call x7, Pallas kernels, call(): pl.pallas_call(kernel, out_shape=out_shape, in_specs=[SMEM if o.dtype ==...  8.55 us
    all_to_all x1, starting transfers between devices, shards(): lax.all_to_all(probs, ('x', 'y'), 0, 0, tiled=True).reshape(half, full)  5.69 us
    unnamed x10, local copies, waits for them, and re-layouts  4.82 us
  transfers between devices with their start and end apart: 31, of which 18 were waited for; matrix products, arithmetic and copies ran while one was open for 0% of the time, Pallas kernels for 0%

profile of v1, /device:TPU:6, one launch (start us, length us, event | category | flops | bytes accessed | tf_op | source)
XLA Modules:
  0.0 148.7 jit_solution(5961020766960796395)
XLA Ops:
  0.0 0.7 reshape.13.gain_ref
  0.7 1.7 %copy-done.1 = bf16[768,3,512]{2,0,1:T(8,128)(2,1)S(1)} copy-done((bf16[768,3,512]{2,0,1:T(8,128)(2,1)S(1)}, bf16[768,3,512]{2,0,1:T(8,128)(2,1)}, u32[]{:S(2)}) %copy-start.1) | copy-done | bytes 2359320
  2.4 1.2 copy-done.2
  3.6 2.4 %shard_map.46 = (bf16[160,256]{1,0:T(8,128)(2,1)S(1)}, bf16[160,256]{1,0:T(8,128)(2,1)S(1)}, bf16[160,256]{1,0:T(8,128)(2,1)S(1)}, bf16[160,256]{1,0:T(8,128)(2,...) custom-call(s32[1]{0:T(128)} %bitcast.pos_ref, ...), custom_call_target="tpu_custom_call" | custom-call | flops 1509949440 | bytes 6690824 | tf_op jit(solution)/shard_map/pallas_call | solution.py:121
  6.0 2.0 %collective-permute-start.7 = (bf16[160,256]{1,0:T(8,128)(2,1)S(1)}, bf16[160,256]{1,0:T(8,128)(2,1)S(1)}, u32[]{:S(2)}, u32[]{:S(2)}) collective-permute-start(bf16[160,256]{1,0:T(8,128)(2,1)S(1)} %get-tuple-element.46), channel_id=1, source_target_pairs={{0,64},{1,65},{64,128},{65,129},{128,192},{129,193},{192,1},{193,0... | collective-permute-start | bytes 245768 | tf_op jit(solution)/shard_map/ppermute | solution.py:136
  8.0 3.3 %collective-permute-start.8 = (bf16[160,256]{1,0:T(8,128)(2,1)S(1)}, bf16[160,256]{1,0:T(8,128)(2,1)S(1)}, u32[]{:S(2)}, u32[]{:S(2)}) collective-permute-start(bf16[160,256]{1,0:T(8,128)(2,1)S(1)} %get-tuple-element.47), channel_id=1, source_target_pairs={{0,128},{1,129},{64,192},{65,193},{128,1},{129,0},{192,65},{193,64... | collective-permute-start | bytes 245768 | tf_op jit(solution)/shard_map/ppermute | solution.py:136
  11.3 4.0 %collective-permute-start.9 = (bf16[160,256]{1,0:T(8,128)(2,1)S(1)}, bf16[160,256]{1,0:T(8,128)(2,1)S(1)}, u32[]{:S(2)}, u32[]{:S(2)}) collective-permute-start(bf16[160,256]{1,0:T(8,128)(2,1)S(1)} %get-tuple-element.48), channel_id=1, source_target_pairs={{0,192},{1,193},{64,1},{65,0},{128,65},{129,64},{192,129},{193,128... | collective-permute-start | bytes 245768 | tf_op jit(solution)/shard_map/ppermute | solution.py:136
  15.3 0.6 collective-permute-start.10
  15.9 4.9 %collective-permute-start.11 = (bf16[160,256]{1,0:T(8,128)(2,1)S(1)}, bf16[160,256]{1,0:T(8,128)(2,1)S(1)}, u32[]{:S(2)}, u32[]{:S(2)}) collective-permute-start(bf16[160,256]{1,0:T(8,128)(2,1)S(1)} %get-tuple-element.50), channel_id=1, source_target_pairs={{0,65},{1,64},{64,129},{65,128},{128,193},{129,192},{192,0},{193,1... | collective-permute-start | bytes 245768 | tf_op jit(solution)/shard_map/ppermute | solution.py:136
  20.8 2.7 %collective-permute-start.12 = (bf16[160,256]{1,0:T(8,128)(2,1)S(1)}, bf16[160,256]{1,0:T(8,128)(2,1)S(1)}, u32[]{:S(2)}, u32[]{:S(2)}) collective-permute-start(bf16[160,256]{1,0:T(8,128)(2,1)S(1)} %get-tuple-element.51), channel_id=1, source_target_pairs={{0,129},{1,128},{64,193},{65,192},{128,0},{129,1},{192,64},{193,65... | collective-permute-start | bytes 245768 | tf_op jit(solution)/shard_map/ppermute | solution.py:136
  23.5 1.0 collective-permute-start.13
  24.5 1.7 %collective-permute-done.9.refs_3_ = bf16[160,256]{1,0:T(8,128)(2,1)S(1)} collective-permute-done((bf16[160,256]{1,0:T(8,128)(2,1)S(1)}, bf16[160,256]{1,0:T(8,128)(2,1)S(1)}, u32[]{:S(2)}, u32[]{:S(2)}) %collective-permute-start.9) | collective-permute-done | bytes 81952 | tf_op jit(solution)/shard_map/ppermute | solution.py:136
  26.2 0.0 collective-permute-done.10.refs_4_
  26.2 5.7 %collective-permute-done.11.refs_5_ = bf16[160,256]{1,0:T(8,128)(2,1)S(1)} collective-permute-done((bf16[160,256]{1,0:T(8,128)(2,1)S(1)}, bf16[160,256]{1,0:T(8,128)(2,1)S(1)}, u32[]{:S(2)}, u32[]{:S(2)}) %collective-permute-start.11) | collective-permute-done | bytes 81952 | tf_op jit(solution)/shard_map/ppermute | solution.py:136
  31.9 0.8 collective-permute-done.13.refs_7_
  32.6 0.1 shard_map.47.refs_8_
  32.7 0.1 collective-permute-start.14
  32.8 2.4 %collective-permute-start = (bf16[160,256]{1,0:T(8,128)(2,1)S(1)}, bf16[160,256]{1,0:T(8,128)(2,1)S(1)}, u32[]{:S(2)}, u32[]{:S(2)}) collective-permute-start(bf16[160,256]{1,0:T(8,128)(2,1)S(1)} %get-tuple-element.38), channel_id=1, source_target_pairs={{0,64},{1,65},{64,128},{65,129},{128,192},{129,193},{192,1},{193,0... | collective-permute-start | bytes 245768 | tf_op jit(solution)/shard_map/ppermute | solution.py:136
  35.2 1.2 collective-permute-start.1
  36.4 1.9 %collective-permute-start.2 = (bf16[160,256]{1,0:T(8,128)(2,1)S(1)}, bf16[160,256]{1,0:T(8,128)(2,1)S(1)}, u32[]{:S(2)}, u32[]{:S(2)}) collective-permute-start(bf16[160,256]{1,0:T(8,128)(2,1)S(1)} %get-tuple-element.40), channel_id=1, source_target_pairs={{0,192},{1,193},{64,1},{65,0},{128,65},{129,64},{192,129},{193,128... | collective-permute-start | bytes 245768 | tf_op jit(solution)/shard_map/ppermute | solution.py:136
  38.3 3.4 %collective-permute-start.3 = (bf16[160,256]{1,0:T(8,128)(2,1)S(1)}, bf16[160,256]{1,0:T(8,128)(2,1)S(1)}, u32[]{:S(2)}, u32[]{:S(2)}) collective-permute-start(bf16[160,256]{1,0:T(8,128)(2,1)S(1)} %get-tuple-element.41), channel_id=1, source_target_pairs={{0,1},{1,0},{64,65},{65,64},{128,129},{129,128},{192,193},{193,192... | collective-permute-start | bytes 245768 | tf_op jit(solution)/shard_map/ppermute | solution.py:136
  41.7 2.7 %collective-permute-start.4 = (bf16[160,256]{1,0:T(8,128)(2,1)S(1)}, bf16[160,256]{1,0:T(8,128)(2,1)S(1)}, u32[]{:S(2)}, u32[]{:S(2)}) collective-permute-start(bf16[160,256]{1,0:T(8,128)(2,1)S(1)} %get-tuple-element.42), channel_id=1, source_target_pairs={{0,65},{1,64},{64,129},{65,128},{128,193},{129,192},{192,0},{193,1... | collective-permute-start | bytes 245768 | tf_op jit(solution)/shard_map/ppermute | solution.py:136
  44.4 1.6 %collective-permute-done.1.refs_2_ = bf16[160,256]{1,0:T(8,128)(2,1)S(1)} collective-permute-done((bf16[160,256]{1,0:T(8,128)(2,1)S(1)}, bf16[160,256]{1,0:T(8,128)(2,1)S(1)}, u32[]{:S(2)}, u32[]{:S(2)}) %collective-permute-start.1) | collective-permute-done | bytes 81952 | tf_op jit(solution)/shard_map/ppermute | solution.py:136
  46.1 0.0 collective-permute-start.5
  46.1 2.6 %collective-permute-done.2.refs_3_ = bf16[160,256]{1,0:T(8,128)(2,1)S(1)} collective-permute-done((bf16[160,256]{1,0:T(8,128)(2,1)S(1)}, bf16[160,256]{1,0:T(8,128)(2,1)S(1)}, u32[]{:S(2)}, u32[]{:S(2)}) %collective-permute-start.2) | collective-permute-done | bytes 81952 | tf_op jit(solution)/shard_map/ppermute | solution.py:136
  48.7 0.0 collective-permute-start.6
  48.7 2.4 %collective-permute-done.3.refs_4_ = bf16[160,256]{1,0:T(8,128)(2,1)S(1)} collective-permute-done((bf16[160,256]{1,0:T(8,128)(2,1)S(1)}, bf16[160,256]{1,0:T(8,128)(2,1)S(1)}, u32[]{:S(2)}, u32[]{:S(2)}) %collective-permute-start.3) | collective-permute-done | bytes 81952 | tf_op jit(solution)/shard_map/ppermute | solution.py:136
  51.1 0.4 collective-permute-done.4.refs_5_
  51.5 4.6 %collective-permute-done.5.refs_6_ = bf16[160,256]{1,0:T(8,128)(2,1)S(1)} collective-permute-done((bf16[160,256]{1,0:T(8,128)(2,1)S(1)}, bf16[160,256]{1,0:T(8,128)(2,1)S(1)}, u32[]{:S(2)}, u32[]{:S(2)}) %collective-permute-start.5) | collective-permute-done | bytes 81952 | tf_op jit(solution)/shard_map/ppermute | solution.py:136
  56.1 1.0 collective-permute-done.6.refs_7_
  57.1 1.2 shard_map.48
  58.3 28.4 %all_to_all.10.x_ref = bf16[16,40,1280]{2,1,0:T(8,128)(2,1)S(1)} all-to-all(bf16[16,40,1280]{2,1,0:T(8,128)(2,1)S(1)} %bitcast.4), channel_id=1, replica_groups=mesh['z'=4,'c'=2,'x'=4,'y'=4,'w'=2] {'x','y'}, dimensions={0} | all-to-all | bytes 3276800 | tf_op jit(solution)/shard_map/all_to_all | solution.py:176
  86.7 1.5 %shard_map.49 = bf16[16,40,1280]{2,1,0:T(8,128)(2,1)} custom-call(bf16[16,40,1280]{2,1,0:T(8,128)(2,1)S(1)} %all_to_all.10.x_ref), custom_call_target="tpu_custom_call" | custom-call | bytes 3276800 | tf_op jit(solution)/shard_map/pallas_call | solution.py:121
  88.3 5.7 %all-to-all-start.1 = ((bf16[16,40,1280]{2,1,0:T(8,128)(2,1)}), bf16[16,40,1280]{2,1,0:T(8,128)(2,1)S(1)}, u32[]{:S(2)}, u32[]{:S(2)}) async-start(bf16[16,40,1280]{2,1,0:T(8,128)(2,1)} %shard_map.49), calls=%async_computation.1 | async-start | bytes 3276800 | tf_op jit(solution)/shard_map/all_to_all | solution.py:178
  93.9 2.0 %collective-permute-start.15 = (bf16[160,256]{1,0:T(8,128)(2,1)S(1)}, bf16[160,256]{1,0:T(8,128)(2,1)S(1)}, u32[]{:S(2)}, u32[]{:S(2)}) collective-permute-start(bf16[160,256]{1,0:T(8,128)(2,1)S(1)} %get-tuple-element.54), channel_id=1, source_target_pairs={{0,64},{1,65},{64,128},{65,129},{128,192},{129,193},{192,1},{193,0... | collective-permute-start | bytes 245768 | tf_op jit(solution)/shard_map/ppermute | solution.py:136
  95.9 2.6 %collective-permute-start.16 = (bf16[160,256]{1,0:T(8,128)(2,1)S(1)}, bf16[160,256]{1,0:T(8,128)(2,1)S(1)}, u32[]{:S(2)}, u32[]{:S(2)}) collective-permute-start(bf16[160,256]{1,0:T(8,128)(2,1)S(1)} %get-tuple-element.55), channel_id=1, source_target_pairs={{0,128},{1,129},{64,192},{65,193},{128,1},{129,0},{192,65},{193,64... | collective-permute-start | bytes 245768 | tf_op jit(solution)/shard_map/ppermute | solution.py:136
  98.5 1.5 collective-permute-start.17
  100.0 2.5 %collective-permute-start.18 = (bf16[160,256]{1,0:T(8,128)(2,1)S(1)}, bf16[160,256]{1,0:T(8,128)(2,1)S(1)}, u32[]{:S(2)}, u32[]{:S(2)}) collective-permute-start(bf16[160,256]{1,0:T(8,128)(2,1)S(1)} %get-tuple-element.57), channel_id=1, source_target_pairs={{0,1},{1,0},{64,65},{65,64},{128,129},{129,128},{192,193},{193,192... | collective-permute-start | bytes 245768 | tf_op jit(solution)/shard_map/ppermute | solution.py:136
  102.5 3.6 %collective-permute-start.19 = (bf16[160,256]{1,0:T(8,128)(2,1)S(1)}, bf16[160,256]{1,0:T(8,128)(2,1)S(1)}, u32[]{:S(2)}, u32[]{:S(2)}) collective-permute-start(bf16[160,256]{1,0:T(8,128)(2,1)S(1)} %get-tuple-element.58), channel_id=1, source_target_pairs={{0,65},{1,64},{64,129},{65,128},{128,193},{129,192},{192,0},{193,1... | collective-permute-start | bytes 245768 | tf_op jit(solution)/shard_map/ppermute | solution.py:136
  106.1 0.0 collective-permute-done.15.refs_1_
  106.1 3.0 %collective-permute-start.20 = (bf16[160,256]{1,0:T(8,128)(2,1)S(1)}, bf16[160,256]{1,0:T(8,128)(2,1)S(1)}, u32[]{:S(2)}, u32[]{:S(2)}) collective-permute-start(bf16[160,256]{1,0:T(8,128)(2,1)S(1)} %get-tuple-element.59), channel_id=1, source_target_pairs={{0,129},{1,128},{64,193},{65,192},{128,0},{129,1},{192,64},{193,65... | collective-permute-start | bytes 245768 | tf_op jit(solution)/shard_map/ppermute | solution.py:136
  109.1 2.0 %collective-permute-done.18.refs_4_ = bf16[160,256]{1,0:T(8,128)(2,1)S(1)} collective-permute-done((bf16[160,256]{1,0:T(8,128)(2,1)S(1)}, bf16[160,256]{1,0:T(8,128)(2,1)S(1)}, u32[]{:S(2)}, u32[]{:S(2)}) %collective-permute-start.18) | collective-permute-done | bytes 81952 | tf_op jit(solution)/shard_map/ppermute | solution.py:136
  111.1 5.0 %collective-permute-done.19.refs_5_ = bf16[160,256]{1,0:T(8,128)(2,1)S(1)} collective-permute-done((bf16[160,256]{1,0:T(8,128)(2,1)S(1)}, bf16[160,256]{1,0:T(8,128)(2,1)S(1)}, u32[]{:S(2)}, u32[]{:S(2)}) %collective-permute-start.19) | collective-permute-done | bytes 81952 | tf_op jit(solution)/shard_map/ppermute | solution.py:136
  116.0 1.6 %collective-permute-done.20.refs_6_ = bf16[160,256]{1,0:T(8,128)(2,1)S(1)} collective-permute-done((bf16[160,256]{1,0:T(8,128)(2,1)S(1)}, bf16[160,256]{1,0:T(8,128)(2,1)S(1)}, u32[]{:S(2)}, u32[]{:S(2)}) %collective-permute-start.20) | collective-permute-done | bytes 81952 | tf_op jit(solution)/shard_map/ppermute | solution.py:136
  117.7 0.1 shard_map.50.v_ref
  117.8 0.0 copy-start
  117.8 0.1 collective-permute-start.22
  117.9 2.1 %collective-permute-done.22.v_far = bf16[2,4,160,256]{3,2,1,0:T(8,128)(2,1)S(1)} collective-permute-done((bf16[2,4,160,256]{3,2,1,0:T(8,128)(2,1)S(1)}, bf16[2,4,160,256]{3,2,1,0:T(8,128)(2,1)S(1)}, u32[]{:S(2)}, u32[]{:S(2)}) %collective-permute-start.22) | collective-permute-done | bytes 655392 | tf_op jit(solution)/shard_map/ppermute | solution.py:141
  120.0 0.9 copy-done.3
  120.8 1.1 copy-done.4
  121.9 1.2 shard_map.51
  123.2 1.5 %collective-permute-start.23 = (bf16[160,256]{1,0:T(8,128)(2,1)S(1)}, bf16[160,256]{1,0:T(8,128)(2,1)S(1)}, u32[]{:S(2)}, u32[]{:S(2)}) collective-permute-start(bf16[160,256]{1,0:T(8,128)(2,1)S(1)} %get-tuple-element.62), channel_id=1, source_target_pairs={{0,64},{1,65},{64,128},{65,129},{128,192},{129,193},{192,1},{193,0... | collective-permute-start | bytes 245768 | tf_op jit(solution)/shard_map/ppermute | solution.py:136
  124.7 1.2 collective-permute-start.24
  125.9 2.7 %collective-permute-start.25 = (bf16[160,256]{1,0:T(8,128)(2,1)S(1)}, bf16[160,256]{1,0:T(8,128)(2,1)S(1)}, u32[]{:S(2)}, u32[]{:S(2)}) collective-permute-start(bf16[160,256]{1,0:T(8,128)(2,1)S(1)} %get-tuple-element.64), channel_id=1, source_target_pairs={{0,192},{1,193},{64,1},{65,0},{128,65},{129,64},{192,129},{193,128... | collective-permute-start | bytes 245768 | tf_op jit(solution)/shard_map/ppermute | solution.py:136
  128.6 2.5 %collective-permute-start.26 = (bf16[160,256]{1,0:T(8,128)(2,1)S(1)}, bf16[160,256]{1,0:T(8,128)(2,1)S(1)}, u32[]{:S(2)}, u32[]{:S(2)}) collective-permute-start(bf16[160,256]{1,0:T(8,128)(2,1)S(1)} %get-tuple-element.65), channel_id=1, source_target_pairs={{0,1},{1,0},{64,65},{65,64},{128,129},{129,128},{192,193},{193,192... | collective-permute-start | bytes 245768 | tf_op jit(solution)/shard_map/ppermute | solution.py:136
  131.2 3.4 %collective-permute-start.27 = (bf16[160,256]{1,0:T(8,128)(2,1)S(1)}, bf16[160,256]{1,0:T(8,128)(2,1)S(1)}, u32[]{:S(2)}, u32[]{:S(2)}) collective-permute-start(bf16[160,256]{1,0:T(8,128)(2,1)S(1)} %get-tuple-element.66), channel_id=1, source_target_pairs={{0,65},{1,64},{64,129},{65,128},{128,193},{129,192},{192,0},{193,1... | collective-permute-start | bytes 245768 | tf_op jit(solution)/shard_map/ppermute | solution.py:136
  134.5 1.8 %collective-permute-start.28 = (bf16[160,256]{1,0:T(8,128)(2,1)S(1)}, bf16[160,256]{1,0:T(8,128)(2,1)S(1)}, u32[]{:S(2)}, u32[]{:S(2)}) collective-permute-start(bf16[160,256]{1,0:T(8,128)(2,1)S(1)} %get-tuple-element.67), channel_id=1, source_target_pairs={{0,129},{1,128},{64,193},{65,192},{128,0},{129,1},{192,64},{193,65... | collective-permute-start | bytes 245768 | tf_op jit(solution)/shard_map/ppermute | solution.py:136
  136.3 0.6 collective-permute-start.29
  136.9 1.5 %collective-permute-done.25.refs_3_ = bf16[160,256]{1,0:T(8,128)(2,1)S(1)} collective-permute-done((bf16[160,256]{1,0:T(8,128)(2,1)S(1)}, bf16[160,256]{1,0:T(8,128)(2,1)S(1)}, u32[]{:S(2)}, u32[]{:S(2)}) %collective-permute-start.25) | collective-permute-done | bytes 81952 | tf_op jit(solution)/shard_map/ppermute | solution.py:136
  138.4 2.6 %collective-permute-done.26.refs_4_ = bf16[160,256]{1,0:T(8,128)(2,1)S(1)} collective-permute-done((bf16[160,256]{1,0:T(8,128)(2,1)S(1)}, bf16[160,256]{1,0:T(8,128)(2,1)S(1)}, u32[]{:S(2)}, u32[]{:S(2)}) %collective-permute-start.26) | collective-permute-done | bytes 81952 | tf_op jit(solution)/shard_map/ppermute | solution.py:136
  141.0 1.5 %collective-permute-done.27.refs_5_ = bf16[160,256]{1,0:T(8,128)(2,1)S(1)} collective-permute-done((bf16[160,256]{1,0:T(8,128)(2,1)S(1)}, bf16[160,256]{1,0:T(8,128)(2,1)S(1)}, u32[]{:S(2)}, u32[]{:S(2)}) %collective-permute-start.27) | collective-permute-done | bytes 81952 | tf_op jit(solution)/shard_map/ppermute | solution.py:136
  142.5 3.7 %collective-permute-done.28.refs_6_ = bf16[160,256]{1,0:T(8,128)(2,1)S(1)} collective-permute-done((bf16[160,256]{1,0:T(8,128)(2,1)S(1)}, bf16[160,256]{1,0:T(8,128)(2,1)S(1)}, u32[]{:S(2)}, u32[]{:S(2)}) %collective-permute-start.28) | collective-permute-done | bytes 81952 | tf_op jit(solution)/shard_map/ppermute | solution.py:136
  146.2 0.4 collective-permute-done.29.refs_7_
  146.7 2.0 %shard_map.52 = f32[4,160,768]{2,1,0:T(8,128)} custom-call(s32[1]{0:T(128)} %bitcast.pos_ref, bf16[512,768]{1,0:T(8,128)(2,1)S(1)} %copy-done, bf16[160,256]{1,0:T(8,128)(2,1)S(1)} %get-tuple-element.61.refs_0_, bf16[160,256]{1,0:T(8,128)(2,1)S(1)} %collective-permute-done.23.refs_1_, bf16[160,256]{1,0:T(8,128)(2,1)S(1)} %collective-permute-done.24.refs_2_, ...), custom_call_target="tpu_custom_call" | custom-call | flops 503316480 | bytes 2883592 | tf_op jit(solution)/shard_map/pallas_call | solution.py:121
  (17 shorter events, 0.0 us)
Async XLA Ops:
  0.7 1.7 %copy-start.1 = (bf16[768,3,512]{2,0,1:T(8,128)(2,1)S(1)}, bf16[768,3,512]{2,0,1:T(8,128)(2,1)}, u32[]{:S(2)}) copy-start(bf16[768,3,512]{2,0,1:T(8,128)(2,1)} %param.6) | copy-start | bytes 7077892
  2.4 1.2 copy-start.2
  6.0 14.8 %collective-permute-start.7 = (bf16[160,256]{1,0:T(8,128)(2,1)S(1)}, bf16[160,256]{1,0:T(8,128)(2,1)S(1)}, u32[]{:S(2)}, u32[]{:S(2)}) collective-permute-start(bf16[160,256]{1,0:T(8,128)(2,1)S(1)} %get-tuple-element.46), channel_id=1, source_target_pairs={{0,64},{1,65},{64,128},{65,129},{128,192},{129,193},{192,1},{193,0... | collective-permute-start | bytes 245768 | tf_op jit(solution)/shard_map/ppermute | solution.py:136
  8.0 15.5 %collective-permute-start.8 = (bf16[160,256]{1,0:T(8,128)(2,1)S(1)}, bf16[160,256]{1,0:T(8,128)(2,1)S(1)}, u32[]{:S(2)}, u32[]{:S(2)}) collective-permute-start(bf16[160,256]{1,0:T(8,128)(2,1)S(1)} %get-tuple-element.47), channel_id=1, source_target_pairs={{0,128},{1,129},{64,192},{65,193},{128,1},{129,0},{192,65},{193,64... | collective-permute-start | bytes 245768 | tf_op jit(solution)/shard_map/ppermute | solution.py:136
  11.3 14.9 %collective-permute-start.9 = (bf16[160,256]{1,0:T(8,128)(2,1)S(1)}, bf16[160,256]{1,0:T(8,128)(2,1)S(1)}, u32[]{:S(2)}, u32[]{:S(2)}) collective-permute-start(bf16[160,256]{1,0:T(8,128)(2,1)S(1)} %get-tuple-element.48), channel_id=1, source_target_pairs={{0,192},{1,193},{64,1},{65,0},{128,65},{129,64},{192,129},{193,128... | collective-permute-start | bytes 245768 | tf_op jit(solution)/shard_map/ppermute | solution.py:136
  15.3 10.9 %collective-permute-start.10 = (bf16[160,256]{1,0:T(8,128)(2,1)S(1)}, bf16[160,256]{1,0:T(8,128)(2,1)S(1)}, u32[]{:S(2)}, u32[]{:S(2)}) collective-permute-start(bf16[160,256]{1,0:T(8,128)(2,1)S(1)} %get-tuple-element.49), channel_id=1, source_target_pairs={{0,1},{1,0},{64,65},{65,64},{128,129},{129,128},{192,193},{193,192... | collective-permute-start | bytes 245768 | tf_op jit(solution)/shard_map/ppermute | solution.py:136
  15.9 16.0 %collective-permute-start.11 = (bf16[160,256]{1,0:T(8,128)(2,1)S(1)}, bf16[160,256]{1,0:T(8,128)(2,1)S(1)}, u32[]{:S(2)}, u32[]{:S(2)}) collective-permute-start(bf16[160,256]{1,0:T(8,128)(2,1)S(1)} %get-tuple-element.50), channel_id=1, source_target_pairs={{0,65},{1,64},{64,129},{65,128},{128,193},{129,192},{192,0},{193,1... | collective-permute-start | bytes 245768 | tf_op jit(solution)/shard_map/ppermute | solution.py:136
  20.8 11.1 %collective-permute-start.12 = (bf16[160,256]{1,0:T(8,128)(2,1)S(1)}, bf16[160,256]{1,0:T(8,128)(2,1)S(1)}, u32[]{:S(2)}, u32[]{:S(2)}) collective-permute-start(bf16[160,256]{1,0:T(8,128)(2,1)S(1)} %get-tuple-element.51), channel_id=1, source_target_pairs={{0,129},{1,128},{64,193},{65,192},{128,0},{129,1},{192,64},{193,65... | collective-permute-start | bytes 245768 | tf_op jit(solution)/shard_map/ppermute | solution.py:136
  23.5 9.2 %collective-permute-start.13 = (bf16[160,256]{1,0:T(8,128)(2,1)S(1)}, bf16[160,256]{1,0:T(8,128)(2,1)S(1)}, u32[]{:S(2)}, u32[]{:S(2)}) collective-permute-start(bf16[160,256]{1,0:T(8,128)(2,1)S(1)} %get-tuple-element.52), channel_id=1, source_target_pairs={{0,193},{1,192},{64,0},{65,1},{128,64},{129,65},{192,128},{193,129... | collective-permute-start | bytes 245768 | tf_op jit(solution)/shard_map/ppermute | solution.py:136
  32.7 24.4 %collective-permute-start.14 = (bf16[2,4,160,256]{3,2,1,0:T(8,128)(2,1)S(1)}, bf16[2,4,160,256]{3,2,1,0:T(8,128)(2,1)S(1)}, u32[]{:S(2)}, u32[]{:S(2)}) collective-permute-start(bf16[2,4,160,256]{3,2,1,0:T(8,128)(2,1)S(1)} %shard_map.47.refs_8_), channel_id=1, source_target_pairs={{0,32},{32,0},{1,33},{33,1},{2,34},{34,2},{3,35},{35,3},{4,36},{36... | collective-permute-start | bytes 1966088 | tf_op jit(solution)/shard_map/ppermute | solution.py:141
  32.8 8.9 %collective-permute-start = (bf16[160,256]{1,0:T(8,128)(2,1)S(1)}, bf16[160,256]{1,0:T(8,128)(2,1)S(1)}, u32[]{:S(2)}, u32[]{:S(2)}) collective-permute-start(bf16[160,256]{1,0:T(8,128)(2,1)S(1)} %get-tuple-element.38), channel_id=1, source_target_pairs={{0,64},{1,65},{64,128},{65,129},{128,192},{129,193},{192,1},{193,0... | collective-permute-start | bytes 245768 | tf_op jit(solution)/shard_map/ppermute | solution.py:136
  35.2 10.9 %collective-permute-start.1 = (bf16[160,256]{1,0:T(8,128)(2,1)S(1)}, bf16[160,256]{1,0:T(8,128)(2,1)S(1)}, u32[]{:S(2)}, u32[]{:S(2)}) collective-permute-start(bf16[160,256]{1,0:T(8,128)(2,1)S(1)} %get-tuple-element.39), channel_id=1, source_target_pairs={{0,128},{1,129},{64,192},{65,193},{128,1},{129,0},{192,65},{193,64... | collective-permute-start | bytes 245768 | tf_op jit(solution)/shard_map/ppermute | solution.py:136
  36.4 12.3 %collective-permute-start.2 = (bf16[160,256]{1,0:T(8,128)(2,1)S(1)}, bf16[160,256]{1,0:T(8,128)(2,1)S(1)}, u32[]{:S(2)}, u32[]{:S(2)}) collective-permute-start(bf16[160,256]{1,0:T(8,128)(2,1)S(1)} %get-tuple-element.40), channel_id=1, source_target_pairs={{0,192},{1,193},{64,1},{65,0},{128,65},{129,64},{192,129},{193,128... | collective-permute-start | bytes 245768 | tf_op jit(solution)/shard_map/ppermute | solution.py:136
  38.3 12.7 %collective-permute-start.3 = (bf16[160,256]{1,0:T(8,128)(2,1)S(1)}, bf16[160,256]{1,0:T(8,128)(2,1)S(1)}, u32[]{:S(2)}, u32[]{:S(2)}) collective-permute-start(bf16[160,256]{1,0:T(8,128)(2,1)S(1)} %get-tuple-element.41), channel_id=1, source_target_pairs={{0,1},{1,0},{64,65},{65,64},{128,129},{129,128},{192,193},{193,192... | collective-permute-start | bytes 245768 | tf_op jit(solution)/shard_map/ppermute | solution.py:136
  41.7 9.7 %collective-permute-start.4 = (bf16[160,256]{1,0:T(8,128)(2,1)S(1)}, bf16[160,256]{1,0:T(8,128)(2,1)S(1)}, u32[]{:S(2)}, u32[]{:S(2)}) collective-permute-start(bf16[160,256]{1,0:T(8,128)(2,1)S(1)} %get-tuple-element.42), channel_id=1, source_target_pairs={{0,65},{1,64},{64,129},{65,128},{128,193},{129,192},{192,0},{193,1... | collective-permute-start | bytes 245768 | tf_op jit(solution)/shard_map/ppermute | solution.py:136
  46.1 10.0 %collective-permute-start.5 = (bf16[160,256]{1,0:T(8,128)(2,1)S(1)}, bf16[160,256]{1,0:T(8,128)(2,1)S(1)}, u32[]{:S(2)}, u32[]{:S(2)}) collective-permute-start(bf16[160,256]{1,0:T(8,128)(2,1)S(1)} %get-tuple-element.43), channel_id=1, source_target_pairs={{0,129},{1,128},{64,193},{65,192},{128,0},{129,1},{192,64},{193,65... | collective-permute-start | bytes 245768 | tf_op jit(solution)/shard_map/ppermute | solution.py:136
  48.7 8.4 %collective-permute-start.6 = (bf16[160,256]{1,0:T(8,128)(2,1)S(1)}, bf16[160,256]{1,0:T(8,128)(2,1)S(1)}, u32[]{:S(2)}, u32[]{:S(2)}) collective-permute-start(bf16[160,256]{1,0:T(8,128)(2,1)S(1)} %get-tuple-element.44), channel_id=1, source_target_pairs={{0,193},{1,192},{64,0},{65,1},{128,64},{129,65},{192,128},{193,129... | collective-permute-start | bytes 245768 | tf_op jit(solution)/shard_map/ppermute | solution.py:136
  88.3 32.6 %all-to-all-start.1 = ((bf16[16,40,1280]{2,1,0:T(8,128)(2,1)}), bf16[16,40,1280]{2,1,0:T(8,128)(2,1)S(1)}, u32[]{:S(2)}, u32[]{:S(2)}) async-start(bf16[16,40,1280]{2,1,0:T(8,128)(2,1)} %shard_map.49), calls=%async_computation.1 | async-start | bytes 3276800 | tf_op jit(solution)/shard_map/all_to_all | solution.py:178
  93.9 12.2 %collective-permute-start.15 = (bf16[160,256]{1,0:T(8,128)(2,1)S(1)}, bf16[160,256]{1,0:T(8,128)(2,1)S(1)}, u32[]{:S(2)}, u32[]{:S(2)}) collective-permute-start(bf16[160,256]{1,0:T(8,128)(2,1)S(1)} %get-tuple-element.54), channel_id=1, source_target_pairs={{0,64},{1,65},{64,128},{65,129},{128,192},{129,193},{192,1},{193,0... | collective-permute-start | bytes 245768 | tf_op jit(solution)/shard_map/ppermute | solution.py:136
  95.9 13.1 %collective-permute-start.16 = (bf16[160,256]{1,0:T(8,128)(2,1)S(1)}, bf16[160,256]{1,0:T(8,128)(2,1)S(1)}, u32[]{:S(2)}, u32[]{:S(2)}) collective-permute-start(bf16[160,256]{1,0:T(8,128)(2,1)S(1)} %get-tuple-element.55), channel_id=1, source_target_pairs={{0,128},{1,129},{64,192},{65,193},{128,1},{129,0},{192,65},{193,64... | collective-permute-start | bytes 245768 | tf_op jit(solution)/shard_map/ppermute | solution.py:136
  98.5 10.6 %collective-permute-start.17 = (bf16[160,256]{1,0:T(8,128)(2,1)S(1)}, bf16[160,256]{1,0:T(8,128)(2,1)S(1)}, u32[]{:S(2)}, u32[]{:S(2)}) collective-permute-start(bf16[160,256]{1,0:T(8,128)(2,1)S(1)} %get-tuple-element.56), channel_id=1, source_target_pairs={{0,192},{1,193},{64,1},{65,0},{128,65},{129,64},{192,129},{193,128... | collective-permute-start | bytes 245768 | tf_op jit(solution)/shard_map/ppermute | solution.py:136
  100.0 11.1 %collective-permute-start.18 = (bf16[160,256]{1,0:T(8,128)(2,1)S(1)}, bf16[160,256]{1,0:T(8,128)(2,1)S(1)}, u32[]{:S(2)}, u32[]{:S(2)}) collective-permute-start(bf16[160,256]{1,0:T(8,128)(2,1)S(1)} %get-tuple-element.57), channel_id=1, source_target_pairs={{0,1},{1,0},{64,65},{65,64},{128,129},{129,128},{192,193},{193,192... | collective-permute-start | bytes 245768 | tf_op jit(solution)/shard_map/ppermute | solution.py:136
  102.5 13.5 %collective-permute-start.19 = (bf16[160,256]{1,0:T(8,128)(2,1)S(1)}, bf16[160,256]{1,0:T(8,128)(2,1)S(1)}, u32[]{:S(2)}, u32[]{:S(2)}) collective-permute-start(bf16[160,256]{1,0:T(8,128)(2,1)S(1)} %get-tuple-element.58), channel_id=1, source_target_pairs={{0,65},{1,64},{64,129},{65,128},{128,193},{129,192},{192,0},{193,1... | collective-permute-start | bytes 245768 | tf_op jit(solution)/shard_map/ppermute | solution.py:136
  106.1 11.6 %collective-permute-start.20 = (bf16[160,256]{1,0:T(8,128)(2,1)S(1)}, bf16[160,256]{1,0:T(8,128)(2,1)S(1)}, u32[]{:S(2)}, u32[]{:S(2)}) collective-permute-start(bf16[160,256]{1,0:T(8,128)(2,1)S(1)} %get-tuple-element.59), channel_id=1, source_target_pairs={{0,129},{1,128},{64,193},{65,192},{128,0},{129,1},{192,64},{193,65... | collective-permute-start | bytes 245768 | tf_op jit(solution)/shard_map/ppermute | solution.py:136
  109.1 8.6 %collective-permute-start.21 = (bf16[160,256]{1,0:T(8,128)(2,1)S(1)}, bf16[160,256]{1,0:T(8,128)(2,1)S(1)}, u32[]{:S(2)}, u32[]{:S(2)}) collective-permute-start(bf16[160,256]{1,0:T(8,128)(2,1)S(1)} %get-tuple-element.60), channel_id=1, source_target_pairs={{0,193},{1,192},{64,0},{65,1},{128,64},{129,65},{192,128},{193,129... | collective-permute-start | bytes 245768 | tf_op jit(solution)/shard_map/ppermute | solution.py:136
  117.8 28.9 %copy-start = (bf16[512,768]{1,0:T(8,128)(2,1)S(1)}, bf16[512,768]{1,0:T(8,128)(2,1)}, u32[]{:S(2)}) copy-start(bf16[512,768]{1,0:T(8,128)(2,1)} %w_ref.1) | copy-start | bytes 2359300
  117.8 2.2 %collective-permute-start.22 = (bf16[2,4,160,256]{3,2,1,0:T(8,128)(2,1)S(1)}, bf16[2,4,160,256]{3,2,1,0:T(8,128)(2,1)S(1)}, u32[]{:S(2)}, u32[]{:S(2)}) collective-permute-start(bf16[2,4,160,256]{3,2,1,0:T(8,128)(2,1)S(1)} %shard_map.50.v_ref), channel_id=1, source_target_pairs={{0,32},{32,0},{1,33},{33,1},{2,34},{34,2},{3,35},{35,3},{4,36},{36... | collective-permute-start | bytes 1966088 | tf_op jit(solution)/shard_map/ppermute | solution.py:141
  120.0 0.9 copy-start.3
  120.8 1.1 copy-start.4
  123.2 11.4 %collective-permute-start.23 = (bf16[160,256]{1,0:T(8,128)(2,1)S(1)}, bf16[160,256]{1,0:T(8,128)(2,1)S(1)}, u32[]{:S(2)}, u32[]{:S(2)}) collective-permute-start(bf16[160,256]{1,0:T(8,128)(2,1)S(1)} %get-tuple-element.62), channel_id=1, source_target_pairs={{0,64},{1,65},{64,128},{65,129},{128,192},{129,193},{192,1},{193,0... | collective-permute-start | bytes 245768 | tf_op jit(solution)/shard_map/ppermute | solution.py:136
  124.7 11.6 %collective-permute-start.24 = (bf16[160,256]{1,0:T(8,128)(2,1)S(1)}, bf16[160,256]{1,0:T(8,128)(2,1)S(1)}, u32[]{:S(2)}, u32[]{:S(2)}) collective-permute-start(bf16[160,256]{1,0:T(8,128)(2,1)S(1)} %get-tuple-element.63), channel_id=1, source_target_pairs={{0,128},{1,129},{64,192},{65,193},{128,1},{129,0},{192,65},{193,64... | collective-permute-start | bytes 245768 | tf_op jit(solution)/shard_map/ppermute | solution.py:136
  125.9 12.5 %collective-permute-start.25 = (bf16[160,256]{1,0:T(8,128)(2,1)S(1)}, bf16[160,256]{1,0:T(8,128)(2,1)S(1)}, u32[]{:S(2)}, u32[]{:S(2)}) collective-permute-start(bf16[160,256]{1,0:T(8,128)(2,1)S(1)} %get-tuple-element.64), channel_id=1, source_target_pairs={{0,192},{1,193},{64,1},{65,0},{128,65},{129,64},{192,129},{193,128... | collective-permute-start | bytes 245768 | tf_op jit(solution)/shard_map/ppermute | solution.py:136
  128.6 12.3 %collective-permute-start.26 = (bf16[160,256]{1,0:T(8,128)(2,1)S(1)}, bf16[160,256]{1,0:T(8,128)(2,1)S(1)}, u32[]{:S(2)}, u32[]{:S(2)}) collective-permute-start(bf16[160,256]{1,0:T(8,128)(2,1)S(1)} %get-tuple-element.65), channel_id=1, source_target_pairs={{0,1},{1,0},{64,65},{65,64},{128,129},{129,128},{192,193},{193,192... | collective-permute-start | bytes 245768 | tf_op jit(solution)/shard_map/ppermute | solution.py:136
  131.2 11.3 %collective-permute-start.27 = (bf16[160,256]{1,0:T(8,128)(2,1)S(1)}, bf16[160,256]{1,0:T(8,128)(2,1)S(1)}, u32[]{:S(2)}, u32[]{:S(2)}) collective-permute-start(bf16[160,256]{1,0:T(8,128)(2,1)S(1)} %get-tuple-element.66), channel_id=1, source_target_pairs={{0,65},{1,64},{64,129},{65,128},{128,193},{129,192},{192,0},{193,1... | collective-permute-start | bytes 245768 | tf_op jit(solution)/shard_map/ppermute | solution.py:136
  134.5 11.7 %collective-permute-start.28 = (bf16[160,256]{1,0:T(8,128)(2,1)S(1)}, bf16[160,256]{1,0:T(8,128)(2,1)S(1)}, u32[]{:S(2)}, u32[]{:S(2)}) collective-permute-start(bf16[160,256]{1,0:T(8,128)(2,1)S(1)} %get-tuple-element.67), channel_id=1, source_target_pairs={{0,129},{1,128},{64,193},{65,192},{128,0},{129,1},{192,64},{193,65... | collective-permute-start | bytes 245768 | tf_op jit(solution)/shard_map/ppermute | solution.py:136
  136.3 10.3 %collective-permute-start.29 = (bf16[160,256]{1,0:T(8,128)(2,1)S(1)}, bf16[160,256]{1,0:T(8,128)(2,1)S(1)}, u32[]{:S(2)}, u32[]{:S(2)}) collective-permute-start(bf16[160,256]{1,0:T(8,128)(2,1)S(1)} %get-tuple-element.68), channel_id=1, source_target_pairs={{0,193},{1,192},{64,0},{65,1},{128,64},{129,65},{192,128},{193,129... | collective-permute-start | bytes 245768 | tf_op jit(solution)/shard_map/ppermute | solution.py:136

commit v2 on v1

--- a/solution.py
+++ b/solution.py
@@ -34,41 +34,46 @@
 
 
 def project_kernel(pos_ref, x_ref, gain_ref, w_ref, *refs):
-    outs, (normed, mine) = refs[:-2], refs[-2:]
+    both, values, (normed, mine) = refs[:RING], refs[RING:-2], refs[-2:]
     seqs, length, width = x_ref.shape
     inner = w_ref.shape[2]
     heads = inner // HEAD_DIM
+    gain = gain_ref[...].reshape(1, width)
     for r in range(seqs):
         x = x_ref[r].astype(F32)
         mean = jnp.mean(x, axis=-1, keepdims=True)
         off = x - mean
         var = jnp.mean(off * off, axis=-1, keepdims=True)
-        normed[r * length : (r + 1) * length] = (off / jnp.sqrt(var + 1e-05) * gain_ref[...]).astype(BF)
+        normed[r * length : (r + 1) * length] = (off / jnp.sqrt(var + 1e-05) * gain).astype(BF)
     pos = pos_ref[0]
-    for c in range(3):
+    for c in (1, 0, 2):
         y = jnp.dot(normed[...], w_ref[c], preferred_element_type=F32)
         for h in range(heads):
             mine[h] = jnp.concatenate(
                 [y[r * length : (r + 1) * length, h * HEAD_DIM : (h + 1) * HEAD_DIM] for r in range(seqs)], axis=1
             ).astype(BF)
         for s in range(RING):
-            outs[c * RING + s][...] = mine[head_at(pos + s)]
-
-
-def gather_kernel(pos_ref, *refs):
-    parts, out = refs[:-1], refs[-1]
-    pos = pos_ref[0]
+            block = mine[head_at(pos + s)]
+            if c == 2:
+                values[s][...] = block
+            else:
+                both[s][(1 - c) * length : (2 - c) * length] = block
+
+
+def put_by_sender(pos, parts, first, out):
+    length = out.shape[2]
     for s in range(RING):
         src = lax.rem(pos + RING - s, RING)
-        out[lax.div(src, Z), lax.rem(src, Z)] = parts[s][...]
+        out[lax.div(src, Z), lax.rem(src, Z)] = parts[s][first : first + length]
+
+
+def keys_kernel(pos_ref, *refs):
+    put_by_sender(pos_ref[0], refs[:-1], 0, refs[-1])
 
 
 def logits_kernel(pos_ref, *refs):
-    q_parts, (k_ref, k_far, out_ref, q) = refs[:RING], refs[RING:]
-    pos = pos_ref[0]
-    for s in range(RING):
-        src = lax.rem(pos + RING - s, RING)
-        q[lax.div(src, Z), lax.rem(src, Z)] = q_parts[s][...]
+    parts, (k_ref, k_far, out_ref, q) = refs[:RING], refs[RING:]
+    put_by_sender(pos_ref[0], parts, q.shape[2], q)
     half = k_ref.shape[1] * k_ref.shape[2]
     for side, keys in enumerate((k_ref, k_far)):
         total = None
@@ -80,7 +85,9 @@
         out_ref[:, side * half : (side + 1) * half] = total.astype(BF)
 
 
-def probs_kernel(scale, x_ref, out_ref):
+def probs_kernel(scale, pos_ref, x_ref, *refs):
+    parts, (out_ref, values) = refs[:RING], refs[RING:]
+    put_by_sender(pos_ref[0], parts, 0, values)
     logits = x_ref[0].astype(F32)
     for i in range(1, x_ref.shape[0]):
         logits = logits + x_ref[i].astype(F32)
@@ -146,6 +153,7 @@
     inner = w_qkv.shape[2]
     lanes = seqs * HEAD_DIM
     pos = (lax.axis_index("w") * Z + lax.axis_index("z")).astype(jnp.int32).reshape(1)
+    pair = jax.ShapeDtypeStruct((2 * length, lanes), BF)
     block = jax.ShapeDtypeStruct((length, lanes), BF)
     whole = jax.ShapeDtypeStruct((W, Z, length, lanes), BF)
     half = Z * length
@@ -154,29 +162,30 @@
 
     outs = call(
         project_kernel,
-        [block] * (3 * RING),
-        [pos, tokens, ln_gain.reshape(1, width), jnp.transpose(w_qkv, (1, 0, 2))],
+        [pair] * RING + [block] * RING,
+        [pos, tokens, ln_gain, jnp.transpose(w_qkv, (1, 0, 2))],
         [pltpu.VMEM((seqs * length, width), BF), pltpu.VMEM((RING, length, lanes), BF)],
         flops=2 * seqs * length * width * 3 * inner,
     )
-    query, keys, values = outs[:RING], outs[RING : 2 * RING], outs[2 * RING :]
-    keys = along_ring(keys)
-    query = along_ring(query)
-    values = along_ring(values)
-    keys = call(gather_kernel, whole, [pos, *keys])
+    both = along_ring(outs[:RING])
+    values = along_ring(outs[RING:])
+    keys = call(keys_kernel, whole, [pos, *both])
     keys_far = other_core(keys)
     term = call(
         logits_kernel,
         jax.ShapeDtypeStruct((half, full), BF),
-        [pos, *query, keys, keys_far],
+        [pos, *both, keys, keys_far],
         [pltpu.VMEM(whole.shape, BF)],
         flops=2 * half * full * W * lanes,
     )
     chunk = (PLANE, half // PLANE, full)
     terms = lax.all_to_all(term.reshape(chunk), ("x", "y"), 0, 0, tiled=True)
-    probs = call(functools.partial(probs_kernel, scale), jax.ShapeDtypeStruct(chunk, BF), [terms])
+    probs, values = call(
+        functools.partial(probs_kernel, scale),
+        [jax.ShapeDtypeStruct(chunk, BF), whole],
+        [pos, terms, *values],
+    )
     probs = lax.all_to_all(probs, ("x", "y"), 0, 0, tiled=True).reshape(half, full)
-    values = call(gather_kernel, whole, [pos, *values])
     values_far = other_core(values)
     context = call(
         context_kernel,

time: 149 us -> 141 us (0.946)
  blocking collectives: 28.4 us -> 0 us
  waiting for transfers between devices: 41.3 us -> 60.1 us
    all_to_all x1 -> x0, blocking collectives: 28.4 us -> none  [shards(): terms = lax.all_to_all(term.reshape(chunk), ('x', 'y'), 0, 0, tiled=True)]
    all_to_all x1, waiting for transfers between devices: 0.01 us -> 17.7 us  [shards(): lax.all_to_all(probs, ('x', 'y'), 0, 0, tiled=True).reshape(half, full)]
    ppermute x28 -> x21, starting transfers between devices: 58.9 us -> 49.9 us  [along_ring(): got[s] = lax.ppermute(parts[s], ('z', 'w'), pairs)]
    all_to_all x0 -> x1, starting transfers between devices: none -> 7.43 us  [shards(): terms = lax.all_to_all(term.reshape(chunk), ('x', 'y'), 0, 0, tiled=True)]
    ppermute x2, waiting for transfers between devices: 2.09 us -> 4.17 us  [other_core(): return lax.ppermute(a, 'c', [(0, 1), (1, 0)])]
    all_to_all x1, starting transfers between devices: 5.69 us -> 7.23 us  [shards(): lax.all_to_all(probs, ('x', 'y'), 0, 0, tiled=True).reshape(half, full)]
    pallas_call x7 -> x6, Pallas kernels: 8.55 us -> 9.61 us  [call(): pl.pallas_call(kernel, out_shape=out_shape, in_specs=[SMEM if o.dtype ==...]
    ppermute x28 -> x21, waiting for transfers between devices: 39.2 us -> 38.3 us  [along_ring(): got[s] = lax.ppermute(parts[s], ('z', 'w'), pairs)]
  transfers between devices with their start and end apart: 31 -> 25, of which waited for: 18 -> 17; matrix products, arithmetic and copies ran while one was open for 0% -> 0% of each run, Pallas kernels for 0% -> 0%
where the time goes in v2:
time: 141 us; the launch traced here: 140 us
  starting transfers between devices  64.8 us (46%)
  waiting for transfers between devices  60.1 us (43%)
  Pallas kernels  9.61 us (7%)
  local copies, waits for them, and re-layouts  5.48 us (4%)
    ppermute x21, starting transfers between devices, along_ring(): got[s] = lax.ppermute(parts[s], ('z', 'w'), pairs)  49.9 us
    ppermute x21, waiting for transfers between devices, along_ring(): got[s] = lax.ppermute(parts[s], ('z', 'w'), pairs)  38.3 us
    all_to_all x1, waiting for transfers between devices, shards(): lax.all_to_all(probs, ('x', 'y'), 0, 0, tiled=True).reshape(half, full)  17.7 us
    pallas_call x6, Pallas kernels, call(): pl.pallas_call(kernel, out_shape=out_shape, in_specs=[SMEM if o.dtype ==...  9.61 us
    all_to_all x1, starting transfers between devices, shards(): terms = lax.all_to_all(term.reshape(chunk), ('x', 'y'), 0, 0, tiled=True)  7.43 us
    all_to_all x1, starting transfers between devices, shards(): lax.all_to_all(probs, ('x', 'y'), 0, 0, tiled=True).reshape(half, full)  7.23 us
    unnamed x12, local copies, waits for them, and re-layouts  5.48 us
    ppermute x2, waiting for transfers between devices, other_core(): return lax.ppermute(a, 'c', [(0, 1), (1, 0)])  4.17 us
  transfers between devices with their start and end apart: 25, of which 17 were waited for; matrix products, arithmetic and copies ran while one was open for 0% of the time, Pallas kernels for 0%

profile of v2, /device:TPU:6, one launch (start us, length us, event | category | flops | bytes accessed | tf_op | source)
XLA Modules:
  0.0 140.1 jit_solution(12879361779008055470)
XLA Ops:
  0.0 0.0 copy-start.1
  0.0 1.7 %copy-done.1 = bf16[768,3,512]{2,0,1:T(8,128)(2,1)S(1)} copy-done((bf16[768,3,512]{2,0,1:T(8,128)(2,1)S(1)}, bf16[768,3,512]{2,0,1:T(8,128)(2,1)}, u32[]{:S(2)}) %copy-start.1) | copy-done | bytes 2359320
  1.7 0.0 copy-start.2
  1.7 1.2 copy-done.2
  2.9 0.7 copy-done.5
  3.6 2.4 %shard_map.46 = (bf16[320,256]{1,0:T(8,128)(2,1)S(1)}, bf16[320,256]{1,0:T(8,128)(2,1)S(1)}, bf16[320,256]{1,0:T(8,128)(2,1)S(1)}, bf16[320,256]{1,0:T(8,128)(2,...) custom-call(s32[1]{0:T(128)} %bitcast.pos_ref, ...), custom_call_target="tpu_custom_call" | custom-call | flops 1509949440 | bytes 6690824 | tf_op jit(solution)/shard_map/pallas_call | solution.py:128
  5.9 2.0 %collective-permute-start = (bf16[320,256]{1,0:T(8,128)(2,1)S(1)}, bf16[320,256]{1,0:T(8,128)(2,1)S(1)}, u32[]{:S(2)}, u32[]{:S(2)}) collective-permute-start(bf16[320,256]{1,0:T(8,128)(2,1)S(1)} %get-tuple-element.32), channel_id=1, source_target_pairs={{0,64},{1,65},{64,128},{65,129},{128,192},{129,193},{192,1},{193,0... | collective-permute-start | bytes 491528 | tf_op jit(solution)/shard_map/ppermute | solution.py:143
  7.9 3.3 %collective-permute-start.1 = (bf16[320,256]{1,0:T(8,128)(2,1)S(1)}, bf16[320,256]{1,0:T(8,128)(2,1)S(1)}, u32[]{:S(2)}, u32[]{:S(2)}) collective-permute-start(bf16[320,256]{1,0:T(8,128)(2,1)S(1)} %get-tuple-element.33), channel_id=1, source_target_pairs={{0,128},{1,129},{64,192},{65,193},{128,1},{129,0},{192,65},{193,64... | collective-permute-start | bytes 491528 | tf_op jit(solution)/shard_map/ppermute | solution.py:143
  11.2 4.0 %collective-permute-start.2 = (bf16[320,256]{1,0:T(8,128)(2,1)S(1)}, bf16[320,256]{1,0:T(8,128)(2,1)S(1)}, u32[]{:S(2)}, u32[]{:S(2)}) collective-permute-start(bf16[320,256]{1,0:T(8,128)(2,1)S(1)} %get-tuple-element.34), channel_id=1, source_target_pairs={{0,192},{1,193},{64,1},{65,0},{128,65},{129,64},{192,129},{193,128... | collective-permute-start | bytes 491528 | tf_op jit(solution)/shard_map/ppermute | solution.py:143
  15.2 0.5 collective-permute-start.3
  15.8 4.9 %collective-permute-start.4 = (bf16[320,256]{1,0:T(8,128)(2,1)S(1)}, bf16[320,256]{1,0:T(8,128)(2,1)S(1)}, u32[]{:S(2)}, u32[]{:S(2)}) collective-permute-start(bf16[320,256]{1,0:T(8,128)(2,1)S(1)} %get-tuple-element.36), channel_id=1, source_target_pairs={{0,65},{1,64},{64,129},{65,128},{128,193},{129,192},{192,0},{193,1... | collective-permute-start | bytes 491528 | tf_op jit(solution)/shard_map/ppermute | solution.py:143
  20.7 0.0 collective-permute-done.refs_1_
  20.7 2.7 %collective-permute-start.5 = (bf16[320,256]{1,0:T(8,128)(2,1)S(1)}, bf16[320,256]{1,0:T(8,128)(2,1)S(1)}, u32[]{:S(2)}, u32[]{:S(2)}) collective-permute-start(bf16[320,256]{1,0:T(8,128)(2,1)S(1)} %get-tuple-element.37), channel_id=1, source_target_pairs={{0,129},{1,128},{64,193},{65,192},{128,0},{129,1},{192,64},{193,65... | collective-permute-start | bytes 491528 | tf_op jit(solution)/shard_map/ppermute | solution.py:143
  23.4 3.6 %collective-permute-done.1.refs_2_ = bf16[320,256]{1,0:T(8,128)(2,1)S(1)} collective-permute-done((bf16[320,256]{1,0:T(8,128)(2,1)S(1)}, bf16[320,256]{1,0:T(8,128)(2,1)S(1)}, u32[]{:S(2)}, u32[]{:S(2)}) %collective-permute-start.1) | collective-permute-done | bytes 163872 | tf_op jit(solution)/shard_map/ppermute | solution.py:143
  27.0 2.0 %collective-permute-start.6 = (bf16[320,256]{1,0:T(8,128)(2,1)S(1)}, bf16[320,256]{1,0:T(8,128)(2,1)S(1)}, u32[]{:S(2)}, u32[]{:S(2)}) collective-permute-start(bf16[320,256]{1,0:T(8,128)(2,1)S(1)} %get-tuple-element.38), channel_id=1, source_target_pairs={{0,193},{1,192},{64,0},{65,1},{128,64},{129,65},{192,128},{193,129... | collective-permute-start | bytes 491528 | tf_op jit(solution)/shard_map/ppermute | solution.py:143
  29.0 8.5 %collective-permute-done.2.refs_3_ = bf16[320,256]{1,0:T(8,128)(2,1)S(1)} collective-permute-done((bf16[320,256]{1,0:T(8,128)(2,1)S(1)}, bf16[320,256]{1,0:T(8,128)(2,1)S(1)}, u32[]{:S(2)}, u32[]{:S(2)}) %collective-permute-start.2) | collective-permute-done | bytes 163872 | tf_op jit(solution)/shard_map/ppermute | solution.py:143
  37.5 0.0 collective-permute-done.3.refs_4_
  37.5 2.3 %collective-permute-done.4.refs_5_ = bf16[320,256]{1,0:T(8,128)(2,1)S(1)} collective-permute-done((bf16[320,256]{1,0:T(8,128)(2,1)S(1)}, bf16[320,256]{1,0:T(8,128)(2,1)S(1)}, u32[]{:S(2)}, u32[]{:S(2)}) %collective-permute-start.4) | collective-permute-done | bytes 163872 | tf_op jit(solution)/shard_map/ppermute | solution.py:143
  39.8 4.2 %collective-permute-done.5.refs_6_ = bf16[320,256]{1,0:T(8,128)(2,1)S(1)} collective-permute-done((bf16[320,256]{1,0:T(8,128)(2,1)S(1)}, bf16[320,256]{1,0:T(8,128)(2,1)S(1)}, u32[]{:S(2)}, u32[]{:S(2)}) %collective-permute-start.5) | collective-permute-done | bytes 163872 | tf_op jit(solution)/shard_map/ppermute | solution.py:143
  44.1 1.5 %collective-permute-done.6.refs_7_ = bf16[320,256]{1,0:T(8,128)(2,1)S(1)} collective-permute-done((bf16[320,256]{1,0:T(8,128)(2,1)S(1)}, bf16[320,256]{1,0:T(8,128)(2,1)S(1)}, u32[]{:S(2)}, u32[]{:S(2)}) %collective-permute-start.6) | collective-permute-done | bytes 163872 | tf_op jit(solution)/shard_map/ppermute | solution.py:143
  45.6 0.1 shard_map.47.refs_8_
  45.7 0.1 collective-permute-start.7
  45.8 2.1 %collective-permute-done.7.refs_9_ = bf16[2,4,160,256]{3,2,1,0:T(8,128)(2,1)S(1)} collective-permute-done((bf16[2,4,160,256]{3,2,1,0:T(8,128)(2,1)S(1)}, bf16[2,4,160,256]{3,2,1,0:T(8,128)(2,1)S(1)}, u32[]{:S(2)}, u32[]{:S(2)}) %collective-permute-start.7) | collective-permute-done | bytes 655392 | tf_op jit(solution)/shard_map/ppermute | solution.py:148
  47.9 2.4 %shard_map.48 = bf16[640,1280]{1,0:T(8,128)(2,1)} custom-call(s32[1]{0:T(128)} %bitcast.pos_ref, bf16[320,256]{1,0:T(8,128)(2,1)S(1)} %get-tuple-element.31.refs_0_, bf16[320,256]{1,0:T(8,128)(2,1)S(1)} %collective-permute-done.refs_1_, bf16[320,256]{1,0:T(8,128)(2,1)S(1)} %collective-permute-done.1.refs_2_, ...), custom_call_target="tpu_custom_call" | custom-call | flops 838860800 | bytes 5242888 | tf_op jit(solution)/shard_map/pallas_call | solution.py:128
  50.3 7.4 %all-to-all-start = ((bf16[16,40,1280]{2,1,0:T(8,128)(2,1)}), bf16[16,40,1280]{2,1,0:T(8,128)(2,1)S(1)}, u32[]{:S(2)}, u32[]{:S(2)}) async-start(bf16[16,40,1280]{2,1,0:T(8,128)(2,1)} %bitcast.2), calls=%async_computation | async-start | bytes 3276800 | tf_op jit(solution)/shard_map/all_to_all | solution.py:182
  57.7 3.4 %collective-permute-start.8 = (bf16[160,256]{1,0:T(8,128)(2,1)S(1)}, bf16[160,256]{1,0:T(8,128)(2,1)S(1)}, u32[]{:S(2)}, u32[]{:S(2)}) collective-permute-start(bf16[160,256]{1,0:T(8,128)(2,1)S(1)} %get-tuple-element.40), channel_id=1, source_target_pairs={{0,64},{1,65},{64,128},{65,129},{128,192},{129,193},{192,1},{193,0... | collective-permute-start | bytes 245768 | tf_op jit(solution)/shard_map/ppermute | solution.py:143
  61.1 1.2 collective-permute-start.9
  62.2 0.6 collective-permute-start.10
  62.8 4.7 %collective-permute-start.11 = (bf16[160,256]{1,0:T(8,128)(2,1)S(1)}, bf16[160,256]{1,0:T(8,128)(2,1)S(1)}, u32[]{:S(2)}, u32[]{:S(2)}) collective-permute-start(bf16[160,256]{1,0:T(8,128)(2,1)S(1)} %get-tuple-element.43), channel_id=1, source_target_pairs={{0,1},{1,0},{64,65},{65,64},{128,129},{129,128},{192,193},{193,192... | collective-permute-start | bytes 245768 | tf_op jit(solution)/shard_map/ppermute | solution.py:143
  67.5 1.7 %collective-permute-start.12 = (bf16[160,256]{1,0:T(8,128)(2,1)S(1)}, bf16[160,256]{1,0:T(8,128)(2,1)S(1)}, u32[]{:S(2)}, u32[]{:S(2)}) collective-permute-start(bf16[160,256]{1,0:T(8,128)(2,1)S(1)} %get-tuple-element.44), channel_id=1, source_target_pairs={{0,65},{1,64},{64,129},{65,128},{128,193},{129,192},{192,0},{193,1... | collective-permute-start | bytes 245768 | tf_op jit(solution)/shard_map/ppermute | solution.py:143
  69.2 0.0 collective-permute-done.8.refs_1_
  69.2 2.2 %collective-permute-start.13 = (bf16[160,256]{1,0:T(8,128)(2,1)S(1)}, bf16[160,256]{1,0:T(8,128)(2,1)S(1)}, u32[]{:S(2)}, u32[]{:S(2)}) collective-permute-start(bf16[160,256]{1,0:T(8,128)(2,1)S(1)} %get-tuple-element.45), channel_id=1, source_target_pairs={{0,129},{1,128},{64,193},{65,192},{128,0},{129,1},{192,64},{193,65... | collective-permute-start | bytes 245768 | tf_op jit(solution)/shard_map/ppermute | solution.py:143
  71.4 1.0 collective-permute-done.9.refs_2_
  72.4 0.5 collective-permute-start.14
  72.9 1.9 %collective-permute-done.10.refs_3_ = bf16[160,256]{1,0:T(8,128)(2,1)S(1)} collective-permute-done((bf16[160,256]{1,0:T(8,128)(2,1)S(1)}, bf16[160,256]{1,0:T(8,128)(2,1)S(1)}, u32[]{:S(2)}, u32[]{:S(2)}) %collective-permute-start.10) | collective-permute-done | bytes 81952 | tf_op jit(solution)/shard_map/ppermute | solution.py:143
  74.8 0.2 collective-permute-done.11.refs_4_
  74.9 2.2 %collective-permute-done.12.refs_5_ = bf16[160,256]{1,0:T(8,128)(2,1)S(1)} collective-permute-done((bf16[160,256]{1,0:T(8,128)(2,1)S(1)}, bf16[160,256]{1,0:T(8,128)(2,1)S(1)}, u32[]{:S(2)}, u32[]{:S(2)}) %collective-permute-start.12) | collective-permute-done | bytes 81952 | tf_op jit(solution)/shard_map/ppermute | solution.py:143
  77.1 3.4 %collective-permute-done.13.refs_6_ = bf16[160,256]{1,0:T(8,128)(2,1)S(1)} collective-permute-done((bf16[160,256]{1,0:T(8,128)(2,1)S(1)}, bf16[160,256]{1,0:T(8,128)(2,1)S(1)}, u32[]{:S(2)}, u32[]{:S(2)}) %collective-permute-start.13) | collective-permute-done | bytes 81952 | tf_op jit(solution)/shard_map/ppermute | solution.py:143
  80.6 1.5 %collective-permute-done.14.refs_7_ = bf16[160,256]{1,0:T(8,128)(2,1)S(1)} collective-permute-done((bf16[160,256]{1,0:T(8,128)(2,1)S(1)}, bf16[160,256]{1,0:T(8,128)(2,1)S(1)}, u32[]{:S(2)}, u32[]{:S(2)}) %collective-permute-start.14) | collective-permute-done | bytes 81952 | tf_op jit(solution)/shard_map/ppermute | solution.py:143
  82.1 0.0 all-to-all-done.x_ref
  82.1 1.5 %shard_map.49 = (bf16[16,40,1280]{2,1,0:T(8,128)(2,1)}, bf16[2,4,160,256]{3,2,1,0:T(8,128)(2,1)S(1)}) custom-call(s32[1]{0:T(128)} %bitcast.pos_ref, bf16[16,40,1280]{2,1,0:T(8,128)(2,1)S(1)} %all-to-all-done.x_ref, bf16[160,256]{1,0:T(8,128)(2,1)S(1)} %get-tuple-element.39.refs_0_, bf16[160,256]{1,0:T(8,128)(2,1)S(1)} %collective-permute-done.8.refs_1_, ...), custom_call_target="tpu_custom_call" | custom-call | bytes 4587528 | tf_op jit(solution)/shard_map/pallas_call | solution.py:128
  83.6 7.2 %all-to-all-start.1 = ((bf16[16,40,1280]{2,1,0:T(8,128)(2,1)}), bf16[16,40,1280]{2,1,0:T(8,128)(2,1)S(1)}, u32[]{:S(2)}, u32[]{:S(2)}) async-start(bf16[16,40,1280]{2,1,0:T(8,128)(2,1)} %get-tuple-element.47), calls=%async_computation.1 | async-start | bytes 3276800 | tf_op jit(solution)/shard_map/all_to_all | solution.py:188
  90.9 0.1 collective-permute-start.15
  91.0 2.1 %collective-permute-done.15.v_far = bf16[2,4,160,256]{3,2,1,0:T(8,128)(2,1)S(1)} collective-permute-done((bf16[2,4,160,256]{3,2,1,0:T(8,128)(2,1)S(1)}, bf16[2,4,160,256]{3,2,1,0:T(8,128)(2,1)S(1)}, u32[]{:S(2)}, u32[]{:S(2)}) %collective-permute-start.15) | collective-permute-done | bytes 655392 | tf_op jit(solution)/shard_map/ppermute | solution.py:148
  93.1 0.8 copy-done.3
  93.9 17.7 %all-to-all-done.1 = bf16[16,40,1280]{2,1,0:T(8,128)(2,1)S(1)} async-done(((bf16[16,40,1280]{2,1,0:T(8,128)(2,1)}), bf16[16,40,1280]{2,1,0:T(8,128)(2,1)S(1)}, u32[]{:S(2)}, u32[]{:S(2)}) %all-to-all-start.1) | async-done | bytes 1638432 | tf_op jit(solution)/shard_map/all_to_all | solution.py:188
  111.6 1.1 copy-done.4
  112.7 1.2 shard_map.50
  113.9 2.9 %collective-permute-start.16 = (bf16[160,256]{1,0:T(8,128)(2,1)S(1)}, bf16[160,256]{1,0:T(8,128)(2,1)S(1)}, u32[]{:S(2)}, u32[]{:S(2)}) collective-permute-start(bf16[160,256]{1,0:T(8,128)(2,1)S(1)} %get-tuple-element.50), channel_id=1, source_target_pairs={{0,64},{1,65},{64,128},{65,129},{128,192},{129,193},{192,1},{193,0... | collective-permute-start | bytes 245768 | tf_op jit(solution)/shard_map/ppermute | solution.py:143
  116.8 2.1 %collective-permute-start.17 = (bf16[160,256]{1,0:T(8,128)(2,1)S(1)}, bf16[160,256]{1,0:T(8,128)(2,1)S(1)}, u32[]{:S(2)}, u32[]{:S(2)}) collective-permute-start(bf16[160,256]{1,0:T(8,128)(2,1)S(1)} %get-tuple-element.51), channel_id=1, source_target_pairs={{0,128},{1,129},{64,192},{65,193},{128,1},{129,0},{192,65},{193,64... | collective-permute-start | bytes 245768 | tf_op jit(solution)/shard_map/ppermute | solution.py:143
  118.9 2.2 %collective-permute-start.18 = (bf16[160,256]{1,0:T(8,128)(2,1)S(1)}, bf16[160,256]{1,0:T(8,128)(2,1)S(1)}, u32[]{:S(2)}, u32[]{:S(2)}) collective-permute-start(bf16[160,256]{1,0:T(8,128)(2,1)S(1)} %get-tuple-element.52), channel_id=1, source_target_pairs={{0,192},{1,193},{64,1},{65,0},{128,65},{129,64},{192,129},{193,128... | collective-permute-start | bytes 245768 | tf_op jit(solution)/shard_map/ppermute | solution.py:143
  121.1 1.8 %collective-permute-start.19 = (bf16[160,256]{1,0:T(8,128)(2,1)S(1)}, bf16[160,256]{1,0:T(8,128)(2,1)S(1)}, u32[]{:S(2)}, u32[]{:S(2)}) collective-permute-start(bf16[160,256]{1,0:T(8,128)(2,1)S(1)} %get-tuple-element.53), channel_id=1, source_target_pairs={{0,1},{1,0},{64,65},{65,64},{128,129},{129,128},{192,193},{193,192... | collective-permute-start | bytes 245768 | tf_op jit(solution)/shard_map/ppermute | solution.py:143
  122.9 4.0 %collective-permute-start.20 = (bf16[160,256]{1,0:T(8,128)(2,1)S(1)}, bf16[160,256]{1,0:T(8,128)(2,1)S(1)}, u32[]{:S(2)}, u32[]{:S(2)}) collective-permute-start(bf16[160,256]{1,0:T(8,128)(2,1)S(1)} %get-tuple-element.54), channel_id=1, source_target_pairs={{0,65},{1,64},{64,129},{65,128},{128,193},{129,192},{192,0},{193,1... | collective-permute-start | bytes 245768 | tf_op jit(solution)/shard_map/ppermute | solution.py:143
  126.8 0.0 collective-permute-done.16.refs_1_
  126.8 3.4 %collective-permute-start.21 = (bf16[160,256]{1,0:T(8,128)(2,1)S(1)}, bf16[160,256]{1,0:T(8,128)(2,1)S(1)}, u32[]{:S(2)}, u32[]{:S(2)}) collective-permute-start(bf16[160,256]{1,0:T(8,128)(2,1)S(1)} %get-tuple-element.55), channel_id=1, source_target_pairs={{0,129},{1,128},{64,193},{65,192},{128,0},{129,1},{192,64},{193,65... | collective-permute-start | bytes 245768 | tf_op jit(solution)/shard_map/ppermute | solution.py:143
  130.2 0.3 collective-permute-done.17.refs_2_
  130.5 0.0 collective-permute-start.22
  130.5 0.0 collective-permute-done.18.refs_3_
  130.5 0.0 collective-permute-done.19.refs_4_
  130.5 5.6 %collective-permute-done.20.refs_5_ = bf16[160,256]{1,0:T(8,128)(2,1)S(1)} collective-permute-done((bf16[160,256]{1,0:T(8,128)(2,1)S(1)}, bf16[160,256]{1,0:T(8,128)(2,1)S(1)}, u32[]{:S(2)}, u32[]{:S(2)}) %collective-permute-start.20) | collective-permute-done | bytes 81952 | tf_op jit(solution)/shard_map/ppermute | solution.py:143
  136.1 2.0 %collective-permute-done.21.refs_6_ = bf16[160,256]{1,0:T(8,128)(2,1)S(1)} collective-permute-done((bf16[160,256]{1,0:T(8,128)(2,1)S(1)}, bf16[160,256]{1,0:T(8,128)(2,1)S(1)}, u32[]{:S(2)}, u32[]{:S(2)}) %collective-permute-start.21) | collective-permute-done | bytes 81952 | tf_op jit(solution)/shard_map/ppermute | solution.py:143
  138.1 0.0 collective-permute-done.22.refs_7_
  138.1 0.0 copy-done
  138.1 2.0 %shard_map.51 = f32[4,160,768]{2,1,0:T(8,128)} custom-call(s32[1]{0:T(128)} %bitcast.pos_ref, bf16[512,768]{1,0:T(8,128)(2,1)S(1)} %copy-done, bf16[160,256]{1,0:T(8,128)(2,1)S(1)} %get-tuple-element.49.refs_0_, bf16[160,256]{1,0:T(8,128)(2,1)S(1)} %collective-permute-done.16.refs_1_, bf16[160,256]{1,0:T(8,128)(2,1)S(1)} %collective-permute-done.17.refs_2_, ...), custom_call_target="tpu_custom_call" | custom-call | flops 503316480 | bytes 2883592 | tf_op jit(solution)/shard_map/pallas_call | solution.py:128
  (4 shorter events, 0.0 us)
Async XLA Ops:
  0.0 1.7 %copy-start.1 = (bf16[768,3,512]{2,0,1:T(8,128)(2,1)S(1)}, bf16[768,3,512]{2,0,1:T(8,128)(2,1)}, u32[]{:S(2)}) copy-start(bf16[768,3,512]{2,0,1:T(8,128)(2,1)} %param.6) | copy-start | bytes 7077892
  1.7 1.2 copy-start.2
  2.9 0.7 copy-start.5
  5.9 14.8 %collective-permute-start = (bf16[320,256]{1,0:T(8,128)(2,1)S(1)}, bf16[320,256]{1,0:T(8,128)(2,1)S(1)}, u32[]{:S(2)}, u32[]{:S(2)}) collective-permute-start(bf16[320,256]{1,0:T(8,128)(2,1)S(1)} %get-tuple-element.32), channel_id=1, source_target_pairs={{0,64},{1,65},{64,128},{65,129},{128,192},{129,193},{192,1},{193,0... | collective-permute-start | bytes 491528 | tf_op jit(solution)/shard_map/ppermute | solution.py:143
  7.9 19.1 %collective-permute-start.1 = (bf16[320,256]{1,0:T(8,128)(2,1)S(1)}, bf16[320,256]{1,0:T(8,128)(2,1)S(1)}, u32[]{:S(2)}, u32[]{:S(2)}) collective-permute-start(bf16[320,256]{1,0:T(8,128)(2,1)S(1)} %get-tuple-element.33), channel_id=1, source_target_pairs={{0,128},{1,129},{64,192},{65,193},{128,1},{129,0},{192,65},{193,64... | collective-permute-start | bytes 491528 | tf_op jit(solution)/shard_map/ppermute | solution.py:143
  11.2 26.3 %collective-permute-start.2 = (bf16[320,256]{1,0:T(8,128)(2,1)S(1)}, bf16[320,256]{1,0:T(8,128)(2,1)S(1)}, u32[]{:S(2)}, u32[]{:S(2)}) collective-permute-start(bf16[320,256]{1,0:T(8,128)(2,1)S(1)} %get-tuple-element.34), channel_id=1, source_target_pairs={{0,192},{1,193},{64,1},{65,0},{128,65},{129,64},{192,129},{193,128... | collective-permute-start | bytes 491528 | tf_op jit(solution)/shard_map/ppermute | solution.py:143
  15.2 22.3 %collective-permute-start.3 = (bf16[320,256]{1,0:T(8,128)(2,1)S(1)}, bf16[320,256]{1,0:T(8,128)(2,1)S(1)}, u32[]{:S(2)}, u32[]{:S(2)}) collective-permute-start(bf16[320,256]{1,0:T(8,128)(2,1)S(1)} %get-tuple-element.35), channel_id=1, source_target_pairs={{0,1},{1,0},{64,65},{65,64},{128,129},{129,128},{192,193},{193,192... | collective-permute-start | bytes 491528 | tf_op jit(solution)/shard_map/ppermute | solution.py:143
  15.8 24.1 %collective-permute-start.4 = (bf16[320,256]{1,0:T(8,128)(2,1)S(1)}, bf16[320,256]{1,0:T(8,128)(2,1)S(1)}, u32[]{:S(2)}, u32[]{:S(2)}) collective-permute-start(bf16[320,256]{1,0:T(8,128)(2,1)S(1)} %get-tuple-element.36), channel_id=1, source_target_pairs={{0,65},{1,64},{64,129},{65,128},{128,193},{129,192},{192,0},{193,1... | collective-permute-start | bytes 491528 | tf_op jit(solution)/shard_map/ppermute | solution.py:143
  20.7 23.4 %collective-permute-start.5 = (bf16[320,256]{1,0:T(8,128)(2,1)S(1)}, bf16[320,256]{1,0:T(8,128)(2,1)S(1)}, u32[]{:S(2)}, u32[]{:S(2)}) collective-permute-start(bf16[320,256]{1,0:T(8,128)(2,1)S(1)} %get-tuple-element.37), channel_id=1, source_target_pairs={{0,129},{1,128},{64,193},{65,192},{128,0},{129,1},{192,64},{193,65... | collective-permute-start | bytes 491528 | tf_op jit(solution)/shard_map/ppermute | solution.py:143
  27.0 18.6 %collective-permute-start.6 = (bf16[320,256]{1,0:T(8,128)(2,1)S(1)}, bf16[320,256]{1,0:T(8,128)(2,1)S(1)}, u32[]{:S(2)}, u32[]{:S(2)}) collective-permute-start(bf16[320,256]{1,0:T(8,128)(2,1)S(1)} %get-tuple-element.38), channel_id=1, source_target_pairs={{0,193},{1,192},{64,0},{65,1},{128,64},{129,65},{192,128},{193,129... | collective-permute-start | bytes 491528 | tf_op jit(solution)/shard_map/ppermute | solution.py:143
  45.7 2.2 %collective-permute-start.7 = (bf16[2,4,160,256]{3,2,1,0:T(8,128)(2,1)S(1)}, bf16[2,4,160,256]{3,2,1,0:T(8,128)(2,1)S(1)}, u32[]{:S(2)}, u32[]{:S(2)}) collective-permute-start(bf16[2,4,160,256]{3,2,1,0:T(8,128)(2,1)S(1)} %shard_map.47.refs_8_), channel_id=1, source_target_pairs={{0,32},{32,0},{1,33},{33,1},{2,34},{34,2},{3,35},{35,3},{4,36},{36... | collective-permute-start | bytes 1966088 | tf_op jit(solution)/shard_map/ppermute | solution.py:148
  50.3 31.8 %all-to-all-start = ((bf16[16,40,1280]{2,1,0:T(8,128)(2,1)}), bf16[16,40,1280]{2,1,0:T(8,128)(2,1)S(1)}, u32[]{:S(2)}, u32[]{:S(2)}) async-start(bf16[16,40,1280]{2,1,0:T(8,128)(2,1)} %bitcast.2), calls=%async_computation | async-start | bytes 3276800 | tf_op jit(solution)/shard_map/all_to_all | solution.py:182
  57.7 11.5 %collective-permute-start.8 = (bf16[160,256]{1,0:T(8,128)(2,1)S(1)}, bf16[160,256]{1,0:T(8,128)(2,1)S(1)}, u32[]{:S(2)}, u32[]{:S(2)}) collective-permute-start(bf16[160,256]{1,0:T(8,128)(2,1)S(1)} %get-tuple-element.40), channel_id=1, source_target_pairs={{0,64},{1,65},{64,128},{65,129},{128,192},{129,193},{192,1},{193,0... | collective-permute-start | bytes 245768 | tf_op jit(solution)/shard_map/ppermute | solution.py:143
  61.1 11.3 %collective-permute-start.9 = (bf16[160,256]{1,0:T(8,128)(2,1)S(1)}, bf16[160,256]{1,0:T(8,128)(2,1)S(1)}, u32[]{:S(2)}, u32[]{:S(2)}) collective-permute-start(bf16[160,256]{1,0:T(8,128)(2,1)S(1)} %get-tuple-element.41), channel_id=1, source_target_pairs={{0,128},{1,129},{64,192},{65,193},{128,1},{129,0},{192,65},{193,64... | collective-permute-start | bytes 245768 | tf_op jit(solution)/shard_map/ppermute | solution.py:143
  62.2 12.5 %collective-permute-start.10 = (bf16[160,256]{1,0:T(8,128)(2,1)S(1)}, bf16[160,256]{1,0:T(8,128)(2,1)S(1)}, u32[]{:S(2)}, u32[]{:S(2)}) collective-permute-start(bf16[160,256]{1,0:T(8,128)(2,1)S(1)} %get-tuple-element.42), channel_id=1, source_target_pairs={{0,192},{1,193},{64,1},{65,0},{128,65},{129,64},{192,129},{193,128... | collective-permute-start | bytes 245768 | tf_op jit(solution)/shard_map/ppermute | solution.py:143
  62.8 12.1 %collective-permute-start.11 = (bf16[160,256]{1,0:T(8,128)(2,1)S(1)}, bf16[160,256]{1,0:T(8,128)(2,1)S(1)}, u32[]{:S(2)}, u32[]{:S(2)}) collective-permute-start(bf16[160,256]{1,0:T(8,128)(2,1)S(1)} %get-tuple-element.43), channel_id=1, source_target_pairs={{0,1},{1,0},{64,65},{65,64},{128,129},{129,128},{192,193},{193,192... | collective-permute-start | bytes 245768 | tf_op jit(solution)/shard_map/ppermute | solution.py:143
  67.5 9.6 %collective-permute-start.12 = (bf16[160,256]{1,0:T(8,128)(2,1)S(1)}, bf16[160,256]{1,0:T(8,128)(2,1)S(1)}, u32[]{:S(2)}, u32[]{:S(2)}) collective-permute-start(bf16[160,256]{1,0:T(8,128)(2,1)S(1)} %get-tuple-element.44), channel_id=1, source_target_pairs={{0,65},{1,64},{64,129},{65,128},{128,193},{129,192},{192,0},{193,1... | collective-permute-start | bytes 245768 | tf_op jit(solution)/shard_map/ppermute | solution.py:143
  69.2 11.3 %collective-permute-start.13 = (bf16[160,256]{1,0:T(8,128)(2,1)S(1)}, bf16[160,256]{1,0:T(8,128)(2,1)S(1)}, u32[]{:S(2)}, u32[]{:S(2)}) collective-permute-start(bf16[160,256]{1,0:T(8,128)(2,1)S(1)} %get-tuple-element.45), channel_id=1, source_target_pairs={{0,129},{1,128},{64,193},{65,192},{128,0},{129,1},{192,64},{193,65... | collective-permute-start | bytes 245768 | tf_op jit(solution)/shard_map/ppermute | solution.py:143
  72.4 9.7 %collective-permute-start.14 = (bf16[160,256]{1,0:T(8,128)(2,1)S(1)}, bf16[160,256]{1,0:T(8,128)(2,1)S(1)}, u32[]{:S(2)}, u32[]{:S(2)}) collective-permute-start(bf16[160,256]{1,0:T(8,128)(2,1)S(1)} %get-tuple-element.46), channel_id=1, source_target_pairs={{0,193},{1,192},{64,0},{65,1},{128,64},{129,65},{192,128},{193,129... | collective-permute-start | bytes 245768 | tf_op jit(solution)/shard_map/ppermute | solution.py:143
  83.6 27.9 %all-to-all-start.1 = ((bf16[16,40,1280]{2,1,0:T(8,128)(2,1)}), bf16[16,40,1280]{2,1,0:T(8,128)(2,1)S(1)}, u32[]{:S(2)}, u32[]{:S(2)}) async-start(bf16[16,40,1280]{2,1,0:T(8,128)(2,1)} %get-tuple-element.47), calls=%async_computation.1 | async-start | bytes 3276800 | tf_op jit(solution)/shard_map/all_to_all | solution.py:188
  90.9 47.2 %copy-start = (bf16[512,768]{1,0:T(8,128)(2,1)S(1)}, bf16[512,768]{1,0:T(8,128)(2,1)}, u32[]{:S(2)}) copy-start(bf16[512,768]{1,0:T(8,128)(2,1)} %w_ref.1) | copy-start | bytes 2359300
  90.9 2.2 %collective-permute-start.15 = (bf16[2,4,160,256]{3,2,1,0:T(8,128)(2,1)S(1)}, bf16[2,4,160,256]{3,2,1,0:T(8,128)(2,1)S(1)}, u32[]{:S(2)}, u32[]{:S(2)}) collective-permute-start(bf16[2,4,160,256]{3,2,1,0:T(8,128)(2,1)S(1)} %get-tuple-element.48.v_ref), channel_id=1, source_target_pairs={{0,32},{32,0},{1,33},{33,1},{2,34},{34,2},{3,35},{35,3},{4,36},{36... | collective-permute-start | bytes 1966088 | tf_op jit(solution)/shard_map/ppermute | solution.py:148
  93.1 0.8 copy-start.3
  111.6 1.1 copy-start.4
  113.9 12.9 %collective-permute-start.16 = (bf16[160,256]{1,0:T(8,128)(2,1)S(1)}, bf16[160,256]{1,0:T(8,128)(2,1)S(1)}, u32[]{:S(2)}, u32[]{:S(2)}) collective-permute-start(bf16[160,256]{1,0:T(8,128)(2,1)S(1)} %get-tuple-element.50), channel_id=1, source_target_pairs={{0,64},{1,65},{64,128},{65,129},{128,192},{129,193},{192,1},{193,0... | collective-permute-start | bytes 245768 | tf_op jit(solution)/shard_map/ppermute | solution.py:143
  116.8 13.7 %collective-permute-start.17 = (bf16[160,256]{1,0:T(8,128)(2,1)S(1)}, bf16[160,256]{1,0:T(8,128)(2,1)S(1)}, u32[]{:S(2)}, u32[]{:S(2)}) collective-permute-start(bf16[160,256]{1,0:T(8,128)(2,1)S(1)} %get-tuple-element.51), channel_id=1, source_target_pairs={{0,128},{1,129},{64,192},{65,193},{128,1},{129,0},{192,65},{193,64... | collective-permute-start | bytes 245768 | tf_op jit(solution)/shard_map/ppermute | solution.py:143
  118.9 11.6 %collective-permute-start.18 = (bf16[160,256]{1,0:T(8,128)(2,1)S(1)}, bf16[160,256]{1,0:T(8,128)(2,1)S(1)}, u32[]{:S(2)}, u32[]{:S(2)}) collective-permute-start(bf16[160,256]{1,0:T(8,128)(2,1)S(1)} %get-tuple-element.52), channel_id=1, source_target_pairs={{0,192},{1,193},{64,1},{65,0},{128,65},{129,64},{192,129},{193,128... | collective-permute-start | bytes 245768 | tf_op jit(solution)/shard_map/ppermute | solution.py:143
  121.1 9.4 %collective-permute-start.19 = (bf16[160,256]{1,0:T(8,128)(2,1)S(1)}, bf16[160,256]{1,0:T(8,128)(2,1)S(1)}, u32[]{:S(2)}, u32[]{:S(2)}) collective-permute-start(bf16[160,256]{1,0:T(8,128)(2,1)S(1)} %get-tuple-element.53), channel_id=1, source_target_pairs={{0,1},{1,0},{64,65},{65,64},{128,129},{129,128},{192,193},{193,192... | collective-permute-start | bytes 245768 | tf_op jit(solution)/shard_map/ppermute | solution.py:143
  122.9 13.2 %collective-permute-start.20 = (bf16[160,256]{1,0:T(8,128)(2,1)S(1)}, bf16[160,256]{1,0:T(8,128)(2,1)S(1)}, u32[]{:S(2)}, u32[]{:S(2)}) collective-permute-start(bf16[160,256]{1,0:T(8,128)(2,1)S(1)} %get-tuple-element.54), channel_id=1, source_target_pairs={{0,65},{1,64},{64,129},{65,128},{128,193},{129,192},{192,0},{193,1... | collective-permute-start | bytes 245768 | tf_op jit(solution)/shard_map/ppermute | solution.py:143
  126.8 11.3 %collective-permute-start.21 = (bf16[160,256]{1,0:T(8,128)(2,1)S(1)}, bf16[160,256]{1,0:T(8,128)(2,1)S(1)}, u32[]{:S(2)}, u32[]{:S(2)}) collective-permute-start(bf16[160,256]{1,0:T(8,128)(2,1)S(1)} %get-tuple-element.55), channel_id=1, source_target_pairs={{0,129},{1,128},{64,193},{65,192},{128,0},{129,1},{192,64},{193,65... | collective-permute-start | bytes 245768 | tf_op jit(solution)/shard_map/ppermute | solution.py:143
  130.5 7.6 %collective-permute-start.22 = (bf16[160,256]{1,0:T(8,128)(2,1)S(1)}, bf16[160,256]{1,0:T(8,128)(2,1)S(1)}, u32[]{:S(2)}, u32[]{:S(2)}) collective-permute-start(bf16[160,256]{1,0:T(8,128)(2,1)S(1)} %get-tuple-element.56), channel_id=1, source_target_pairs={{0,193},{1,192},{64,0},{65,1},{128,64},{129,65},{192,128},{193,129... | collective-permute-start | bytes 245768 | tf_op jit(solution)/shard_map/ppermute | solution.py:143

commit v3 on v2

v3 whole, which is shorter than its diff:
```python
import functools
import math

import jax
import jax.numpy as jnp
from jax import lax
from jax.experimental import pallas as pl
from jax.experimental.pallas import tpu as pltpu
from jax.sharding import Mesh
from jax.sharding import PartitionSpec as P

HEAD_DIM = 64
Z, CORE, X, Y, W = 4, 2, 4, 4, 2
RING = Z * W
PLANE = X * Y
STEPS = (0, 4, 3, 5, 2, 6, 1, 7)
BF = jnp.bfloat16
F32 = jnp.float32
VMEM = pl.BlockSpec(memory_space=pltpu.VMEM)
HBM = pl.BlockSpec(memory_space=pltpu.HBM)
ANY = pl.BlockSpec(memory_space=pl.ANY)
SMEM = pl.BlockSpec(memory_space=pltpu.SMEM)
MIB = 1024 * 1024


def place(index):
    return (index % W) * Z + index // W


def index_of(position):
    return (position % Z) * W + position // Z


def head_at(position):
    pos = lax.rem(position, RING)
    return lax.rem(pos, Z) * W + lax.div(pos, Z)


def blocks_by_head(y, seqs, mine):
    length = y.shape[0] // seqs
    for h in range(mine.shape[0]):
        mine[h] = jnp.concatenate(
            [y[r * length : (r + 1) * length, h * HEAD_DIM : (h + 1) * HEAD_DIM] for r in range(seqs)], axis=1
        ).astype(BF)


def keys_queries_kernel(pos_ref, gain_ref, x_hbm, w_hbm, *refs):
    both, (normed, mine, x_ref, w_ref, x_sem, w_sem) = refs[:RING], refs[RING:]
    seqs, length, width = x_hbm.shape
    x_copies = [pltpu.make_async_copy(x_hbm.at[r], x_ref.at[r], x_sem.at[r]) for r in range(seqs)]
    w_copies = [pltpu.make_async_copy(w_hbm.at[c], w_ref.at[c], w_sem.at[c]) for c in range(2)]
    for copy in (*x_copies, w_copies[1], w_copies[0]):
        copy.start()
    gain = gain_ref[...].reshape(1, width)
    for r in range(seqs):
        x_copies[r].wait()
        x = x_ref[r].astype(F32)
        mean = jnp.mean(x, axis=-1, keepdims=True)
        off = x - mean
        var = jnp.mean(off * off, axis=-1, keepdims=True)
        normed[r * length : (r + 1) * length] = (off / jnp.sqrt(var + 1e-05) * gain).astype(BF)
    pos = pos_ref[0]
    for c in (1, 0):
        w_copies[c].wait()
        blocks_by_head(jnp.dot(normed[...], w_ref[c], preferred_element_type=F32), seqs, mine)
        for i, s in enumerate(STEPS):
            both[i][(1 - c) * length : (2 - c) * length] = mine[head_at(pos + s)]


def values_kernel(seqs, pos_ref, normed, w_hbm, *refs):
    outs, (mine, w_ref, w_sem) = refs[:RING], refs[RING:]
    copy = pltpu.make_async_copy(w_hbm.at[2], w_ref, w_sem)
    copy.start()
    copy.wait()
    blocks_by_head(jnp.dot(normed[...], w_ref[...], preferred_element_type=F32), seqs, mine)
    pos = pos_ref[0]
    for i, s in enumerate(STEPS):
        outs[i][...] = mine[head_at(pos + s)]


def put_by_sender(pos, parts, first, out):
    length = out.shape[2]
    for part, s in zip(parts, STEPS):
        src = lax.rem(pos + RING - s, RING)
        out[lax.div(src, Z), lax.rem(src, Z)] = part[first : first + length]


def place_kernel(pos_ref, *refs):
    put_by_sender(pos_ref[0], refs[:-1], 0, refs[-1])


def logits_kernel(pos_ref, *refs):
    parts, (k_ref, k_far, out_ref, q) = refs[:RING], refs[RING:]
    put_by_sender(pos_ref[0], parts, q.shape[2], q)
    half = k_ref.shape[1] * k_ref.shape[2]
    for side, keys in enumerate((k_ref, k_far)):
        total = None
        for w in range(W):
            a = q[w].reshape(half, -1)
            b = keys[w].reshape(half, -1)
            term = lax.dot_general(a, b, (((1,), (1,)), ((), ())), preferred_element_type=F32)
            total = term if total is None else total + term
        out_ref[:, side * half : (side + 1) * half] = total.astype(BF)


def probs_kernel(scale, x_ref, *refs):
    out_ref = refs[-1]
    logits = x_ref[0].astype(F32)
    for i in range(1, x_ref.shape[0]):
        logits = logits + x_ref[i].astype(F32)
    expo = jnp.exp(logits * scale)
    probs = (expo / jnp.sum(expo, axis=-1, keepdims=True)).astype(BF)
    for i in range(out_ref.shape[0]):
        out_ref[i] = probs


def context_kernel(pos_ref, p_ref, v_ref, far_hbm, *refs):
    outs, (mine, v_far, sem) = refs[:RING], refs[RING:]
    copy = pltpu.make_async_copy(far_hbm, v_far, sem)
    copy.start()
    half = v_ref.shape[1] * v_ref.shape[2]
    length = v_ref.shape[2]
    near = [jnp.dot(p_ref[:, :half], v_ref[w].reshape(half, -1), preferred_element_type=F32) for w in range(W)]
    copy.wait()
    for w in range(W):
        a = near[w] + jnp.dot(p_ref[:, half:], v_far[w].reshape(half, -1), preferred_element_type=F32)
        a = a.astype(BF)
        for z in range(Z):
            mine[w * Z + z] = a[z * length : (z + 1) * length]
    pos = pos_ref[0]
    for i, s in enumerate(STEPS):
        outs[i][...] = mine[lax.rem(pos + s, RING)]


def mix_kernel(pos_ref, w_ref, *refs):
    parts, (out_hbm, rows, mixed, sem) = refs[:RING], refs[RING:]
    pos = pos_ref[0]
    for i, s in enumerate(STEPS):
        h = head_at(pos + RING - s)
        rows[i * HEAD_DIM : (i + 1) * HEAD_DIM] = w_ref[pl.ds(pl.multiple_of(h * HEAD_DIM, HEAD_DIM), HEAD_DIM)]
    copies = []
    for r in range(mixed.shape[0]):
        lhs = jnp.concatenate([part[:, r * HEAD_DIM : (r + 1) * HEAD_DIM] for part in parts], axis=1)
        mixed[r] = jnp.dot(lhs, rows[...], preferred_element_type=F32)
        copies.append(pltpu.make_async_copy(mixed.at[r], out_hbm.at[r], sem.at[r]))
        copies[r].start()
    for copy in copies:
        copy.wait()


def call(kernel, out_shape, operands, scratch=(), flops=0, hbm=(), unread=(), out_specs=None, vmem=20):
    moved = sum(math.prod(o.shape) * o.dtype.itemsize for o in operands)
    specs = [
        SMEM if o.dtype == jnp.int32 else HBM if i in hbm else ANY if i in unread else VMEM for i, o in enumerate(operands)
    ]
    return pl.pallas_call(
        kernel,
        out_shape=out_shape,
        in_specs=specs,
        out_specs=out_specs or jax.tree.map(lambda _: VMEM, out_shape),
        scratch_shapes=list(scratch),
        compiler_params=pltpu.CompilerParams(vmem_limit_bytes=vmem * MIB),
        cost_estimate=pl.CostEstimate(flops=flops, bytes_accessed=2 * moved, transcendentals=0),
    )(*operands)


def along_ring(parts):
    got = []
    for part, s in zip(parts, STEPS):
        pairs = [(i, index_of((place(i) + s) % RING)) for i in range(RING)]
        got.append(lax.ppermute(part, ("z", "w"), pairs) if s else part)
    return got


def other_core(a):
    return lax.ppermute(a, "c", [(0, 1), (1, 0)])


def shards(tokens, ln_gain, w_qkv, w_out):
    seqs, length, width = tokens.shape
    inner = w_qkv.shape[2]
    lanes = seqs * HEAD_DIM
    pos = (lax.axis_index("w") * Z + lax.axis_index("z")).astype(jnp.int32).reshape(1)
    pair = jax.ShapeDtypeStruct((2 * length, lanes), BF)
    block = jax.ShapeDtypeStruct((length, lanes), BF)
    whole = jax.ShapeDtypeStruct((W, Z, length, lanes), BF)
    half = Z * length
    full = CORE * half
    scale = 1.0 / math.sqrt(HEAD_DIM * seqs * W * PLANE)

    weights = jnp.transpose(w_qkv, (1, 0, 2))
    dma = pltpu.SemaphoreType.DMA
    *both, normed = call(
        keys_queries_kernel,
        [pair] * RING + [jax.ShapeDtypeStruct((seqs * length, width), BF)],
        [pos, ln_gain, tokens, weights],
        [
            pltpu.VMEM((RING, length, lanes), BF),
            pltpu.VMEM(tokens.shape, BF),
            pltpu.VMEM((2, width, inner), BF),
            dma((seqs,)),
            dma((2,)),
        ],
        flops=2 * seqs * length * width * 2 * inner,
        hbm=(2, 3),
        vmem=57,
    )
    both = along_ring(both)
    values = call(
        functools.partial(values_kernel, seqs),
        [block] * RING,
        [pos, normed, weights],
        [pltpu.VMEM((RING, length, lanes), BF), pltpu.VMEM((width, inner), BF), dma],
        flops=2 * seqs * length * width * inner,
        hbm=(2,),
        vmem=20,
    )
    values = along_ring(values)
    keys = call(place_kernel, whole, [pos, *both])
    keys_far = other_core(keys)
    term = call(
        logits_kernel,
        jax.ShapeDtypeStruct((half, full), BF),
        [pos, *both, keys, keys_far],
        [pltpu.VMEM(whole.shape, BF)],
        flops=2 * half * full * W * lanes,
    )
    chunk = (PLANE, half // PLANE, full)
    terms = lax.all_to_all(term.reshape(chunk), ("x", "y"), 0, 0, tiled=True)
    early = values[1:5]
    probs = call(
        functools.partial(probs_kernel, scale),
        jax.ShapeDtypeStruct(chunk, BF),
        [terms, *early],
        unread=range(1, 5),
    )
    probs = lax.all_to_all(probs, ("x", "y"), 0, 0, tiled=True).reshape(half, full)
    values = call(place_kernel, whole, [pos, *values])
    values_far = other_core(values)
    context = call(
        context_kernel,
        [block] * RING,
        [pos, probs, values, values_far],
        [pltpu.VMEM((RING, length, lanes), BF), pltpu.VMEM(whole.shape, BF), dma],
        flops=2 * half * full * W * lanes,
        hbm=(3,),
        vmem=20,
    )
    context = along_ring(context)
    return call(
        mix_kernel,
        jax.ShapeDtypeStruct((seqs, length, width), F32),
        [pos, w_out, *context],
        [pltpu.VMEM(w_out.shape, BF), pltpu.VMEM((seqs, length, width), F32), dma((seqs,))],
        flops=2 * seqs * length * inner * width,
        out_specs=HBM,
    )


def solution(mesh):
    cut = Mesh(mesh.devices.reshape(Z, CORE, X, Y, W), ("z", "c", "x", "y", "w"))
    split = P(("x", "y", "w"), ("z", "c"), None)
    return jax.shard_map(shards, mesh=cut, in_specs=(split, P(), P(), P()), out_specs=split, check_vma=False)
```

time: 141 us -> 131 us (0.929)
  waiting for transfers between devices: 60.1 us -> 51.5 us
  starting transfers between devices: 64.8 us -> 60 us
  Pallas kernels: 9.61 us -> 13.8 us
    all_to_all x1, waiting for transfers between devices: 17.7 us -> 8.82 us  [shards(): lax.all_to_all(probs, ('x', 'y'), 0, 0, tiled=True).reshape(half, full)]
    pallas_call x6 -> x8, Pallas kernels: 9.61 us -> 13.8 us  [call(): pl.pallas_call(kernel, out_shape=out_shape, in_specs=specs, out_specs=out...]
    ppermute x21, starting transfers between devices: 49.9 us -> 46 us  [along_ring(): got.append(lax.ppermute(part, ('z', 'w'), pairs) if s else part)]
    all_to_all x1, waiting for transfers between devices: 0.01 us -> 3.22 us  [shards(): terms = lax.all_to_all(term.reshape(chunk), ('x', 'y'), 0, 0, tiled=True)]
    ppermute x21, waiting for transfers between devices: 38.3 us -> 35.3 us  [along_ring(): got.append(lax.ppermute(part, ('z', 'w'), pairs) if s else part)]
  transfers between devices with their start and end apart: 25 -> 25, of which waited for: 17 -> 20; matrix products, arithmetic and copies ran while one was open for 0% -> 0% of each run, Pallas kernels for 0% -> 1%
where the time goes in v3:
time: 131 us; the launch traced here: 130 us
  starting transfers between devices  60 us (46%)
  waiting for transfers between devices  51.5 us (39%)
  Pallas kernels  13.8 us (11%)
  local copies, waits for them, and re-layouts  4.51 us (3%)
    ppermute x21, starting transfers between devices, along_ring(): got.append(lax.ppermute(part, ('z', 'w'), pairs) if s else part)  46 us
    ppermute x21, waiting for transfers between devices, along_ring(): got.append(lax.ppermute(part, ('z', 'w'), pairs) if s else part)  35.3 us
    pallas_call x8, Pallas kernels, call(): pl.pallas_call(kernel, out_shape=out_shape, in_specs=specs, out_specs=out...  13.8 us
    all_to_all x1, waiting for transfers between devices, shards(): lax.all_to_all(probs, ('x', 'y'), 0, 0, tiled=True).reshape(half, full)  8.82 us
    all_to_all x1, starting transfers between devices, shards(): terms = lax.all_to_all(term.reshape(chunk), ('x', 'y'), 0, 0, tiled=True)  7.56 us
    all_to_all x1, starting transfers between devices, shards(): lax.all_to_all(probs, ('x', 'y'), 0, 0, tiled=True).reshape(half, full)  6.23 us
    unnamed x12, local copies, waits for them, and re-layouts  4.51 us
    ppermute x2, waiting for transfers between devices, other_core(): return lax.ppermute(a, 'c', [(0, 1), (1, 0)])  4.17 us
  transfers between devices with their start and end apart: 25, of which 20 were waited for; matrix products, arithmetic and copies ran while one was open for 0% of the time, Pallas kernels for 1%

profile of v3, /device:TPU:6, one launch (start us, length us, event | category | flops | bytes accessed | tf_op | source)
XLA Modules:
  0.0 130.0 jit_solution(83981307432535540)
XLA Ops:
  0.0 5.6 %shard_map.46 = (bf16[320,256]{1,0:T(8,128)(2,1)}, bf16[320,256]{1,0:T(8,128)(2,1)}, bf16[320,256]{1,0:T(8,128)(2,1)}, bf16[320,256]{1,0:T(8,128)(2,1)}, bf16[32...) custom-call(s32[1]{0:T(128)} %bitcast.pos_ref, ...), custom_call_target="tpu_custom_call" | custom-call | flops 1006632960 | bytes 6690824 | tf_op jit(solution)/shard_map/pallas_call | solution.py:156
  5.6 7.3 %collective-permute-start = (bf16[320,256]{1,0:T(8,128)(2,1)}, bf16[320,256]{1,0:T(8,128)(2,1)S(1)}, u32[]{:S(2)}, u32[]{:S(2)}) collective-permute-start(bf16[320,256]{1,0:T(8,128)(2,1)} %get-tuple-element.31), channel_id=1, source_target_pairs={{0,1},{1,0},{64,65},{65,64},{128,129},{129,128},{192,193},{193,192... | collective-permute-start | bytes 491528 | tf_op jit(solution)/shard_map/ppermute | solution.py:171
  12.9 1.9 %collective-permute-start.1 = (bf16[320,256]{1,0:T(8,128)(2,1)}, bf16[320,256]{1,0:T(8,128)(2,1)S(1)}, u32[]{:S(2)}, u32[]{:S(2)}) collective-permute-start(bf16[320,256]{1,0:T(8,128)(2,1)} %get-tuple-element.32), channel_id=1, source_target_pairs={{0,192},{1,193},{64,1},{65,0},{128,65},{129,64},{192,129},{193,128... | collective-permute-start | bytes 491528 | tf_op jit(solution)/shard_map/ppermute | solution.py:171
  14.8 3.1 %collective-permute-start.2 = (bf16[320,256]{1,0:T(8,128)(2,1)}, bf16[320,256]{1,0:T(8,128)(2,1)S(1)}, u32[]{:S(2)}, u32[]{:S(2)}) collective-permute-start(bf16[320,256]{1,0:T(8,128)(2,1)} %get-tuple-element.33), channel_id=1, source_target_pairs={{0,65},{1,64},{64,129},{65,128},{128,193},{129,192},{192,0},{193,1... | collective-permute-start | bytes 491528 | tf_op jit(solution)/shard_map/ppermute | solution.py:171
  17.9 1.5 %collective-permute-start.3 = (bf16[320,256]{1,0:T(8,128)(2,1)}, bf16[320,256]{1,0:T(8,128)(2,1)S(1)}, u32[]{:S(2)}, u32[]{:S(2)}) collective-permute-start(bf16[320,256]{1,0:T(8,128)(2,1)} %get-tuple-element.34), channel_id=1, source_target_pairs={{0,128},{1,129},{64,192},{65,193},{128,1},{129,0},{192,65},{193,64... | collective-permute-start | bytes 491528 | tf_op jit(solution)/shard_map/ppermute | solution.py:171
  19.4 2.7 %collective-permute-start.4 = (bf16[320,256]{1,0:T(8,128)(2,1)}, bf16[320,256]{1,0:T(8,128)(2,1)S(1)}, u32[]{:S(2)}, u32[]{:S(2)}) collective-permute-start(bf16[320,256]{1,0:T(8,128)(2,1)} %get-tuple-element.35), channel_id=1, source_target_pairs={{0,129},{1,128},{64,193},{65,192},{128,0},{129,1},{192,64},{193,65... | collective-permute-start | bytes 491528 | tf_op jit(solution)/shard_map/ppermute | solution.py:171
  22.1 3.2 %collective-permute-done.refs_1_ = bf16[320,256]{1,0:T(8,128)(2,1)S(1)} collective-permute-done((bf16[320,256]{1,0:T(8,128)(2,1)}, bf16[320,256]{1,0:T(8,128)(2,1)S(1)}, u32[]{:S(2)}, u32[]{:S(2)}) %collective-permute-start) | collective-permute-done | bytes 163872 | tf_op jit(solution)/shard_map/ppermute | solution.py:171
  25.2 0.2 collective-permute-start.5
  25.5 8.8 %collective-permute-done.1.refs_2_ = bf16[320,256]{1,0:T(8,128)(2,1)S(1)} collective-permute-done((bf16[320,256]{1,0:T(8,128)(2,1)}, bf16[320,256]{1,0:T(8,128)(2,1)S(1)}, u32[]{:S(2)}, u32[]{:S(2)}) %collective-permute-start.1) | collective-permute-done | bytes 163872 | tf_op jit(solution)/shard_map/ppermute | solution.py:171
  34.3 0.0 collective-permute-start.6
  34.3 0.0 collective-permute-done.2.refs_3_
  34.3 4.2 %collective-permute-done.3.refs_4_ = bf16[320,256]{1,0:T(8,128)(2,1)S(1)} collective-permute-done((bf16[320,256]{1,0:T(8,128)(2,1)}, bf16[320,256]{1,0:T(8,128)(2,1)S(1)}, u32[]{:S(2)}, u32[]{:S(2)}) %collective-permute-start.3) | collective-permute-done | bytes 163872 | tf_op jit(solution)/shard_map/ppermute | solution.py:171
  38.5 0.9 collective-permute-done.4.refs_5_
  39.4 2.2 %collective-permute-done.5.refs_6_ = bf16[320,256]{1,0:T(8,128)(2,1)S(1)} collective-permute-done((bf16[320,256]{1,0:T(8,128)(2,1)}, bf16[320,256]{1,0:T(8,128)(2,1)S(1)}, u32[]{:S(2)}, u32[]{:S(2)}) %collective-permute-start.5) | collective-permute-done | bytes 163872 | tf_op jit(solution)/shard_map/ppermute | solution.py:171
  41.6 1.1 collective-permute-done.6.refs_7_
  42.7 0.9 copy-done.3
  43.6 0.1 shard_map.47.refs_8_
  43.7 0.1 collective-permute-start.7
  43.8 2.1 %collective-permute-done.7.refs_9_ = bf16[2,4,160,256]{3,2,1,0:T(8,128)(2,1)S(1)} collective-permute-done((bf16[2,4,160,256]{3,2,1,0:T(8,128)(2,1)S(1)}, bf16[2,4,160,256]{3,2,1,0:T(8,128)(2,1)S(1)}, u32[]{:S(2)}, u32[]{:S(2)}) %collective-permute-start.7) | collective-permute-done | bytes 655392 | tf_op jit(solution)/shard_map/ppermute | solution.py:176
  45.9 2.4 %shard_map.48 = bf16[640,1280]{1,0:T(8,128)(2,1)} custom-call(s32[1]{0:T(128)} %bitcast.pos_ref, bf16[320,256]{1,0:T(8,128)(2,1)S(1)} %copy-done.3, bf16[320,256]{1,0:T(8,128)(2,1)S(1)} %collective-permute-done.refs_1_, bf16[320,256]{1,0:T(8,128)(2,1)S(1)} %collective-permute-done.1.refs_2_, bf16[320,256]{1,0:T(8,128)(2,1)S(1)} %collective-permute-done.2.refs_3_, ...), custom_call_target="tpu_custom_call" | custom-call | flops 838860800 | bytes 5242888 | tf_op jit(solution)/shard_map/pallas_call | solution.py:156
  48.2 7.6 %all-to-all-start = ((bf16[16,40,1280]{2,1,0:T(8,128)(2,1)}), bf16[16,40,1280]{2,1,0:T(8,128)(2,1)S(1)}, u32[]{:S(2)}, u32[]{:S(2)}) async-start(bf16[16,40,1280]{2,1,0:T(8,128)(2,1)} %bitcast.2), calls=%async_computation | async-start | bytes 3276800 | tf_op jit(solution)/shard_map/all_to_all | solution.py:229
  55.8 0.0 copy-start
  55.8 1.7 %copy-done = bf16[768,3,512]{2,0,1:T(8,128)(2,1)S(1)} copy-done((bf16[768,3,512]{2,0,1:T(8,128)(2,1)S(1)}, bf16[768,3,512]{2,0,1:T(8,128)(2,1)}, u32[]{:S(2)}) %copy-start) | copy-done | bytes 2359320
  57.5 0.9 shard_map.49
  58.4 3.6 %collective-permute-start.8 = (bf16[160,256]{1,0:T(8,128)(2,1)S(1)}, bf16[160,256]{1,0:T(8,128)(2,1)S(1)}, u32[]{:S(2)}, u32[]{:S(2)}) collective-permute-start(bf16[160,256]{1,0:T(8,128)(2,1)S(1)} %get-tuple-element.39), channel_id=1, source_target_pairs={{0,1},{1,0},{64,65},{65,64},{128,129},{129,128},{192,193},{193,192... | collective-permute-start | bytes 245768 | tf_op jit(solution)/shard_map/ppermute | solution.py:171
  62.0 2.3 %collective-permute-start.9 = (bf16[160,256]{1,0:T(8,128)(2,1)S(1)}, bf16[160,256]{1,0:T(8,128)(2,1)S(1)}, u32[]{:S(2)}, u32[]{:S(2)}) collective-permute-start(bf16[160,256]{1,0:T(8,128)(2,1)S(1)} %get-tuple-element.40), channel_id=1, source_target_pairs={{0,192},{1,193},{64,1},{65,0},{128,65},{129,64},{192,129},{193,128... | collective-permute-start | bytes 245768 | tf_op jit(solution)/shard_map/ppermute | solution.py:171
  64.3 2.7 %collective-permute-start.10 = (bf16[160,256]{1,0:T(8,128)(2,1)S(1)}, bf16[160,256]{1,0:T(8,128)(2,1)S(1)}, u32[]{:S(2)}, u32[]{:S(2)}) collective-permute-start(bf16[160,256]{1,0:T(8,128)(2,1)S(1)} %get-tuple-element.41), channel_id=1, source_target_pairs={{0,65},{1,64},{64,129},{65,128},{128,193},{129,192},{192,0},{193,1... | collective-permute-start | bytes 245768 | tf_op jit(solution)/shard_map/ppermute | solution.py:171
  67.0 0.2 collective-permute-start.11
  67.2 2.6 %collective-permute-done.8.refs_0_.refs_1_ = bf16[160,256]{1,0:T(8,128)(2,1)S(1)} collective-permute-done((bf16[160,256]{1,0:T(8,128)(2,1)S(1)}, bf16[160,256]{1,0:T(8,128)(2,1)S(1)}, u32[]{:S(2)}, u32[]{:S(2)}) %collective-permute-start.8) | collective-permute-done | bytes 81952 | tf_op jit(solution)/shard_map/ppermute | solution.py:171
  69.9 5.3 %collective-permute-done.9.refs_1_.refs_2_ = bf16[160,256]{1,0:T(8,128)(2,1)S(1)} collective-permute-done((bf16[160,256]{1,0:T(8,128)(2,1)S(1)}, bf16[160,256]{1,0:T(8,128)(2,1)S(1)}, u32[]{:S(2)}, u32[]{:S(2)}) %collective-permute-start.9) | collective-permute-done | bytes 81952 | tf_op jit(solution)/shard_map/ppermute | solution.py:171
  75.2 0.0 collective-permute-done.10.refs_2_.refs_3_
  75.2 0.0 collective-permute-done.11.refs_3_.refs_4_
  75.2 3.2 %all-to-all-done.x_ref = bf16[16,40,1280]{2,1,0:T(8,128)(2,1)S(1)} async-done(((bf16[16,40,1280]{2,1,0:T(8,128)(2,1)}), bf16[16,40,1280]{2,1,0:T(8,128)(2,1)S(1)}, u32[]{:S(2)}, u32[]{:S(2)}) %all-to-all-start) | async-done | bytes 1638432 | tf_op jit(solution)/shard_map/all_to_all | solution.py:229
  78.4 1.5 %shard_map.50 = bf16[16,40,1280]{2,1,0:T(8,128)(2,1)} custom-call(bf16[16,40,1280]{2,1,0:T(8,128)(2,1)S(1)} %all-to-all-done.x_ref, bf16[160,256]{1,0:T(8,128)(2,1)S(1)} %collective-permute-done.8.refs_0_.refs_1_, bf16[160,256]{1,0:T(8,128)(2,1)S(1)} %collective-permute-done.9.refs_1_.refs_2_, bf16[160,256]{1,0:T(8,128)(2,1)S(1)} %collective-permute-done.10.refs_2_.refs_3_, ...), custom_call_target="tpu_custom_call" | custom-call | bytes 3932160 | tf_op jit(solution)/shard_map/pallas_call | solution.py:156
  79.9 6.2 %all-to-all-start.1 = ((bf16[16,40,1280]{2,1,0:T(8,128)(2,1)}), bf16[16,40,1280]{2,1,0:T(8,128)(2,1)S(1)}, u32[]{:S(2)}, u32[]{:S(2)}) async-start(bf16[16,40,1280]{2,1,0:T(8,128)(2,1)} %shard_map.50), calls=%async_computation.1 | async-start | bytes 3276800 | tf_op jit(solution)/shard_map/all_to_all | solution.py:237
  86.2 1.4 %collective-permute-start.12 = (bf16[160,256]{1,0:T(8,128)(2,1)S(1)}, bf16[160,256]{1,0:T(8,128)(2,1)S(1)}, u32[]{:S(2)}, u32[]{:S(2)}) collective-permute-start(bf16[160,256]{1,0:T(8,128)(2,1)S(1)} %get-tuple-element.44), channel_id=1, source_target_pairs={{0,129},{1,128},{64,193},{65,192},{128,0},{129,1},{192,64},{193,65... | collective-permute-start | bytes 245768 | tf_op jit(solution)/shard_map/ppermute | solution.py:171
  87.5 2.7 %collective-permute-start.13 = (bf16[160,256]{1,0:T(8,128)(2,1)S(1)}, bf16[160,256]{1,0:T(8,128)(2,1)S(1)}, u32[]{:S(2)}, u32[]{:S(2)}) collective-permute-start(bf16[160,256]{1,0:T(8,128)(2,1)S(1)} %get-tuple-element.45), channel_id=1, source_target_pairs={{0,64},{1,65},{64,128},{65,129},{128,192},{129,193},{192,1},{193,0... | collective-permute-start | bytes 245768 | tf_op jit(solution)/shard_map/ppermute | solution.py:171
  90.3 0.5 collective-permute-start.14
  90.8 1.9 %collective-permute-done.12.refs_5_ = bf16[160,256]{1,0:T(8,128)(2,1)S(1)} collective-permute-done((bf16[160,256]{1,0:T(8,128)(2,1)S(1)}, bf16[160,256]{1,0:T(8,128)(2,1)S(1)}, u32[]{:S(2)}, u32[]{:S(2)}) %collective-permute-start.12) | collective-permute-done | bytes 81952 | tf_op jit(solution)/shard_map/ppermute | solution.py:171
  92.7 0.5 collective-permute-done.13.refs_6_
  93.2 1.5 %collective-permute-done.14.refs_7_ = bf16[160,256]{1,0:T(8,128)(2,1)S(1)} collective-permute-done((bf16[160,256]{1,0:T(8,128)(2,1)S(1)}, bf16[160,256]{1,0:T(8,128)(2,1)S(1)}, u32[]{:S(2)}, u32[]{:S(2)}) %collective-permute-start.14) | collective-permute-done | bytes 81952 | tf_op jit(solution)/shard_map/ppermute | solution.py:171
  94.7 0.1 shard_map.51.v_ref
  94.8 0.0 copy-start.2
  94.8 0.1 collective-permute-start.15
  94.9 2.1 %collective-permute-done.15.far_hbm = bf16[2,4,160,256]{3,2,1,0:T(8,128)(2,1)S(1)} collective-permute-done((bf16[2,4,160,256]{3,2,1,0:T(8,128)(2,1)S(1)}, bf16[2,4,160,256]{3,2,1,0:T(8,128)(2,1)S(1)}, u32[]{:S(2)}, u32[]{:S(2)}) %collective-permute-start.15) | collective-permute-done | bytes 655392 | tf_op jit(solution)/shard_map/ppermute | solution.py:176
  97.0 0.8 copy-done.4
  97.8 8.8 %all-to-all-done.1 = bf16[16,40,1280]{2,1,0:T(8,128)(2,1)S(1)} async-done(((bf16[16,40,1280]{2,1,0:T(8,128)(2,1)}), bf16[16,40,1280]{2,1,0:T(8,128)(2,1)S(1)}, u32[]{:S(2)}, u32[]{:S(2)}) %all-to-all-start.1) | async-done | bytes 1638432 | tf_op jit(solution)/shard_map/all_to_all | solution.py:237
  106.6 1.1 copy-done.5
  107.7 1.5 %shard_map.52 = (bf16[160,256]{1,0:T(8,128)(2,1)S(1)}, bf16[160,256]{1,0:T(8,128)(2,1)S(1)}, bf16[160,256]{1,0:T(8,128)(2,1)S(1)}, bf16[160,256]{1,0:T(8,128)(2,...) custom-call(s32[1]{0:T(128)} %bitcast.pos_ref, ...), custom_call_target="tpu_custom_call" | custom-call | flops 838860800 | bytes 5898248 | tf_op jit(solution)/shard_map/pallas_call | solution.py:156
  109.3 3.6 %collective-permute-start.16 = (bf16[160,256]{1,0:T(8,128)(2,1)S(1)}, bf16[160,256]{1,0:T(8,128)(2,1)S(1)}, u32[]{:S(2)}, u32[]{:S(2)}) collective-permute-start(bf16[160,256]{1,0:T(8,128)(2,1)S(1)} %get-tuple-element.48), channel_id=1, source_target_pairs={{0,1},{1,0},{64,65},{65,64},{128,129},{129,128},{192,193},{193,192... | collective-permute-start | bytes 245768 | tf_op jit(solution)/shard_map/ppermute | solution.py:171
  112.9 2.3 %collective-permute-start.17 = (bf16[160,256]{1,0:T(8,128)(2,1)S(1)}, bf16[160,256]{1,0:T(8,128)(2,1)S(1)}, u32[]{:S(2)}, u32[]{:S(2)}) collective-permute-start(bf16[160,256]{1,0:T(8,128)(2,1)S(1)} %get-tuple-element.49), channel_id=1, source_target_pairs={{0,192},{1,193},{64,1},{65,0},{128,65},{129,64},{192,129},{193,128... | collective-permute-start | bytes 245768 | tf_op jit(solution)/shard_map/ppermute | solution.py:171
  115.2 2.7 %collective-permute-start.18 = (bf16[160,256]{1,0:T(8,128)(2,1)S(1)}, bf16[160,256]{1,0:T(8,128)(2,1)S(1)}, u32[]{:S(2)}, u32[]{:S(2)}) collective-permute-start(bf16[160,256]{1,0:T(8,128)(2,1)S(1)} %get-tuple-element.50), channel_id=1, source_target_pairs={{0,65},{1,64},{64,129},{65,128},{128,193},{129,192},{192,0},{193,1... | collective-permute-start | bytes 245768 | tf_op jit(solution)/shard_map/ppermute | solution.py:171
  117.9 0.2 collective-permute-start.19
  118.1 3.9 %collective-permute-start.20 = (bf16[160,256]{1,0:T(8,128)(2,1)S(1)}, bf16[160,256]{1,0:T(8,128)(2,1)S(1)}, u32[]{:S(2)}, u32[]{:S(2)}) collective-permute-start(bf16[160,256]{1,0:T(8,128)(2,1)S(1)} %get-tuple-element.52), channel_id=1, source_target_pairs={{0,129},{1,128},{64,193},{65,192},{128,0},{129,1},{192,64},{193,65... | collective-permute-start | bytes 245768 | tf_op jit(solution)/shard_map/ppermute | solution.py:171
  122.1 0.0 collective-permute-done.16.refs_1_
  122.1 1.2 collective-permute-start.21
  123.3 0.2 collective-permute-done.17.refs_2_
  123.4 1.9 %collective-permute-start.22 = (bf16[160,256]{1,0:T(8,128)(2,1)S(1)}, bf16[160,256]{1,0:T(8,128)(2,1)S(1)}, u32[]{:S(2)}, u32[]{:S(2)}) collective-permute-start(bf16[160,256]{1,0:T(8,128)(2,1)S(1)} %get-tuple-element.54), channel_id=1, source_target_pairs={{0,193},{1,192},{64,0},{65,1},{128,64},{129,65},{192,128},{193,129... | collective-permute-start | bytes 245768 | tf_op jit(solution)/shard_map/ppermute | solution.py:171
  125.3 0.6 collective-permute-done.18.refs_3_
  125.9 0.7 collective-permute-done.19.refs_4_
  126.6 0.0 collective-permute-done.20.refs_5_
  126.6 1.1 collective-permute-done.21.refs_6_
  127.7 0.4 collective-permute-done.22.refs_7_
  128.2 1.7 %shard_map.53 = f32[4,160,768]{2,1,0:T(8,128)} custom-call(s32[1]{0:T(128)} %bitcast.pos_ref, bf16[512,768]{1,0:T(8,128)(2,1)S(1)} %copy-done.2, bf16[160,256]{1,0:T(8,128)(2,1)S(1)} %get-tuple-element.47.refs_0_, bf16[160,256]{1,0:T(8,128)(2,1)S(1)} %collective-permute-done.16.refs_1_, bf16[160,256]{1,0:T(8,128)(2,1)S(1)} %collective-permute-done.17.refs_2_, ...), custom_call_target="tpu_custom_call" | custom-call | flops 503316480 | bytes 2883592 | tf_op jit(solution)/shard_map/pallas_call | solution.py:156
  (6 shorter events, 0.0 us)
Async XLA Ops:
  5.6 19.6 %collective-permute-start = (bf16[320,256]{1,0:T(8,128)(2,1)}, bf16[320,256]{1,0:T(8,128)(2,1)S(1)}, u32[]{:S(2)}, u32[]{:S(2)}) collective-permute-start(bf16[320,256]{1,0:T(8,128)(2,1)} %get-tuple-element.31), channel_id=1, source_target_pairs={{0,1},{1,0},{64,65},{65,64},{128,129},{129,128},{192,193},{193,192... | collective-permute-start | bytes 491528 | tf_op jit(solution)/shard_map/ppermute | solution.py:171
  12.9 21.4 %collective-permute-start.1 = (bf16[320,256]{1,0:T(8,128)(2,1)}, bf16[320,256]{1,0:T(8,128)(2,1)S(1)}, u32[]{:S(2)}, u32[]{:S(2)}) collective-permute-start(bf16[320,256]{1,0:T(8,128)(2,1)} %get-tuple-element.32), channel_id=1, source_target_pairs={{0,192},{1,193},{64,1},{65,0},{128,65},{129,64},{192,129},{193,128... | collective-permute-start | bytes 491528 | tf_op jit(solution)/shard_map/ppermute | solution.py:171
  14.8 19.5 %collective-permute-start.2 = (bf16[320,256]{1,0:T(8,128)(2,1)}, bf16[320,256]{1,0:T(8,128)(2,1)S(1)}, u32[]{:S(2)}, u32[]{:S(2)}) collective-permute-start(bf16[320,256]{1,0:T(8,128)(2,1)} %get-tuple-element.33), channel_id=1, source_target_pairs={{0,65},{1,64},{64,129},{65,128},{128,193},{129,192},{192,0},{193,1... | collective-permute-start | bytes 491528 | tf_op jit(solution)/shard_map/ppermute | solution.py:171
  17.9 20.6 %collective-permute-start.3 = (bf16[320,256]{1,0:T(8,128)(2,1)}, bf16[320,256]{1,0:T(8,128)(2,1)S(1)}, u32[]{:S(2)}, u32[]{:S(2)}) collective-permute-start(bf16[320,256]{1,0:T(8,128)(2,1)} %get-tuple-element.34), channel_id=1, source_target_pairs={{0,128},{1,129},{64,192},{65,193},{128,1},{129,0},{192,65},{193,64... | collective-permute-start | bytes 491528 | tf_op jit(solution)/shard_map/ppermute | solution.py:171
  19.4 20.0 %collective-permute-start.4 = (bf16[320,256]{1,0:T(8,128)(2,1)}, bf16[320,256]{1,0:T(8,128)(2,1)S(1)}, u32[]{:S(2)}, u32[]{:S(2)}) collective-permute-start(bf16[320,256]{1,0:T(8,128)(2,1)} %get-tuple-element.35), channel_id=1, source_target_pairs={{0,129},{1,128},{64,193},{65,192},{128,0},{129,1},{192,64},{193,65... | collective-permute-start | bytes 491528 | tf_op jit(solution)/shard_map/ppermute | solution.py:171
  25.2 16.3 %collective-permute-start.5 = (bf16[320,256]{1,0:T(8,128)(2,1)}, bf16[320,256]{1,0:T(8,128)(2,1)S(1)}, u32[]{:S(2)}, u32[]{:S(2)}) collective-permute-start(bf16[320,256]{1,0:T(8,128)(2,1)} %get-tuple-element.36), channel_id=1, source_target_pairs={{0,64},{1,65},{64,128},{65,129},{128,192},{129,193},{192,1},{193,0... | collective-permute-start | bytes 491528 | tf_op jit(solution)/shard_map/ppermute | solution.py:171
  34.3 8.4 %collective-permute-start.6 = (bf16[320,256]{1,0:T(8,128)(2,1)}, bf16[320,256]{1,0:T(8,128)(2,1)S(1)}, u32[]{:S(2)}, u32[]{:S(2)}) collective-permute-start(bf16[320,256]{1,0:T(8,128)(2,1)} %get-tuple-element.37), channel_id=1, source_target_pairs={{0,193},{1,192},{64,0},{65,1},{128,64},{129,65},{192,128},{193,129... | collective-permute-start | bytes 491528 | tf_op jit(solution)/shard_map/ppermute | solution.py:171
  42.7 0.9 copy-start.3
  43.7 2.2 %collective-permute-start.7 = (bf16[2,4,160,256]{3,2,1,0:T(8,128)(2,1)S(1)}, bf16[2,4,160,256]{3,2,1,0:T(8,128)(2,1)S(1)}, u32[]{:S(2)}, u32[]{:S(2)}) collective-permute-start(bf16[2,4,160,256]{3,2,1,0:T(8,128)(2,1)S(1)} %shard_map.47.refs_8_), channel_id=1, source_target_pairs={{0,32},{32,0},{1,33},{33,1},{2,34},{34,2},{3,35},{35,3},{4,36},{36... | collective-permute-start | bytes 1966088 | tf_op jit(solution)/shard_map/ppermute | solution.py:176
  48.2 7.6 %copy-start.1 = (bf16[640,768]{1,0:T(8,128)(2,1)S(1)}, bf16[640,768]{1,0:T(8,128)(2,1)}, u32[]{:S(2)}) copy-start(bf16[640,768]{1,0:T(8,128)(2,1)} %get-tuple-element.38.normed) | copy-start | bytes 2949124
  48.2 30.2 %all-to-all-start = ((bf16[16,40,1280]{2,1,0:T(8,128)(2,1)}), bf16[16,40,1280]{2,1,0:T(8,128)(2,1)S(1)}, u32[]{:S(2)}, u32[]{:S(2)}) async-start(bf16[16,40,1280]{2,1,0:T(8,128)(2,1)} %bitcast.2), calls=%async_computation | async-start | bytes 3276800 | tf_op jit(solution)/shard_map/all_to_all | solution.py:229
  55.8 1.7 %copy-start = (bf16[768,3,512]{2,0,1:T(8,128)(2,1)S(1)}, bf16[768,3,512]{2,0,1:T(8,128)(2,1)}, u32[]{:S(2)}) copy-start(bf16[768,3,512]{2,0,1:T(8,128)(2,1)} %param.6) | copy-start | bytes 7077892
  58.4 11.5 %collective-permute-start.8 = (bf16[160,256]{1,0:T(8,128)(2,1)S(1)}, bf16[160,256]{1,0:T(8,128)(2,1)S(1)}, u32[]{:S(2)}, u32[]{:S(2)}) collective-permute-start(bf16[160,256]{1,0:T(8,128)(2,1)S(1)} %get-tuple-element.39), channel_id=1, source_target_pairs={{0,1},{1,0},{64,65},{65,64},{128,129},{129,128},{192,193},{193,192... | collective-permute-start | bytes 245768 | tf_op jit(solution)/shard_map/ppermute | solution.py:171
  62.0 13.2 %collective-permute-start.9 = (bf16[160,256]{1,0:T(8,128)(2,1)S(1)}, bf16[160,256]{1,0:T(8,128)(2,1)S(1)}, u32[]{:S(2)}, u32[]{:S(2)}) collective-permute-start(bf16[160,256]{1,0:T(8,128)(2,1)S(1)} %get-tuple-element.40), channel_id=1, source_target_pairs={{0,192},{1,193},{64,1},{65,0},{128,65},{129,64},{192,129},{193,128... | collective-permute-start | bytes 245768 | tf_op jit(solution)/shard_map/ppermute | solution.py:171
  64.3 10.9 %collective-permute-start.10 = (bf16[160,256]{1,0:T(8,128)(2,1)S(1)}, bf16[160,256]{1,0:T(8,128)(2,1)S(1)}, u32[]{:S(2)}, u32[]{:S(2)}) collective-permute-start(bf16[160,256]{1,0:T(8,128)(2,1)S(1)} %get-tuple-element.41), channel_id=1, source_target_pairs={{0,65},{1,64},{64,129},{65,128},{128,193},{129,192},{192,0},{193,1... | collective-permute-start | bytes 245768 | tf_op jit(solution)/shard_map/ppermute | solution.py:171
  67.0 8.2 %collective-permute-start.11 = (bf16[160,256]{1,0:T(8,128)(2,1)S(1)}, bf16[160,256]{1,0:T(8,128)(2,1)S(1)}, u32[]{:S(2)}, u32[]{:S(2)}) collective-permute-start(bf16[160,256]{1,0:T(8,128)(2,1)S(1)} %get-tuple-element.42), channel_id=1, source_target_pairs={{0,128},{1,129},{64,192},{65,193},{128,1},{129,0},{192,65},{193,64... | collective-permute-start | bytes 245768 | tf_op jit(solution)/shard_map/ppermute | solution.py:171
  79.9 26.7 %all-to-all-start.1 = ((bf16[16,40,1280]{2,1,0:T(8,128)(2,1)}), bf16[16,40,1280]{2,1,0:T(8,128)(2,1)S(1)}, u32[]{:S(2)}, u32[]{:S(2)}) async-start(bf16[16,40,1280]{2,1,0:T(8,128)(2,1)} %shard_map.50), calls=%async_computation.1 | async-start | bytes 3276800 | tf_op jit(solution)/shard_map/all_to_all | solution.py:237
  86.2 6.5 %collective-permute-start.12 = (bf16[160,256]{1,0:T(8,128)(2,1)S(1)}, bf16[160,256]{1,0:T(8,128)(2,1)S(1)}, u32[]{:S(2)}, u32[]{:S(2)}) collective-permute-start(bf16[160,256]{1,0:T(8,128)(2,1)S(1)} %get-tuple-element.44), channel_id=1, source_target_pairs={{0,129},{1,128},{64,193},{65,192},{128,0},{129,1},{192,64},{193,65... | collective-permute-start | bytes 245768 | tf_op jit(solution)/shard_map/ppermute | solution.py:171
  87.5 5.7 %collective-permute-start.13 = (bf16[160,256]{1,0:T(8,128)(2,1)S(1)}, bf16[160,256]{1,0:T(8,128)(2,1)S(1)}, u32[]{:S(2)}, u32[]{:S(2)}) collective-permute-start(bf16[160,256]{1,0:T(8,128)(2,1)S(1)} %get-tuple-element.45), channel_id=1, source_target_pairs={{0,64},{1,65},{64,128},{65,129},{128,192},{129,193},{192,1},{193,0... | collective-permute-start | bytes 245768 | tf_op jit(solution)/shard_map/ppermute | solution.py:171
  90.3 4.4 %collective-permute-start.14 = (bf16[160,256]{1,0:T(8,128)(2,1)S(1)}, bf16[160,256]{1,0:T(8,128)(2,1)S(1)}, u32[]{:S(2)}, u32[]{:S(2)}) collective-permute-start(bf16[160,256]{1,0:T(8,128)(2,1)S(1)} %get-tuple-element.46), channel_id=1, source_target_pairs={{0,193},{1,192},{64,0},{65,1},{128,64},{129,65},{192,128},{193,129... | collective-permute-start | bytes 245768 | tf_op jit(solution)/shard_map/ppermute | solution.py:171
  94.8 33.4 %copy-start.2 = (bf16[512,768]{1,0:T(8,128)(2,1)S(1)}, bf16[512,768]{1,0:T(8,128)(2,1)}, u32[]{:S(2)}) copy-start(bf16[512,768]{1,0:T(8,128)(2,1)} %w_ref.1) | copy-start | bytes 2359300
  94.8 2.2 %collective-permute-start.15 = (bf16[2,4,160,256]{3,2,1,0:T(8,128)(2,1)S(1)}, bf16[2,4,160,256]{3,2,1,0:T(8,128)(2,1)S(1)}, u32[]{:S(2)}, u32[]{:S(2)}) collective-permute-start(bf16[2,4,160,256]{3,2,1,0:T(8,128)(2,1)S(1)} %shard_map.51.v_ref), channel_id=1, source_target_pairs={{0,32},{32,0},{1,33},{33,1},{2,34},{34,2},{3,35},{35,3},{4,36},{36... | collective-permute-start | bytes 1966088 | tf_op jit(solution)/shard_map/ppermute | solution.py:176
  97.0 0.8 copy-start.4
  106.6 1.1 copy-start.5
  109.3 12.8 %collective-permute-start.16 = (bf16[160,256]{1,0:T(8,128)(2,1)S(1)}, bf16[160,256]{1,0:T(8,128)(2,1)S(1)}, u32[]{:S(2)}, u32[]{:S(2)}) collective-permute-start(bf16[160,256]{1,0:T(8,128)(2,1)S(1)} %get-tuple-element.48), channel_id=1, source_target_pairs={{0,1},{1,0},{64,65},{65,64},{128,129},{129,128},{192,193},{193,192... | collective-permute-start | bytes 245768 | tf_op jit(solution)/shard_map/ppermute | solution.py:171
  112.9 10.5 %collective-permute-start.17 = (bf16[160,256]{1,0:T(8,128)(2,1)S(1)}, bf16[160,256]{1,0:T(8,128)(2,1)S(1)}, u32[]{:S(2)}, u32[]{:S(2)}) collective-permute-start(bf16[160,256]{1,0:T(8,128)(2,1)S(1)} %get-tuple-element.49), channel_id=1, source_target_pairs={{0,192},{1,193},{64,1},{65,0},{128,65},{129,64},{192,129},{193,128... | collective-permute-start | bytes 245768 | tf_op jit(solution)/shard_map/ppermute | solution.py:171
  115.2 10.7 %collective-permute-start.18 = (bf16[160,256]{1,0:T(8,128)(2,1)S(1)}, bf16[160,256]{1,0:T(8,128)(2,1)S(1)}, u32[]{:S(2)}, u32[]{:S(2)}) collective-permute-start(bf16[160,256]{1,0:T(8,128)(2,1)S(1)} %get-tuple-element.50), channel_id=1, source_target_pairs={{0,65},{1,64},{64,129},{65,128},{128,193},{129,192},{192,0},{193,1... | collective-permute-start | bytes 245768 | tf_op jit(solution)/shard_map/ppermute | solution.py:171
  117.9 8.6 %collective-permute-start.19 = (bf16[160,256]{1,0:T(8,128)(2,1)S(1)}, bf16[160,256]{1,0:T(8,128)(2,1)S(1)}, u32[]{:S(2)}, u32[]{:S(2)}) collective-permute-start(bf16[160,256]{1,0:T(8,128)(2,1)S(1)} %get-tuple-element.51), channel_id=1, source_target_pairs={{0,128},{1,129},{64,192},{65,193},{128,1},{129,0},{192,65},{193,64... | collective-permute-start | bytes 245768 | tf_op jit(solution)/shard_map/ppermute | solution.py:171
  118.1 8.5 %collective-permute-start.20 = (bf16[160,256]{1,0:T(8,128)(2,1)S(1)}, bf16[160,256]{1,0:T(8,128)(2,1)S(1)}, u32[]{:S(2)}, u32[]{:S(2)}) collective-permute-start(bf16[160,256]{1,0:T(8,128)(2,1)S(1)} %get-tuple-element.52), channel_id=1, source_target_pairs={{0,129},{1,128},{64,193},{65,192},{128,0},{129,1},{192,64},{193,65... | collective-permute-start | bytes 245768 | tf_op jit(solution)/shard_map/ppermute | solution.py:171
  122.1 5.7 %collective-permute-start.21 = (bf16[160,256]{1,0:T(8,128)(2,1)S(1)}, bf16[160,256]{1,0:T(8,128)(2,1)S(1)}, u32[]{:S(2)}, u32[]{:S(2)}) collective-permute-start(bf16[160,256]{1,0:T(8,128)(2,1)S(1)} %get-tuple-element.53), channel_id=1, source_target_pairs={{0,64},{1,65},{64,128},{65,129},{128,192},{129,193},{192,1},{193,0... | collective-permute-start | bytes 245768 | tf_op jit(solution)/shard_map/ppermute | solution.py:171
  123.4 4.7 %collective-permute-start.22 = (bf16[160,256]{1,0:T(8,128)(2,1)S(1)}, bf16[160,256]{1,0:T(8,128)(2,1)S(1)}, u32[]{:S(2)}, u32[]{:S(2)}) collective-permute-start(bf16[160,256]{1,0:T(8,128)(2,1)S(1)} %get-tuple-element.54), channel_id=1, source_target_pairs={{0,193},{1,192},{64,0},{65,1},{128,64},{129,65},{192,128},{193,129... | collective-permute-start | bytes 245768 | tf_op jit(solution)/shard_map/ppermute | solution.py:171

commit v4 on v3

--- a/solution.py
+++ b/solution.py
@@ -44,13 +44,15 @@
         ).astype(BF)
 
 
-def keys_queries_kernel(pos_ref, gain_ref, x_hbm, w_hbm, *refs):
-    both, (normed, mine, x_ref, w_ref, x_sem, w_sem) = refs[:RING], refs[RING:]
+def keys_queries_kernel(pos_ref, gain_hbm, x_hbm, w_hbm, *refs):
+    both, (normed, mine, gain_ref, x_ref, w_ref, gain_sem, x_sem, w_sem) = refs[:RING], refs[RING:]
     seqs, length, width = x_hbm.shape
     x_copies = [pltpu.make_async_copy(x_hbm.at[r], x_ref.at[r], x_sem.at[r]) for r in range(seqs)]
     w_copies = [pltpu.make_async_copy(w_hbm.at[c], w_ref.at[c], w_sem.at[c]) for c in range(2)]
-    for copy in (*x_copies, w_copies[1], w_copies[0]):
+    gain_copy = pltpu.make_async_copy(gain_hbm, gain_ref, gain_sem)
+    for copy in (x_copies[0], gain_copy, *x_copies[1:], w_copies[1], w_copies[0]):
         copy.start()
+    gain_copy.wait()
     gain = gain_ref[...].reshape(1, width)
     for r in range(seqs):
         x_copies[r].wait()
@@ -85,22 +87,30 @@
         out[lax.div(src, Z), lax.rem(src, Z)] = part[first : first + length]
 
 
-def place_kernel(pos_ref, *refs):
-    put_by_sender(pos_ref[0], refs[:-1], 0, refs[-1])
+def place_kernel(count, pos_ref, *refs):
+    put_by_sender(pos_ref[0], refs[:count], 0, refs[-1])
 
 
 def logits_kernel(pos_ref, *refs):
-    parts, (k_ref, k_far, out_ref, q) = refs[:RING], refs[RING:]
+    parts, (k_ref, k_far, out_hbm, q, terms, sem) = refs[:RING], refs[RING:]
     put_by_sender(pos_ref[0], parts, q.shape[2], q)
-    half = k_ref.shape[1] * k_ref.shape[2]
-    for side, keys in enumerate((k_ref, k_far)):
-        total = None
-        for w in range(W):
-            a = q[w].reshape(half, -1)
-            b = keys[w].reshape(half, -1)
-            term = lax.dot_general(a, b, (((1,), (1,)), ((), ())), preferred_element_type=F32)
-            total = term if total is None else total + term
-        out_ref[:, side * half : (side + 1) * half] = total.astype(BF)
+    length = k_ref.shape[2]
+    half = k_ref.shape[1] * length
+    copies = []
+    for z in range(Z):
+        rows = slice(z * length, (z + 1) * length)
+        for side, keys in enumerate((k_ref, k_far)):
+            total = None
+            for w in range(W):
+                term = lax.dot_general(
+                    q[w, z], keys[w].reshape(half, -1), (((1,), (1,)), ((), ())), preferred_element_type=F32
+                )
+                total = term if total is None else total + term
+            terms[rows, side * half : (side + 1) * half] = total.astype(BF)
+        copies.append(pltpu.make_async_copy(terms.at[rows], out_hbm.at[rows], sem.at[z]))
+        copies[z].start()
+    for copy in copies:
+        copy.wait()
 
 
 def probs_kernel(scale, x_ref, *refs):
@@ -196,14 +206,16 @@
         [pos, ln_gain, tokens, weights],
         [
             pltpu.VMEM((RING, length, lanes), BF),
+            pltpu.VMEM(ln_gain.shape, F32),
             pltpu.VMEM(tokens.shape, BF),
             pltpu.VMEM((2, width, inner), BF),
+            dma,
             dma((seqs,)),
             dma((2,)),
         ],
         flops=2 * seqs * length * width * 2 * inner,
-        hbm=(2, 3),
-        vmem=57,
+        hbm=(1, 2, 3),
+        vmem=51,
     )
     both = along_ring(both)
     values = call(
@@ -215,15 +227,16 @@
         hbm=(2,),
         vmem=20,
     )
+    keys = call(functools.partial(place_kernel, RING), whole, [pos, *both, values[0]], unread=(1 + RING,))
+    keys_far = other_core(keys)
     values = along_ring(values)
-    keys = call(place_kernel, whole, [pos, *both])
-    keys_far = other_core(keys)
     term = call(
         logits_kernel,
         jax.ShapeDtypeStruct((half, full), BF),
         [pos, *both, keys, keys_far],
-        [pltpu.VMEM(whole.shape, BF)],
+        [pltpu.VMEM(whole.shape, BF), pltpu.VMEM((half, full), BF), dma((Z,))],
         flops=2 * half * full * W * lanes,
+        out_specs=HBM,
     )
     chunk = (PLANE, half // PLANE, full)
     terms = lax.all_to_all(term.reshape(chunk), ("x", "y"), 0, 0, tiled=True)
@@ -235,7 +248,7 @@
         unread=range(1, 5),
     )
     probs = lax.all_to_all(probs, ("x", "y"), 0, 0, tiled=True).reshape(half, full)
-    values = call(place_kernel, whole, [pos, *values])
+    values = call(functools.partial(place_kernel, RING), whole, [pos, *values])
     values_far = other_core(values)
     context = call(
         context_kernel,

time: 131 us -> 129 us (0.985)
  waiting for transfers between devices: 51.5 us -> 56.1 us
  starting transfers between devices: 60 us -> 57.4 us
  local copies, waits for them, and re-layouts: 4.51 us -> 2.61 us
  Pallas kernels: 13.8 us -> 12 us
    ppermute x21, starting transfers between devices: 46 us -> 43.6 us  [along_ring(): got.append(lax.ppermute(part, ('z', 'w'), pairs) if s else part)]
    all_to_all x1, waiting for transfers between devices: 3.22 us -> 5.58 us  [shards(): terms = lax.all_to_all(term.reshape(chunk), ('x', 'y'), 0, 0, tiled=True)]
    ppermute x21, waiting for transfers between devices: 35.3 us -> 37.5 us  [along_ring(): got.append(lax.ppermute(part, ('z', 'w'), pairs) if s else part)]
    unnamed x12 -> x10, local copies, waits for them, and re-layouts: 4.51 us -> 2.61 us
    pallas_call x8, Pallas kernels: 13.8 us -> 12 us  [call(): pl.pallas_call(kernel, out_shape=out_shape, in_specs=specs, out_specs=out...]
  transfers between devices with their start and end apart: 25 -> 25, of which waited for: 20 -> 19; matrix products, arithmetic and copies ran while one was open for 0% -> 0% of each run, Pallas kernels for 1% -> 1%
where the time goes in v4:
time: 129 us; the launch traced here: 128 us
  starting transfers between devices  57.4 us (44%)
  waiting for transfers between devices  56.1 us (43%)
  Pallas kernels  12 us (9%)
  local copies, waits for them, and re-layouts  2.61 us (2%)
    ppermute x21, starting transfers between devices, along_ring(): got.append(lax.ppermute(part, ('z', 'w'), pairs) if s else part)  43.6 us
    ppermute x21, waiting for transfers between devices, along_ring(): got.append(lax.ppermute(part, ('z', 'w'), pairs) if s else part)  37.5 us
    pallas_call x8, Pallas kernels, call(): pl.pallas_call(kernel, out_shape=out_shape, in_specs=specs, out_specs=out...  12 us
    all_to_all x1, waiting for transfers between devices, shards(): lax.all_to_all(probs, ('x', 'y'), 0, 0, tiled=True).reshape(half, full)  8.83 us
    all_to_all x1, starting transfers between devices, shards(): terms = lax.all_to_all(term.reshape(chunk), ('x', 'y'), 0, 0, tiled=True)  7.44 us
    all_to_all x1, starting transfers between devices, shards(): lax.all_to_all(probs, ('x', 'y'), 0, 0, tiled=True).reshape(half, full)  6.23 us
    all_to_all x1, waiting for transfers between devices, shards(): terms = lax.all_to_all(term.reshape(chunk), ('x', 'y'), 0, 0, tiled=True)  5.58 us
    ppermute x2, waiting for transfers between devices, other_core(): return lax.ppermute(a, 'c', [(0, 1), (1, 0)])  4.17 us
  transfers between devices with their start and end apart: 25, of which 19 were waited for; matrix products, arithmetic and copies ran while one was open for 0% of the time, Pallas kernels for 1%

profile of v4, /device:TPU:6, one launch (start us, length us, event | category | flops | bytes accessed | tf_op | source)
XLA Modules:
  0.0 128.4 jit_solution(17612053978783372494)
XLA Ops:
  0.0 0.7 copy-done.4
  0.7 3.8 %shard_map.46 = (bf16[320,256]{1,0:T(8,128)(2,1)S(1)}, bf16[320,256]{1,0:T(8,128)(2,1)S(1)}, bf16[320,256]{1,0:T(8,128)(2,1)S(1)}, bf16[320,256]{1,0:T(8,128)(2,...) custom-call(s32[1]{0:T(128)} %bitcast.pos_ref, ...), custom_call_target="tpu_custom_call" | custom-call | flops 1006632960 | bytes 6690824 | tf_op jit(solution)/shard_map/pallas_call | solution.py:166
  4.5 7.3 %collective-permute-start = (bf16[320,256]{1,0:T(8,128)(2,1)S(1)}, bf16[320,256]{1,0:T(8,128)(2,1)S(1)}, u32[]{:S(2)}, u32[]{:S(2)}) collective-permute-start(bf16[320,256]{1,0:T(8,128)(2,1)S(1)} %get-tuple-element.31), channel_id=1, source_target_pairs={{0,1},{1,0},{64,65},{65,64},{128,129},{129,128},{192,193},{193,192... | collective-permute-start | bytes 491528 | tf_op jit(solution)/shard_map/ppermute | solution.py:181
  11.8 1.9 %collective-permute-start.1 = (bf16[320,256]{1,0:T(8,128)(2,1)S(1)}, bf16[320,256]{1,0:T(8,128)(2,1)S(1)}, u32[]{:S(2)}, u32[]{:S(2)}) collective-permute-start(bf16[320,256]{1,0:T(8,128)(2,1)S(1)} %get-tuple-element.32), channel_id=1, source_target_pairs={{0,192},{1,193},{64,1},{65,0},{128,65},{129,64},{192,129},{193,128... | collective-permute-start | bytes 491528 | tf_op jit(solution)/shard_map/ppermute | solution.py:181
  13.7 3.1 %collective-permute-start.2 = (bf16[320,256]{1,0:T(8,128)(2,1)S(1)}, bf16[320,256]{1,0:T(8,128)(2,1)S(1)}, u32[]{:S(2)}, u32[]{:S(2)}) collective-permute-start(bf16[320,256]{1,0:T(8,128)(2,1)S(1)} %get-tuple-element.33), channel_id=1, source_target_pairs={{0,65},{1,64},{64,129},{65,128},{128,193},{129,192},{192,0},{193,1... | collective-permute-start | bytes 491528 | tf_op jit(solution)/shard_map/ppermute | solution.py:181
  16.8 1.5 %collective-permute-start.3 = (bf16[320,256]{1,0:T(8,128)(2,1)S(1)}, bf16[320,256]{1,0:T(8,128)(2,1)S(1)}, u32[]{:S(2)}, u32[]{:S(2)}) collective-permute-start(bf16[320,256]{1,0:T(8,128)(2,1)S(1)} %get-tuple-element.34), channel_id=1, source_target_pairs={{0,128},{1,129},{64,192},{65,193},{128,1},{129,0},{192,65},{193,64... | collective-permute-start | bytes 491528 | tf_op jit(solution)/shard_map/ppermute | solution.py:181
  18.3 2.7 %collective-permute-start.4 = (bf16[320,256]{1,0:T(8,128)(2,1)S(1)}, bf16[320,256]{1,0:T(8,128)(2,1)S(1)}, u32[]{:S(2)}, u32[]{:S(2)}) collective-permute-start(bf16[320,256]{1,0:T(8,128)(2,1)S(1)} %get-tuple-element.35), channel_id=1, source_target_pairs={{0,129},{1,128},{64,193},{65,192},{128,0},{129,1},{192,64},{193,65... | collective-permute-start | bytes 491528 | tf_op jit(solution)/shard_map/ppermute | solution.py:181
  20.9 2.8 %collective-permute-done.refs_1_ = bf16[320,256]{1,0:T(8,128)(2,1)S(1)} collective-permute-done((bf16[320,256]{1,0:T(8,128)(2,1)S(1)}, bf16[320,256]{1,0:T(8,128)(2,1)S(1)}, u32[]{:S(2)}, u32[]{:S(2)}) %collective-permute-start) | collective-permute-done | bytes 163872 | tf_op jit(solution)/shard_map/ppermute | solution.py:181
  23.8 0.3 collective-permute-start.5
  24.1 8.8 %collective-permute-done.1.refs_2_ = bf16[320,256]{1,0:T(8,128)(2,1)S(1)} collective-permute-done((bf16[320,256]{1,0:T(8,128)(2,1)S(1)}, bf16[320,256]{1,0:T(8,128)(2,1)S(1)}, u32[]{:S(2)}, u32[]{:S(2)}) %collective-permute-start.1) | collective-permute-done | bytes 163872 | tf_op jit(solution)/shard_map/ppermute | solution.py:181
  32.9 0.0 collective-permute-start.6
  32.9 0.0 copy-done
  32.9 0.9 shard_map.47
  33.8 0.0 collective-permute-done.2.refs_3_
  33.8 3.3 %collective-permute-done.3.refs_4_ = bf16[320,256]{1,0:T(8,128)(2,1)S(1)} collective-permute-done((bf16[320,256]{1,0:T(8,128)(2,1)S(1)}, bf16[320,256]{1,0:T(8,128)(2,1)S(1)}, u32[]{:S(2)}, u32[]{:S(2)}) %collective-permute-start.3) | collective-permute-done | bytes 163872 | tf_op jit(solution)/shard_map/ppermute | solution.py:181
  37.1 0.9 collective-permute-done.4.refs_5_
  38.0 2.2 %collective-permute-done.5.refs_6_ = bf16[320,256]{1,0:T(8,128)(2,1)S(1)} collective-permute-done((bf16[320,256]{1,0:T(8,128)(2,1)S(1)}, bf16[320,256]{1,0:T(8,128)(2,1)S(1)}, u32[]{:S(2)}, u32[]{:S(2)}) %collective-permute-start.5) | collective-permute-done | bytes 163872 | tf_op jit(solution)/shard_map/ppermute | solution.py:181
  40.2 1.1 collective-permute-done.6.refs_7_
  41.3 0.1 shard_map.48.refs_8_
  41.4 0.1 collective-permute-start.7
  41.5 2.1 %collective-permute-done.7.refs_9_ = bf16[2,4,160,256]{3,2,1,0:T(8,128)(2,1)S(1)} collective-permute-done((bf16[2,4,160,256]{3,2,1,0:T(8,128)(2,1)S(1)}, bf16[2,4,160,256]{3,2,1,0:T(8,128)(2,1)S(1)}, u32[]{:S(2)}, u32[]{:S(2)}) %collective-permute-start.7) | collective-permute-done | bytes 655392 | tf_op jit(solution)/shard_map/ppermute | solution.py:186
  43.6 2.4 %shard_map.49 = bf16[640,1280]{1,0:T(8,128)(2,1)} custom-call(s32[1]{0:T(128)} %bitcast.pos_ref, bf16[320,256]{1,0:T(8,128)(2,1)S(1)} %get-tuple-element.30.refs_0_, bf16[320,256]{1,0:T(8,128)(2,1)S(1)} %collective-permute-done.refs_1_, bf16[320,256]{1,0:T(8,128)(2,1)S(1)} %collective-permute-done.1.refs_2_, ...), custom_call_target="tpu_custom_call" | custom-call | flops 838860800 | bytes 5242888 | tf_op jit(solution)/shard_map/pallas_call | solution.py:166
  46.0 7.4 %all-to-all-start = ((bf16[16,40,1280]{2,1,0:T(8,128)(2,1)}), bf16[16,40,1280]{2,1,0:T(8,128)(2,1)S(1)}, u32[]{:S(2)}, u32[]{:S(2)}) async-start(bf16[16,40,1280]{2,1,0:T(8,128)(2,1)} %bitcast.2), calls=%async_computation | async-start | bytes 3276800 | tf_op jit(solution)/shard_map/all_to_all | solution.py:242
  53.5 3.5 %collective-permute-start.8 = (bf16[160,256]{1,0:T(8,128)(2,1)S(1)}, bf16[160,256]{1,0:T(8,128)(2,1)S(1)}, u32[]{:S(2)}, u32[]{:S(2)}) collective-permute-start(bf16[160,256]{1,0:T(8,128)(2,1)S(1)} %get-tuple-element.40), channel_id=1, source_target_pairs={{0,1},{1,0},{64,65},{65,64},{128,129},{129,128},{192,193},{193,192... | collective-permute-start | bytes 245768 | tf_op jit(solution)/shard_map/ppermute | solution.py:181
  57.0 2.3 %collective-permute-start.9 = (bf16[160,256]{1,0:T(8,128)(2,1)S(1)}, bf16[160,256]{1,0:T(8,128)(2,1)S(1)}, u32[]{:S(2)}, u32[]{:S(2)}) collective-permute-start(bf16[160,256]{1,0:T(8,128)(2,1)S(1)} %get-tuple-element.41), channel_id=1, source_target_pairs={{0,192},{1,193},{64,1},{65,0},{128,65},{129,64},{192,129},{193,128... | collective-permute-start | bytes 245768 | tf_op jit(solution)/shard_map/ppermute | solution.py:181
  59.3 2.7 %collective-permute-start.10 = (bf16[160,256]{1,0:T(8,128)(2,1)S(1)}, bf16[160,256]{1,0:T(8,128)(2,1)S(1)}, u32[]{:S(2)}, u32[]{:S(2)}) collective-permute-start(bf16[160,256]{1,0:T(8,128)(2,1)S(1)} %get-tuple-element.42), channel_id=1, source_target_pairs={{0,65},{1,64},{64,129},{65,128},{128,193},{129,192},{192,0},{193,1... | collective-permute-start | bytes 245768 | tf_op jit(solution)/shard_map/ppermute | solution.py:181
  62.0 0.1 collective-permute-start.11
  62.1 2.9 %collective-permute-done.8.refs_0_.refs_1_ = bf16[160,256]{1,0:T(8,128)(2,1)S(1)} collective-permute-done((bf16[160,256]{1,0:T(8,128)(2,1)S(1)}, bf16[160,256]{1,0:T(8,128)(2,1)S(1)}, u32[]{:S(2)}, u32[]{:S(2)}) %collective-permute-start.8) | collective-permute-done | bytes 81952 | tf_op jit(solution)/shard_map/ppermute | solution.py:181
  65.0 5.4 %collective-permute-done.9.refs_1_.refs_2_ = bf16[160,256]{1,0:T(8,128)(2,1)S(1)} collective-permute-done((bf16[160,256]{1,0:T(8,128)(2,1)S(1)}, bf16[160,256]{1,0:T(8,128)(2,1)S(1)}, u32[]{:S(2)}, u32[]{:S(2)}) %collective-permute-start.9) | collective-permute-done | bytes 81952 | tf_op jit(solution)/shard_map/ppermute | solution.py:181
  70.5 0.0 collective-permute-done.10.refs_2_.refs_3_
  70.5 0.0 collective-permute-done.11.refs_3_.refs_4_
  70.5 5.6 %all-to-all-done.x_ref = bf16[16,40,1280]{2,1,0:T(8,128)(2,1)S(1)} async-done(((bf16[16,40,1280]{2,1,0:T(8,128)(2,1)}), bf16[16,40,1280]{2,1,0:T(8,128)(2,1)S(1)}, u32[]{:S(2)}, u32[]{:S(2)}) %all-to-all-start) | async-done | bytes 1638432 | tf_op jit(solution)/shard_map/all_to_all | solution.py:242
  76.1 1.5 %shard_map.50 = bf16[16,40,1280]{2,1,0:T(8,128)(2,1)} custom-call(bf16[16,40,1280]{2,1,0:T(8,128)(2,1)S(1)} %all-to-all-done.x_ref, bf16[160,256]{1,0:T(8,128)(2,1)S(1)} %collective-permute-done.8.refs_0_.refs_1_, bf16[160,256]{1,0:T(8,128)(2,1)S(1)} %collective-permute-done.9.refs_1_.refs_2_, bf16[160,256]{1,0:T(8,128)(2,1)S(1)} %collective-permute-done.10.refs_2_.refs_3_, ...), custom_call_target="tpu_custom_call" | custom-call | bytes 3932160 | tf_op jit(solution)/shard_map/pallas_call | solution.py:166
  77.6 6.2 %all-to-all-start.1 = ((bf16[16,40,1280]{2,1,0:T(8,128)(2,1)}), bf16[16,40,1280]{2,1,0:T(8,128)(2,1)S(1)}, u32[]{:S(2)}, u32[]{:S(2)}) async-start(bf16[16,40,1280]{2,1,0:T(8,128)(2,1)} %shard_map.50), calls=%async_computation.1 | async-start | bytes 3276800 | tf_op jit(solution)/shard_map/all_to_all | solution.py:250
  83.8 1.3 collective-permute-start.12
  85.1 2.8 %collective-permute-start.13 = (bf16[160,256]{1,0:T(8,128)(2,1)S(1)}, bf16[160,256]{1,0:T(8,128)(2,1)S(1)}, u32[]{:S(2)}, u32[]{:S(2)}) collective-permute-start(bf16[160,256]{1,0:T(8,128)(2,1)S(1)} %get-tuple-element.45), channel_id=1, source_target_pairs={{0,64},{1,65},{64,128},{65,129},{128,192},{129,193},{192,1},{193,0... | collective-permute-start | bytes 245768 | tf_op jit(solution)/shard_map/ppermute | solution.py:181
  87.9 0.4 collective-permute-start.14
  88.3 1.8 %collective-permute-done.12.refs_5_ = bf16[160,256]{1,0:T(8,128)(2,1)S(1)} collective-permute-done((bf16[160,256]{1,0:T(8,128)(2,1)S(1)}, bf16[160,256]{1,0:T(8,128)(2,1)S(1)}, u32[]{:S(2)}, u32[]{:S(2)}) %collective-permute-start.12) | collective-permute-done | bytes 81952 | tf_op jit(solution)/shard_map/ppermute | solution.py:181
  90.1 0.6 collective-permute-done.13.refs_6_
  90.7 1.6 %collective-permute-done.14.refs_7_ = bf16[160,256]{1,0:T(8,128)(2,1)S(1)} collective-permute-done((bf16[160,256]{1,0:T(8,128)(2,1)S(1)}, bf16[160,256]{1,0:T(8,128)(2,1)S(1)}, u32[]{:S(2)}, u32[]{:S(2)}) %collective-permute-start.14) | collective-permute-done | bytes 81952 | tf_op jit(solution)/shard_map/ppermute | solution.py:181
  92.3 0.1 shard_map.51.v_ref
  92.4 0.0 copy-start.1
  92.4 0.1 collective-permute-start.15
  92.5 2.1 %collective-permute-done.15.far_hbm = bf16[2,4,160,256]{3,2,1,0:T(8,128)(2,1)S(1)} collective-permute-done((bf16[2,4,160,256]{3,2,1,0:T(8,128)(2,1)S(1)}, bf16[2,4,160,256]{3,2,1,0:T(8,128)(2,1)S(1)}, u32[]{:S(2)}, u32[]{:S(2)}) %collective-permute-start.15) | collective-permute-done | bytes 655392 | tf_op jit(solution)/shard_map/ppermute | solution.py:186
  94.6 0.8 copy-done.2
  95.5 8.8 %all-to-all-done.1 = bf16[16,40,1280]{2,1,0:T(8,128)(2,1)S(1)} async-done(((bf16[16,40,1280]{2,1,0:T(8,128)(2,1)}), bf16[16,40,1280]{2,1,0:T(8,128)(2,1)S(1)}, u32[]{:S(2)}, u32[]{:S(2)}) %all-to-all-start.1) | async-done | bytes 1638432 | tf_op jit(solution)/shard_map/all_to_all | solution.py:250
  104.3 1.1 copy-done.3
  105.4 1.5 %shard_map.52 = (bf16[160,256]{1,0:T(8,128)(2,1)S(1)}, bf16[160,256]{1,0:T(8,128)(2,1)S(1)}, bf16[160,256]{1,0:T(8,128)(2,1)S(1)}, bf16[160,256]{1,0:T(8,128)(2,...) custom-call(s32[1]{0:T(128)} %bitcast.pos_ref, ...), custom_call_target="tpu_custom_call" | custom-call | flops 838860800 | bytes 5898248 | tf_op jit(solution)/shard_map/pallas_call | solution.py:166
  106.9 3.6 %collective-permute-start.16 = (bf16[160,256]{1,0:T(8,128)(2,1)S(1)}, bf16[160,256]{1,0:T(8,128)(2,1)S(1)}, u32[]{:S(2)}, u32[]{:S(2)}) collective-permute-start(bf16[160,256]{1,0:T(8,128)(2,1)S(1)} %get-tuple-element.48), channel_id=1, source_target_pairs={{0,1},{1,0},{64,65},{65,64},{128,129},{129,128},{192,193},{193,192... | collective-permute-start | bytes 245768 | tf_op jit(solution)/shard_map/ppermute | solution.py:181
  110.6 2.3 %collective-permute-start.17 = (bf16[160,256]{1,0:T(8,128)(2,1)S(1)}, bf16[160,256]{1,0:T(8,128)(2,1)S(1)}, u32[]{:S(2)}, u32[]{:S(2)}) collective-permute-start(bf16[160,256]{1,0:T(8,128)(2,1)S(1)} %get-tuple-element.49), channel_id=1, source_target_pairs={{0,192},{1,193},{64,1},{65,0},{128,65},{129,64},{192,129},{193,128... | collective-permute-start | bytes 245768 | tf_op jit(solution)/shard_map/ppermute | solution.py:181
  112.9 2.7 %collective-permute-start.18 = (bf16[160,256]{1,0:T(8,128)(2,1)S(1)}, bf16[160,256]{1,0:T(8,128)(2,1)S(1)}, u32[]{:S(2)}, u32[]{:S(2)}) collective-permute-start(bf16[160,256]{1,0:T(8,128)(2,1)S(1)} %get-tuple-element.50), channel_id=1, source_target_pairs={{0,65},{1,64},{64,129},{65,128},{128,193},{129,192},{192,0},{193,1... | collective-permute-start | bytes 245768 | tf_op jit(solution)/shard_map/ppermute | solution.py:181
  115.6 0.1 collective-permute-start.19
  115.7 4.1 %collective-permute-start.20 = (bf16[160,256]{1,0:T(8,128)(2,1)S(1)}, bf16[160,256]{1,0:T(8,128)(2,1)S(1)}, u32[]{:S(2)}, u32[]{:S(2)}) collective-permute-start(bf16[160,256]{1,0:T(8,128)(2,1)S(1)} %get-tuple-element.52), channel_id=1, source_target_pairs={{0,129},{1,128},{64,193},{65,192},{128,0},{129,1},{192,64},{193,65... | collective-permute-start | bytes 245768 | tf_op jit(solution)/shard_map/ppermute | solution.py:181
  119.7 0.0 collective-permute-done.16.refs_1_
  119.7 0.0 collective-permute-start.21
  119.7 2.4 %collective-permute-done.17.refs_2_ = bf16[160,256]{1,0:T(8,128)(2,1)S(1)} collective-permute-done((bf16[160,256]{1,0:T(8,128)(2,1)S(1)}, bf16[160,256]{1,0:T(8,128)(2,1)S(1)}, u32[]{:S(2)}, u32[]{:S(2)}) %collective-permute-start.17) | collective-permute-done | bytes 81952 | tf_op jit(solution)/shard_map/ppermute | solution.py:181
  122.1 0.9 collective-permute-start.22
  123.0 0.0 collective-permute-done.18.refs_3_
  123.0 0.0 collective-permute-done.19.refs_4_
  123.0 1.4 %collective-permute-done.20.refs_5_ = bf16[160,256]{1,0:T(8,128)(2,1)S(1)} collective-permute-done((bf16[160,256]{1,0:T(8,128)(2,1)S(1)}, bf16[160,256]{1,0:T(8,128)(2,1)S(1)}, u32[]{:S(2)}, u32[]{:S(2)}) %collective-permute-start.20) | collective-permute-done | bytes 81952 | tf_op jit(solution)/shard_map/ppermute | solution.py:181
  124.4 1.0 collective-permute-done.21.refs_6_
  125.4 1.2 collective-permute-done.22.refs_7_
  126.6 0.0 copy-done.1
  126.6 1.7 %shard_map.53 = f32[4,160,768]{2,1,0:T(8,128)} custom-call(s32[1]{0:T(128)} %bitcast.pos_ref, bf16[512,768]{1,0:T(8,128)(2,1)S(1)} %copy-done.1, bf16[160,256]{1,0:T(8,128)(2,1)S(1)} %get-tuple-element.47.refs_0_, bf16[160,256]{1,0:T(8,128)(2,1)S(1)} %collective-permute-done.16.refs_1_, bf16[160,256]{1,0:T(8,128)(2,1)S(1)} %collective-permute-done.17.refs_2_, ...), custom_call_target="tpu_custom_call" | custom-call | flops 503316480 | bytes 2883592 | tf_op jit(solution)/shard_map/pallas_call | solution.py:166
  (4 shorter events, 0.0 us)
Async XLA Ops:
  0.0 0.7 copy-start.4
  0.7 32.3 %copy-start = (bf16[768,3,512]{2,0,1:T(8,128)(2,1)S(1)}, bf16[768,3,512]{2,0,1:T(8,128)(2,1)}, u32[]{:S(2)}) copy-start(bf16[768,3,512]{2,0,1:T(8,128)(2,1)} %param.6) | copy-start | bytes 7077892
  4.5 19.3 %collective-permute-start = (bf16[320,256]{1,0:T(8,128)(2,1)S(1)}, bf16[320,256]{1,0:T(8,128)(2,1)S(1)}, u32[]{:S(2)}, u32[]{:S(2)}) collective-permute-start(bf16[320,256]{1,0:T(8,128)(2,1)S(1)} %get-tuple-element.31), channel_id=1, source_target_pairs={{0,1},{1,0},{64,65},{65,64},{128,129},{129,128},{192,193},{193,192... | collective-permute-start | bytes 491528 | tf_op jit(solution)/shard_map/ppermute | solution.py:181
  11.8 21.2 %collective-permute-start.1 = (bf16[320,256]{1,0:T(8,128)(2,1)S(1)}, bf16[320,256]{1,0:T(8,128)(2,1)S(1)}, u32[]{:S(2)}, u32[]{:S(2)}) collective-permute-start(bf16[320,256]{1,0:T(8,128)(2,1)S(1)} %get-tuple-element.32), channel_id=1, source_target_pairs={{0,192},{1,193},{64,1},{65,0},{128,65},{129,64},{192,129},{193,128... | collective-permute-start | bytes 491528 | tf_op jit(solution)/shard_map/ppermute | solution.py:181
  13.7 20.1 %collective-permute-start.2 = (bf16[320,256]{1,0:T(8,128)(2,1)S(1)}, bf16[320,256]{1,0:T(8,128)(2,1)S(1)}, u32[]{:S(2)}, u32[]{:S(2)}) collective-permute-start(bf16[320,256]{1,0:T(8,128)(2,1)S(1)} %get-tuple-element.33), channel_id=1, source_target_pairs={{0,65},{1,64},{64,129},{65,128},{128,193},{129,192},{192,0},{193,1... | collective-permute-start | bytes 491528 | tf_op jit(solution)/shard_map/ppermute | solution.py:181
  16.8 20.4 %collective-permute-start.3 = (bf16[320,256]{1,0:T(8,128)(2,1)S(1)}, bf16[320,256]{1,0:T(8,128)(2,1)S(1)}, u32[]{:S(2)}, u32[]{:S(2)}) collective-permute-start(bf16[320,256]{1,0:T(8,128)(2,1)S(1)} %get-tuple-element.34), channel_id=1, source_target_pairs={{0,128},{1,129},{64,192},{65,193},{128,1},{129,0},{192,65},{193,64... | collective-permute-start | bytes 491528 | tf_op jit(solution)/shard_map/ppermute | solution.py:181
  18.3 19.8 %collective-permute-start.4 = (bf16[320,256]{1,0:T(8,128)(2,1)S(1)}, bf16[320,256]{1,0:T(8,128)(2,1)S(1)}, u32[]{:S(2)}, u32[]{:S(2)}) collective-permute-start(bf16[320,256]{1,0:T(8,128)(2,1)S(1)} %get-tuple-element.35), channel_id=1, source_target_pairs={{0,129},{1,128},{64,193},{65,192},{128,0},{129,1},{192,64},{193,65... | collective-permute-start | bytes 491528 | tf_op jit(solution)/shard_map/ppermute | solution.py:181
  23.8 16.4 %collective-permute-start.5 = (bf16[320,256]{1,0:T(8,128)(2,1)S(1)}, bf16[320,256]{1,0:T(8,128)(2,1)S(1)}, u32[]{:S(2)}, u32[]{:S(2)}) collective-permute-start(bf16[320,256]{1,0:T(8,128)(2,1)S(1)} %get-tuple-element.36), channel_id=1, source_target_pairs={{0,64},{1,65},{64,128},{65,129},{128,192},{129,193},{192,1},{193,0... | collective-permute-start | bytes 491528 | tf_op jit(solution)/shard_map/ppermute | solution.py:181
  32.9 8.4 %collective-permute-start.6 = (bf16[320,256]{1,0:T(8,128)(2,1)S(1)}, bf16[320,256]{1,0:T(8,128)(2,1)S(1)}, u32[]{:S(2)}, u32[]{:S(2)}) collective-permute-start(bf16[320,256]{1,0:T(8,128)(2,1)S(1)} %get-tuple-element.37), channel_id=1, source_target_pairs={{0,193},{1,192},{64,0},{65,1},{128,64},{129,65},{192,128},{193,129... | collective-permute-start | bytes 491528 | tf_op jit(solution)/shard_map/ppermute | solution.py:181
  41.4 2.2 %collective-permute-start.7 = (bf16[2,4,160,256]{3,2,1,0:T(8,128)(2,1)S(1)}, bf16[2,4,160,256]{3,2,1,0:T(8,128)(2,1)S(1)}, u32[]{:S(2)}, u32[]{:S(2)}) collective-permute-start(bf16[2,4,160,256]{3,2,1,0:T(8,128)(2,1)S(1)} %shard_map.48.refs_8_), channel_id=1, source_target_pairs={{0,32},{32,0},{1,33},{33,1},{2,34},{34,2},{3,35},{35,3},{4,36},{36... | collective-permute-start | bytes 1966088 | tf_op jit(solution)/shard_map/ppermute | solution.py:186
  46.0 30.0 %all-to-all-start = ((bf16[16,40,1280]{2,1,0:T(8,128)(2,1)}), bf16[16,40,1280]{2,1,0:T(8,128)(2,1)S(1)}, u32[]{:S(2)}, u32[]{:S(2)}) async-start(bf16[16,40,1280]{2,1,0:T(8,128)(2,1)} %bitcast.2), calls=%async_computation | async-start | bytes 3276800 | tf_op jit(solution)/shard_map/all_to_all | solution.py:242
  53.5 11.6 %collective-permute-start.8 = (bf16[160,256]{1,0:T(8,128)(2,1)S(1)}, bf16[160,256]{1,0:T(8,128)(2,1)S(1)}, u32[]{:S(2)}, u32[]{:S(2)}) collective-permute-start(bf16[160,256]{1,0:T(8,128)(2,1)S(1)} %get-tuple-element.40), channel_id=1, source_target_pairs={{0,1},{1,0},{64,65},{65,64},{128,129},{129,128},{192,193},{193,192... | collective-permute-start | bytes 245768 | tf_op jit(solution)/shard_map/ppermute | solution.py:181
  57.0 13.5 %collective-permute-start.9 = (bf16[160,256]{1,0:T(8,128)(2,1)S(1)}, bf16[160,256]{1,0:T(8,128)(2,1)S(1)}, u32[]{:S(2)}, u32[]{:S(2)}) collective-permute-start(bf16[160,256]{1,0:T(8,128)(2,1)S(1)} %get-tuple-element.41), channel_id=1, source_target_pairs={{0,192},{1,193},{64,1},{65,0},{128,65},{129,64},{192,129},{193,128... | collective-permute-start | bytes 245768 | tf_op jit(solution)/shard_map/ppermute | solution.py:181
  59.3 11.1 %collective-permute-start.10 = (bf16[160,256]{1,0:T(8,128)(2,1)S(1)}, bf16[160,256]{1,0:T(8,128)(2,1)S(1)}, u32[]{:S(2)}, u32[]{:S(2)}) collective-permute-start(bf16[160,256]{1,0:T(8,128)(2,1)S(1)} %get-tuple-element.42), channel_id=1, source_target_pairs={{0,65},{1,64},{64,129},{65,128},{128,193},{129,192},{192,0},{193,1... | collective-permute-start | bytes 245768 | tf_op jit(solution)/shard_map/ppermute | solution.py:181
  62.0 8.4 %collective-permute-start.11 = (bf16[160,256]{1,0:T(8,128)(2,1)S(1)}, bf16[160,256]{1,0:T(8,128)(2,1)S(1)}, u32[]{:S(2)}, u32[]{:S(2)}) collective-permute-start(bf16[160,256]{1,0:T(8,128)(2,1)S(1)} %get-tuple-element.43), channel_id=1, source_target_pairs={{0,128},{1,129},{64,192},{65,193},{128,1},{129,0},{192,65},{193,64... | collective-permute-start | bytes 245768 | tf_op jit(solution)/shard_map/ppermute | solution.py:181
  77.6 26.7 %all-to-all-start.1 = ((bf16[16,40,1280]{2,1,0:T(8,128)(2,1)}), bf16[16,40,1280]{2,1,0:T(8,128)(2,1)S(1)}, u32[]{:S(2)}, u32[]{:S(2)}) async-start(bf16[16,40,1280]{2,1,0:T(8,128)(2,1)} %shard_map.50), calls=%async_computation.1 | async-start | bytes 3276800 | tf_op jit(solution)/shard_map/all_to_all | solution.py:250
  83.8 6.3 %collective-permute-start.12 = (bf16[160,256]{1,0:T(8,128)(2,1)S(1)}, bf16[160,256]{1,0:T(8,128)(2,1)S(1)}, u32[]{:S(2)}, u32[]{:S(2)}) collective-permute-start(bf16[160,256]{1,0:T(8,128)(2,1)S(1)} %get-tuple-element.44), channel_id=1, source_target_pairs={{0,129},{1,128},{64,193},{65,192},{128,0},{129,1},{192,64},{193,65... | collective-permute-start | bytes 245768 | tf_op jit(solution)/shard_map/ppermute | solution.py:181
  85.1 5.7 %collective-permute-start.13 = (bf16[160,256]{1,0:T(8,128)(2,1)S(1)}, bf16[160,256]{1,0:T(8,128)(2,1)S(1)}, u32[]{:S(2)}, u32[]{:S(2)}) collective-permute-start(bf16[160,256]{1,0:T(8,128)(2,1)S(1)} %get-tuple-element.45), channel_id=1, source_target_pairs={{0,64},{1,65},{64,128},{65,129},{128,192},{129,193},{192,1},{193,0... | collective-permute-start | bytes 245768 | tf_op jit(solution)/shard_map/ppermute | solution.py:181
  87.9 4.4 %collective-permute-start.14 = (bf16[160,256]{1,0:T(8,128)(2,1)S(1)}, bf16[160,256]{1,0:T(8,128)(2,1)S(1)}, u32[]{:S(2)}, u32[]{:S(2)}) collective-permute-start(bf16[160,256]{1,0:T(8,128)(2,1)S(1)} %get-tuple-element.46), channel_id=1, source_target_pairs={{0,193},{1,192},{64,0},{65,1},{128,64},{129,65},{192,128},{193,129... | collective-permute-start | bytes 245768 | tf_op jit(solution)/shard_map/ppermute | solution.py:181
  92.4 34.1 %copy-start.1 = (bf16[512,768]{1,0:T(8,128)(2,1)S(1)}, bf16[512,768]{1,0:T(8,128)(2,1)}, u32[]{:S(2)}) copy-start(bf16[512,768]{1,0:T(8,128)(2,1)} %w_ref.1) | copy-start | bytes 2359300
  92.4 2.2 %collective-permute-start.15 = (bf16[2,4,160,256]{3,2,1,0:T(8,128)(2,1)S(1)}, bf16[2,4,160,256]{3,2,1,0:T(8,128)(2,1)S(1)}, u32[]{:S(2)}, u32[]{:S(2)}) collective-permute-start(bf16[2,4,160,256]{3,2,1,0:T(8,128)(2,1)S(1)} %shard_map.51.v_ref), channel_id=1, source_target_pairs={{0,32},{32,0},{1,33},{33,1},{2,34},{34,2},{3,35},{35,3},{4,36},{36... | collective-permute-start | bytes 1966088 | tf_op jit(solution)/shard_map/ppermute | solution.py:186
  94.6 0.8 copy-start.2
  104.3 1.1 copy-start.3
  106.9 12.8 %collective-permute-start.16 = (bf16[160,256]{1,0:T(8,128)(2,1)S(1)}, bf16[160,256]{1,0:T(8,128)(2,1)S(1)}, u32[]{:S(2)}, u32[]{:S(2)}) collective-permute-start(bf16[160,256]{1,0:T(8,128)(2,1)S(1)} %get-tuple-element.48), channel_id=1, source_target_pairs={{0,1},{1,0},{64,65},{65,64},{128,129},{129,128},{192,193},{193,192... | collective-permute-start | bytes 245768 | tf_op jit(solution)/shard_map/ppermute | solution.py:181
  110.6 11.6 %collective-permute-start.17 = (bf16[160,256]{1,0:T(8,128)(2,1)S(1)}, bf16[160,256]{1,0:T(8,128)(2,1)S(1)}, u32[]{:S(2)}, u32[]{:S(2)}) collective-permute-start(bf16[160,256]{1,0:T(8,128)(2,1)S(1)} %get-tuple-element.49), channel_id=1, source_target_pairs={{0,192},{1,193},{64,1},{65,0},{128,65},{129,64},{192,129},{193,128... | collective-permute-start | bytes 245768 | tf_op jit(solution)/shard_map/ppermute | solution.py:181
  112.9 10.1 %collective-permute-start.18 = (bf16[160,256]{1,0:T(8,128)(2,1)S(1)}, bf16[160,256]{1,0:T(8,128)(2,1)S(1)}, u32[]{:S(2)}, u32[]{:S(2)}) collective-permute-start(bf16[160,256]{1,0:T(8,128)(2,1)S(1)} %get-tuple-element.50), channel_id=1, source_target_pairs={{0,65},{1,64},{64,129},{65,128},{128,193},{129,192},{192,0},{193,1... | collective-permute-start | bytes 245768 | tf_op jit(solution)/shard_map/ppermute | solution.py:181
  115.6 7.4 %collective-permute-start.19 = (bf16[160,256]{1,0:T(8,128)(2,1)S(1)}, bf16[160,256]{1,0:T(8,128)(2,1)S(1)}, u32[]{:S(2)}, u32[]{:S(2)}) collective-permute-start(bf16[160,256]{1,0:T(8,128)(2,1)S(1)} %get-tuple-element.51), channel_id=1, source_target_pairs={{0,128},{1,129},{64,192},{65,193},{128,1},{129,0},{192,65},{193,64... | collective-permute-start | bytes 245768 | tf_op jit(solution)/shard_map/ppermute | solution.py:181
  115.7 8.7 %collective-permute-start.20 = (bf16[160,256]{1,0:T(8,128)(2,1)S(1)}, bf16[160,256]{1,0:T(8,128)(2,1)S(1)}, u32[]{:S(2)}, u32[]{:S(2)}) collective-permute-start(bf16[160,256]{1,0:T(8,128)(2,1)S(1)} %get-tuple-element.52), channel_id=1, source_target_pairs={{0,129},{1,128},{64,193},{65,192},{128,0},{129,1},{192,64},{193,65... | collective-permute-start | bytes 245768 | tf_op jit(solution)/shard_map/ppermute | solution.py:181
  119.7 5.7 %collective-permute-start.21 = (bf16[160,256]{1,0:T(8,128)(2,1)S(1)}, bf16[160,256]{1,0:T(8,128)(2,1)S(1)}, u32[]{:S(2)}, u32[]{:S(2)}) collective-permute-start(bf16[160,256]{1,0:T(8,128)(2,1)S(1)} %get-tuple-element.53), channel_id=1, source_target_pairs={{0,64},{1,65},{64,128},{65,129},{128,192},{129,193},{192,1},{193,0... | collective-permute-start | bytes 245768 | tf_op jit(solution)/shard_map/ppermute | solution.py:181
  122.1 4.4 %collective-permute-start.22 = (bf16[160,256]{1,0:T(8,128)(2,1)S(1)}, bf16[160,256]{1,0:T(8,128)(2,1)S(1)}, u32[]{:S(2)}, u32[]{:S(2)}) collective-permute-start(bf16[160,256]{1,0:T(8,128)(2,1)S(1)} %get-tuple-element.54), channel_id=1, source_target_pairs={{0,193},{1,192},{64,0},{65,1},{128,64},{129,65},{192,128},{193,129... | collective-permute-start | bytes 245768 | tf_op jit(solution)/shard_map/ppermute | solution.py:181

commit v5 on v4

--- a/solution.py
+++ b/solution.py
@@ -20,6 +20,9 @@
 HBM = pl.BlockSpec(memory_space=pltpu.HBM)
 ANY = pl.BlockSpec(memory_space=pl.ANY)
 SMEM = pl.BlockSpec(memory_space=pltpu.SMEM)
+X_STEPS = (0, 2, 1, 3)
+Y_STEPS = (0, 1, 3, 2)
+EARLY = 6
 MIB = 1024 * 1024
 
 
@@ -84,7 +87,7 @@
     length = out.shape[2]
     for part, s in zip(parts, STEPS):
         src = lax.rem(pos + RING - s, RING)
-        out[lax.div(src, Z), lax.rem(src, Z)] = part[first : first + length]
+        out[lax.div(src, Z), -s % Z] = part[first : first + length]
 
 
 def place_kernel(count, pos_ref, *refs):
@@ -96,19 +99,25 @@
     put_by_sender(pos_ref[0], parts, q.shape[2], q)
     length = k_ref.shape[2]
     half = k_ref.shape[1] * length
+    rows = terms.shape[1]
     copies = []
-    for z in range(Z):
-        rows = slice(z * length, (z + 1) * length)
-        for side, keys in enumerate((k_ref, k_far)):
-            total = None
-            for w in range(W):
-                term = lax.dot_general(
-                    q[w, z], keys[w].reshape(half, -1), (((1,), (1,)), ((), ())), preferred_element_type=F32
-                )
-                total = term if total is None else total + term
-            terms[rows, side * half : (side + 1) * half] = total.astype(BF)
-        copies.append(pltpu.make_async_copy(terms.at[rows], out_hbm.at[rows], sem.at[z]))
-        copies[z].start()
+    for side, keys in enumerate((k_ref, k_far)):
+        total = None
+        for w in range(W):
+            term = lax.dot_general(
+                q[w].reshape(half, -1),
+                keys[w].reshape(half, -1),
+                (((1,), (1,)), ((), ())),
+                preferred_element_type=F32,
+            )
+            total = term if total is None else total + term
+        columns = slice(side * half, (side + 1) * half)
+        for t in range(Z):
+            for x in range(X):
+                first = t * length + x * rows
+                terms[x * Y + t, :, columns] = total[first : first + rows].astype(BF)
+        copies.append(pltpu.make_async_copy(terms.at[:, :, columns], out_hbm.at[:, :, columns], sem.at[side]))
+        copies[side].start()
     for copy in copies:
         copy.wait()
 
@@ -119,34 +128,32 @@
     for i in range(1, x_ref.shape[0]):
         logits = logits + x_ref[i].astype(F32)
     expo = jnp.exp(logits * scale)
-    probs = (expo / jnp.sum(expo, axis=-1, keepdims=True)).astype(BF)
-    for i in range(out_ref.shape[0]):
-        out_ref[i] = probs
-
-
-def context_kernel(pos_ref, p_ref, v_ref, far_hbm, *refs):
-    outs, (mine, v_far, sem) = refs[:RING], refs[RING:]
-    copy = pltpu.make_async_copy(far_hbm, v_far, sem)
-    copy.start()
+    out_ref[...] = (expo / jnp.sum(expo, axis=-1, keepdims=True)).astype(BF)
+
+
+def rows_kernel(pos_ref, *refs):
+    parts, out = refs[:-1], refs[-1]
+    for s, part in zip(X_STEPS, parts):
+        out[lax.rem(pos_ref[1] + X - s, X)] = part[...]
+
+
+def context_kernel(step, pos_ref, p_ref, v_ref, v_far, near, far, mine):
     half = v_ref.shape[1] * v_ref.shape[2]
-    length = v_ref.shape[2]
-    near = [jnp.dot(p_ref[:, :half], v_ref[w].reshape(half, -1), preferred_element_type=F32) for w in range(W)]
-    copy.wait()
     for w in range(W):
-        a = near[w] + jnp.dot(p_ref[:, half:], v_far[w].reshape(half, -1), preferred_element_type=F32)
-        a = a.astype(BF)
-        for z in range(Z):
-            mine[w * Z + z] = a[z * length : (z + 1) * length]
-    pos = pos_ref[0]
-    for i, s in enumerate(STEPS):
-        outs[i][...] = mine[lax.rem(pos + s, RING)]
+        a = jnp.dot(p_ref[:, :half], v_ref[w].reshape(half, -1), preferred_element_type=F32)
+        a = a + jnp.dot(p_ref[:, half:], v_far[w].reshape(half, -1), preferred_element_type=F32)
+        mine[w] = a.astype(BF)
+    block = lax.rem(pos_ref[2] + Y - step, Y)
+    run = lax.div(lax.rem(pos_ref[0] + block, RING), Z)
+    near[...] = mine[run]
+    far[...] = mine[1 - run]
 
 
 def mix_kernel(pos_ref, w_ref, *refs):
     parts, (out_hbm, rows, mixed, sem) = refs[:RING], refs[RING:]
-    pos = pos_ref[0]
-    for i, s in enumerate(STEPS):
-        h = head_at(pos + RING - s)
+    for i in range(RING):
+        block = lax.rem(pos_ref[2] + Y - Y_STEPS[i // W], Y)
+        h = head_at(pos_ref[0] + RING - block - Z * (i % W))
         rows[i * HEAD_DIM : (i + 1) * HEAD_DIM] = w_ref[pl.ds(pl.multiple_of(h * HEAD_DIM, HEAD_DIM), HEAD_DIM)]
     copies = []
     for r in range(mixed.shape[0]):
@@ -182,6 +189,19 @@
     return got
 
 
+def along(a, axis, size, s):
+    return lax.ppermute(a, axis, [(i, (i + s) % size) for i in range(size)]) if s else a
+
+
+def to_block(part, step, more):
+    pairs = []
+    for i in range(Z * Y * W):
+        z, y, w = i // (Y * W), i // W % Y, i % W
+        there = index_of((place(z * W + w) + (y - step) % Y + more) % RING)
+        pairs.append((i, (there // W * Y + y) * W + there % W))
+    return lax.ppermute(part, ("z", "y", "w"), pairs)
+
+
 def other_core(a):
     return lax.ppermute(a, "c", [(0, 1), (1, 0)])
 
@@ -190,7 +210,8 @@
     seqs, length, width = tokens.shape
     inner = w_qkv.shape[2]
     lanes = seqs * HEAD_DIM
-    pos = (lax.axis_index("w") * Z + lax.axis_index("z")).astype(jnp.int32).reshape(1)
+    ring = lax.axis_index("w") * Z + lax.axis_index("z")
+    pos = jnp.stack([ring, lax.axis_index("x"), lax.axis_index("y")]).astype(jnp.int32)
     pair = jax.ShapeDtypeStruct((2 * length, lanes), BF)
     block = jax.ShapeDtypeStruct((length, lanes), BF)
     whole = jax.ShapeDtypeStruct((W, Z, length, lanes), BF)
@@ -230,36 +251,39 @@
     keys = call(functools.partial(place_kernel, RING), whole, [pos, *both, values[0]], unread=(1 + RING,))
     keys_far = other_core(keys)
     values = along_ring(values)
+    chunk = (PLANE, half // PLANE, full)
     term = call(
         logits_kernel,
-        jax.ShapeDtypeStruct((half, full), BF),
+        jax.ShapeDtypeStruct(chunk, BF),
         [pos, *both, keys, keys_far],
-        [pltpu.VMEM(whole.shape, BF), pltpu.VMEM((half, full), BF), dma((Z,))],
+        [pltpu.VMEM(whole.shape, BF), pltpu.VMEM(chunk, BF), dma((CORE,))],
         flops=2 * half * full * W * lanes,
         out_specs=HBM,
     )
-    chunk = (PLANE, half // PLANE, full)
-    terms = lax.all_to_all(term.reshape(chunk), ("x", "y"), 0, 0, tiled=True)
-    early = values[1:5]
+    terms = lax.all_to_all(term, ("x", "y"), 0, 0, tiled=True)
     probs = call(
         functools.partial(probs_kernel, scale),
-        jax.ShapeDtypeStruct(chunk, BF),
-        [terms, *early],
-        unread=range(1, 5),
-    )
-    probs = lax.all_to_all(probs, ("x", "y"), 0, 0, tiled=True).reshape(half, full)
+        jax.ShapeDtypeStruct(chunk[1:], BF),
+        [terms, *values[1:EARLY]],
+        unread=range(1, EARLY),
+    )
     values = call(functools.partial(place_kernel, RING), whole, [pos, *values])
     values_far = other_core(values)
-    context = call(
-        context_kernel,
-        [block] * RING,
-        [pos, probs, values, values_far],
-        [pltpu.VMEM((RING, length, lanes), BF), pltpu.VMEM(whole.shape, BF), dma],
-        flops=2 * half * full * W * lanes,
-        hbm=(3,),
-        vmem=20,
-    )
-    context = along_ring(context)
+    rows = call(
+        rows_kernel,
+        jax.ShapeDtypeStruct((X, *chunk[1:]), BF),
+        [pos, *(along(probs, "x", X, s) for s in X_STEPS)],
+    ).reshape(length, full)
+    context = []
+    for step in Y_STEPS:
+        near, far = call(
+            functools.partial(context_kernel, step),
+            [block] * 2,
+            [pos, along(rows, "y", Y, step), values, values_far],
+            [pltpu.VMEM((W, length, lanes), BF)],
+            flops=2 * length * full * W * lanes,
+        )
+        context += [to_block(near, step, 0), to_block(far, step, Z)]
     return call(
         mix_kernel,
         jax.ShapeDtypeStruct((seqs, length, width), F32),

time: 129 us -> 134 us (1.039)
  starting transfers between devices: 57.4 us -> 71.9 us
  waiting for transfers between devices: 56.1 us -> 41.8 us
  Pallas kernels: 12 us -> 17.2 us
  local copies, waits for them, and re-layouts: 2.61 us -> 0.86 us
    ppermute x0 -> x14, starting transfers between devices: none -> 34.6 us  [the longest x8 26.7 us: to_block(): return lax.ppermute(part, ('z', 'y', 'w'), pairs)]
    ppermute x21 -> x14, starting transfers between devices: 43.6 us -> 29.5 us  [along_ring(): got.append(lax.ppermute(part, ('z', 'w'), pairs) if s else part)]
    all_to_all x2 -> x1, waiting for transfers between devices: 14.4 us -> 0.79 us  [shards(): terms = lax.all_to_all(term, ('x', 'y'), 0, 0, tiled=True)]
    ppermute x0 -> x14, waiting for transfers between devices: none -> 12.7 us  [the longest x6 9.64 us: along(): lax.ppermute(a, axis, [(i, (i + s) % size) for i in range(size)])]
    ppermute x21 -> x14, waiting for transfers between devices: 37.5 us -> 26.2 us  [along_ring(): got.append(lax.ppermute(part, ('z', 'w'), pairs) if s else part)]
    all_to_all x2 -> x1, starting transfers between devices: 13.7 us -> 7.57 us  [shards(): terms = lax.all_to_all(term, ('x', 'y'), 0, 0, tiled=True)]
    pallas_call x8 -> x12, Pallas kernels: 12 us -> 17.2 us  [call(): pl.pallas_call(kernel, out_shape=out_shape, in_specs=specs, out_specs=out...]
    ppermute x2, waiting for transfers between devices: 4.17 us -> 2.09 us  [other_core(): return lax.ppermute(a, 'c', [(0, 1), (1, 0)])]
  transfers between devices with their start and end apart: 25 -> 31, of which waited for: 19 -> 20; matrix products, arithmetic and copies ran while one was open for 0% -> 0% of each run, Pallas kernels for 1% -> 6%
where the time goes in v5:
time: 134 us; the launch traced here: 132 us
  starting transfers between devices  71.9 us (54%)
  waiting for transfers between devices  41.8 us (31%)
  Pallas kernels  17.2 us (13%)
    ppermute x14, starting transfers between devices, along_ring(): got.append(lax.ppermute(part, ('z', 'w'), pairs) if s else part)  29.5 us
    ppermute x8, starting transfers between devices, to_block(): return lax.ppermute(part, ('z', 'y', 'w'), pairs)  26.7 us
    ppermute x14, waiting for transfers between devices, along_ring(): got.append(lax.ppermute(part, ('z', 'w'), pairs) if s else part)  26.2 us
    pallas_call x12, Pallas kernels, call(): pl.pallas_call(kernel, out_shape=out_shape, in_specs=specs, out_specs=out...  17.2 us
    ppermute x6, waiting for transfers between devices, along(): lax.ppermute(a, axis, [(i, (i + s) % size) for i in range(size)])  9.64 us
    ppermute x6, starting transfers between devices, along(): lax.ppermute(a, axis, [(i, (i + s) % size) for i in range(size)])  7.94 us
    all_to_all x1, starting transfers between devices, shards(): terms = lax.all_to_all(term, ('x', 'y'), 0, 0, tiled=True)  7.57 us
    ppermute x8, waiting for transfers between devices, to_block(): return lax.ppermute(part, ('z', 'y', 'w'), pairs)  3.07 us
  transfers between devices with their start and end apart: 31, of which 20 were waited for; matrix products, arithmetic and copies ran while one was open for 0% of the time, Pallas kernels for 6%

profile of v5, /device:TPU:6, one launch (start us, length us, event | category | flops | bytes accessed | tf_op | source)
XLA Modules:
  0.0 132.2 jit_solution(5430889962498961441)
XLA Ops:
  0.0 0.1 pad_add_fusion.pos_ref
  0.1 0.8 copy-done.6
  0.9 4.2 %shard_map.46 = (bf16[320,256]{1,0:T(8,128)(2,1)S(1)}, bf16[320,256]{1,0:T(8,128)(2,1)S(1)}, bf16[320,256]{1,0:T(8,128)(2,1)S(1)}, bf16[320,256]{1,0:T(8,128)(2,...) custom-call(s32[3]{0:T(128)S(1)} %pad_add_fusion.pos_ref, ...), custom_call_target="tpu_custom_call" | custom-call | flops 1006632960 | bytes 6690840 | tf_op jit(solution)/shard_map/pallas_call | solution.py:173
  5.1 7.3 %collective-permute-start = (bf16[320,256]{1,0:T(8,128)(2,1)S(1)}, bf16[320,256]{1,0:T(8,128)(2,1)S(1)}, u32[]{:S(2)}, u32[]{:S(2)}) collective-permute-start(bf16[320,256]{1,0:T(8,128)(2,1)S(1)} %get-tuple-element.31), channel_id=1, source_target_pairs={{0,1},{1,0},{64,65},{65,64},{128,129},{129,128},{192,193},{193,192... | collective-permute-start | bytes 491528 | tf_op jit(solution)/shard_map/ppermute | solution.py:188
  12.4 1.9 %collective-permute-start.1 = (bf16[320,256]{1,0:T(8,128)(2,1)S(1)}, bf16[320,256]{1,0:T(8,128)(2,1)S(1)}, u32[]{:S(2)}, u32[]{:S(2)}) collective-permute-start(bf16[320,256]{1,0:T(8,128)(2,1)S(1)} %get-tuple-element.32), channel_id=1, source_target_pairs={{0,192},{1,193},{64,1},{65,0},{128,65},{129,64},{192,129},{193,128... | collective-permute-start | bytes 491528 | tf_op jit(solution)/shard_map/ppermute | solution.py:188
  14.3 3.1 %collective-permute-start.2 = (bf16[320,256]{1,0:T(8,128)(2,1)S(1)}, bf16[320,256]{1,0:T(8,128)(2,1)S(1)}, u32[]{:S(2)}, u32[]{:S(2)}) collective-permute-start(bf16[320,256]{1,0:T(8,128)(2,1)S(1)} %get-tuple-element.33), channel_id=1, source_target_pairs={{0,65},{1,64},{64,129},{65,128},{128,193},{129,192},{192,0},{193,1... | collective-permute-start | bytes 491528 | tf_op jit(solution)/shard_map/ppermute | solution.py:188
  17.4 1.5 %collective-permute-start.3 = (bf16[320,256]{1,0:T(8,128)(2,1)S(1)}, bf16[320,256]{1,0:T(8,128)(2,1)S(1)}, u32[]{:S(2)}, u32[]{:S(2)}) collective-permute-start(bf16[320,256]{1,0:T(8,128)(2,1)S(1)} %get-tuple-element.34), channel_id=1, source_target_pairs={{0,128},{1,129},{64,192},{65,193},{128,1},{129,0},{192,65},{193,64... | collective-permute-start | bytes 491528 | tf_op jit(solution)/shard_map/ppermute | solution.py:188
  18.9 2.7 %collective-permute-start.4 = (bf16[320,256]{1,0:T(8,128)(2,1)S(1)}, bf16[320,256]{1,0:T(8,128)(2,1)S(1)}, u32[]{:S(2)}, u32[]{:S(2)}) collective-permute-start(bf16[320,256]{1,0:T(8,128)(2,1)S(1)} %get-tuple-element.35), channel_id=1, source_target_pairs={{0,129},{1,128},{64,193},{65,192},{128,0},{129,1},{192,64},{193,65... | collective-permute-start | bytes 491528 | tf_op jit(solution)/shard_map/ppermute | solution.py:188
  21.5 2.8 %collective-permute-done.refs_1_ = bf16[320,256]{1,0:T(8,128)(2,1)S(1)} collective-permute-done((bf16[320,256]{1,0:T(8,128)(2,1)S(1)}, bf16[320,256]{1,0:T(8,128)(2,1)S(1)}, u32[]{:S(2)}, u32[]{:S(2)}) %collective-permute-start) | collective-permute-done | bytes 163872 | tf_op jit(solution)/shard_map/ppermute | solution.py:188
  24.4 0.3 collective-permute-start.5
  24.7 8.9 %collective-permute-done.1.refs_2_ = bf16[320,256]{1,0:T(8,128)(2,1)S(1)} collective-permute-done((bf16[320,256]{1,0:T(8,128)(2,1)S(1)}, bf16[320,256]{1,0:T(8,128)(2,1)S(1)}, u32[]{:S(2)}, u32[]{:S(2)}) %collective-permute-start.1) | collective-permute-done | bytes 163872 | tf_op jit(solution)/shard_map/ppermute | solution.py:188
  33.6 2.1 %shard_map.47 = (bf16[160,256]{1,0:T(8,128)(2,1)S(1)}, bf16[160,256]{1,0:T(8,128)(2,1)}, bf16[160,256]{1,0:T(8,128)(2,1)}, bf16[160,256]{1,0:T(8,128)(2,1)}, bf1...) custom-call(s32[3]{0:T(128)S(1)} %pad_add_fusion.pos_ref, ...), custom_call_target="tpu_custom_call" | custom-call | flops 503316480 | bytes 6684696 | tf_op jit(solution)/shard_map/pallas_call | solution.py:173
  35.7 0.0 collective-permute-done.2.refs_3_
  35.7 2.0 %collective-permute-done.3.refs_4_ = bf16[320,256]{1,0:T(8,128)(2,1)S(1)} collective-permute-done((bf16[320,256]{1,0:T(8,128)(2,1)S(1)}, bf16[320,256]{1,0:T(8,128)(2,1)S(1)}, u32[]{:S(2)}, u32[]{:S(2)}) %collective-permute-start.3) | collective-permute-done | bytes 163872 | tf_op jit(solution)/shard_map/ppermute | solution.py:188
  37.8 0.9 collective-permute-done.4.refs_5_
  38.6 2.2 %collective-permute-done.5.refs_6_ = bf16[320,256]{1,0:T(8,128)(2,1)S(1)} collective-permute-done((bf16[320,256]{1,0:T(8,128)(2,1)S(1)}, bf16[320,256]{1,0:T(8,128)(2,1)S(1)}, u32[]{:S(2)}, u32[]{:S(2)}) %collective-permute-start.5) | collective-permute-done | bytes 163872 | tf_op jit(solution)/shard_map/ppermute | solution.py:188
  40.8 1.1 collective-permute-done.6.refs_7_
  41.9 0.6 shard_map.48.refs_8_
  42.5 0.1 collective-permute-start.7
  42.6 2.1 %collective-permute-done.7.refs_9_ = bf16[2,4,160,256]{3,2,1,0:T(8,128)(2,1)S(1)} collective-permute-done((bf16[2,4,160,256]{3,2,1,0:T(8,128)(2,1)S(1)}, bf16[2,4,160,256]{3,2,1,0:T(8,128)(2,1)S(1)}, u32[]{:S(2)}, u32[]{:S(2)}) %collective-permute-start.7) | collective-permute-done | bytes 655392 | tf_op jit(solution)/shard_map/ppermute | solution.py:206
  44.7 2.7 %shard_map.49 = bf16[16,40,1280]{2,1,0:T(8,128)(2,1)} custom-call(s32[3]{0:T(128)S(1)} %pad_add_fusion.pos_ref, bf16[320,256]{1,0:T(8,128)(2,1)S(1)} %get-tuple-element.30.refs_0_, bf16[320,256]{1,0:T(8,128)(2,1)S(1)} %collective-permute-done.refs_1_, bf16[320,256]{1,0:T(8,128)(2,1)S(1)} %collective-permute-done.1.refs_2_, ...), custom_call_target="tpu_custom_call" | custom-call | flops 838860800 | bytes 5242904 | tf_op jit(solution)/shard_map/pallas_call | solution.py:173
  47.4 7.6 %all-to-all-start = ((bf16[16,40,1280]{2,1,0:T(8,128)(2,1)}), bf16[16,40,1280]{2,1,0:T(8,128)(2,1)S(1)}, u32[]{:S(2)}, u32[]{:S(2)}) async-start(bf16[16,40,1280]{2,1,0:T(8,128)(2,1)} %shard_map.49), calls=%async_computation | async-start | bytes 3276800 | tf_op jit(solution)/shard_map/all_to_all | solution.py:263
  55.0 3.5 %collective-permute-start.8 = (bf16[160,256]{1,0:T(8,128)(2,1)}, bf16[160,256]{1,0:T(8,128)(2,1)S(1)}, u32[]{:S(2)}, u32[]{:S(2)}) collective-permute-start(bf16[160,256]{1,0:T(8,128)(2,1)} %get-tuple-element.40), channel_id=1, source_target_pairs={{0,1},{1,0},{64,65},{65,64},{128,129},{129,128},{192,193},{193,192... | collective-permute-start | bytes 245768 | tf_op jit(solution)/shard_map/ppermute | solution.py:188
  58.5 2.3 %collective-permute-start.9 = (bf16[160,256]{1,0:T(8,128)(2,1)}, bf16[160,256]{1,0:T(8,128)(2,1)S(1)}, u32[]{:S(2)}, u32[]{:S(2)}) collective-permute-start(bf16[160,256]{1,0:T(8,128)(2,1)} %get-tuple-element.41), channel_id=1, source_target_pairs={{0,192},{1,193},{64,1},{65,0},{128,65},{129,64},{192,129},{193,128... | collective-permute-start | bytes 245768 | tf_op jit(solution)/shard_map/ppermute | solution.py:188
  60.9 2.7 %collective-permute-start.10 = (bf16[160,256]{1,0:T(8,128)(2,1)}, bf16[160,256]{1,0:T(8,128)(2,1)S(1)}, u32[]{:S(2)}, u32[]{:S(2)}) collective-permute-start(bf16[160,256]{1,0:T(8,128)(2,1)} %get-tuple-element.42), channel_id=1, source_target_pairs={{0,65},{1,64},{64,129},{65,128},{128,193},{129,192},{192,0},{193,1... | collective-permute-start | bytes 245768 | tf_op jit(solution)/shard_map/ppermute | solution.py:188
  63.6 0.1 collective-permute-start.11
  63.7 4.1 %collective-permute-start.12 = (bf16[160,256]{1,0:T(8,128)(2,1)S(1)}, bf16[160,256]{1,0:T(8,128)(2,1)S(1)}, u32[]{:S(2)}, u32[]{:S(2)}) collective-permute-start(bf16[160,256]{1,0:T(8,128)(2,1)S(1)} %copy-done.5), channel_id=1, source_target_pairs={{0,129},{1,128},{64,193},{65,192},{128,0},{129,1},{192,64},{193,65... | collective-permute-start | bytes 245768 | tf_op jit(solution)/shard_map/ppermute | solution.py:188
  67.7 0.0 collective-permute-done.8.refs_0_.refs_1_
  67.7 3.9 %collective-permute-done.9.refs_1_.refs_2_ = bf16[160,256]{1,0:T(8,128)(2,1)S(1)} collective-permute-done((bf16[160,256]{1,0:T(8,128)(2,1)}, bf16[160,256]{1,0:T(8,128)(2,1)S(1)}, u32[]{:S(2)}, u32[]{:S(2)}) %collective-permute-start.9) | collective-permute-done | bytes 81952 | tf_op jit(solution)/shard_map/ppermute | solution.py:188
  71.7 0.1 collective-permute-done.10.refs_2_.refs_3_
  71.8 0.4 collective-permute-done.11.refs_3_.refs_4_
  72.2 1.2 collective-permute-done.12.refs_4_.refs_5_
  73.4 1.0 collective-permute-done.16.refs_6_
  74.5 1.6 %collective-permute-done.17.refs_7_ = bf16[160,256]{1,0:T(8,128)(2,1)S(1)} collective-permute-done((bf16[160,256]{1,0:T(8,128)(2,1)S(1)}, bf16[160,256]{1,0:T(8,128)(2,1)S(1)}, u32[]{:S(2)}, u32[]{:S(2)}) %collective-permute-start.17) | collective-permute-done | bytes 81952 | tf_op jit(solution)/shard_map/ppermute | solution.py:188
  76.1 0.6 shard_map.52.v_ref
  76.7 0.1 collective-permute-start.18
  76.8 0.8 all-to-all-done.x_ref
  77.6 0.3 shard_map.50.refs_0_
  77.9 1.3 collective-permute-start.13
  79.2 2.5 %collective-permute-start.14 = (bf16[40,1280]{1,0:T(8,128)(2,1)S(1)}, bf16[40,1280]{1,0:T(8,128)(2,1)S(1)}, u32[]{:S(2)}, u32[]{:S(2)}) collective-permute-start(bf16[40,1280]{1,0:T(8,128)(2,1)S(1)} %shard_map.50.refs_0_), channel_id=1, source_target_pairs={{0,8},{8,16},{16,24},{24,0},{1,9},{9,17},{17,25},{25,1},{2,10},{10... | collective-permute-start | bytes 307208 | tf_op jit(solution)/shard_map/ppermute | solution.py:193
  81.8 3.3 %collective-permute-done.13.refs_1_ = bf16[40,1280]{1,0:T(8,128)(2,1)S(1)} collective-permute-done((bf16[40,1280]{1,0:T(8,128)(2,1)S(1)}, bf16[40,1280]{1,0:T(8,128)(2,1)S(1)}, u32[]{:S(2)}, u32[]{:S(2)}) %collective-permute-start.13) | collective-permute-done | bytes 102432 | tf_op jit(solution)/shard_map/ppermute | solution.py:193
  85.0 0.2 collective-permute-done.14.refs_2_
  85.3 2.4 %collective-permute-done.15.refs_3_ = bf16[40,1280]{1,0:T(8,128)(2,1)S(1)} collective-permute-done((bf16[40,1280]{1,0:T(8,128)(2,1)S(1)}, bf16[40,1280]{1,0:T(8,128)(2,1)S(1)}, u32[]{:S(2)}, u32[]{:S(2)}) %collective-permute-start.15) | collective-permute-done | bytes 102432 | tf_op jit(solution)/shard_map/ppermute | solution.py:193
  87.6 0.6 shard_map.51
  88.2 0.6 collective-permute-start.21
  88.9 2.7 %collective-permute-start.24 = (bf16[160,1280]{1,0:T(8,128)(2,1)S(1)}, bf16[160,1280]{1,0:T(8,128)(2,1)S(1)}, u32[]{:S(2)}, u32[]{:S(2)}) collective-permute-start(bf16[160,1280]{1,0:T(8,128)(2,1)S(1)} %bitcast.8), channel_id=1, source_target_pairs={{0,6},{2,0},{4,2},{6,4},{1,7},{3,1},{5,3},{7,5},{8,14},{10,8},{12,... | collective-permute-start | bytes 1228808 | tf_op jit(solution)/shard_map/ppermute | solution.py:193
  91.5 0.8 collective-permute-start.27
  92.3 1.0 shard_map.53
  93.3 0.7 collective-permute-start.19
  94.0 3.3 %collective-permute-start.20 = (bf16[160,256]{1,0:T(8,128)(2,1)S(1)}, bf16[160,256]{1,0:T(8,128)(2,1)S(1)}, u32[]{:S(2)}, u32[]{:S(2)}) collective-permute-start(bf16[160,256]{1,0:T(8,128)(2,1)S(1)} %get-tuple-element.48), channel_id=1, source_target_pairs={{0,1},{1,0},{2,67},{3,66},{4,133},{5,132},{6,199},{7,198},{64,65},... | collective-permute-start | bytes 245768 | tf_op jit(solution)/shard_map/ppermute | solution.py:202
  97.3 2.7 %collective-permute-done.21.p_ref = bf16[160,1280]{1,0:T(8,128)(2,1)S(1)} collective-permute-done((bf16[160,1280]{1,0:T(8,128)(2,1)S(1)}, bf16[160,1280]{1,0:T(8,128)(2,1)S(1)}, u32[]{:S(2)}, u32[]{:S(2)}) %collective-permute-start.21) | collective-permute-done | bytes 409632 | tf_op jit(solution)/shard_map/ppermute | solution.py:193
  99.9 1.0 shard_map.54
  100.9 0.0 copy-start.1
  100.9 4.9 %collective-permute-start.22 = (bf16[160,256]{1,0:T(8,128)(2,1)S(1)}, bf16[160,256]{1,0:T(8,128)(2,1)S(1)}, u32[]{:S(2)}, u32[]{:S(2)}) collective-permute-start(bf16[160,256]{1,0:T(8,128)(2,1)S(1)} %get-tuple-element.49), channel_id=1, source_target_pairs={{0,192},{1,193},{2,2},{3,3},{4,68},{5,69},{6,134},{7,135},{64,1},{... | collective-permute-start | bytes 245768 | tf_op jit(solution)/shard_map/ppermute | solution.py:202
  105.9 1.1 collective-permute-done.24.p_ref
  107.0 5.9 %collective-permute-start.23 = (bf16[160,256]{1,0:T(8,128)(2,1)S(1)}, bf16[160,256]{1,0:T(8,128)(2,1)S(1)}, u32[]{:S(2)}, u32[]{:S(2)}) collective-permute-start(bf16[160,256]{1,0:T(8,128)(2,1)S(1)} %get-tuple-element.50), channel_id=1, source_target_pairs={{0,193},{1,192},{2,3},{3,2},{4,69},{5,68},{6,135},{7,134},{64,0},{... | collective-permute-start | bytes 245768 | tf_op jit(solution)/shard_map/ppermute | solution.py:202
  112.8 1.0 shard_map.55
  113.8 1.9 %collective-permute-start.25 = (bf16[160,256]{1,0:T(8,128)(2,1)S(1)}, bf16[160,256]{1,0:T(8,128)(2,1)S(1)}, u32[]{:S(2)}, u32[]{:S(2)}) collective-permute-start(bf16[160,256]{1,0:T(8,128)(2,1)S(1)} %get-tuple-element.51), channel_id=1, source_target_pairs={{0,64},{1,65},{2,130},{3,131},{4,196},{5,197},{6,6},{7,7},{64,128}... | collective-permute-start | bytes 245768 | tf_op jit(solution)/shard_map/ppermute | solution.py:202
  115.8 1.0 shard_map.56
  116.8 3.9 %collective-permute-start.26 = (bf16[160,256]{1,0:T(8,128)(2,1)S(1)}, bf16[160,256]{1,0:T(8,128)(2,1)S(1)}, u32[]{:S(2)}, u32[]{:S(2)}) collective-permute-start(bf16[160,256]{1,0:T(8,128)(2,1)S(1)} %get-tuple-element.52), channel_id=1, source_target_pairs={{0,65},{1,64},{2,131},{3,130},{4,197},{5,196},{6,7},{7,6},{64,129}... | collective-permute-start | bytes 245768 | tf_op jit(solution)/shard_map/ppermute | solution.py:202
  120.6 3.7 %collective-permute-start.28 = (bf16[160,256]{1,0:T(8,128)(2,1)S(1)}, bf16[160,256]{1,0:T(8,128)(2,1)S(1)}, u32[]{:S(2)}, u32[]{:S(2)}) collective-permute-start(bf16[160,256]{1,0:T(8,128)(2,1)S(1)} %get-tuple-element.53), channel_id=1, source_target_pairs={{0,128},{1,129},{2,194},{3,195},{4,4},{5,5},{6,70},{7,71},{64,192}... | collective-permute-start | bytes 245768 | tf_op jit(solution)/shard_map/ppermute | solution.py:202
  124.3 2.4 %collective-permute-start.29 = (bf16[160,256]{1,0:T(8,128)(2,1)S(1)}, bf16[160,256]{1,0:T(8,128)(2,1)S(1)}, u32[]{:S(2)}, u32[]{:S(2)}) collective-permute-start(bf16[160,256]{1,0:T(8,128)(2,1)S(1)} %get-tuple-element.54), channel_id=1, source_target_pairs={{0,129},{1,128},{2,195},{3,194},{4,5},{5,4},{6,71},{7,70},{64,193}... | collective-permute-start | bytes 245768 | tf_op jit(solution)/shard_map/ppermute | solution.py:202
  126.8 3.0 %collective-permute-done.28.refs_6_ = bf16[160,256]{1,0:T(8,128)(2,1)S(1)} collective-permute-done((bf16[160,256]{1,0:T(8,128)(2,1)S(1)}, bf16[160,256]{1,0:T(8,128)(2,1)S(1)}, u32[]{:S(2)}, u32[]{:S(2)}) %collective-permute-start.28) | collective-permute-done | bytes 81952 | tf_op jit(solution)/shard_map/ppermute | solution.py:202
  129.8 2.2 %shard_map.57 = f32[4,160,768]{2,1,0:T(8,128)} custom-call(s32[3]{0:T(128)S(1)} %pad_add_fusion.pos_ref, bf16[512,768]{1,0:T(8,128)(2,1)S(1)} %copy-done.1, bf16[160,256]{1,0:T(8,128)(2,1)S(1)} %collective-permute-done.19.refs_0_, bf16[160,256]{1,0:T(8,128)(2,1)S(1)} %collective-permute-done.20.refs_1_, ...), custom_call_target="tpu_custom_call" | custom-call | flops 503316480 | bytes 2883608 | tf_op jit(solution)/shard_map/pallas_call | solution.py:173
  (25 shorter events, 0.1 us)
Async XLA Ops:
  0.0 33.6 %copy-start = (bf16[768,3,512]{2,0,1:T(8,128)(2,1)S(1)}, bf16[768,3,512]{2,0,1:T(8,128)(2,1)}, u32[]{:S(2)}) copy-start(bf16[768,3,512]{2,0,1:T(8,128)(2,1)} %param.6) | copy-start | bytes 7077892
  0.1 0.8 copy-start.6
  5.1 19.3 %collective-permute-start = (bf16[320,256]{1,0:T(8,128)(2,1)S(1)}, bf16[320,256]{1,0:T(8,128)(2,1)S(1)}, u32[]{:S(2)}, u32[]{:S(2)}) collective-permute-start(bf16[320,256]{1,0:T(8,128)(2,1)S(1)} %get-tuple-element.31), channel_id=1, source_target_pairs={{0,1},{1,0},{64,65},{65,64},{128,129},{129,128},{192,193},{193,192... | collective-permute-start | bytes 491528 | tf_op jit(solution)/shard_map/ppermute | solution.py:188
  12.4 21.2 %collective-permute-start.1 = (bf16[320,256]{1,0:T(8,128)(2,1)S(1)}, bf16[320,256]{1,0:T(8,128)(2,1)S(1)}, u32[]{:S(2)}, u32[]{:S(2)}) collective-permute-start(bf16[320,256]{1,0:T(8,128)(2,1)S(1)} %get-tuple-element.32), channel_id=1, source_target_pairs={{0,192},{1,193},{64,1},{65,0},{128,65},{129,64},{192,129},{193,128... | collective-permute-start | bytes 491528 | tf_op jit(solution)/shard_map/ppermute | solution.py:188
  14.3 21.4 %collective-permute-start.2 = (bf16[320,256]{1,0:T(8,128)(2,1)S(1)}, bf16[320,256]{1,0:T(8,128)(2,1)S(1)}, u32[]{:S(2)}, u32[]{:S(2)}) collective-permute-start(bf16[320,256]{1,0:T(8,128)(2,1)S(1)} %get-tuple-element.33), channel_id=1, source_target_pairs={{0,65},{1,64},{64,129},{65,128},{128,193},{129,192},{192,0},{193,1... | collective-permute-start | bytes 491528 | tf_op jit(solution)/shard_map/ppermute | solution.py:188
  17.4 20.4 %collective-permute-start.3 = (bf16[320,256]{1,0:T(8,128)(2,1)S(1)}, bf16[320,256]{1,0:T(8,128)(2,1)S(1)}, u32[]{:S(2)}, u32[]{:S(2)}) collective-permute-start(bf16[320,256]{1,0:T(8,128)(2,1)S(1)} %get-tuple-element.34), channel_id=1, source_target_pairs={{0,128},{1,129},{64,192},{65,193},{128,1},{129,0},{192,65},{193,64... | collective-permute-start | bytes 491528 | tf_op jit(solution)/shard_map/ppermute | solution.py:188
  18.9 19.8 %collective-permute-start.4 = (bf16[320,256]{1,0:T(8,128)(2,1)S(1)}, bf16[320,256]{1,0:T(8,128)(2,1)S(1)}, u32[]{:S(2)}, u32[]{:S(2)}) collective-permute-start(bf16[320,256]{1,0:T(8,128)(2,1)S(1)} %get-tuple-element.35), channel_id=1, source_target_pairs={{0,129},{1,128},{64,193},{65,192},{128,0},{129,1},{192,64},{193,65... | collective-permute-start | bytes 491528 | tf_op jit(solution)/shard_map/ppermute | solution.py:188
  24.4 16.4 %collective-permute-start.5 = (bf16[320,256]{1,0:T(8,128)(2,1)S(1)}, bf16[320,256]{1,0:T(8,128)(2,1)S(1)}, u32[]{:S(2)}, u32[]{:S(2)}) collective-permute-start(bf16[320,256]{1,0:T(8,128)(2,1)S(1)} %get-tuple-element.36), channel_id=1, source_target_pairs={{0,64},{1,65},{64,128},{65,129},{128,192},{129,193},{192,1},{193,0... | collective-permute-start | bytes 491528 | tf_op jit(solution)/shard_map/ppermute | solution.py:188
  33.6 8.3 %collective-permute-start.6 = (bf16[320,256]{1,0:T(8,128)(2,1)S(1)}, bf16[320,256]{1,0:T(8,128)(2,1)S(1)}, u32[]{:S(2)}, u32[]{:S(2)}) collective-permute-start(bf16[320,256]{1,0:T(8,128)(2,1)S(1)} %get-tuple-element.37), channel_id=1, source_target_pairs={{0,193},{1,192},{64,0},{65,1},{128,64},{129,65},{192,128},{193,129... | collective-permute-start | bytes 491528 | tf_op jit(solution)/shard_map/ppermute | solution.py:188
  35.7 9.0 %copy-start.2 = (bf16[160,256]{1,0:T(8,128)(2,1)}, bf16[160,256]{1,0:T(8,128)(2,1)S(1)}, u32[]{:S(2)}) copy-start(bf16[160,256]{1,0:T(8,128)(2,1)S(1)} %get-tuple-element.45) | copy-start | bytes 245764
  35.7 9.0 %copy-start.4 = (bf16[160,256]{1,0:T(8,128)(2,1)}, bf16[160,256]{1,0:T(8,128)(2,1)S(1)}, u32[]{:S(2)}) copy-start(bf16[160,256]{1,0:T(8,128)(2,1)S(1)} %get-tuple-element.44) | copy-start | bytes 245764
  42.5 2.2 %collective-permute-start.7 = (bf16[2,4,160,256]{3,2,1,0:T(8,128)(2,1)S(1)}, bf16[2,4,160,256]{3,2,1,0:T(8,128)(2,1)S(1)}, u32[]{:S(2)}, u32[]{:S(2)}) collective-permute-start(bf16[2,4,160,256]{3,2,1,0:T(8,128)(2,1)S(1)} %shard_map.48.refs_8_), channel_id=1, source_target_pairs={{0,32},{32,0},{1,33},{33,1},{2,34},{34,2},{3,35},{35,3},{4,36},{36... | collective-permute-start | bytes 1966088 | tf_op jit(solution)/shard_map/ppermute | solution.py:206
  47.4 16.2 %copy-start.5 = (bf16[160,256]{1,0:T(8,128)(2,1)S(1)}, bf16[160,256]{1,0:T(8,128)(2,1)}, u32[]{:S(2)}) copy-start(bf16[160,256]{1,0:T(8,128)(2,1)} %copy-done.4) | copy-start | bytes 245764
  47.4 20.3 %copy-start.3 = (bf16[160,256]{1,0:T(8,128)(2,1)S(1)}, bf16[160,256]{1,0:T(8,128)(2,1)}, u32[]{:S(2)}) copy-start(bf16[160,256]{1,0:T(8,128)(2,1)} %copy-done.2) | copy-start | bytes 245764
  47.4 30.2 %all-to-all-start = ((bf16[16,40,1280]{2,1,0:T(8,128)(2,1)}), bf16[16,40,1280]{2,1,0:T(8,128)(2,1)S(1)}, u32[]{:S(2)}, u32[]{:S(2)}) async-start(bf16[16,40,1280]{2,1,0:T(8,128)(2,1)} %shard_map.49), calls=%async_computation | async-start | bytes 3276800 | tf_op jit(solution)/shard_map/all_to_all | solution.py:263
  55.0 12.7 %collective-permute-start.8 = (bf16[160,256]{1,0:T(8,128)(2,1)}, bf16[160,256]{1,0:T(8,128)(2,1)S(1)}, u32[]{:S(2)}, u32[]{:S(2)}) collective-permute-start(bf16[160,256]{1,0:T(8,128)(2,1)} %get-tuple-element.40), channel_id=1, source_target_pairs={{0,1},{1,0},{64,65},{65,64},{128,129},{129,128},{192,193},{193,192... | collective-permute-start | bytes 245768 | tf_op jit(solution)/shard_map/ppermute | solution.py:188
  58.5 13.1 %collective-permute-start.9 = (bf16[160,256]{1,0:T(8,128)(2,1)}, bf16[160,256]{1,0:T(8,128)(2,1)S(1)}, u32[]{:S(2)}, u32[]{:S(2)}) collective-permute-start(bf16[160,256]{1,0:T(8,128)(2,1)} %get-tuple-element.41), channel_id=1, source_target_pairs={{0,192},{1,193},{64,1},{65,0},{128,65},{129,64},{192,129},{193,128... | collective-permute-start | bytes 245768 | tf_op jit(solution)/shard_map/ppermute | solution.py:188
  60.9 10.9 %collective-permute-start.10 = (bf16[160,256]{1,0:T(8,128)(2,1)}, bf16[160,256]{1,0:T(8,128)(2,1)S(1)}, u32[]{:S(2)}, u32[]{:S(2)}) collective-permute-start(bf16[160,256]{1,0:T(8,128)(2,1)} %get-tuple-element.42), channel_id=1, source_target_pairs={{0,65},{1,64},{64,129},{65,128},{128,193},{129,192},{192,0},{193,1... | collective-permute-start | bytes 245768 | tf_op jit(solution)/shard_map/ppermute | solution.py:188
  63.6 8.6 %collective-permute-start.11 = (bf16[160,256]{1,0:T(8,128)(2,1)}, bf16[160,256]{1,0:T(8,128)(2,1)S(1)}, u32[]{:S(2)}, u32[]{:S(2)}) collective-permute-start(bf16[160,256]{1,0:T(8,128)(2,1)} %get-tuple-element.43), channel_id=1, source_target_pairs={{0,128},{1,129},{64,192},{65,193},{128,1},{129,0},{192,65},{193,64... | collective-permute-start | bytes 245768 | tf_op jit(solution)/shard_map/ppermute | solution.py:188
  63.7 9.8 %collective-permute-start.12 = (bf16[160,256]{1,0:T(8,128)(2,1)S(1)}, bf16[160,256]{1,0:T(8,128)(2,1)S(1)}, u32[]{:S(2)}, u32[]{:S(2)}) collective-permute-start(bf16[160,256]{1,0:T(8,128)(2,1)S(1)} %copy-done.5), channel_id=1, source_target_pairs={{0,129},{1,128},{64,193},{65,192},{128,0},{129,1},{192,64},{193,65... | collective-permute-start | bytes 245768 | tf_op jit(solution)/shard_map/ppermute | solution.py:188
  67.7 6.7 %collective-permute-start.16 = (bf16[160,256]{1,0:T(8,128)(2,1)S(1)}, bf16[160,256]{1,0:T(8,128)(2,1)S(1)}, u32[]{:S(2)}, u32[]{:S(2)}) collective-permute-start(bf16[160,256]{1,0:T(8,128)(2,1)S(1)} %copy-done.3), channel_id=1, source_target_pairs={{0,64},{1,65},{64,128},{65,129},{128,192},{129,193},{192,1},{193,0... | collective-permute-start | bytes 245768 | tf_op jit(solution)/shard_map/ppermute | solution.py:188
  71.7 4.4 %collective-permute-start.17 = (bf16[160,256]{1,0:T(8,128)(2,1)S(1)}, bf16[160,256]{1,0:T(8,128)(2,1)S(1)}, u32[]{:S(2)}, u32[]{:S(2)}) collective-permute-start(bf16[160,256]{1,0:T(8,128)(2,1)S(1)} %get-tuple-element.46), channel_id=1, source_target_pairs={{0,193},{1,192},{64,0},{65,1},{128,64},{129,65},{192,128},{193,129... | collective-permute-start | bytes 245768 | tf_op jit(solution)/shard_map/ppermute | solution.py:188
  76.7 15.6 %collective-permute-start.18 = (bf16[2,4,160,256]{3,2,1,0:T(8,128)(2,1)S(1)}, bf16[2,4,160,256]{3,2,1,0:T(8,128)(2,1)S(1)}, u32[]{:S(2)}, u32[]{:S(2)}) collective-permute-start(bf16[2,4,160,256]{3,2,1,0:T(8,128)(2,1)S(1)} %shard_map.52.v_ref), channel_id=1, source_target_pairs={{0,32},{32,0},{1,33},{33,1},{2,34},{34,2},{3,35},{35,3},{4,36},{36... | collective-permute-start | bytes 1966088 | tf_op jit(solution)/shard_map/ppermute | solution.py:206
  77.9 7.1 %collective-permute-start.13 = (bf16[40,1280]{1,0:T(8,128)(2,1)S(1)}, bf16[40,1280]{1,0:T(8,128)(2,1)S(1)}, u32[]{:S(2)}, u32[]{:S(2)}) collective-permute-start(bf16[40,1280]{1,0:T(8,128)(2,1)S(1)} %shard_map.50.refs_0_), channel_id=1, source_target_pairs={{0,16},{8,24},{16,0},{24,8},{1,17},{9,25},{17,1},{25,9},{2,18},{10... | collective-permute-start | bytes 307208 | tf_op jit(solution)/shard_map/ppermute | solution.py:193
  79.2 6.0 %collective-permute-start.14 = (bf16[40,1280]{1,0:T(8,128)(2,1)S(1)}, bf16[40,1280]{1,0:T(8,128)(2,1)S(1)}, u32[]{:S(2)}, u32[]{:S(2)}) collective-permute-start(bf16[40,1280]{1,0:T(8,128)(2,1)S(1)} %shard_map.50.refs_0_), channel_id=1, source_target_pairs={{0,8},{8,16},{16,24},{24,0},{1,9},{9,17},{17,25},{25,1},{2,10},{10... | collective-permute-start | bytes 307208 | tf_op jit(solution)/shard_map/ppermute | solution.py:193
  81.8 5.9 %collective-permute-start.15 = (bf16[40,1280]{1,0:T(8,128)(2,1)S(1)}, bf16[40,1280]{1,0:T(8,128)(2,1)S(1)}, u32[]{:S(2)}, u32[]{:S(2)}) collective-permute-start(bf16[40,1280]{1,0:T(8,128)(2,1)S(1)} %shard_map.50.refs_0_), channel_id=1, source_target_pairs={{0,24},{8,0},{16,8},{24,16},{1,25},{9,1},{17,9},{25,17},{2,26},{10... | collective-permute-start | bytes 307208 | tf_op jit(solution)/shard_map/ppermute | solution.py:193
  88.2 11.7 %collective-permute-start.21 = (bf16[160,1280]{1,0:T(8,128)(2,1)S(1)}, bf16[160,1280]{1,0:T(8,128)(2,1)S(1)}, u32[]{:S(2)}, u32[]{:S(2)}) collective-permute-start(bf16[160,1280]{1,0:T(8,128)(2,1)S(1)} %bitcast.7), channel_id=1, source_target_pairs={{0,2},{2,4},{4,6},{6,0},{1,3},{3,5},{5,7},{7,1},{8,10},{10,12},{12... | collective-permute-start | bytes 1228808 | tf_op jit(solution)/shard_map/ppermute | solution.py:193
  88.9 18.1 %collective-permute-start.24 = (bf16[160,1280]{1,0:T(8,128)(2,1)S(1)}, bf16[160,1280]{1,0:T(8,128)(2,1)S(1)}, u32[]{:S(2)}, u32[]{:S(2)}) collective-permute-start(bf16[160,1280]{1,0:T(8,128)(2,1)S(1)} %bitcast.8), channel_id=1, source_target_pairs={{0,6},{2,0},{4,2},{6,4},{1,7},{3,1},{5,3},{7,5},{8,14},{10,8},{12,... | collective-permute-start | bytes 1228808 | tf_op jit(solution)/shard_map/ppermute | solution.py:193
  91.5 22.3 %collective-permute-start.27 = (bf16[160,1280]{1,0:T(8,128)(2,1)S(1)}, bf16[160,1280]{1,0:T(8,128)(2,1)S(1)}, u32[]{:S(2)}, u32[]{:S(2)}) collective-permute-start(bf16[160,1280]{1,0:T(8,128)(2,1)S(1)} %bitcast.9), channel_id=1, source_target_pairs={{0,4},{2,6},{4,0},{6,2},{1,5},{3,7},{5,1},{7,3},{8,12},{10,14},{12... | collective-permute-start | bytes 1228808 | tf_op jit(solution)/shard_map/ppermute | solution.py:193
  93.3 23.5 %collective-permute-start.19 = (bf16[160,256]{1,0:T(8,128)(2,1)S(1)}, bf16[160,256]{1,0:T(8,128)(2,1)S(1)}, u32[]{:S(2)}, u32[]{:S(2)}) collective-permute-start(bf16[160,256]{1,0:T(8,128)(2,1)S(1)} %get-tuple-element.47), channel_id=1, source_target_pairs={{0,0},{1,1},{2,66},{3,67},{4,132},{5,133},{6,198},{7,199},{64,64},... | collective-permute-start | bytes 245768 | tf_op jit(solution)/shard_map/ppermute | solution.py:202
  94.0 26.7 %collective-permute-start.20 = (bf16[160,256]{1,0:T(8,128)(2,1)S(1)}, bf16[160,256]{1,0:T(8,128)(2,1)S(1)}, u32[]{:S(2)}, u32[]{:S(2)}) collective-permute-start(bf16[160,256]{1,0:T(8,128)(2,1)S(1)} %get-tuple-element.48), channel_id=1, source_target_pairs={{0,1},{1,0},{2,67},{3,66},{4,133},{5,132},{6,199},{7,198},{64,65},... | collective-permute-start | bytes 245768 | tf_op jit(solution)/shard_map/ppermute | solution.py:202
  100.9 28.9 %copy-start.1 = (bf16[512,768]{1,0:T(8,128)(2,1)S(1)}, bf16[512,768]{1,0:T(8,128)(2,1)}, u32[]{:S(2)}) copy-start(bf16[512,768]{1,0:T(8,128)(2,1)} %w_ref.1) | copy-start | bytes 2359300
  100.9 23.4 %collective-permute-start.22 = (bf16[160,256]{1,0:T(8,128)(2,1)S(1)}, bf16[160,256]{1,0:T(8,128)(2,1)S(1)}, u32[]{:S(2)}, u32[]{:S(2)}) collective-permute-start(bf16[160,256]{1,0:T(8,128)(2,1)S(1)} %get-tuple-element.49), channel_id=1, source_target_pairs={{0,192},{1,193},{2,2},{3,3},{4,68},{5,69},{6,134},{7,135},{64,1},{... | collective-permute-start | bytes 245768 | tf_op jit(solution)/shard_map/ppermute | solution.py:202
  107.0 19.8 %collective-permute-start.23 = (bf16[160,256]{1,0:T(8,128)(2,1)S(1)}, bf16[160,256]{1,0:T(8,128)(2,1)S(1)}, u32[]{:S(2)}, u32[]{:S(2)}) collective-permute-start(bf16[160,256]{1,0:T(8,128)(2,1)S(1)} %get-tuple-element.50), channel_id=1, source_target_pairs={{0,193},{1,192},{2,3},{3,2},{4,69},{5,68},{6,135},{7,134},{64,0},{... | collective-permute-start | bytes 245768 | tf_op jit(solution)/shard_map/ppermute | solution.py:202
  113.8 12.9 %collective-permute-start.25 = (bf16[160,256]{1,0:T(8,128)(2,1)S(1)}, bf16[160,256]{1,0:T(8,128)(2,1)S(1)}, u32[]{:S(2)}, u32[]{:S(2)}) collective-permute-start(bf16[160,256]{1,0:T(8,128)(2,1)S(1)} %get-tuple-element.51), channel_id=1, source_target_pairs={{0,64},{1,65},{2,130},{3,131},{4,196},{5,197},{6,6},{7,7},{64,128}... | collective-permute-start | bytes 245768 | tf_op jit(solution)/shard_map/ppermute | solution.py:202
  116.8 10.0 %collective-permute-start.26 = (bf16[160,256]{1,0:T(8,128)(2,1)S(1)}, bf16[160,256]{1,0:T(8,128)(2,1)S(1)}, u32[]{:S(2)}, u32[]{:S(2)}) collective-permute-start(bf16[160,256]{1,0:T(8,128)(2,1)S(1)} %get-tuple-element.52), channel_id=1, source_target_pairs={{0,65},{1,64},{2,131},{3,130},{4,197},{5,196},{6,7},{7,6},{64,129}... | collective-permute-start | bytes 245768 | tf_op jit(solution)/shard_map/ppermute | solution.py:202
  120.6 9.2 %collective-permute-start.28 = (bf16[160,256]{1,0:T(8,128)(2,1)S(1)}, bf16[160,256]{1,0:T(8,128)(2,1)S(1)}, u32[]{:S(2)}, u32[]{:S(2)}) collective-permute-start(bf16[160,256]{1,0:T(8,128)(2,1)S(1)} %get-tuple-element.53), channel_id=1, source_target_pairs={{0,128},{1,129},{2,194},{3,195},{4,4},{5,5},{6,70},{7,71},{64,192}... | collective-permute-start | bytes 245768 | tf_op jit(solution)/shard_map/ppermute | solution.py:202
  124.3 5.5 %collective-permute-start.29 = (bf16[160,256]{1,0:T(8,128)(2,1)S(1)}, bf16[160,256]{1,0:T(8,128)(2,1)S(1)}, u32[]{:S(2)}, u32[]{:S(2)}) collective-permute-start(bf16[160,256]{1,0:T(8,128)(2,1)S(1)} %get-tuple-element.54), channel_id=1, source_target_pairs={{0,129},{1,128},{2,195},{3,194},{4,5},{5,4},{6,71},{7,70},{64,193}... | collective-permute-start | bytes 245768 | tf_op jit(solution)/shard_map/ppermute | solution.py:202

commit v6 on v4

--- a/solution.py
+++ b/solution.py
@@ -20,6 +20,7 @@
 HBM = pl.BlockSpec(memory_space=pltpu.HBM)
 ANY = pl.BlockSpec(memory_space=pl.ANY)
 SMEM = pl.BlockSpec(memory_space=pltpu.SMEM)
+CUTS = 4
 MIB = 1024 * 1024
 
 
@@ -48,9 +49,12 @@
     both, (normed, mine, gain_ref, x_ref, w_ref, gain_sem, x_sem, w_sem) = refs[:RING], refs[RING:]
     seqs, length, width = x_hbm.shape
     x_copies = [pltpu.make_async_copy(x_hbm.at[r], x_ref.at[r], x_sem.at[r]) for r in range(seqs)]
-    w_copies = [pltpu.make_async_copy(w_hbm.at[c], w_ref.at[c], w_sem.at[c]) for c in range(2)]
+    w_copies = [
+        [pltpu.make_async_copy(w_hbm.at[c, part], w_ref.at[c, part], w_sem.at[c, i]) for i, part in enumerate(cuts(width, CUTS))]
+        for c in range(2)
+    ]
     gain_copy = pltpu.make_async_copy(gain_hbm, gain_ref, gain_sem)
-    for copy in (x_copies[0], gain_copy, *x_copies[1:], w_copies[1], w_copies[0]):
+    for copy in (x_copies[0], gain_copy, *x_copies[1:], *w_copies[1], *w_copies[0]):
         copy.start()
     gain_copy.wait()
     gain = gain_ref[...].reshape(1, width)
@@ -63,7 +67,8 @@
         normed[r * length : (r + 1) * length] = (off / jnp.sqrt(var + 1e-05) * gain).astype(BF)
     pos = pos_ref[0]
     for c in (1, 0):
-        w_copies[c].wait()
+        for copy in w_copies[c]:
+            copy.wait()
         blocks_by_head(jnp.dot(normed[...], w_ref[c], preferred_element_type=F32), seqs, mine)
         for i, s in enumerate(STEPS):
             both[i][(1 - c) * length : (2 - c) * length] = mine[head_at(pos + s)]
@@ -80,6 +85,10 @@
         outs[i][...] = mine[head_at(pos + s)]
 
 
+def cuts(rows, count):
+    return [pl.ds(i * (rows // count), rows // count) for i in range(count)]
+
+
 def put_by_sender(pos, parts, first, out):
     length = out.shape[2]
     for part, s in zip(parts, STEPS):
@@ -91,49 +100,56 @@
     put_by_sender(pos_ref[0], refs[:count], 0, refs[-1])
 
 
-def logits_kernel(pos_ref, *refs):
-    parts, (k_ref, k_far, out_hbm, q, terms, sem) = refs[:RING], refs[RING:]
-    put_by_sender(pos_ref[0], parts, q.shape[2], q)
-    length = k_ref.shape[2]
-    half = k_ref.shape[1] * length
+def half_terms(q, keys, side, out_hbm, terms, sem):
+    length = keys.shape[2]
+    half = keys.shape[1] * length
+    columns = pl.ds(side * half, half)
+    total = None
+    for w in range(W):
+        term = lax.dot_general(
+            q[w].reshape(half, -1), keys[w].reshape(half, -1), (((1,), (1,)), ((), ())), preferred_element_type=F32
+        )
+        total = term if total is None else total + term
     copies = []
-    for z in range(Z):
-        rows = slice(z * length, (z + 1) * length)
-        for side, keys in enumerate((k_ref, k_far)):
-            total = None
-            for w in range(W):
-                term = lax.dot_general(
-                    q[w, z], keys[w].reshape(half, -1), (((1,), (1,)), ((), ())), preferred_element_type=F32
-                )
-                total = term if total is None else total + term
-            terms[rows, side * half : (side + 1) * half] = total.astype(BF)
-        copies.append(pltpu.make_async_copy(terms.at[rows], out_hbm.at[rows], sem.at[z]))
-        copies[z].start()
+    for i, rows in enumerate(cuts(half, Z)):
+        terms[rows] = total[i * length : (i + 1) * length].astype(BF)
+        copies.append(pltpu.make_async_copy(terms.at[rows], out_hbm.at[rows, columns], sem.at[i]))
+        copies[i].start()
     for copy in copies:
         copy.wait()
 
 
+def near_kernel(pos_ref, *refs):
+    parts, (k_ref, out_hbm, q, terms, sem) = refs[:RING], refs[RING:]
+    put_by_sender(pos_ref[0], parts, q.shape[2], q)
+    half_terms(q, k_ref, 0, out_hbm, terms, sem)
+
+
+def far_kernel(_, q, k_far, out_hbm, terms, sem):
+    half_terms(q, k_far, 1, out_hbm, terms, sem)
+
+
 def probs_kernel(scale, x_ref, *refs):
-    out_ref = refs[-1]
+    out_hbm, probs, sem = refs[-3:]
     logits = x_ref[0].astype(F32)
     for i in range(1, x_ref.shape[0]):
         logits = logits + x_ref[i].astype(F32)
     expo = jnp.exp(logits * scale)
-    probs = (expo / jnp.sum(expo, axis=-1, keepdims=True)).astype(BF)
-    for i in range(out_ref.shape[0]):
-        out_ref[i] = probs
-
-
-def context_kernel(pos_ref, p_ref, v_ref, far_hbm, *refs):
-    outs, (mine, v_far, sem) = refs[:RING], refs[RING:]
-    copy = pltpu.make_async_copy(far_hbm, v_far, sem)
-    copy.start()
+    probs[...] = (expo / jnp.sum(expo, axis=-1, keepdims=True)).astype(BF)
+    copies = [pltpu.make_async_copy(probs, out_hbm.at[i], sem.at[i]) for i in range(PLANE)]
+    for copy in copies:
+        copy.start()
+    for copy in copies:
+        copy.wait()
+
+
+def context_kernel(pos_ref, p_ref, v_ref, v_far, *refs):
+    outs, mine = refs[:RING], refs[RING]
     half = v_ref.shape[1] * v_ref.shape[2]
     length = v_ref.shape[2]
-    near = [jnp.dot(p_ref[:, :half], v_ref[w].reshape(half, -1), preferred_element_type=F32) for w in range(W)]
-    copy.wait()
     for w in range(W):
-        a = near[w] + jnp.dot(p_ref[:, half:], v_far[w].reshape(half, -1), preferred_element_type=F32)
+        a = jnp.dot(p_ref[:, :half], v_ref[w].reshape(half, -1), preferred_element_type=F32)
+        a = a + jnp.dot(p_ref[:, half:], v_far[w].reshape(half, -1), preferred_element_type=F32)
         a = a.astype(BF)
         for z in range(Z):
             mine[w * Z + z] = a[z * length : (z + 1) * length]
@@ -152,13 +168,14 @@
     for r in range(mixed.shape[0]):
         lhs = jnp.concatenate([part[:, r * HEAD_DIM : (r + 1) * HEAD_DIM] for part in parts], axis=1)
         mixed[r] = jnp.dot(lhs, rows[...], preferred_element_type=F32)
-        copies.append(pltpu.make_async_copy(mixed.at[r], out_hbm.at[r], sem.at[r]))
-        copies[r].start()
+        for i, part in enumerate(cuts(mixed.shape[1], CUTS)):
+            copies.append(pltpu.make_async_copy(mixed.at[r, part], out_hbm.at[r, part], sem.at[r, i]))
+            copies[-1].start()
     for copy in copies:
         copy.wait()
 
 
-def call(kernel, out_shape, operands, scratch=(), flops=0, hbm=(), unread=(), out_specs=None, vmem=20):
+def call(kernel, out_shape, operands, scratch=(), flops=0, hbm=(), unread=(), out_specs=None, aliases=None, vmem=20):
     moved = sum(math.prod(o.shape) * o.dtype.itemsize for o in operands)
     specs = [
         SMEM if o.dtype == jnp.int32 else HBM if i in hbm else ANY if i in unread else VMEM for i, o in enumerate(operands)
@@ -169,6 +186,7 @@
         in_specs=specs,
         out_specs=out_specs or jax.tree.map(lambda _: VMEM, out_shape),
         scratch_shapes=list(scratch),
+        input_output_aliases=aliases or {},
         compiler_params=pltpu.CompilerParams(vmem_limit_bytes=vmem * MIB),
         cost_estimate=pl.CostEstimate(flops=flops, bytes_accessed=2 * moved, transcendentals=0),
     )(*operands)
@@ -211,7 +229,7 @@
             pltpu.VMEM((2, width, inner), BF),
             dma,
             dma((seqs,)),
-            dma((2,)),
+            dma((2, CUTS)),
         ],
         flops=2 * seqs * length * width * 2 * inner,
         hbm=(1, 2, 3),
@@ -230,13 +248,23 @@
     keys = call(functools.partial(place_kernel, RING), whole, [pos, *both, values[0]], unread=(1 + RING,))
     keys_far = other_core(keys)
     values = along_ring(values)
+    term, query = call(
+        near_kernel,
+        [jax.ShapeDtypeStruct((half, full), BF), whole],
+        [pos, *both, keys],
+        [pltpu.VMEM((half, half), BF), dma((Z,))],
+        flops=2 * half * half * W * lanes,
+        out_specs=[HBM, VMEM],
+    )
     term = call(
-        logits_kernel,
+        far_kernel,
         jax.ShapeDtypeStruct((half, full), BF),
-        [pos, *both, keys, keys_far],
-        [pltpu.VMEM(whole.shape, BF), pltpu.VMEM((half, full), BF), dma((Z,))],
-        flops=2 * half * full * W * lanes,
+        [term, query, keys_far],
+        [pltpu.VMEM((half, half), BF), dma((Z,))],
+        flops=2 * half * half * W * lanes,
+        hbm=(0,),
         out_specs=HBM,
+        aliases={0: 0},
     )
     chunk = (PLANE, half // PLANE, full)
     terms = lax.all_to_all(term.reshape(chunk), ("x", "y"), 0, 0, tiled=True)
@@ -245,7 +273,9 @@
         functools.partial(probs_kernel, scale),
         jax.ShapeDtypeStruct(chunk, BF),
         [terms, *early],
+        [pltpu.VMEM(chunk[1:], BF), dma((PLANE,))],
         unread=range(1, 5),
+        out_specs=HBM,
     )
     probs = lax.all_to_all(probs, ("x", "y"), 0, 0, tiled=True).reshape(half, full)
     values = call(functools.partial(place_kernel, RING), whole, [pos, *values])
@@ -254,17 +284,15 @@
         context_kernel,
         [block] * RING,
         [pos, probs, values, values_far],
-        [pltpu.VMEM((RING, length, lanes), BF), pltpu.VMEM(whole.shape, BF), dma],
+        [pltpu.VMEM((RING, length, lanes), BF)],
         flops=2 * half * full * W * lanes,
-        hbm=(3,),
-        vmem=20,
     )
     context = along_ring(context)
     return call(
         mix_kernel,
         jax.ShapeDtypeStruct((seqs, length, width), F32),
         [pos, w_out, *context],
-        [pltpu.VMEM(w_out.shape, BF), pltpu.VMEM((seqs, length, width), F32), dma((seqs,))],
+        [pltpu.VMEM(w_out.shape, BF), pltpu.VMEM((seqs, length, width), F32), dma((seqs, CUTS))],
         flops=2 * seqs * length * inner * width,
         out_specs=HBM,
     )

time: 129 us -> 128 us (level)
  waiting for transfers between devices: 56.1 us -> 54.6 us
    ppermute x2, waiting for transfers between devices: 4.17 us -> 2.65 us  [other_core(): return lax.ppermute(a, 'c', [(0, 1), (1, 0)])]
    pallas_call x8 -> x9, Pallas kernels: 12 us -> 12.7 us  [call(): pl.pallas_call(kernel, out_shape=out_shape, in_specs=specs, out_specs=out...]
  transfers between devices with their start and end apart: 25 -> 25, of which waited for: 19 -> 19; matrix products, arithmetic and copies ran while one was open for 0% -> 0% of each run, Pallas kernels for 1% -> 2%
where the time goes in v6:
time: 128 us
  starting transfers between devices  57.5 us (45%)
  waiting for transfers between devices  54.6 us (43%)
  Pallas kernels  12.7 us (10%)
  local copies, waits for them, and re-layouts  2.62 us (2%)
    ppermute x21, starting transfers between devices, along_ring(): got.append(lax.ppermute(part, ('z', 'w'), pairs) if s else part)  43.6 us
    ppermute x21, waiting for transfers between devices, along_ring(): got.append(lax.ppermute(part, ('z', 'w'), pairs) if s else part)  37.5 us
    pallas_call x9, Pallas kernels, call(): pl.pallas_call(kernel, out_shape=out_shape, in_specs=specs, out_specs=out...  12.7 us
    all_to_all x1, waiting for transfers between devices, shards(): lax.all_to_all(probs, ('x', 'y'), 0, 0, tiled=True).reshape(half, full)  8.82 us
    all_to_all x1, starting transfers between devices, shards(): terms = lax.all_to_all(term.reshape(chunk), ('x', 'y'), 0, 0, tiled=True)  7.44 us
    all_to_all x1, starting transfers between devices, shards(): lax.all_to_all(probs, ('x', 'y'), 0, 0, tiled=True).reshape(half, full)  6.24 us
    all_to_all x1, waiting for transfers between devices, shards(): terms = lax.all_to_all(term.reshape(chunk), ('x', 'y'), 0, 0, tiled=True)  5.57 us
    ppermute x2, waiting for transfers between devices, other_core(): return lax.ppermute(a, 'c', [(0, 1), (1, 0)])  2.65 us
  transfers between devices with their start and end apart: 25, of which 19 were waited for; matrix products, arithmetic and copies ran while one was open for 0% of the time, Pallas kernels for 2%

profile of v6, /device:TPU:6, one launch (start us, length us, event | category | flops | bytes accessed | tf_op | source)
XLA Modules:
  0.0 127.7 jit_solution(1024636449386342247)
XLA Ops:
  0.0 0.7 copy-done.4
  0.7 4.1 %shard_map.46 = (bf16[320,256]{1,0:T(8,128)(2,1)S(1)}, bf16[320,256]{1,0:T(8,128)(2,1)S(1)}, bf16[320,256]{1,0:T(8,128)(2,1)S(1)}, bf16[320,256]{1,0:T(8,128)(2,...) custom-call(s32[1]{0:T(128)} %bitcast.pos_ref, ...), custom_call_target="tpu_custom_call" | custom-call | flops 1006632960 | bytes 6690824 | tf_op jit(solution)/shard_map/pallas_call | solution.py:183
  4.8 7.3 %collective-permute-start = (bf16[320,256]{1,0:T(8,128)(2,1)S(1)}, bf16[320,256]{1,0:T(8,128)(2,1)S(1)}, u32[]{:S(2)}, u32[]{:S(2)}) collective-permute-start(bf16[320,256]{1,0:T(8,128)(2,1)S(1)} %get-tuple-element.33), channel_id=1, source_target_pairs={{0,1},{1,0},{64,65},{65,64},{128,129},{129,128},{192,193},{193,192... | collective-permute-start | bytes 491528 | tf_op jit(solution)/shard_map/ppermute | solution.py:199
  12.0 1.9 %collective-permute-start.1 = (bf16[320,256]{1,0:T(8,128)(2,1)S(1)}, bf16[320,256]{1,0:T(8,128)(2,1)S(1)}, u32[]{:S(2)}, u32[]{:S(2)}) collective-permute-start(bf16[320,256]{1,0:T(8,128)(2,1)S(1)} %get-tuple-element.34), channel_id=1, source_target_pairs={{0,192},{1,193},{64,1},{65,0},{128,65},{129,64},{192,129},{193,128... | collective-permute-start | bytes 491528 | tf_op jit(solution)/shard_map/ppermute | solution.py:199
  14.0 3.1 %collective-permute-start.2 = (bf16[320,256]{1,0:T(8,128)(2,1)S(1)}, bf16[320,256]{1,0:T(8,128)(2,1)S(1)}, u32[]{:S(2)}, u32[]{:S(2)}) collective-permute-start(bf16[320,256]{1,0:T(8,128)(2,1)S(1)} %get-tuple-element.35), channel_id=1, source_target_pairs={{0,65},{1,64},{64,129},{65,128},{128,193},{129,192},{192,0},{193,1... | collective-permute-start | bytes 491528 | tf_op jit(solution)/shard_map/ppermute | solution.py:199
  17.1 1.5 %collective-permute-start.3 = (bf16[320,256]{1,0:T(8,128)(2,1)S(1)}, bf16[320,256]{1,0:T(8,128)(2,1)S(1)}, u32[]{:S(2)}, u32[]{:S(2)}) collective-permute-start(bf16[320,256]{1,0:T(8,128)(2,1)S(1)} %get-tuple-element.36), channel_id=1, source_target_pairs={{0,128},{1,129},{64,192},{65,193},{128,1},{129,0},{192,65},{193,64... | collective-permute-start | bytes 491528 | tf_op jit(solution)/shard_map/ppermute | solution.py:199
  18.6 2.7 %collective-permute-start.4 = (bf16[320,256]{1,0:T(8,128)(2,1)S(1)}, bf16[320,256]{1,0:T(8,128)(2,1)S(1)}, u32[]{:S(2)}, u32[]{:S(2)}) collective-permute-start(bf16[320,256]{1,0:T(8,128)(2,1)S(1)} %get-tuple-element.37), channel_id=1, source_target_pairs={{0,129},{1,128},{64,193},{65,192},{128,0},{129,1},{192,64},{193,65... | collective-permute-start | bytes 491528 | tf_op jit(solution)/shard_map/ppermute | solution.py:199
  21.2 2.8 %collective-permute-done.refs_1_ = bf16[320,256]{1,0:T(8,128)(2,1)S(1)} collective-permute-done((bf16[320,256]{1,0:T(8,128)(2,1)S(1)}, bf16[320,256]{1,0:T(8,128)(2,1)S(1)}, u32[]{:S(2)}, u32[]{:S(2)}) %collective-permute-start) | collective-permute-done | bytes 163872 | tf_op jit(solution)/shard_map/ppermute | solution.py:199
  24.0 0.3 collective-permute-start.5
  24.4 8.8 %collective-permute-done.1.refs_2_ = bf16[320,256]{1,0:T(8,128)(2,1)S(1)} collective-permute-done((bf16[320,256]{1,0:T(8,128)(2,1)S(1)}, bf16[320,256]{1,0:T(8,128)(2,1)S(1)}, u32[]{:S(2)}, u32[]{:S(2)}) %collective-permute-start.1) | collective-permute-done | bytes 163872 | tf_op jit(solution)/shard_map/ppermute | solution.py:199
  33.2 0.0 collective-permute-start.6
  33.2 0.0 copy-done
  33.2 0.9 shard_map.47
  34.1 0.0 collective-permute-done.2.refs_3_
  34.1 3.3 %collective-permute-done.3.refs_4_ = bf16[320,256]{1,0:T(8,128)(2,1)S(1)} collective-permute-done((bf16[320,256]{1,0:T(8,128)(2,1)S(1)}, bf16[320,256]{1,0:T(8,128)(2,1)S(1)}, u32[]{:S(2)}, u32[]{:S(2)}) %collective-permute-start.3) | collective-permute-done | bytes 163872 | tf_op jit(solution)/shard_map/ppermute | solution.py:199
  37.4 0.9 collective-permute-done.4.refs_5_
  38.3 2.2 %collective-permute-done.5.refs_6_ = bf16[320,256]{1,0:T(8,128)(2,1)S(1)} collective-permute-done((bf16[320,256]{1,0:T(8,128)(2,1)S(1)}, bf16[320,256]{1,0:T(8,128)(2,1)S(1)}, u32[]{:S(2)}, u32[]{:S(2)}) %collective-permute-start.5) | collective-permute-done | bytes 163872 | tf_op jit(solution)/shard_map/ppermute | solution.py:199
  40.5 1.1 collective-permute-done.6.refs_7_
  41.6 0.1 shard_map.48.refs_8_
  41.7 0.1 collective-permute-start.7
  41.8 1.5 %shard_map.49 = (bf16[640,1280]{1,0:T(8,128)(2,1)}, bf16[2,4,160,256]{3,2,1,0:T(8,128)(2,1)S(1)}) custom-call(s32[1]{0:T(128)} %bitcast.pos_ref, bf16[320,256]{1,0:T(8,128)(2,1)S(1)} %get-tuple-element.32.refs_0_, bf16[320,256]{1,0:T(8,128)(2,1)S(1)} %collective-permute-done.refs_1_, bf16[320,256]{1,0:T(8,128)(2,1)S(1)} %collective-permute-done.1.refs_2_, ...), custom_call_target="tpu_custom_call" | custom-call | flops 419430400 | bytes 3932168 | tf_op jit(solution)/shard_map/pallas_call | solution.py:183
  43.3 0.6 collective-permute-done.7.k_far
  43.9 1.5 %shard_map.50 = bf16[640,1280]{1,0:T(8,128)(2,1)} custom-call(bf16[640,1280]{1,0:T(8,128)(2,1)} %get-tuple-element.42._, bf16[2,4,160,256]{3,2,1,0:T(8,128)(2,1)S(1)} %get-tuple-element.43.q, bf16[2,4,160,256]{3,2,1,0:T(8,128)(2,1)S(1)} %collective-permute-done.7.k_far), custom_call_target="tpu_custom_call", output_to_operand_aliasing={{}: (0, {})} | custom-call | flops 419430400 | bytes 5898240 | tf_op jit(solution)/shard_map/pallas_call | solution.py:183
  45.4 7.4 %all-to-all-start = ((bf16[16,40,1280]{2,1,0:T(8,128)(2,1)}), bf16[16,40,1280]{2,1,0:T(8,128)(2,1)S(1)}, u32[]{:S(2)}, u32[]{:S(2)}) async-start(bf16[16,40,1280]{2,1,0:T(8,128)(2,1)} %bitcast.2), calls=%async_computation | async-start | bytes 3276800 | tf_op jit(solution)/shard_map/all_to_all | solution.py:270
  52.8 3.5 %collective-permute-start.8 = (bf16[160,256]{1,0:T(8,128)(2,1)S(1)}, bf16[160,256]{1,0:T(8,128)(2,1)S(1)}, u32[]{:S(2)}, u32[]{:S(2)}) collective-permute-start(bf16[160,256]{1,0:T(8,128)(2,1)S(1)} %get-tuple-element.44), channel_id=1, source_target_pairs={{0,1},{1,0},{64,65},{65,64},{128,129},{129,128},{192,193},{193,192... | collective-permute-start | bytes 245768 | tf_op jit(solution)/shard_map/ppermute | solution.py:199
  56.4 2.3 %collective-permute-start.9 = (bf16[160,256]{1,0:T(8,128)(2,1)S(1)}, bf16[160,256]{1,0:T(8,128)(2,1)S(1)}, u32[]{:S(2)}, u32[]{:S(2)}) collective-permute-start(bf16[160,256]{1,0:T(8,128)(2,1)S(1)} %get-tuple-element.45), channel_id=1, source_target_pairs={{0,192},{1,193},{64,1},{65,0},{128,65},{129,64},{192,129},{193,128... | collective-permute-start | bytes 245768 | tf_op jit(solution)/shard_map/ppermute | solution.py:199
  58.7 2.7 %collective-permute-start.10 = (bf16[160,256]{1,0:T(8,128)(2,1)S(1)}, bf16[160,256]{1,0:T(8,128)(2,1)S(1)}, u32[]{:S(2)}, u32[]{:S(2)}) collective-permute-start(bf16[160,256]{1,0:T(8,128)(2,1)S(1)} %get-tuple-element.46), channel_id=1, source_target_pairs={{0,65},{1,64},{64,129},{65,128},{128,193},{129,192},{192,0},{193,1... | collective-permute-start | bytes 245768 | tf_op jit(solution)/shard_map/ppermute | solution.py:199
  61.4 0.1 collective-permute-start.11
  61.5 2.9 %collective-permute-done.8.refs_0_.refs_1_ = bf16[160,256]{1,0:T(8,128)(2,1)S(1)} collective-permute-done((bf16[160,256]{1,0:T(8,128)(2,1)S(1)}, bf16[160,256]{1,0:T(8,128)(2,1)S(1)}, u32[]{:S(2)}, u32[]{:S(2)}) %collective-permute-start.8) | collective-permute-done | bytes 81952 | tf_op jit(solution)/shard_map/ppermute | solution.py:199
  64.4 5.4 %collective-permute-done.9.refs_1_.refs_2_ = bf16[160,256]{1,0:T(8,128)(2,1)S(1)} collective-permute-done((bf16[160,256]{1,0:T(8,128)(2,1)S(1)}, bf16[160,256]{1,0:T(8,128)(2,1)S(1)}, u32[]{:S(2)}, u32[]{:S(2)}) %collective-permute-start.9) | collective-permute-done | bytes 81952 | tf_op jit(solution)/shard_map/ppermute | solution.py:199
  69.8 0.0 collective-permute-done.10.refs_2_.refs_3_
  69.8 0.0 collective-permute-done.11.refs_3_.refs_4_
  69.8 5.6 %all-to-all-done.x_ref = bf16[16,40,1280]{2,1,0:T(8,128)(2,1)S(1)} async-done(((bf16[16,40,1280]{2,1,0:T(8,128)(2,1)}), bf16[16,40,1280]{2,1,0:T(8,128)(2,1)S(1)}, u32[]{:S(2)}, u32[]{:S(2)}) %all-to-all-start) | async-done | bytes 1638432 | tf_op jit(solution)/shard_map/all_to_all | solution.py:270
  75.4 1.6 %shard_map.51 = bf16[16,40,1280]{2,1,0:T(8,128)(2,1)} custom-call(bf16[16,40,1280]{2,1,0:T(8,128)(2,1)S(1)} %all-to-all-done.x_ref, bf16[160,256]{1,0:T(8,128)(2,1)S(1)} %collective-permute-done.8.refs_0_.refs_1_, bf16[160,256]{1,0:T(8,128)(2,1)S(1)} %collective-permute-done.9.refs_1_.refs_2_, bf16[160,256]{1,0:T(8,128)(2,1)S(1)} %collective-permute-done.10.refs_2_.refs_3_, ...), custom_call_target="tpu_custom_call" | custom-call | bytes 3932160 | tf_op jit(solution)/shard_map/pallas_call | solution.py:183
  77.0 6.2 %all-to-all-start.1 = ((bf16[16,40,1280]{2,1,0:T(8,128)(2,1)}), bf16[16,40,1280]{2,1,0:T(8,128)(2,1)S(1)}, u32[]{:S(2)}, u32[]{:S(2)}) async-start(bf16[16,40,1280]{2,1,0:T(8,128)(2,1)} %shard_map.51), calls=%async_computation.1 | async-start | bytes 3276800 | tf_op jit(solution)/shard_map/all_to_all | solution.py:280
  83.3 1.3 collective-permute-start.12
  84.5 2.8 %collective-permute-start.13 = (bf16[160,256]{1,0:T(8,128)(2,1)S(1)}, bf16[160,256]{1,0:T(8,128)(2,1)S(1)}, u32[]{:S(2)}, u32[]{:S(2)}) collective-permute-start(bf16[160,256]{1,0:T(8,128)(2,1)S(1)} %get-tuple-element.49), channel_id=1, source_target_pairs={{0,64},{1,65},{64,128},{65,129},{128,192},{129,193},{192,1},{193,0... | collective-permute-start | bytes 245768 | tf_op jit(solution)/shard_map/ppermute | solution.py:199
  87.4 0.4 collective-permute-start.14
  87.8 1.8 %collective-permute-done.12.refs_5_ = bf16[160,256]{1,0:T(8,128)(2,1)S(1)} collective-permute-done((bf16[160,256]{1,0:T(8,128)(2,1)S(1)}, bf16[160,256]{1,0:T(8,128)(2,1)S(1)}, u32[]{:S(2)}, u32[]{:S(2)}) %collective-permute-start.12) | collective-permute-done | bytes 81952 | tf_op jit(solution)/shard_map/ppermute | solution.py:199
  89.6 0.6 collective-permute-done.13.refs_6_
  90.2 1.6 %collective-permute-done.14.refs_7_ = bf16[160,256]{1,0:T(8,128)(2,1)S(1)} collective-permute-done((bf16[160,256]{1,0:T(8,128)(2,1)S(1)}, bf16[160,256]{1,0:T(8,128)(2,1)S(1)}, u32[]{:S(2)}, u32[]{:S(2)}) %collective-permute-start.14) | collective-permute-done | bytes 81952 | tf_op jit(solution)/shard_map/ppermute | solution.py:199
  91.8 0.1 shard_map.52.v_ref
  91.9 0.0 copy-start.1
  91.9 0.1 collective-permute-start.15
  92.0 2.1 %collective-permute-done.15.v_far = bf16[2,4,160,256]{3,2,1,0:T(8,128)(2,1)S(1)} collective-permute-done((bf16[2,4,160,256]{3,2,1,0:T(8,128)(2,1)S(1)}, bf16[2,4,160,256]{3,2,1,0:T(8,128)(2,1)S(1)}, u32[]{:S(2)}, u32[]{:S(2)}) %collective-permute-start.15) | collective-permute-done | bytes 655392 | tf_op jit(solution)/shard_map/ppermute | solution.py:204
  94.1 0.8 copy-done.2
  94.9 8.8 %all-to-all-done.1 = bf16[16,40,1280]{2,1,0:T(8,128)(2,1)S(1)} async-done(((bf16[16,40,1280]{2,1,0:T(8,128)(2,1)}), bf16[16,40,1280]{2,1,0:T(8,128)(2,1)S(1)}, u32[]{:S(2)}, u32[]{:S(2)}) %all-to-all-start.1) | async-done | bytes 1638432 | tf_op jit(solution)/shard_map/all_to_all | solution.py:280
  103.8 1.1 copy-done.3
  104.8 1.2 shard_map.53
  106.1 3.6 %collective-permute-start.16 = (bf16[160,256]{1,0:T(8,128)(2,1)S(1)}, bf16[160,256]{1,0:T(8,128)(2,1)S(1)}, u32[]{:S(2)}, u32[]{:S(2)}) collective-permute-start(bf16[160,256]{1,0:T(8,128)(2,1)S(1)} %get-tuple-element.52), channel_id=1, source_target_pairs={{0,1},{1,0},{64,65},{65,64},{128,129},{129,128},{192,193},{193,192... | collective-permute-start | bytes 245768 | tf_op jit(solution)/shard_map/ppermute | solution.py:199
  109.7 2.3 %collective-permute-start.17 = (bf16[160,256]{1,0:T(8,128)(2,1)S(1)}, bf16[160,256]{1,0:T(8,128)(2,1)S(1)}, u32[]{:S(2)}, u32[]{:S(2)}) collective-permute-start(bf16[160,256]{1,0:T(8,128)(2,1)S(1)} %get-tuple-element.53), channel_id=1, source_target_pairs={{0,192},{1,193},{64,1},{65,0},{128,65},{129,64},{192,129},{193,128... | collective-permute-start | bytes 245768 | tf_op jit(solution)/shard_map/ppermute | solution.py:199
  112.0 2.7 %collective-permute-start.18 = (bf16[160,256]{1,0:T(8,128)(2,1)S(1)}, bf16[160,256]{1,0:T(8,128)(2,1)S(1)}, u32[]{:S(2)}, u32[]{:S(2)}) collective-permute-start(bf16[160,256]{1,0:T(8,128)(2,1)S(1)} %get-tuple-element.54), channel_id=1, source_target_pairs={{0,65},{1,64},{64,129},{65,128},{128,193},{129,192},{192,0},{193,1... | collective-permute-start | bytes 245768 | tf_op jit(solution)/shard_map/ppermute | solution.py:199
  114.7 0.1 collective-permute-start.19
  114.8 4.0 %collective-permute-start.20 = (bf16[160,256]{1,0:T(8,128)(2,1)S(1)}, bf16[160,256]{1,0:T(8,128)(2,1)S(1)}, u32[]{:S(2)}, u32[]{:S(2)}) collective-permute-start(bf16[160,256]{1,0:T(8,128)(2,1)S(1)} %get-tuple-element.56), channel_id=1, source_target_pairs={{0,129},{1,128},{64,193},{65,192},{128,0},{129,1},{192,64},{193,65... | collective-permute-start | bytes 245768 | tf_op jit(solution)/shard_map/ppermute | solution.py:199
  118.9 0.0 collective-permute-done.16.refs_1_
  118.9 0.0 collective-permute-start.21
  118.9 2.4 %collective-permute-done.17.refs_2_ = bf16[160,256]{1,0:T(8,128)(2,1)S(1)} collective-permute-done((bf16[160,256]{1,0:T(8,128)(2,1)S(1)}, bf16[160,256]{1,0:T(8,128)(2,1)S(1)}, u32[]{:S(2)}, u32[]{:S(2)}) %collective-permute-start.17) | collective-permute-done | bytes 81952 | tf_op jit(solution)/shard_map/ppermute | solution.py:199
  121.3 0.8 collective-permute-start.22
  122.1 0.0 collective-permute-done.18.refs_3_
  122.1 0.0 collective-permute-done.19.refs_4_
  122.1 1.4 %collective-permute-done.20.refs_5_ = bf16[160,256]{1,0:T(8,128)(2,1)S(1)} collective-permute-done((bf16[160,256]{1,0:T(8,128)(2,1)S(1)}, bf16[160,256]{1,0:T(8,128)(2,1)S(1)}, u32[]{:S(2)}, u32[]{:S(2)}) %collective-permute-start.20) | collective-permute-done | bytes 81952 | tf_op jit(solution)/shard_map/ppermute | solution.py:199
  123.5 1.0 collective-permute-done.21.refs_6_
  124.5 1.2 collective-permute-done.22.refs_7_
  125.7 1.8 %shard_map.54 = f32[4,160,768]{2,1,0:T(8,128)} custom-call(s32[1]{0:T(128)} %bitcast.pos_ref, bf16[512,768]{1,0:T(8,128)(2,1)S(1)} %copy-done.1, bf16[160,256]{1,0:T(8,128)(2,1)S(1)} %get-tuple-element.51.refs_0_, bf16[160,256]{1,0:T(8,128)(2,1)S(1)} %collective-permute-done.16.refs_1_, bf16[160,256]{1,0:T(8,128)(2,1)S(1)} %collective-permute-done.17.refs_2_, ...), custom_call_target="tpu_custom_call" | custom-call | flops 503316480 | bytes 2883592 | tf_op jit(solution)/shard_map/pallas_call | solution.py:183
  (5 shorter events, 0.0 us)
Async XLA Ops:
  0.0 0.7 copy-start.4
  0.7 32.6 %copy-start = (bf16[768,3,512]{2,0,1:T(8,128)(2,1)S(1)}, bf16[768,3,512]{2,0,1:T(8,128)(2,1)}, u32[]{:S(2)}) copy-start(bf16[768,3,512]{2,0,1:T(8,128)(2,1)} %param.6) | copy-start | bytes 7077892
  4.8 19.3 %collective-permute-start = (bf16[320,256]{1,0:T(8,128)(2,1)S(1)}, bf16[320,256]{1,0:T(8,128)(2,1)S(1)}, u32[]{:S(2)}, u32[]{:S(2)}) collective-permute-start(bf16[320,256]{1,0:T(8,128)(2,1)S(1)} %get-tuple-element.33), channel_id=1, source_target_pairs={{0,1},{1,0},{64,65},{65,64},{128,129},{129,128},{192,193},{193,192... | collective-permute-start | bytes 491528 | tf_op jit(solution)/shard_map/ppermute | solution.py:199
  12.0 21.2 %collective-permute-start.1 = (bf16[320,256]{1,0:T(8,128)(2,1)S(1)}, bf16[320,256]{1,0:T(8,128)(2,1)S(1)}, u32[]{:S(2)}, u32[]{:S(2)}) collective-permute-start(bf16[320,256]{1,0:T(8,128)(2,1)S(1)} %get-tuple-element.34), channel_id=1, source_target_pairs={{0,192},{1,193},{64,1},{65,0},{128,65},{129,64},{192,129},{193,128... | collective-permute-start | bytes 491528 | tf_op jit(solution)/shard_map/ppermute | solution.py:199
  14.0 20.2 %collective-permute-start.2 = (bf16[320,256]{1,0:T(8,128)(2,1)S(1)}, bf16[320,256]{1,0:T(8,128)(2,1)S(1)}, u32[]{:S(2)}, u32[]{:S(2)}) collective-permute-start(bf16[320,256]{1,0:T(8,128)(2,1)S(1)} %get-tuple-element.35), channel_id=1, source_target_pairs={{0,65},{1,64},{64,129},{65,128},{128,193},{129,192},{192,0},{193,1... | collective-permute-start | bytes 491528 | tf_op jit(solution)/shard_map/ppermute | solution.py:199
  17.1 20.4 %collective-permute-start.3 = (bf16[320,256]{1,0:T(8,128)(2,1)S(1)}, bf16[320,256]{1,0:T(8,128)(2,1)S(1)}, u32[]{:S(2)}, u32[]{:S(2)}) collective-permute-start(bf16[320,256]{1,0:T(8,128)(2,1)S(1)} %get-tuple-element.36), channel_id=1, source_target_pairs={{0,128},{1,129},{64,192},{65,193},{128,1},{129,0},{192,65},{193,64... | collective-permute-start | bytes 491528 | tf_op jit(solution)/shard_map/ppermute | solution.py:199
  18.6 19.8 %collective-permute-start.4 = (bf16[320,256]{1,0:T(8,128)(2,1)S(1)}, bf16[320,256]{1,0:T(8,128)(2,1)S(1)}, u32[]{:S(2)}, u32[]{:S(2)}) collective-permute-start(bf16[320,256]{1,0:T(8,128)(2,1)S(1)} %get-tuple-element.37), channel_id=1, source_target_pairs={{0,129},{1,128},{64,193},{65,192},{128,0},{129,1},{192,64},{193,65... | collective-permute-start | bytes 491528 | tf_op jit(solution)/shard_map/ppermute | solution.py:199
  24.0 16.4 %collective-permute-start.5 = (bf16[320,256]{1,0:T(8,128)(2,1)S(1)}, bf16[320,256]{1,0:T(8,128)(2,1)S(1)}, u32[]{:S(2)}, u32[]{:S(2)}) collective-permute-start(bf16[320,256]{1,0:T(8,128)(2,1)S(1)} %get-tuple-element.38), channel_id=1, source_target_pairs={{0,64},{1,65},{64,128},{65,129},{128,192},{129,193},{192,1},{193,0... | collective-permute-start | bytes 491528 | tf_op jit(solution)/shard_map/ppermute | solution.py:199
  33.2 8.4 %collective-permute-start.6 = (bf16[320,256]{1,0:T(8,128)(2,1)S(1)}, bf16[320,256]{1,0:T(8,128)(2,1)S(1)}, u32[]{:S(2)}, u32[]{:S(2)}) collective-permute-start(bf16[320,256]{1,0:T(8,128)(2,1)S(1)} %get-tuple-element.39), channel_id=1, source_target_pairs={{0,193},{1,192},{64,0},{65,1},{128,64},{129,65},{192,128},{193,129... | collective-permute-start | bytes 491528 | tf_op jit(solution)/shard_map/ppermute | solution.py:199
  41.7 2.2 %collective-permute-start.7 = (bf16[2,4,160,256]{3,2,1,0:T(8,128)(2,1)S(1)}, bf16[2,4,160,256]{3,2,1,0:T(8,128)(2,1)S(1)}, u32[]{:S(2)}, u32[]{:S(2)}) collective-permute-start(bf16[2,4,160,256]{3,2,1,0:T(8,128)(2,1)S(1)} %shard_map.48.refs_8_), channel_id=1, source_target_pairs={{0,32},{32,0},{1,33},{33,1},{2,34},{34,2},{3,35},{35,3},{4,36},{36... | collective-permute-start | bytes 1966088 | tf_op jit(solution)/shard_map/ppermute | solution.py:204
  45.4 30.0 %all-to-all-start = ((bf16[16,40,1280]{2,1,0:T(8,128)(2,1)}), bf16[16,40,1280]{2,1,0:T(8,128)(2,1)S(1)}, u32[]{:S(2)}, u32[]{:S(2)}) async-start(bf16[16,40,1280]{2,1,0:T(8,128)(2,1)} %bitcast.2), calls=%async_computation | async-start | bytes 3276800 | tf_op jit(solution)/shard_map/all_to_all | solution.py:270
  52.8 11.6 %collective-permute-start.8 = (bf16[160,256]{1,0:T(8,128)(2,1)S(1)}, bf16[160,256]{1,0:T(8,128)(2,1)S(1)}, u32[]{:S(2)}, u32[]{:S(2)}) collective-permute-start(bf16[160,256]{1,0:T(8,128)(2,1)S(1)} %get-tuple-element.44), channel_id=1, source_target_pairs={{0,1},{1,0},{64,65},{65,64},{128,129},{129,128},{192,193},{193,192... | collective-permute-start | bytes 245768 | tf_op jit(solution)/shard_map/ppermute | solution.py:199
  56.4 13.5 %collective-permute-start.9 = (bf16[160,256]{1,0:T(8,128)(2,1)S(1)}, bf16[160,256]{1,0:T(8,128)(2,1)S(1)}, u32[]{:S(2)}, u32[]{:S(2)}) collective-permute-start(bf16[160,256]{1,0:T(8,128)(2,1)S(1)} %get-tuple-element.45), channel_id=1, source_target_pairs={{0,192},{1,193},{64,1},{65,0},{128,65},{129,64},{192,129},{193,128... | collective-permute-start | bytes 245768 | tf_op jit(solution)/shard_map/ppermute | solution.py:199
  58.7 11.1 %collective-permute-start.10 = (bf16[160,256]{1,0:T(8,128)(2,1)S(1)}, bf16[160,256]{1,0:T(8,128)(2,1)S(1)}, u32[]{:S(2)}, u32[]{:S(2)}) collective-permute-start(bf16[160,256]{1,0:T(8,128)(2,1)S(1)} %get-tuple-element.46), channel_id=1, source_target_pairs={{0,65},{1,64},{64,129},{65,128},{128,193},{129,192},{192,0},{193,1... | collective-permute-start | bytes 245768 | tf_op jit(solution)/shard_map/ppermute | solution.py:199
  61.4 8.4 %collective-permute-start.11 = (bf16[160,256]{1,0:T(8,128)(2,1)S(1)}, bf16[160,256]{1,0:T(8,128)(2,1)S(1)}, u32[]{:S(2)}, u32[]{:S(2)}) collective-permute-start(bf16[160,256]{1,0:T(8,128)(2,1)S(1)} %get-tuple-element.47), channel_id=1, source_target_pairs={{0,128},{1,129},{64,192},{65,193},{128,1},{129,0},{192,65},{193,64... | collective-permute-start | bytes 245768 | tf_op jit(solution)/shard_map/ppermute | solution.py:199
  77.0 26.7 %all-to-all-start.1 = ((bf16[16,40,1280]{2,1,0:T(8,128)(2,1)}), bf16[16,40,1280]{2,1,0:T(8,128)(2,1)S(1)}, u32[]{:S(2)}, u32[]{:S(2)}) async-start(bf16[16,40,1280]{2,1,0:T(8,128)(2,1)} %shard_map.51), calls=%async_computation.1 | async-start | bytes 3276800 | tf_op jit(solution)/shard_map/all_to_all | solution.py:280
  83.3 6.3 %collective-permute-start.12 = (bf16[160,256]{1,0:T(8,128)(2,1)S(1)}, bf16[160,256]{1,0:T(8,128)(2,1)S(1)}, u32[]{:S(2)}, u32[]{:S(2)}) collective-permute-start(bf16[160,256]{1,0:T(8,128)(2,1)S(1)} %get-tuple-element.48), channel_id=1, source_target_pairs={{0,129},{1,128},{64,193},{65,192},{128,0},{129,1},{192,64},{193,65... | collective-permute-start | bytes 245768 | tf_op jit(solution)/shard_map/ppermute | solution.py:199
  84.5 5.7 %collective-permute-start.13 = (bf16[160,256]{1,0:T(8,128)(2,1)S(1)}, bf16[160,256]{1,0:T(8,128)(2,1)S(1)}, u32[]{:S(2)}, u32[]{:S(2)}) collective-permute-start(bf16[160,256]{1,0:T(8,128)(2,1)S(1)} %get-tuple-element.49), channel_id=1, source_target_pairs={{0,64},{1,65},{64,128},{65,129},{128,192},{129,193},{192,1},{193,0... | collective-permute-start | bytes 245768 | tf_op jit(solution)/shard_map/ppermute | solution.py:199
  87.4 4.4 %collective-permute-start.14 = (bf16[160,256]{1,0:T(8,128)(2,1)S(1)}, bf16[160,256]{1,0:T(8,128)(2,1)S(1)}, u32[]{:S(2)}, u32[]{:S(2)}) collective-permute-start(bf16[160,256]{1,0:T(8,128)(2,1)S(1)} %get-tuple-element.50), channel_id=1, source_target_pairs={{0,193},{1,192},{64,0},{65,1},{128,64},{129,65},{192,128},{193,129... | collective-permute-start | bytes 245768 | tf_op jit(solution)/shard_map/ppermute | solution.py:199
  91.9 33.8 %copy-start.1 = (bf16[512,768]{1,0:T(8,128)(2,1)S(1)}, bf16[512,768]{1,0:T(8,128)(2,1)}, u32[]{:S(2)}) copy-start(bf16[512,768]{1,0:T(8,128)(2,1)} %w_ref.1) | copy-start | bytes 2359300
  91.9 2.2 %collective-permute-start.15 = (bf16[2,4,160,256]{3,2,1,0:T(8,128)(2,1)S(1)}, bf16[2,4,160,256]{3,2,1,0:T(8,128)(2,1)S(1)}, u32[]{:S(2)}, u32[]{:S(2)}) collective-permute-start(bf16[2,4,160,256]{3,2,1,0:T(8,128)(2,1)S(1)} %shard_map.52.v_ref), channel_id=1, source_target_pairs={{0,32},{32,0},{1,33},{33,1},{2,34},{34,2},{3,35},{35,3},{4,36},{36... | collective-permute-start | bytes 1966088 | tf_op jit(solution)/shard_map/ppermute | solution.py:204
  94.1 0.8 copy-start.2
  103.8 1.1 copy-start.3
  106.1 12.8 %collective-permute-start.16 = (bf16[160,256]{1,0:T(8,128)(2,1)S(1)}, bf16[160,256]{1,0:T(8,128)(2,1)S(1)}, u32[]{:S(2)}, u32[]{:S(2)}) collective-permute-start(bf16[160,256]{1,0:T(8,128)(2,1)S(1)} %get-tuple-element.52), channel_id=1, source_target_pairs={{0,1},{1,0},{64,65},{65,64},{128,129},{129,128},{192,193},{193,192... | collective-permute-start | bytes 245768 | tf_op jit(solution)/shard_map/ppermute | solution.py:199
  109.7 11.6 %collective-permute-start.17 = (bf16[160,256]{1,0:T(8,128)(2,1)S(1)}, bf16[160,256]{1,0:T(8,128)(2,1)S(1)}, u32[]{:S(2)}, u32[]{:S(2)}) collective-permute-start(bf16[160,256]{1,0:T(8,128)(2,1)S(1)} %get-tuple-element.53), channel_id=1, source_target_pairs={{0,192},{1,193},{64,1},{65,0},{128,65},{129,64},{192,129},{193,128... | collective-permute-start | bytes 245768 | tf_op jit(solution)/shard_map/ppermute | solution.py:199
  112.0 10.1 %collective-permute-start.18 = (bf16[160,256]{1,0:T(8,128)(2,1)S(1)}, bf16[160,256]{1,0:T(8,128)(2,1)S(1)}, u32[]{:S(2)}, u32[]{:S(2)}) collective-permute-start(bf16[160,256]{1,0:T(8,128)(2,1)S(1)} %get-tuple-element.54), channel_id=1, source_target_pairs={{0,65},{1,64},{64,129},{65,128},{128,193},{129,192},{192,0},{193,1... | collective-permute-start | bytes 245768 | tf_op jit(solution)/shard_map/ppermute | solution.py:199
  114.7 7.4 %collective-permute-start.19 = (bf16[160,256]{1,0:T(8,128)(2,1)S(1)}, bf16[160,256]{1,0:T(8,128)(2,1)S(1)}, u32[]{:S(2)}, u32[]{:S(2)}) collective-permute-start(bf16[160,256]{1,0:T(8,128)(2,1)S(1)} %get-tuple-element.55), channel_id=1, source_target_pairs={{0,128},{1,129},{64,192},{65,193},{128,1},{129,0},{192,65},{193,64... | collective-permute-start | bytes 245768 | tf_op jit(solution)/shard_map/ppermute | solution.py:199
  114.8 8.6 %collective-permute-start.20 = (bf16[160,256]{1,0:T(8,128)(2,1)S(1)}, bf16[160,256]{1,0:T(8,128)(2,1)S(1)}, u32[]{:S(2)}, u32[]{:S(2)}) collective-permute-start(bf16[160,256]{1,0:T(8,128)(2,1)S(1)} %get-tuple-element.56), channel_id=1, source_target_pairs={{0,129},{1,128},{64,193},{65,192},{128,0},{129,1},{192,64},{193,65... | collective-permute-start | bytes 245768 | tf_op jit(solution)/shard_map/ppermute | solution.py:199
  118.9 5.7 %collective-permute-start.21 = (bf16[160,256]{1,0:T(8,128)(2,1)S(1)}, bf16[160,256]{1,0:T(8,128)(2,1)S(1)}, u32[]{:S(2)}, u32[]{:S(2)}) collective-permute-start(bf16[160,256]{1,0:T(8,128)(2,1)S(1)} %get-tuple-element.57), channel_id=1, source_target_pairs={{0,64},{1,65},{64,128},{65,129},{128,192},{129,193},{192,1},{193,0... | collective-permute-start | bytes 245768 | tf_op jit(solution)/shard_map/ppermute | solution.py:199
  121.3 4.4 %collective-permute-start.22 = (bf16[160,256]{1,0:T(8,128)(2,1)S(1)}, bf16[160,256]{1,0:T(8,128)(2,1)S(1)}, u32[]{:S(2)}, u32[]{:S(2)}) collective-permute-start(bf16[160,256]{1,0:T(8,128)(2,1)S(1)} %get-tuple-element.58), channel_id=1, source_target_pairs={{0,193},{1,192},{64,0},{65,1},{128,64},{129,65},{192,128},{193,129... | collective-permute-start | bytes 245768 | tf_op jit(solution)/shard_map/ppermute | solution.py:199

commit v7 on v6

--- a/solution.py
+++ b/solution.py
@@ -20,6 +20,8 @@
 HBM = pl.BlockSpec(memory_space=pltpu.HBM)
 ANY = pl.BlockSpec(memory_space=pl.ANY)
 SMEM = pl.BlockSpec(memory_space=pltpu.SMEM)
+LINE = 4
+LINE_STEPS = (0, 2, 1, 3)
 CUTS = 4
 MIB = 1024 * 1024
 
@@ -74,15 +76,11 @@
             both[i][(1 - c) * length : (2 - c) * length] = mine[head_at(pos + s)]
 
 
-def values_kernel(seqs, pos_ref, normed, w_hbm, *refs):
-    outs, (mine, w_ref, w_sem) = refs[:RING], refs[RING:]
+def values_kernel(seqs, normed, w_hbm, out_ref, w_ref, w_sem):
     copy = pltpu.make_async_copy(w_hbm.at[2], w_ref, w_sem)
     copy.start()
     copy.wait()
-    blocks_by_head(jnp.dot(normed[...], w_ref[...], preferred_element_type=F32), seqs, mine)
-    pos = pos_ref[0]
-    for i, s in enumerate(STEPS):
-        outs[i][...] = mine[head_at(pos + s)]
+    blocks_by_head(jnp.dot(normed[...], w_ref[...], preferred_element_type=F32), seqs, out_ref)
 
 
 def cuts(rows, count):
@@ -100,62 +98,66 @@
     put_by_sender(pos_ref[0], refs[:count], 0, refs[-1])
 
 
-def half_terms(q, keys, side, out_hbm, terms, sem):
-    length = keys.shape[2]
-    half = keys.shape[1] * length
-    columns = pl.ds(side * half, half)
-    total = None
+def logits_kernel(pos_ref, *refs):
+    parts, k_ref, k_far = refs[:RING], refs[RING], refs[RING + 1]
+    outs, q = refs[RING + 2 : -1], refs[-1]
+    rows = q.shape[2]
+    length = k_ref.shape[2]
+    half = k_ref.shape[1] * length
+    for part, s in zip(parts, STEPS):
+        run = lax.div(lax.rem(pos_ref[0] + RING - s, RING), Z)
+        block = -s % Z
+        side = block * 2 // Z
+        for i in range(length // rows):
+            chunk = block * length // rows + i - side * LINE
+            slot = lax.rem(chunk + LINE - pos_ref[1 + side], LINE)
+            q[run, side * LINE + slot] = part[length + i * rows : length + (i + 1) * rows]
+    for core, keys in enumerate((k_ref, k_far)):
+        total = None
+        for w in range(W):
+            term = lax.dot_general(
+                q[w].reshape(half, -1), keys[w].reshape(half, -1), (((1,), (1,)), ((), ())), preferred_element_type=F32
+            )
+            total = term if total is None else total + term
+        total = total.astype(BF)
+        for i, out in enumerate(outs):
+            out[:, core * half : (core + 1) * half] = total[i * rows : (i + 1) * rows]
+
+
+def added(parts):
+    total = parts[0][...].astype(F32)
+    for part in parts[1:]:
+        total = total + part[...].astype(F32)
+    return total
+
+
+def sum_kernel(*refs):
+    for side in range(2):
+        refs[2 * LINE + side][...] = added(refs[side * LINE : (side + 1) * LINE]).astype(BF)
+
+
+def probs_kernel(scale, *refs):
+    for side in range(2):
+        expo = jnp.exp(added(refs[side * LINE : (side + 1) * LINE]) * scale)
+        refs[side - 2][...] = (expo / jnp.sum(expo, axis=-1, keepdims=True)).astype(BF)
+
+
+def context_kernel(pos_ref, *refs):
+    parts, v_ref, v_far = refs[: 2 * LINE], refs[2 * LINE], refs[2 * LINE + 1]
+    outs, (probs, mine) = refs[2 * LINE + 2 : -2], refs[-2:]
+    for side in range(2):
+        for part, s in zip(parts[side * LINE : (side + 1) * LINE], LINE_STEPS):
+            probs[side * LINE + lax.rem(pos_ref[1 + side] + LINE - s, LINE)] = part[...]
+    length = v_ref.shape[1]
+    half = Z * length
+    p = probs[...].reshape(half, -1)
     for w in range(W):
-        term = lax.dot_general(
-            q[w].reshape(half, -1), keys[w].reshape(half, -1), (((1,), (1,)), ((), ())), preferred_element_type=F32
-        )
-        total = term if total is None else total + term
-    copies = []
-    for i, rows in enumerate(cuts(half, Z)):
-        terms[rows] = total[i * length : (i + 1) * length].astype(BF)
-        copies.append(pltpu.make_async_copy(terms.at[rows], out_hbm.at[rows, columns], sem.at[i]))
-        copies[i].start()
-    for copy in copies:
-        copy.wait()
-
-
-def near_kernel(pos_ref, *refs):
-    parts, (k_ref, out_hbm, q, terms, sem) = refs[:RING], refs[RING:]
-    put_by_sender(pos_ref[0], parts, q.shape[2], q)
-    half_terms(q, k_ref, 0, out_hbm, terms, sem)
-
-
-def far_kernel(_, q, k_far, out_hbm, terms, sem):
-    half_terms(q, k_far, 1, out_hbm, terms, sem)
-
-
-def probs_kernel(scale, x_ref, *refs):
-    out_hbm, probs, sem = refs[-3:]
-    logits = x_ref[0].astype(F32)
-    for i in range(1, x_ref.shape[0]):
-        logits = logits + x_ref[i].astype(F32)
-    expo = jnp.exp(logits * scale)
-    probs[...] = (expo / jnp.sum(expo, axis=-1, keepdims=True)).astype(BF)
-    copies = [pltpu.make_async_copy(probs, out_hbm.at[i], sem.at[i]) for i in range(PLANE)]
-    for copy in copies:
-        copy.start()
-    for copy in copies:
-        copy.wait()
-
-
-def context_kernel(pos_ref, p_ref, v_ref, v_far, *refs):
-    outs, mine = refs[:RING], refs[RING]
-    half = v_ref.shape[1] * v_ref.shape[2]
-    length = v_ref.shape[2]
-    for w in range(W):
-        a = jnp.dot(p_ref[:, :half], v_ref[w].reshape(half, -1), preferred_element_type=F32)
-        a = a + jnp.dot(p_ref[:, half:], v_far[w].reshape(half, -1), preferred_element_type=F32)
-        a = a.astype(BF)
-        for z in range(Z):
-            mine[w * Z + z] = a[z * length : (z + 1) * length]
-    pos = pos_ref[0]
+        near, far = (jnp.concatenate([v[z * W + w] for z in range(Z)], axis=0) for v in (v_ref, v_far))
+        a = jnp.dot(p[:, :half], near, preferred_element_type=F32)
+        a = a + jnp.dot(p[:, half:], far, preferred_element_type=F32)
+        mine[w] = a.astype(BF).reshape(mine.shape[1:])
     for i, s in enumerate(STEPS):
-        outs[i][...] = mine[lax.rem(pos + s, RING)]
+        outs[i][...] = mine[lax.div(lax.rem(pos_ref[0] + s, RING), Z), s % Z]
 
 
 def mix_kernel(pos_ref, w_ref, *refs):
@@ -200,6 +202,13 @@
     return got
 
 
+def along_line(parts, axis):
+    return [
+        lax.ppermute(part, axis, [(i, (i + s) % LINE) for i in range(LINE)]) if s else part
+        for part, s in zip(parts, LINE_STEPS)
+    ]
+
+
 def other_core(a):
     return lax.ppermute(a, "c", [(0, 1), (1, 0)])
 
@@ -208,7 +217,8 @@
     seqs, length, width = tokens.shape
     inner = w_qkv.shape[2]
     lanes = seqs * HEAD_DIM
-    pos = (lax.axis_index("w") * Z + lax.axis_index("z")).astype(jnp.int32).reshape(1)
+    ring = lax.axis_index("w") * Z + lax.axis_index("z")
+    pos = jnp.stack([ring, lax.axis_index("x"), lax.axis_index("y")]).astype(jnp.int32)
     pair = jax.ShapeDtypeStruct((2 * length, lanes), BF)
     block = jax.ShapeDtypeStruct((length, lanes), BF)
     whole = jax.ShapeDtypeStruct((W, Z, length, lanes), BF)
@@ -238,53 +248,39 @@
     both = along_ring(both)
     values = call(
         functools.partial(values_kernel, seqs),
-        [block] * RING,
-        [pos, normed, weights],
-        [pltpu.VMEM((RING, length, lanes), BF), pltpu.VMEM((width, inner), BF), dma],
+        jax.ShapeDtypeStruct((RING, length, lanes), BF),
+        [normed, weights],
+        [pltpu.VMEM((width, inner), BF), dma],
         flops=2 * seqs * length * width * inner,
-        hbm=(2,),
-        vmem=20,
-    )
-    keys = call(functools.partial(place_kernel, RING), whole, [pos, *both, values[0]], unread=(1 + RING,))
+        hbm=(1,),
+    )
+    keys = call(functools.partial(place_kernel, RING), whole, [pos, *both, values], unread=(1 + RING,))
     keys_far = other_core(keys)
-    values = along_ring(values)
-    term, query = call(
-        near_kernel,
-        [jax.ShapeDtypeStruct((half, full), BF), whole],
-        [pos, *both, keys],
-        [pltpu.VMEM((half, half), BF), dma((Z,))],
-        flops=2 * half * half * W * lanes,
-        out_specs=[HBM, VMEM],
-    )
-    term = call(
-        far_kernel,
-        jax.ShapeDtypeStruct((half, full), BF),
-        [term, query, keys_far],
-        [pltpu.VMEM((half, half), BF), dma((Z,))],
-        flops=2 * half * half * W * lanes,
-        hbm=(0,),
-        out_specs=HBM,
-        aliases={0: 0},
-    )
-    chunk = (PLANE, half // PLANE, full)
-    terms = lax.all_to_all(term.reshape(chunk), ("x", "y"), 0, 0, tiled=True)
-    early = values[1:5]
-    probs = call(
-        functools.partial(probs_kernel, scale),
-        jax.ShapeDtypeStruct(chunk, BF),
-        [terms, *early],
-        [pltpu.VMEM(chunk[1:], BF), dma((PLANE,))],
-        unread=range(1, 5),
-        out_specs=HBM,
-    )
-    probs = lax.all_to_all(probs, ("x", "y"), 0, 0, tiled=True).reshape(half, full)
-    values = call(functools.partial(place_kernel, RING), whole, [pos, *values])
+    values = lax.all_to_all(values, ("z", "w"), 0, 0, tiled=True)
+    strip = jax.ShapeDtypeStruct((half // (2 * LINE), full), BF)
+    terms = call(
+        logits_kernel,
+        [strip] * (2 * LINE),
+        [pos, *both, keys, keys_far],
+        [pltpu.VMEM((W, 2 * LINE, strip.shape[0], lanes), BF)],
+        flops=2 * half * full * W * lanes,
+    )
+    by_x = along_line([terms[s] for s in LINE_STEPS], "x")
+    by_y = along_line([terms[LINE + s] for s in LINE_STEPS], "y")
+    by_x, by_y = call(sum_kernel, [strip] * 2, [*by_x, *by_y])
+    by_x = along_line([by_x] * LINE, "y")
+    by_y = along_line([by_y] * LINE, "x")
+    by_x, by_y = call(
+        functools.partial(probs_kernel, scale), [strip] * 2, [*by_x, *by_y, values], unread=(2 * LINE,)
+    )
+    by_x = along_line([by_x] * LINE, "x")
+    by_y = along_line([by_y] * LINE, "y")
     values_far = other_core(values)
     context = call(
         context_kernel,
         [block] * RING,
-        [pos, probs, values, values_far],
-        [pltpu.VMEM((RING, length, lanes), BF)],
+        [pos, *by_x, *by_y, values, values_far],
+        [pltpu.VMEM((2 * LINE, *strip.shape), BF), pltpu.VMEM(whole.shape, BF)],
         flops=2 * half * full * W * lanes,
     )
     context = along_ring(context)

time: 128 us -> 135 us (1.055)
  starting transfers between devices: 57.5 us -> 63.8 us
    ppermute x0 -> x18, waiting for transfers between devices: none -> 32.8 us  [along_line(): lax.ppermute(part, axis, [(i, (i + s) % LINE) for i in range(LINE)])]
    ppermute x0 -> x18, starting transfers between devices: none -> 24.2 us  [along_line(): lax.ppermute(part, axis, [(i, (i + s) % LINE) for i in range(LINE)])]
    ppermute x21 -> x14, waiting for transfers between devices: 37.5 us -> 20.8 us  [along_ring(): got.append(lax.ppermute(part, ('z', 'w'), pairs) if s else part)]
    all_to_all x2 -> x1, waiting for transfers between devices: 14.4 us -> 0.01 us  [shards(): values = lax.all_to_all(values, ('z', 'w'), 0, 0, tiled=True)]
    all_to_all x2 -> x1, starting transfers between devices: 13.7 us -> 4.82 us  [shards(): values = lax.all_to_all(values, ('z', 'w'), 0, 0, tiled=True)]
    ppermute x21 -> x14, starting transfers between devices: 43.6 us -> 34.7 us  [along_ring(): got.append(lax.ppermute(part, ('z', 'w'), pairs) if s else part)]
    ppermute x2, waiting for transfers between devices: 2.65 us -> 0.01 us  [other_core(): return lax.ppermute(a, 'c', [(0, 1), (1, 0)])]
    pallas_call x9 -> x8, Pallas kernels: 12.7 us -> 13.2 us  [call(): pl.pallas_call(kernel, out_shape=out_shape, in_specs=specs, out_specs=out...]
  transfers between devices with their start and end apart: 25 -> 35, of which waited for: 19 -> 18; matrix products, arithmetic and copies ran while one was open for 0% -> 0% of each run, Pallas kernels for 2% -> 3%
where the time goes in v7:
time: 135 us; the launch traced here: 133 us
  starting transfers between devices  63.8 us (47%)
  waiting for transfers between devices  53.6 us (40%)
  Pallas kernels  13.2 us (10%)
  local copies, waits for them, and re-layouts  2.41 us (2%)
    ppermute x14, starting transfers between devices, along_ring(): got.append(lax.ppermute(part, ('z', 'w'), pairs) if s else part)  34.7 us
    ppermute x18, waiting for transfers between devices, along_line(): lax.ppermute(part, axis, [(i, (i + s) % LINE) for i in range(LINE)])  32.8 us
    ppermute x18, starting transfers between devices, along_line(): lax.ppermute(part, axis, [(i, (i + s) % LINE) for i in range(LINE)])  24.2 us
    ppermute x14, waiting for transfers between devices, along_ring(): got.append(lax.ppermute(part, ('z', 'w'), pairs) if s else part)  20.8 us
    pallas_call x8, Pallas kernels, call(): pl.pallas_call(kernel, out_shape=out_shape, in_specs=specs, out_specs=out...  13.2 us
    all_to_all x1, starting transfers between devices, shards(): values = lax.all_to_all(values, ('z', 'w'), 0, 0, tiled=True)  4.82 us
  transfers between devices with their start and end apart: 35, of which 18 were waited for; matrix products, arithmetic and copies ran while one was open for 0% of the time, Pallas kernels for 3%

profile of v7, /device:TPU:6, one launch (start us, length us, event | category | flops | bytes accessed | tf_op | source)
XLA Modules:
  0.0 133.4 jit_solution(17792049842297327398)
XLA Ops:
  0.0 0.1 pad_add_fusion.pos_ref
  0.1 0.8 copy-done.4
  0.9 4.5 %shard_map.46 = (bf16[320,256]{1,0:T(8,128)(2,1)S(1)}, bf16[320,256]{1,0:T(8,128)(2,1)S(1)}, bf16[320,256]{1,0:T(8,128)(2,1)S(1)}, bf16[320,256]{1,0:T(8,128)(2,...) custom-call(s32[3]{0:T(128)S(1)} %pad_add_fusion.pos_ref, ...), custom_call_target="tpu_custom_call" | custom-call | flops 1006632960 | bytes 6690840 | tf_op jit(solution)/shard_map/pallas_call | solution.py:185
  5.4 7.3 %collective-permute-start = (bf16[320,256]{1,0:T(8,128)(2,1)S(1)}, bf16[320,256]{1,0:T(8,128)(2,1)S(1)}, u32[]{:S(2)}, u32[]{:S(2)}) collective-permute-start(bf16[320,256]{1,0:T(8,128)(2,1)S(1)} %get-tuple-element.35), channel_id=1, source_target_pairs={{0,1},{1,0},{64,65},{65,64},{128,129},{129,128},{192,193},{193,192... | collective-permute-start | bytes 491528 | tf_op jit(solution)/shard_map/ppermute | solution.py:201
  12.7 1.9 %collective-permute-start.1 = (bf16[320,256]{1,0:T(8,128)(2,1)S(1)}, bf16[320,256]{1,0:T(8,128)(2,1)S(1)}, u32[]{:S(2)}, u32[]{:S(2)}) collective-permute-start(bf16[320,256]{1,0:T(8,128)(2,1)S(1)} %get-tuple-element.36), channel_id=1, source_target_pairs={{0,192},{1,193},{64,1},{65,0},{128,65},{129,64},{192,129},{193,128... | collective-permute-start | bytes 491528 | tf_op jit(solution)/shard_map/ppermute | solution.py:201
  14.6 3.1 %collective-permute-start.2 = (bf16[320,256]{1,0:T(8,128)(2,1)S(1)}, bf16[320,256]{1,0:T(8,128)(2,1)S(1)}, u32[]{:S(2)}, u32[]{:S(2)}) collective-permute-start(bf16[320,256]{1,0:T(8,128)(2,1)S(1)} %get-tuple-element.37), channel_id=1, source_target_pairs={{0,65},{1,64},{64,129},{65,128},{128,193},{129,192},{192,0},{193,1... | collective-permute-start | bytes 491528 | tf_op jit(solution)/shard_map/ppermute | solution.py:201
  17.7 1.5 %collective-permute-start.3 = (bf16[320,256]{1,0:T(8,128)(2,1)S(1)}, bf16[320,256]{1,0:T(8,128)(2,1)S(1)}, u32[]{:S(2)}, u32[]{:S(2)}) collective-permute-start(bf16[320,256]{1,0:T(8,128)(2,1)S(1)} %get-tuple-element.38), channel_id=1, source_target_pairs={{0,128},{1,129},{64,192},{65,193},{128,1},{129,0},{192,65},{193,64... | collective-permute-start | bytes 491528 | tf_op jit(solution)/shard_map/ppermute | solution.py:201
  19.2 2.7 %collective-permute-start.4 = (bf16[320,256]{1,0:T(8,128)(2,1)S(1)}, bf16[320,256]{1,0:T(8,128)(2,1)S(1)}, u32[]{:S(2)}, u32[]{:S(2)}) collective-permute-start(bf16[320,256]{1,0:T(8,128)(2,1)S(1)} %get-tuple-element.39), channel_id=1, source_target_pairs={{0,129},{1,128},{64,193},{65,192},{128,0},{129,1},{192,64},{193,65... | collective-permute-start | bytes 491528 | tf_op jit(solution)/shard_map/ppermute | solution.py:201
  21.8 2.8 %collective-permute-done.refs_1_ = bf16[320,256]{1,0:T(8,128)(2,1)S(1)} collective-permute-done((bf16[320,256]{1,0:T(8,128)(2,1)S(1)}, bf16[320,256]{1,0:T(8,128)(2,1)S(1)}, u32[]{:S(2)}, u32[]{:S(2)}) %collective-permute-start) | collective-permute-done | bytes 163872 | tf_op jit(solution)/shard_map/ppermute | solution.py:201
  24.7 0.3 collective-permute-start.5
  25.0 8.8 %collective-permute-done.1.refs_2_ = bf16[320,256]{1,0:T(8,128)(2,1)S(1)} collective-permute-done((bf16[320,256]{1,0:T(8,128)(2,1)S(1)}, bf16[320,256]{1,0:T(8,128)(2,1)S(1)}, u32[]{:S(2)}, u32[]{:S(2)}) %collective-permute-start.1) | collective-permute-done | bytes 163872 | tf_op jit(solution)/shard_map/ppermute | solution.py:201
  33.9 0.0 collective-permute-start.6
  33.9 1.7 %shard_map.47.refs_8_ = bf16[8,160,256]{2,1,0:T(8,128)(2,1)} custom-call(bf16[640,768]{1,0:T(8,128)(2,1)S(1)} %get-tuple-element.42.normed, bf16[3,768,512]{2,1,0:T(8,128)(2,1)S(1)} %bitcast.5), custom_call_target="tpu_custom_call" | custom-call | flops 503316480 | bytes 6684672 | tf_op jit(solution)/shard_map/pallas_call | solution.py:185
  35.6 2.5 %collective-permute-done.3.refs_4_ = bf16[320,256]{1,0:T(8,128)(2,1)S(1)} collective-permute-done((bf16[320,256]{1,0:T(8,128)(2,1)S(1)}, bf16[320,256]{1,0:T(8,128)(2,1)S(1)}, u32[]{:S(2)}, u32[]{:S(2)}) %collective-permute-start.3) | collective-permute-done | bytes 163872 | tf_op jit(solution)/shard_map/ppermute | solution.py:201
  38.1 0.9 collective-permute-done.4.refs_5_
  38.9 2.2 %collective-permute-done.5.refs_6_ = bf16[320,256]{1,0:T(8,128)(2,1)S(1)} collective-permute-done((bf16[320,256]{1,0:T(8,128)(2,1)S(1)}, bf16[320,256]{1,0:T(8,128)(2,1)S(1)}, u32[]{:S(2)}, u32[]{:S(2)}) %collective-permute-start.5) | collective-permute-done | bytes 163872 | tf_op jit(solution)/shard_map/ppermute | solution.py:201
  41.1 1.1 collective-permute-done.6.refs_7_
  42.2 0.6 shard_map.48.refs_8_
  42.9 0.7 copy-done.2
  43.5 0.0 collective-permute-start.7
  43.5 4.8 %all-to-all-start = ((bf16[8,160,256]{2,1,0:T(8,128)(2,1)}), bf16[8,160,256]{2,1,0:T(8,128)(2,1)S(1)}, u32[]{:S(2)}, u32[]{:S(2)}) async-start(bf16[8,160,256]{2,1,0:T(8,128)(2,1)} %shard_map.47.refs_8_), calls=%async_computation | async-start | bytes 1310720 | tf_op jit(solution)/shard_map/all_to_all | solution.py:259
  48.3 0.0 collective-permute-done.7.refs_9_
  48.4 0.9 copy-done.3
  49.3 1.8 %shard_map.49 = (bf16[80,1280]{1,0:T(8,128)(2,1)S(1)}, bf16[80,1280]{1,0:T(8,128)(2,1)S(1)}, bf16[80,1280]{1,0:T(8,128)(2,1)S(1)}, bf16[80,1280]{1,0:T(8,128)(2,...) custom-call(s32[3]{0:T(128)S(1)} %pad_add_fusion.pos_ref, ...), custom_call_target="tpu_custom_call" | custom-call | flops 838860800 | bytes 5242904 | tf_op jit(solution)/shard_map/pallas_call | solution.py:185
  51.0 1.5 %collective-permute-start.8 = (bf16[80,1280]{1,0:T(8,128)(2,1)S(1)}, bf16[80,1280]{1,0:T(8,128)(2,1)S(1)}, u32[]{:S(2)}, u32[]{:S(2)}) collective-permute-start(bf16[80,1280]{1,0:T(8,128)(2,1)S(1)} %get-tuple-element.44), channel_id=1, source_target_pairs={{0,16},{8,24},{16,0},{24,8},{1,17},{9,25},{17,1},{25,9},{2,18},{10... | collective-permute-start | bytes 614408 | tf_op jit(solution)/shard_map/ppermute | solution.py:207
  52.5 2.1 %collective-permute-start.9 = (bf16[80,1280]{1,0:T(8,128)(2,1)S(1)}, bf16[80,1280]{1,0:T(8,128)(2,1)S(1)}, u32[]{:S(2)}, u32[]{:S(2)}) collective-permute-start(bf16[80,1280]{1,0:T(8,128)(2,1)S(1)} %get-tuple-element.45), channel_id=1, source_target_pairs={{0,8},{8,16},{16,24},{24,0},{1,9},{9,17},{17,25},{25,1},{2,10},{10... | collective-permute-start | bytes 614408 | tf_op jit(solution)/shard_map/ppermute | solution.py:207
  54.6 0.0 collective-permute-start.10
  54.6 3.2 %collective-permute-start.11 = (bf16[80,1280]{1,0:T(8,128)(2,1)S(1)}, bf16[80,1280]{1,0:T(8,128)(2,1)S(1)}, u32[]{:S(2)}, u32[]{:S(2)}) collective-permute-start(bf16[80,1280]{1,0:T(8,128)(2,1)S(1)} %get-tuple-element.48), channel_id=1, source_target_pairs={{0,4},{2,6},{4,0},{6,2},{1,5},{3,7},{5,1},{7,3},{8,12},{10,14},{12... | collective-permute-start | bytes 614408 | tf_op jit(solution)/shard_map/ppermute | solution.py:207
  57.8 0.7 collective-permute-start.12
  58.5 2.0 %collective-permute-done.8.refs_1_ = bf16[80,1280]{1,0:T(8,128)(2,1)S(1)} collective-permute-done((bf16[80,1280]{1,0:T(8,128)(2,1)S(1)}, bf16[80,1280]{1,0:T(8,128)(2,1)S(1)}, u32[]{:S(2)}, u32[]{:S(2)}) %collective-permute-start.8) | collective-permute-done | bytes 204832 | tf_op jit(solution)/shard_map/ppermute | solution.py:207
  60.5 3.0 %collective-permute-start.13 = (bf16[80,1280]{1,0:T(8,128)(2,1)S(1)}, bf16[80,1280]{1,0:T(8,128)(2,1)S(1)}, u32[]{:S(2)}, u32[]{:S(2)}) collective-permute-start(bf16[80,1280]{1,0:T(8,128)(2,1)S(1)} %get-tuple-element.50), channel_id=1, source_target_pairs={{0,6},{2,0},{4,2},{6,4},{1,7},{3,1},{5,3},{7,5},{8,14},{10,8},{12,... | collective-permute-start | bytes 614408 | tf_op jit(solution)/shard_map/ppermute | solution.py:207
  63.6 0.7 collective-permute-done.10.refs_3_
  64.2 0.0 collective-permute-done.11.refs_5_
  64.2 2.9 %collective-permute-done.12.refs_6_ = bf16[80,1280]{1,0:T(8,128)(2,1)S(1)} collective-permute-done((bf16[80,1280]{1,0:T(8,128)(2,1)S(1)}, bf16[80,1280]{1,0:T(8,128)(2,1)S(1)}, u32[]{:S(2)}, u32[]{:S(2)}) %collective-permute-start.12) | collective-permute-done | bytes 204832 | tf_op jit(solution)/shard_map/ppermute | solution.py:207
  67.2 0.3 collective-permute-done.13.refs_7_
  67.5 0.2 shard_map.50
  67.7 3.5 %collective-permute-start.16 = (bf16[80,1280]{1,0:T(8,128)(2,1)S(1)}, bf16[80,1280]{1,0:T(8,128)(2,1)S(1)}, u32[]{:S(2)}, u32[]{:S(2)}) collective-permute-start(bf16[80,1280]{1,0:T(8,128)(2,1)S(1)} %get-tuple-element.51.refs_0_), channel_id=1, source_target_pairs={{0,6},{2,0},{4,2},{6,4},{1,7},{3,1},{5,3},{7,5},{8,14},{10,8},{12,... | collective-permute-start | bytes 614408 | tf_op jit(solution)/shard_map/ppermute | solution.py:207
  71.2 0.0 collective-permute-start.15
  71.2 1.5 %collective-permute-start.14 = (bf16[80,1280]{1,0:T(8,128)(2,1)S(1)}, bf16[80,1280]{1,0:T(8,128)(2,1)S(1)}, u32[]{:S(2)}, u32[]{:S(2)}) collective-permute-start(bf16[80,1280]{1,0:T(8,128)(2,1)S(1)} %get-tuple-element.51.refs_0_), channel_id=1, source_target_pairs={{0,4},{2,6},{4,0},{6,2},{1,5},{3,7},{5,1},{7,3},{8,12},{10,14},{12... | collective-permute-start | bytes 614408 | tf_op jit(solution)/shard_map/ppermute | solution.py:207
  72.8 0.5 collective-permute-start.19
  73.3 1.2 collective-permute-done.16.refs_3_
  74.5 2.6 %collective-permute-start.18 = (bf16[80,1280]{1,0:T(8,128)(2,1)S(1)}, bf16[80,1280]{1,0:T(8,128)(2,1)S(1)}, u32[]{:S(2)}, u32[]{:S(2)}) collective-permute-start(bf16[80,1280]{1,0:T(8,128)(2,1)S(1)} %get-tuple-element.52.refs_4_), channel_id=1, source_target_pairs={{0,8},{8,16},{16,24},{24,0},{1,9},{9,17},{17,25},{25,1},{2,10},{10... | collective-permute-start | bytes 614408 | tf_op jit(solution)/shard_map/ppermute | solution.py:207
  77.1 5.4 %collective-permute-done.15.refs_2_ = bf16[80,1280]{1,0:T(8,128)(2,1)S(1)} collective-permute-done((bf16[80,1280]{1,0:T(8,128)(2,1)S(1)}, bf16[80,1280]{1,0:T(8,128)(2,1)S(1)}, u32[]{:S(2)}, u32[]{:S(2)}) %collective-permute-start.15) | collective-permute-done | bytes 204832 | tf_op jit(solution)/shard_map/ppermute | solution.py:207
  82.5 1.8 %collective-permute-start.17 = (bf16[80,1280]{1,0:T(8,128)(2,1)S(1)}, bf16[80,1280]{1,0:T(8,128)(2,1)S(1)}, u32[]{:S(2)}, u32[]{:S(2)}) collective-permute-start(bf16[80,1280]{1,0:T(8,128)(2,1)S(1)} %get-tuple-element.52.refs_4_), channel_id=1, source_target_pairs={{0,16},{8,24},{16,0},{24,8},{1,17},{9,25},{17,1},{25,9},{2,18},{10... | collective-permute-start | bytes 614408 | tf_op jit(solution)/shard_map/ppermute | solution.py:207
  84.4 0.0 collective-permute-done.14.refs_1_
  84.4 7.7 %collective-permute-done.17.refs_5_ = bf16[80,1280]{1,0:T(8,128)(2,1)S(1)} collective-permute-done((bf16[80,1280]{1,0:T(8,128)(2,1)S(1)}, bf16[80,1280]{1,0:T(8,128)(2,1)S(1)}, u32[]{:S(2)}, u32[]{:S(2)}) %collective-permute-start.17) | collective-permute-done | bytes 204832 | tf_op jit(solution)/shard_map/ppermute | solution.py:207
  92.1 0.4 shard_map.51
  92.5 0.1 collective-permute-start.22
  92.6 3.2 %collective-permute-start.21 = (bf16[80,1280]{1,0:T(8,128)(2,1)S(1)}, bf16[80,1280]{1,0:T(8,128)(2,1)S(1)}, u32[]{:S(2)}, u32[]{:S(2)}) collective-permute-start(bf16[80,1280]{1,0:T(8,128)(2,1)S(1)} %get-tuple-element.53.refs_0_), channel_id=1, source_target_pairs={{0,8},{8,16},{16,24},{24,0},{1,9},{9,17},{17,25},{25,1},{2,10},{10... | collective-permute-start | bytes 614408 | tf_op jit(solution)/shard_map/ppermute | solution.py:207
  95.8 0.5 collective-permute-start.20
  96.3 3.2 %collective-permute-done.22.refs_3_ = bf16[80,1280]{1,0:T(8,128)(2,1)S(1)} collective-permute-done((bf16[80,1280]{1,0:T(8,128)(2,1)S(1)}, bf16[80,1280]{1,0:T(8,128)(2,1)S(1)}, u32[]{:S(2)}, u32[]{:S(2)}) %collective-permute-start.22) | collective-permute-done | bytes 204832 | tf_op jit(solution)/shard_map/ppermute | solution.py:207
  99.5 1.8 %collective-permute-done.21.refs_2_ = bf16[80,1280]{1,0:T(8,128)(2,1)S(1)} collective-permute-done((bf16[80,1280]{1,0:T(8,128)(2,1)S(1)}, bf16[80,1280]{1,0:T(8,128)(2,1)S(1)}, u32[]{:S(2)}, u32[]{:S(2)}) %collective-permute-start.21) | collective-permute-done | bytes 204832 | tf_op jit(solution)/shard_map/ppermute | solution.py:207
  101.3 1.8 %collective-permute-done.20.refs_1_ = bf16[80,1280]{1,0:T(8,128)(2,1)S(1)} collective-permute-done((bf16[80,1280]{1,0:T(8,128)(2,1)S(1)}, bf16[80,1280]{1,0:T(8,128)(2,1)S(1)}, u32[]{:S(2)}, u32[]{:S(2)}) %collective-permute-start.20) | collective-permute-done | bytes 204832 | tf_op jit(solution)/shard_map/ppermute | solution.py:207
  103.1 5.6 %collective-permute-done.24.refs_6_ = bf16[80,1280]{1,0:T(8,128)(2,1)S(1)} collective-permute-done((bf16[80,1280]{1,0:T(8,128)(2,1)S(1)}, bf16[80,1280]{1,0:T(8,128)(2,1)S(1)}, u32[]{:S(2)}, u32[]{:S(2)}) %collective-permute-start.24) | collective-permute-done | bytes 204832 | tf_op jit(solution)/shard_map/ppermute | solution.py:207
  108.7 1.8 %shard_map.52 = (bf16[160,256]{1,0:T(8,128)(2,1)S(1)}, bf16[160,256]{1,0:T(8,128)(2,1)S(1)}, bf16[160,256]{1,0:T(8,128)(2,1)S(1)}, bf16[160,256]{1,0:T(8,128)(2,...) custom-call(s32[3]{0:T(128)S(1)} %pad_add_fusion.pos_ref, ...), custom_call_target="tpu_custom_call" | custom-call | flops 838860800 | bytes 5898264 | tf_op jit(solution)/shard_map/pallas_call | solution.py:185
  110.5 5.5 %collective-permute-start.27 = (bf16[160,256]{1,0:T(8,128)(2,1)S(1)}, bf16[160,256]{1,0:T(8,128)(2,1)S(1)}, u32[]{:S(2)}, u32[]{:S(2)}) collective-permute-start(bf16[160,256]{1,0:T(8,128)(2,1)S(1)} %get-tuple-element.56), channel_id=1, source_target_pairs={{0,1},{1,0},{64,65},{65,64},{128,129},{129,128},{192,193},{193,192... | collective-permute-start | bytes 245768 | tf_op jit(solution)/shard_map/ppermute | solution.py:201
  116.1 0.6 collective-permute-start.28
  116.6 4.5 %collective-permute-start.29 = (bf16[160,256]{1,0:T(8,128)(2,1)S(1)}, bf16[160,256]{1,0:T(8,128)(2,1)S(1)}, u32[]{:S(2)}, u32[]{:S(2)}) collective-permute-start(bf16[160,256]{1,0:T(8,128)(2,1)S(1)} %get-tuple-element.58), channel_id=1, source_target_pairs={{0,65},{1,64},{64,129},{65,128},{128,193},{129,192},{192,0},{193,1... | collective-permute-start | bytes 245768 | tf_op jit(solution)/shard_map/ppermute | solution.py:201
  121.1 0.5 collective-permute-start.30
  121.6 3.6 %collective-permute-start.31 = (bf16[160,256]{1,0:T(8,128)(2,1)S(1)}, bf16[160,256]{1,0:T(8,128)(2,1)S(1)}, u32[]{:S(2)}, u32[]{:S(2)}) collective-permute-start(bf16[160,256]{1,0:T(8,128)(2,1)S(1)} %get-tuple-element.60), channel_id=1, source_target_pairs={{0,129},{1,128},{64,193},{65,192},{128,0},{129,1},{192,64},{193,65... | collective-permute-start | bytes 245768 | tf_op jit(solution)/shard_map/ppermute | solution.py:201
  125.2 0.6 collective-permute-start.32
  125.8 2.7 %collective-permute-start.33 = (bf16[160,256]{1,0:T(8,128)(2,1)S(1)}, bf16[160,256]{1,0:T(8,128)(2,1)S(1)}, u32[]{:S(2)}, u32[]{:S(2)}) collective-permute-start(bf16[160,256]{1,0:T(8,128)(2,1)S(1)} %get-tuple-element.62), channel_id=1, source_target_pairs={{0,193},{1,192},{64,0},{65,1},{128,64},{129,65},{192,128},{193,129... | collective-permute-start | bytes 245768 | tf_op jit(solution)/shard_map/ppermute | solution.py:201
  128.5 2.4 %collective-permute-done.32.refs_6_ = bf16[160,256]{1,0:T(8,128)(2,1)S(1)} collective-permute-done((bf16[160,256]{1,0:T(8,128)(2,1)S(1)}, bf16[160,256]{1,0:T(8,128)(2,1)S(1)}, u32[]{:S(2)}, u32[]{:S(2)}) %collective-permute-start.32) | collective-permute-done | bytes 81952 | tf_op jit(solution)/shard_map/ppermute | solution.py:201
  130.9 2.3 %shard_map.53 = f32[4,160,768]{2,1,0:T(8,128)} custom-call(s32[3]{0:T(128)S(1)} %pad_add_fusion.pos_ref, bf16[512,768]{1,0:T(8,128)(2,1)S(1)} %copy-done.1, bf16[160,256]{1,0:T(8,128)(2,1)S(1)} %get-tuple-element.55.refs_0_, bf16[160,256]{1,0:T(8,128)(2,1)S(1)} %collective-permute-done.27.refs_1_, bf16[160,256]{1,0:T(8,128)(2,1)S(1)} %collective-permute-done.28.refs_2_, ...), custom_call_target="tpu_custom_call" | custom-call | flops 503316480 | bytes 2883608 | tf_op jit(solution)/shard_map/pallas_call | solution.py:185
  (25 shorter events, 0.1 us)
Async XLA Ops:
  0.0 33.9 %copy-start = (bf16[768,3,512]{2,0,1:T(8,128)(2,1)S(1)}, bf16[768,3,512]{2,0,1:T(8,128)(2,1)}, u32[]{:S(2)}) copy-start(bf16[768,3,512]{2,0,1:T(8,128)(2,1)} %param.6) | copy-start | bytes 7077892
  0.1 0.8 copy-start.4
  5.4 19.3 %collective-permute-start = (bf16[320,256]{1,0:T(8,128)(2,1)S(1)}, bf16[320,256]{1,0:T(8,128)(2,1)S(1)}, u32[]{:S(2)}, u32[]{:S(2)}) collective-permute-start(bf16[320,256]{1,0:T(8,128)(2,1)S(1)} %get-tuple-element.35), channel_id=1, source_target_pairs={{0,1},{1,0},{64,65},{65,64},{128,129},{129,128},{192,193},{193,192... | collective-permute-start | bytes 491528 | tf_op jit(solution)/shard_map/ppermute | solution.py:201
  12.7 21.2 %collective-permute-start.1 = (bf16[320,256]{1,0:T(8,128)(2,1)S(1)}, bf16[320,256]{1,0:T(8,128)(2,1)S(1)}, u32[]{:S(2)}, u32[]{:S(2)}) collective-permute-start(bf16[320,256]{1,0:T(8,128)(2,1)S(1)} %get-tuple-element.36), channel_id=1, source_target_pairs={{0,192},{1,193},{64,1},{65,0},{128,65},{129,64},{192,129},{193,128... | collective-permute-start | bytes 491528 | tf_op jit(solution)/shard_map/ppermute | solution.py:201
  14.6 20.9 %collective-permute-start.2 = (bf16[320,256]{1,0:T(8,128)(2,1)S(1)}, bf16[320,256]{1,0:T(8,128)(2,1)S(1)}, u32[]{:S(2)}, u32[]{:S(2)}) collective-permute-start(bf16[320,256]{1,0:T(8,128)(2,1)S(1)} %get-tuple-element.37), channel_id=1, source_target_pairs={{0,65},{1,64},{64,129},{65,128},{128,193},{129,192},{192,0},{193,1... | collective-permute-start | bytes 491528 | tf_op jit(solution)/shard_map/ppermute | solution.py:201
  17.7 20.4 %collective-permute-start.3 = (bf16[320,256]{1,0:T(8,128)(2,1)S(1)}, bf16[320,256]{1,0:T(8,128)(2,1)S(1)}, u32[]{:S(2)}, u32[]{:S(2)}) collective-permute-start(bf16[320,256]{1,0:T(8,128)(2,1)S(1)} %get-tuple-element.38), channel_id=1, source_target_pairs={{0,128},{1,129},{64,192},{65,193},{128,1},{129,0},{192,65},{193,64... | collective-permute-start | bytes 491528 | tf_op jit(solution)/shard_map/ppermute | solution.py:201
  19.2 19.8 %collective-permute-start.4 = (bf16[320,256]{1,0:T(8,128)(2,1)S(1)}, bf16[320,256]{1,0:T(8,128)(2,1)S(1)}, u32[]{:S(2)}, u32[]{:S(2)}) collective-permute-start(bf16[320,256]{1,0:T(8,128)(2,1)S(1)} %get-tuple-element.39), channel_id=1, source_target_pairs={{0,129},{1,128},{64,193},{65,192},{128,0},{129,1},{192,64},{193,65... | collective-permute-start | bytes 491528 | tf_op jit(solution)/shard_map/ppermute | solution.py:201
  24.7 16.4 %collective-permute-start.5 = (bf16[320,256]{1,0:T(8,128)(2,1)S(1)}, bf16[320,256]{1,0:T(8,128)(2,1)S(1)}, u32[]{:S(2)}, u32[]{:S(2)}) collective-permute-start(bf16[320,256]{1,0:T(8,128)(2,1)S(1)} %get-tuple-element.40), channel_id=1, source_target_pairs={{0,64},{1,65},{64,128},{65,129},{128,192},{129,193},{192,1},{193,0... | collective-permute-start | bytes 491528 | tf_op jit(solution)/shard_map/ppermute | solution.py:201
  33.9 8.4 %collective-permute-start.6 = (bf16[320,256]{1,0:T(8,128)(2,1)S(1)}, bf16[320,256]{1,0:T(8,128)(2,1)S(1)}, u32[]{:S(2)}, u32[]{:S(2)}) collective-permute-start(bf16[320,256]{1,0:T(8,128)(2,1)S(1)} %get-tuple-element.41), channel_id=1, source_target_pairs={{0,193},{1,192},{64,0},{65,1},{128,64},{129,65},{192,128},{193,129... | collective-permute-start | bytes 491528 | tf_op jit(solution)/shard_map/ppermute | solution.py:201
  42.9 0.7 copy-start.2
  43.5 4.8 %collective-permute-start.7 = (bf16[2,4,160,256]{3,2,1,0:T(8,128)(2,1)S(1)}, bf16[2,4,160,256]{3,2,1,0:T(8,128)(2,1)S(1)}, u32[]{:S(2)}, u32[]{:S(2)}) collective-permute-start(bf16[2,4,160,256]{3,2,1,0:T(8,128)(2,1)S(1)} %shard_map.48.refs_8_), channel_id=1, source_target_pairs={{0,32},{32,0},{1,33},{33,1},{2,34},{34,2},{3,35},{35,3},{4,36},{36... | collective-permute-start | bytes 1966088 | tf_op jit(solution)/shard_map/ppermute | solution.py:213
  43.5 27.7 %all-to-all-start = ((bf16[8,160,256]{2,1,0:T(8,128)(2,1)}), bf16[8,160,256]{2,1,0:T(8,128)(2,1)S(1)}, u32[]{:S(2)}, u32[]{:S(2)}) async-start(bf16[8,160,256]{2,1,0:T(8,128)(2,1)} %shard_map.47.refs_8_), calls=%async_computation | async-start | bytes 1310720 | tf_op jit(solution)/shard_map/all_to_all | solution.py:259
  48.4 0.9 copy-start.3
  51.0 9.5 %collective-permute-start.8 = (bf16[80,1280]{1,0:T(8,128)(2,1)S(1)}, bf16[80,1280]{1,0:T(8,128)(2,1)S(1)}, u32[]{:S(2)}, u32[]{:S(2)}) collective-permute-start(bf16[80,1280]{1,0:T(8,128)(2,1)S(1)} %get-tuple-element.44), channel_id=1, source_target_pairs={{0,16},{8,24},{16,0},{24,8},{1,17},{9,25},{17,1},{25,9},{2,18},{10... | collective-permute-start | bytes 614408 | tf_op jit(solution)/shard_map/ppermute | solution.py:207
  52.5 11.0 %collective-permute-start.9 = (bf16[80,1280]{1,0:T(8,128)(2,1)S(1)}, bf16[80,1280]{1,0:T(8,128)(2,1)S(1)}, u32[]{:S(2)}, u32[]{:S(2)}) collective-permute-start(bf16[80,1280]{1,0:T(8,128)(2,1)S(1)} %get-tuple-element.45), channel_id=1, source_target_pairs={{0,8},{8,16},{16,24},{24,0},{1,9},{9,17},{17,25},{25,1},{2,10},{10... | collective-permute-start | bytes 614408 | tf_op jit(solution)/shard_map/ppermute | solution.py:207
  54.6 9.6 %collective-permute-start.10 = (bf16[80,1280]{1,0:T(8,128)(2,1)S(1)}, bf16[80,1280]{1,0:T(8,128)(2,1)S(1)}, u32[]{:S(2)}, u32[]{:S(2)}) collective-permute-start(bf16[80,1280]{1,0:T(8,128)(2,1)S(1)} %get-tuple-element.46), channel_id=1, source_target_pairs={{0,24},{8,0},{16,8},{24,16},{1,25},{9,1},{17,9},{25,17},{2,26},{10... | collective-permute-start | bytes 614408 | tf_op jit(solution)/shard_map/ppermute | solution.py:207
  54.6 9.6 %collective-permute-start.11 = (bf16[80,1280]{1,0:T(8,128)(2,1)S(1)}, bf16[80,1280]{1,0:T(8,128)(2,1)S(1)}, u32[]{:S(2)}, u32[]{:S(2)}) collective-permute-start(bf16[80,1280]{1,0:T(8,128)(2,1)S(1)} %get-tuple-element.48), channel_id=1, source_target_pairs={{0,4},{2,6},{4,0},{6,2},{1,5},{3,7},{5,1},{7,3},{8,12},{10,14},{12... | collective-permute-start | bytes 614408 | tf_op jit(solution)/shard_map/ppermute | solution.py:207
  57.8 9.3 %collective-permute-start.12 = (bf16[80,1280]{1,0:T(8,128)(2,1)S(1)}, bf16[80,1280]{1,0:T(8,128)(2,1)S(1)}, u32[]{:S(2)}, u32[]{:S(2)}) collective-permute-start(bf16[80,1280]{1,0:T(8,128)(2,1)S(1)} %get-tuple-element.49), channel_id=1, source_target_pairs={{0,2},{2,4},{4,6},{6,0},{1,3},{3,5},{5,7},{7,1},{8,10},{10,12},{12... | collective-permute-start | bytes 614408 | tf_op jit(solution)/shard_map/ppermute | solution.py:207
  60.5 7.0 %collective-permute-start.13 = (bf16[80,1280]{1,0:T(8,128)(2,1)S(1)}, bf16[80,1280]{1,0:T(8,128)(2,1)S(1)}, u32[]{:S(2)}, u32[]{:S(2)}) collective-permute-start(bf16[80,1280]{1,0:T(8,128)(2,1)S(1)} %get-tuple-element.50), channel_id=1, source_target_pairs={{0,6},{2,0},{4,2},{6,4},{1,7},{3,1},{5,3},{7,5},{8,14},{10,8},{12,... | collective-permute-start | bytes 614408 | tf_op jit(solution)/shard_map/ppermute | solution.py:207
  67.7 6.8 %collective-permute-start.16 = (bf16[80,1280]{1,0:T(8,128)(2,1)S(1)}, bf16[80,1280]{1,0:T(8,128)(2,1)S(1)}, u32[]{:S(2)}, u32[]{:S(2)}) collective-permute-start(bf16[80,1280]{1,0:T(8,128)(2,1)S(1)} %get-tuple-element.51.refs_0_), channel_id=1, source_target_pairs={{0,6},{2,0},{4,2},{6,4},{1,7},{3,1},{5,3},{7,5},{8,14},{10,8},{12,... | collective-permute-start | bytes 614408 | tf_op jit(solution)/shard_map/ppermute | solution.py:207
  71.2 11.3 %collective-permute-start.15 = (bf16[80,1280]{1,0:T(8,128)(2,1)S(1)}, bf16[80,1280]{1,0:T(8,128)(2,1)S(1)}, u32[]{:S(2)}, u32[]{:S(2)}) collective-permute-start(bf16[80,1280]{1,0:T(8,128)(2,1)S(1)} %get-tuple-element.51.refs_0_), channel_id=1, source_target_pairs={{0,2},{2,4},{4,6},{6,0},{1,3},{3,5},{5,7},{7,1},{8,10},{10,12},{12... | collective-permute-start | bytes 614408 | tf_op jit(solution)/shard_map/ppermute | solution.py:207
  71.2 37.5 %collective-permute-start.26 = (bf16[8,160,256]{2,1,0:T(8,128)(2,1)S(1)}, bf16[8,160,256]{2,1,0:T(8,128)(2,1)S(1)}, u32[]{:S(2)}, u32[]{:S(2)}) collective-permute-start(bf16[8,160,256]{2,1,0:T(8,128)(2,1)S(1)} %all-to-all-done.refs_8_), channel_id=1, source_target_pairs={{0,32},{32,0},{1,33},{33,1},{2,34},{34,2},{3,35},{35,3},{4,36},{36... | collective-permute-start | bytes 1966088 | tf_op jit(solution)/shard_map/ppermute | solution.py:213
  71.2 13.1 %collective-permute-start.14 = (bf16[80,1280]{1,0:T(8,128)(2,1)S(1)}, bf16[80,1280]{1,0:T(8,128)(2,1)S(1)}, u32[]{:S(2)}, u32[]{:S(2)}) collective-permute-start(bf16[80,1280]{1,0:T(8,128)(2,1)S(1)} %get-tuple-element.51.refs_0_), channel_id=1, source_target_pairs={{0,4},{2,6},{4,0},{6,2},{1,5},{3,7},{5,1},{7,3},{8,12},{10,14},{12... | collective-permute-start | bytes 614408 | tf_op jit(solution)/shard_map/ppermute | solution.py:207
  72.8 58.1 %copy-start.1 = (bf16[512,768]{1,0:T(8,128)(2,1)S(1)}, bf16[512,768]{1,0:T(8,128)(2,1)}, u32[]{:S(2)}) copy-start(bf16[512,768]{1,0:T(8,128)(2,1)} %w_ref.1) | copy-start | bytes 2359300
  72.8 11.6 %collective-permute-start.19 = (bf16[80,1280]{1,0:T(8,128)(2,1)S(1)}, bf16[80,1280]{1,0:T(8,128)(2,1)S(1)}, u32[]{:S(2)}, u32[]{:S(2)}) collective-permute-start(bf16[80,1280]{1,0:T(8,128)(2,1)S(1)} %get-tuple-element.52.refs_4_), channel_id=1, source_target_pairs={{0,24},{8,0},{16,8},{24,16},{1,25},{9,1},{17,9},{25,17},{2,26},{10... | collective-permute-start | bytes 614408 | tf_op jit(solution)/shard_map/ppermute | solution.py:207
  74.5 9.9 %collective-permute-start.18 = (bf16[80,1280]{1,0:T(8,128)(2,1)S(1)}, bf16[80,1280]{1,0:T(8,128)(2,1)S(1)}, u32[]{:S(2)}, u32[]{:S(2)}) collective-permute-start(bf16[80,1280]{1,0:T(8,128)(2,1)S(1)} %get-tuple-element.52.refs_4_), channel_id=1, source_target_pairs={{0,8},{8,16},{16,24},{24,0},{1,9},{9,17},{17,25},{25,1},{2,10},{10... | collective-permute-start | bytes 614408 | tf_op jit(solution)/shard_map/ppermute | solution.py:207
  82.5 9.6 %collective-permute-start.17 = (bf16[80,1280]{1,0:T(8,128)(2,1)S(1)}, bf16[80,1280]{1,0:T(8,128)(2,1)S(1)}, u32[]{:S(2)}, u32[]{:S(2)}) collective-permute-start(bf16[80,1280]{1,0:T(8,128)(2,1)S(1)} %get-tuple-element.52.refs_4_), channel_id=1, source_target_pairs={{0,16},{8,24},{16,0},{24,8},{1,17},{9,25},{17,1},{25,9},{2,18},{10... | collective-permute-start | bytes 614408 | tf_op jit(solution)/shard_map/ppermute | solution.py:207
  92.5 7.0 %collective-permute-start.22 = (bf16[80,1280]{1,0:T(8,128)(2,1)S(1)}, bf16[80,1280]{1,0:T(8,128)(2,1)S(1)}, u32[]{:S(2)}, u32[]{:S(2)}) collective-permute-start(bf16[80,1280]{1,0:T(8,128)(2,1)S(1)} %get-tuple-element.53.refs_0_), channel_id=1, source_target_pairs={{0,24},{8,0},{16,8},{24,16},{1,25},{9,1},{17,9},{25,17},{2,26},{10... | collective-permute-start | bytes 614408 | tf_op jit(solution)/shard_map/ppermute | solution.py:207
  92.6 8.7 %collective-permute-start.21 = (bf16[80,1280]{1,0:T(8,128)(2,1)S(1)}, bf16[80,1280]{1,0:T(8,128)(2,1)S(1)}, u32[]{:S(2)}, u32[]{:S(2)}) collective-permute-start(bf16[80,1280]{1,0:T(8,128)(2,1)S(1)} %get-tuple-element.53.refs_0_), channel_id=1, source_target_pairs={{0,8},{8,16},{16,24},{24,0},{1,9},{9,17},{17,25},{25,1},{2,10},{10... | collective-permute-start | bytes 614408 | tf_op jit(solution)/shard_map/ppermute | solution.py:207
  95.8 7.3 %collective-permute-start.20 = (bf16[80,1280]{1,0:T(8,128)(2,1)S(1)}, bf16[80,1280]{1,0:T(8,128)(2,1)S(1)}, u32[]{:S(2)}, u32[]{:S(2)}) collective-permute-start(bf16[80,1280]{1,0:T(8,128)(2,1)S(1)} %get-tuple-element.53.refs_0_), channel_id=1, source_target_pairs={{0,16},{8,24},{16,0},{24,8},{1,17},{9,25},{17,1},{25,9},{2,18},{10... | collective-permute-start | bytes 614408 | tf_op jit(solution)/shard_map/ppermute | solution.py:207
  96.3 6.8 %collective-permute-start.25 = (bf16[80,1280]{1,0:T(8,128)(2,1)S(1)}, bf16[80,1280]{1,0:T(8,128)(2,1)S(1)}, u32[]{:S(2)}, u32[]{:S(2)}) collective-permute-start(bf16[80,1280]{1,0:T(8,128)(2,1)S(1)} %get-tuple-element.54.refs_4_), channel_id=1, source_target_pairs={{0,6},{2,0},{4,2},{6,4},{1,7},{3,1},{5,3},{7,5},{8,14},{10,8},{12,... | collective-permute-start | bytes 614408 | tf_op jit(solution)/shard_map/ppermute | solution.py:207
  99.5 9.2 %collective-permute-start.24 = (bf16[80,1280]{1,0:T(8,128)(2,1)S(1)}, bf16[80,1280]{1,0:T(8,128)(2,1)S(1)}, u32[]{:S(2)}, u32[]{:S(2)}) collective-permute-start(bf16[80,1280]{1,0:T(8,128)(2,1)S(1)} %get-tuple-element.54.refs_4_), channel_id=1, source_target_pairs={{0,2},{2,4},{4,6},{6,0},{1,3},{3,5},{5,7},{7,1},{8,10},{10,12},{12... | collective-permute-start | bytes 614408 | tf_op jit(solution)/shard_map/ppermute | solution.py:207
  101.3 7.4 %collective-permute-start.23 = (bf16[80,1280]{1,0:T(8,128)(2,1)S(1)}, bf16[80,1280]{1,0:T(8,128)(2,1)S(1)}, u32[]{:S(2)}, u32[]{:S(2)}) collective-permute-start(bf16[80,1280]{1,0:T(8,128)(2,1)S(1)} %get-tuple-element.54.refs_4_), channel_id=1, source_target_pairs={{0,4},{2,6},{4,0},{6,2},{1,5},{3,7},{5,1},{7,3},{8,12},{10,14},{12... | collective-permute-start | bytes 614408 | tf_op jit(solution)/shard_map/ppermute | solution.py:207
  110.5 14.7 %collective-permute-start.27 = (bf16[160,256]{1,0:T(8,128)(2,1)S(1)}, bf16[160,256]{1,0:T(8,128)(2,1)S(1)}, u32[]{:S(2)}, u32[]{:S(2)}) collective-permute-start(bf16[160,256]{1,0:T(8,128)(2,1)S(1)} %get-tuple-element.56), channel_id=1, source_target_pairs={{0,1},{1,0},{64,65},{65,64},{128,129},{129,128},{192,193},{193,192... | collective-permute-start | bytes 245768 | tf_op jit(solution)/shard_map/ppermute | solution.py:201
  116.1 9.8 %collective-permute-start.28 = (bf16[160,256]{1,0:T(8,128)(2,1)S(1)}, bf16[160,256]{1,0:T(8,128)(2,1)S(1)}, u32[]{:S(2)}, u32[]{:S(2)}) collective-permute-start(bf16[160,256]{1,0:T(8,128)(2,1)S(1)} %get-tuple-element.57), channel_id=1, source_target_pairs={{0,192},{1,193},{64,1},{65,0},{128,65},{129,64},{192,129},{193,128... | collective-permute-start | bytes 245768 | tf_op jit(solution)/shard_map/ppermute | solution.py:201
  116.6 11.8 %collective-permute-start.29 = (bf16[160,256]{1,0:T(8,128)(2,1)S(1)}, bf16[160,256]{1,0:T(8,128)(2,1)S(1)}, u32[]{:S(2)}, u32[]{:S(2)}) collective-permute-start(bf16[160,256]{1,0:T(8,128)(2,1)S(1)} %get-tuple-element.58), channel_id=1, source_target_pairs={{0,65},{1,64},{64,129},{65,128},{128,193},{129,192},{192,0},{193,1... | collective-permute-start | bytes 245768 | tf_op jit(solution)/shard_map/ppermute | solution.py:201
  121.1 7.4 %collective-permute-start.30 = (bf16[160,256]{1,0:T(8,128)(2,1)S(1)}, bf16[160,256]{1,0:T(8,128)(2,1)S(1)}, u32[]{:S(2)}, u32[]{:S(2)}) collective-permute-start(bf16[160,256]{1,0:T(8,128)(2,1)S(1)} %get-tuple-element.59), channel_id=1, source_target_pairs={{0,128},{1,129},{64,192},{65,193},{128,1},{129,0},{192,65},{193,64... | collective-permute-start | bytes 245768 | tf_op jit(solution)/shard_map/ppermute | solution.py:201
  121.6 6.8 %collective-permute-start.31 = (bf16[160,256]{1,0:T(8,128)(2,1)S(1)}, bf16[160,256]{1,0:T(8,128)(2,1)S(1)}, u32[]{:S(2)}, u32[]{:S(2)}) collective-permute-start(bf16[160,256]{1,0:T(8,128)(2,1)S(1)} %get-tuple-element.60), channel_id=1, source_target_pairs={{0,129},{1,128},{64,193},{65,192},{128,0},{129,1},{192,64},{193,65... | collective-permute-start | bytes 245768 | tf_op jit(solution)/shard_map/ppermute | solution.py:201
  125.2 5.7 %collective-permute-start.32 = (bf16[160,256]{1,0:T(8,128)(2,1)S(1)}, bf16[160,256]{1,0:T(8,128)(2,1)S(1)}, u32[]{:S(2)}, u32[]{:S(2)}) collective-permute-start(bf16[160,256]{1,0:T(8,128)(2,1)S(1)} %get-tuple-element.61), channel_id=1, source_target_pairs={{0,64},{1,65},{64,128},{65,129},{128,192},{129,193},{192,1},{193,0... | collective-permute-start | bytes 245768 | tf_op jit(solution)/shard_map/ppermute | solution.py:201
  125.8 5.1 %collective-permute-start.33 = (bf16[160,256]{1,0:T(8,128)(2,1)S(1)}, bf16[160,256]{1,0:T(8,128)(2,1)S(1)}, u32[]{:S(2)}, u32[]{:S(2)}) collective-permute-start(bf16[160,256]{1,0:T(8,128)(2,1)S(1)} %get-tuple-element.62), channel_id=1, source_target_pairs={{0,193},{1,192},{64,0},{65,1},{128,64},{129,65},{192,128},{193,129... | collective-permute-start | bytes 245768 | tf_op jit(solution)/shard_map/ppermute | solution.py:201

commit v8 on v6

--- a/solution.py
+++ b/solution.py
@@ -20,7 +20,7 @@
 HBM = pl.BlockSpec(memory_space=pltpu.HBM)
 ANY = pl.BlockSpec(memory_space=pl.ANY)
 SMEM = pl.BlockSpec(memory_space=pltpu.SMEM)
-CUTS = 4
+CONTEXT_STEPS = (0, 4, 3, 7, 5, 2, 6, 1)
 MIB = 1024 * 1024
 
 
@@ -49,12 +49,9 @@
     both, (normed, mine, gain_ref, x_ref, w_ref, gain_sem, x_sem, w_sem) = refs[:RING], refs[RING:]
     seqs, length, width = x_hbm.shape
     x_copies = [pltpu.make_async_copy(x_hbm.at[r], x_ref.at[r], x_sem.at[r]) for r in range(seqs)]
-    w_copies = [
-        [pltpu.make_async_copy(w_hbm.at[c, part], w_ref.at[c, part], w_sem.at[c, i]) for i, part in enumerate(cuts(width, CUTS))]
-        for c in range(2)
-    ]
+    w_copies = [pltpu.make_async_copy(w_hbm.at[c], w_ref.at[c], w_sem.at[c]) for c in range(2)]
     gain_copy = pltpu.make_async_copy(gain_hbm, gain_ref, gain_sem)
-    for copy in (x_copies[0], gain_copy, *x_copies[1:], *w_copies[1], *w_copies[0]):
+    for copy in (x_copies[0], gain_copy, *x_copies[1:], w_copies[1], w_copies[0]):
         copy.start()
     gain_copy.wait()
     gain = gain_ref[...].reshape(1, width)
@@ -67,8 +64,7 @@
         normed[r * length : (r + 1) * length] = (off / jnp.sqrt(var + 1e-05) * gain).astype(BF)
     pos = pos_ref[0]
     for c in (1, 0):
-        for copy in w_copies[c]:
-            copy.wait()
+        w_copies[c].wait()
         blocks_by_head(jnp.dot(normed[...], w_ref[c], preferred_element_type=F32), seqs, mine)
         for i, s in enumerate(STEPS):
             both[i][(1 - c) * length : (2 - c) * length] = mine[head_at(pos + s)]
@@ -93,7 +89,7 @@
     length = out.shape[2]
     for part, s in zip(parts, STEPS):
         src = lax.rem(pos + RING - s, RING)
-        out[lax.div(src, Z), lax.rem(src, Z)] = part[first : first + length]
+        out[lax.div(src, Z), -s % Z] = part[first : first + length]
 
 
 def place_kernel(count, pos_ref, *refs):
@@ -143,34 +139,35 @@
         copy.wait()
 
 
-def context_kernel(pos_ref, p_ref, v_ref, v_far, *refs):
-    outs, mine = refs[:RING], refs[RING]
+def seen_kernel(_, out_ref):
+    out_ref[...] = jnp.zeros_like(out_ref)
+
+
+def context_kernel(blocks, steps, pos_ref, p_ref, v_ref, v_far, _, *refs):
+    outs, mine = refs[: len(steps)], refs[-1]
     half = v_ref.shape[1] * v_ref.shape[2]
     length = v_ref.shape[2]
+    p = jnp.concatenate([p_ref[t * length : (t + 1) * length] for t in blocks], axis=0)
     for w in range(W):
-        a = jnp.dot(p_ref[:, :half], v_ref[w].reshape(half, -1), preferred_element_type=F32)
-        a = a + jnp.dot(p_ref[:, half:], v_far[w].reshape(half, -1), preferred_element_type=F32)
-        a = a.astype(BF)
-        for z in range(Z):
-            mine[w * Z + z] = a[z * length : (z + 1) * length]
-    pos = pos_ref[0]
-    for i, s in enumerate(STEPS):
-        outs[i][...] = mine[lax.rem(pos + s, RING)]
+        a = jnp.dot(p[:, :half], v_ref[w].reshape(half, -1), preferred_element_type=F32)
+        a = a + jnp.dot(p[:, half:], v_far[w].reshape(half, -1), preferred_element_type=F32)
+        mine[w] = a.astype(BF).reshape(mine.shape[1:])
+    for out, s in zip(outs, steps):
+        out[...] = mine[lax.div(lax.rem(pos_ref[0] + s, RING), Z), blocks.index(s % Z)]
 
 
 def mix_kernel(pos_ref, w_ref, *refs):
     parts, (out_hbm, rows, mixed, sem) = refs[:RING], refs[RING:]
     pos = pos_ref[0]
-    for i, s in enumerate(STEPS):
+    for i, s in enumerate(CONTEXT_STEPS):
         h = head_at(pos + RING - s)
         rows[i * HEAD_DIM : (i + 1) * HEAD_DIM] = w_ref[pl.ds(pl.multiple_of(h * HEAD_DIM, HEAD_DIM), HEAD_DIM)]
     copies = []
     for r in range(mixed.shape[0]):
         lhs = jnp.concatenate([part[:, r * HEAD_DIM : (r + 1) * HEAD_DIM] for part in parts], axis=1)
         mixed[r] = jnp.dot(lhs, rows[...], preferred_element_type=F32)
-        for i, part in enumerate(cuts(mixed.shape[1], CUTS)):
-            copies.append(pltpu.make_async_copy(mixed.at[r, part], out_hbm.at[r, part], sem.at[r, i]))
-            copies[-1].start()
+        copies.append(pltpu.make_async_copy(mixed.at[r], out_hbm.at[r], sem.at[r]))
+        copies[r].start()
     for copy in copies:
         copy.wait()
 
@@ -192,9 +189,9 @@
     )(*operands)
 
 
-def along_ring(parts):
+def along_ring(parts, steps=STEPS):
     got = []
-    for part, s in zip(parts, STEPS):
+    for part, s in zip(parts, steps):
         pairs = [(i, index_of((place(i) + s) % RING)) for i in range(RING)]
         got.append(lax.ppermute(part, ("z", "w"), pairs) if s else part)
     return got
@@ -229,7 +226,7 @@
             pltpu.VMEM((2, width, inner), BF),
             dma,
             dma((seqs,)),
-            dma((2, CUTS)),
+            dma((2,)),
         ],
         flops=2 * seqs * length * width * 2 * inner,
         hbm=(1, 2, 3),
@@ -280,19 +277,24 @@
     probs = lax.all_to_all(probs, ("x", "y"), 0, 0, tiled=True).reshape(half, full)
     values = call(functools.partial(place_kernel, RING), whole, [pos, *values])
     values_far = other_core(values)
-    context = call(
-        context_kernel,
-        [block] * RING,
-        [pos, probs, values, values_far],
-        [pltpu.VMEM((RING, length, lanes), BF)],
-        flops=2 * half * full * W * lanes,
-    )
-    context = along_ring(context)
+    seen = call(seen_kernel, jax.ShapeDtypeStruct((8, 128), F32), [values_far], unread=(0,))
+    context = []
+    for blocks in ((0, 3), (1, 2)):
+        steps = [s for s in CONTEXT_STEPS if s % Z in blocks]
+        parts = call(
+            functools.partial(context_kernel, blocks, steps),
+            [block] * len(steps),
+            [pos, probs, values, values_far, seen],
+            [pltpu.VMEM((W, len(blocks), length, lanes), BF)],
+            flops=half * full * W * lanes,
+            unread=(4,),
+        )
+        context += along_ring(parts, steps)
     return call(
         mix_kernel,
         jax.ShapeDtypeStruct((seqs, length, width), F32),
         [pos, w_out, *context],
-        [pltpu.VMEM(w_out.shape, BF), pltpu.VMEM((seqs, length, width), F32), dma((seqs, CUTS))],
+        [pltpu.VMEM(w_out.shape, BF), pltpu.VMEM((seqs, length, width), F32), dma((seqs,))],
         flops=2 * seqs * length * inner * width,
         out_specs=HBM,
     )

time: 128 us -> 127 us (level)
  local copies, waits for them, and re-layouts: 2.62 us -> 0.7 us
    unnamed x10 -> x6, local copies, waits for them, and re-layouts: 2.62 us -> 0.7 us
    pallas_call x9 -> x11, Pallas kernels: 12.7 us -> 12.5 us  [call(): pl.pallas_call(kernel, out_shape=out_shape, in_specs=specs, out_specs=out...]
where the time goes in v8:
time: 127 us
  starting transfers between devices  57.4 us (45%)
  waiting for transfers between devices  55.8 us (44%)
  Pallas kernels  12.5 us (10%)
    ppermute x21, starting transfers between devices, along_ring(): got.append(lax.ppermute(part, ('z', 'w'), pairs) if s else part)  43.5 us
    ppermute x21, waiting for transfers between devices, along_ring(): got.append(lax.ppermute(part, ('z', 'w'), pairs) if s else part)  37.8 us
    pallas_call x11, Pallas kernels, call(): pl.pallas_call(kernel, out_shape=out_shape, in_specs=specs, out_specs=out...  12.5 us
    all_to_all x1, waiting for transfers between devices, shards(): lax.all_to_all(probs, ('x', 'y'), 0, 0, tiled=True).reshape(half, full)  9.7 us
    all_to_all x1, starting transfers between devices, shards(): terms = lax.all_to_all(term.reshape(chunk), ('x', 'y'), 0, 0, tiled=True)  7.43 us
    all_to_all x1, starting transfers between devices, shards(): lax.all_to_all(probs, ('x', 'y'), 0, 0, tiled=True).reshape(half, full)  6.25 us
    all_to_all x1, waiting for transfers between devices, shards(): terms = lax.all_to_all(term.reshape(chunk), ('x', 'y'), 0, 0, tiled=True)  5.58 us
    ppermute x2, waiting for transfers between devices, other_core(): return lax.ppermute(a, 'c', [(0, 1), (1, 0)])  2.65 us
  transfers between devices with their start and end apart: 25, of which 19 were waited for; matrix products, arithmetic and copies ran while one was open for 0% of the time, Pallas kernels for 2%

profile of v8, /device:TPU:6, one launch (start us, length us, event | category | flops | bytes accessed | tf_op | source)
XLA Modules:
  0.0 126.6 jit_solution(11056279650241242733)
XLA Ops:
  0.0 0.7 copy-done.2
  0.7 3.8 %shard_map.46 = (bf16[320,256]{1,0:T(8,128)(2,1)S(1)}, bf16[320,256]{1,0:T(8,128)(2,1)S(1)}, bf16[320,256]{1,0:T(8,128)(2,1)S(1)}, bf16[320,256]{1,0:T(8,128)(2,...) custom-call(s32[1]{0:T(128)} %bitcast.pos_ref, ...), custom_call_target="tpu_custom_call" | custom-call | flops 1006632960 | bytes 6690824 | tf_op jit(solution)/shard_map/pallas_call | solution.py:180
  4.5 7.3 %collective-permute-start = (bf16[320,256]{1,0:T(8,128)(2,1)S(1)}, bf16[320,256]{1,0:T(8,128)(2,1)S(1)}, u32[]{:S(2)}, u32[]{:S(2)}) collective-permute-start(bf16[320,256]{1,0:T(8,128)(2,1)S(1)} %get-tuple-element.33), channel_id=1, source_target_pairs={{0,1},{1,0},{64,65},{65,64},{128,129},{129,128},{192,193},{193,192... | collective-permute-start | bytes 491528 | tf_op jit(solution)/shard_map/ppermute | solution.py:196
  11.8 1.9 %collective-permute-start.1 = (bf16[320,256]{1,0:T(8,128)(2,1)S(1)}, bf16[320,256]{1,0:T(8,128)(2,1)S(1)}, u32[]{:S(2)}, u32[]{:S(2)}) collective-permute-start(bf16[320,256]{1,0:T(8,128)(2,1)S(1)} %get-tuple-element.34), channel_id=1, source_target_pairs={{0,192},{1,193},{64,1},{65,0},{128,65},{129,64},{192,129},{193,128... | collective-permute-start | bytes 491528 | tf_op jit(solution)/shard_map/ppermute | solution.py:196
  13.7 3.1 %collective-permute-start.2 = (bf16[320,256]{1,0:T(8,128)(2,1)S(1)}, bf16[320,256]{1,0:T(8,128)(2,1)S(1)}, u32[]{:S(2)}, u32[]{:S(2)}) collective-permute-start(bf16[320,256]{1,0:T(8,128)(2,1)S(1)} %get-tuple-element.35), channel_id=1, source_target_pairs={{0,65},{1,64},{64,129},{65,128},{128,193},{129,192},{192,0},{193,1... | collective-permute-start | bytes 491528 | tf_op jit(solution)/shard_map/ppermute | solution.py:196
  16.8 1.5 %collective-permute-start.3 = (bf16[320,256]{1,0:T(8,128)(2,1)S(1)}, bf16[320,256]{1,0:T(8,128)(2,1)S(1)}, u32[]{:S(2)}, u32[]{:S(2)}) collective-permute-start(bf16[320,256]{1,0:T(8,128)(2,1)S(1)} %get-tuple-element.36), channel_id=1, source_target_pairs={{0,128},{1,129},{64,192},{65,193},{128,1},{129,0},{192,65},{193,64... | collective-permute-start | bytes 491528 | tf_op jit(solution)/shard_map/ppermute | solution.py:196
  18.3 2.7 %collective-permute-start.4 = (bf16[320,256]{1,0:T(8,128)(2,1)S(1)}, bf16[320,256]{1,0:T(8,128)(2,1)S(1)}, u32[]{:S(2)}, u32[]{:S(2)}) collective-permute-start(bf16[320,256]{1,0:T(8,128)(2,1)S(1)} %get-tuple-element.37), channel_id=1, source_target_pairs={{0,129},{1,128},{64,193},{65,192},{128,0},{129,1},{192,64},{193,65... | collective-permute-start | bytes 491528 | tf_op jit(solution)/shard_map/ppermute | solution.py:196
  20.9 2.8 %collective-permute-done.refs_1_ = bf16[320,256]{1,0:T(8,128)(2,1)S(1)} collective-permute-done((bf16[320,256]{1,0:T(8,128)(2,1)S(1)}, bf16[320,256]{1,0:T(8,128)(2,1)S(1)}, u32[]{:S(2)}, u32[]{:S(2)}) %collective-permute-start) | collective-permute-done | bytes 163872 | tf_op jit(solution)/shard_map/ppermute | solution.py:196
  23.8 0.3 collective-permute-start.5
  24.1 8.8 %collective-permute-done.1.refs_2_ = bf16[320,256]{1,0:T(8,128)(2,1)S(1)} collective-permute-done((bf16[320,256]{1,0:T(8,128)(2,1)S(1)}, bf16[320,256]{1,0:T(8,128)(2,1)S(1)}, u32[]{:S(2)}, u32[]{:S(2)}) %collective-permute-start.1) | collective-permute-done | bytes 163872 | tf_op jit(solution)/shard_map/ppermute | solution.py:196
  32.9 0.0 collective-permute-start.6
  32.9 0.0 copy-done
  32.9 0.9 shard_map.47
  33.8 0.0 collective-permute-done.2.refs_3_
  33.8 3.3 %collective-permute-done.3.refs_4_ = bf16[320,256]{1,0:T(8,128)(2,1)S(1)} collective-permute-done((bf16[320,256]{1,0:T(8,128)(2,1)S(1)}, bf16[320,256]{1,0:T(8,128)(2,1)S(1)}, u32[]{:S(2)}, u32[]{:S(2)}) %collective-permute-start.3) | collective-permute-done | bytes 163872 | tf_op jit(solution)/shard_map/ppermute | solution.py:196
  37.1 0.9 collective-permute-done.4.refs_5_
  38.0 2.2 %collective-permute-done.5.refs_6_ = bf16[320,256]{1,0:T(8,128)(2,1)S(1)} collective-permute-done((bf16[320,256]{1,0:T(8,128)(2,1)S(1)}, bf16[320,256]{1,0:T(8,128)(2,1)S(1)}, u32[]{:S(2)}, u32[]{:S(2)}) %collective-permute-start.5) | collective-permute-done | bytes 163872 | tf_op jit(solution)/shard_map/ppermute | solution.py:196
  40.2 1.1 collective-permute-done.6.refs_7_
  41.3 0.1 shard_map.48.refs_8_
  41.4 0.1 collective-permute-start.7
  41.5 1.5 %shard_map.49 = (bf16[640,1280]{1,0:T(8,128)(2,1)}, bf16[2,4,160,256]{3,2,1,0:T(8,128)(2,1)S(1)}) custom-call(s32[1]{0:T(128)} %bitcast.pos_ref, bf16[320,256]{1,0:T(8,128)(2,1)S(1)} %get-tuple-element.32.refs_0_, bf16[320,256]{1,0:T(8,128)(2,1)S(1)} %collective-permute-done.refs_1_, bf16[320,256]{1,0:T(8,128)(2,1)S(1)} %collective-permute-done.1.refs_2_, ...), custom_call_target="tpu_custom_call" | custom-call | flops 419430400 | bytes 3932168 | tf_op jit(solution)/shard_map/pallas_call | solution.py:180
  43.0 0.6 collective-permute-done.7.k_far
  43.6 1.5 %shard_map.50 = bf16[640,1280]{1,0:T(8,128)(2,1)} custom-call(bf16[640,1280]{1,0:T(8,128)(2,1)} %get-tuple-element.42._, bf16[2,4,160,256]{3,2,1,0:T(8,128)(2,1)S(1)} %get-tuple-element.43.q, bf16[2,4,160,256]{3,2,1,0:T(8,128)(2,1)S(1)} %collective-permute-done.7.k_far), custom_call_target="tpu_custom_call", output_to_operand_aliasing={{}: (0, {})} | custom-call | flops 419430400 | bytes 5898240 | tf_op jit(solution)/shard_map/pallas_call | solution.py:180
  45.1 7.4 %all-to-all-start = ((bf16[16,40,1280]{2,1,0:T(8,128)(2,1)}), bf16[16,40,1280]{2,1,0:T(8,128)(2,1)S(1)}, u32[]{:S(2)}, u32[]{:S(2)}) async-start(bf16[16,40,1280]{2,1,0:T(8,128)(2,1)} %bitcast.2), calls=%async_computation | async-start | bytes 3276800 | tf_op jit(solution)/shard_map/all_to_all | solution.py:267
  52.5 3.5 %collective-permute-start.8 = (bf16[160,256]{1,0:T(8,128)(2,1)S(1)}, bf16[160,256]{1,0:T(8,128)(2,1)S(1)}, u32[]{:S(2)}, u32[]{:S(2)}) collective-permute-start(bf16[160,256]{1,0:T(8,128)(2,1)S(1)} %get-tuple-element.44), channel_id=1, source_target_pairs={{0,1},{1,0},{64,65},{65,64},{128,129},{129,128},{192,193},{193,192... | collective-permute-start | bytes 245768 | tf_op jit(solution)/shard_map/ppermute | solution.py:196
  56.0 2.3 %collective-permute-start.9 = (bf16[160,256]{1,0:T(8,128)(2,1)S(1)}, bf16[160,256]{1,0:T(8,128)(2,1)S(1)}, u32[]{:S(2)}, u32[]{:S(2)}) collective-permute-start(bf16[160,256]{1,0:T(8,128)(2,1)S(1)} %get-tuple-element.45), channel_id=1, source_target_pairs={{0,192},{1,193},{64,1},{65,0},{128,65},{129,64},{192,129},{193,128... | collective-permute-start | bytes 245768 | tf_op jit(solution)/shard_map/ppermute | solution.py:196
  58.4 2.7 %collective-permute-start.10 = (bf16[160,256]{1,0:T(8,128)(2,1)S(1)}, bf16[160,256]{1,0:T(8,128)(2,1)S(1)}, u32[]{:S(2)}, u32[]{:S(2)}) collective-permute-start(bf16[160,256]{1,0:T(8,128)(2,1)S(1)} %get-tuple-element.46), channel_id=1, source_target_pairs={{0,65},{1,64},{64,129},{65,128},{128,193},{129,192},{192,0},{193,1... | collective-permute-start | bytes 245768 | tf_op jit(solution)/shard_map/ppermute | solution.py:196
  61.1 0.1 collective-permute-start.11
  61.2 2.9 %collective-permute-done.8.refs_0_.refs_1_ = bf16[160,256]{1,0:T(8,128)(2,1)S(1)} collective-permute-done((bf16[160,256]{1,0:T(8,128)(2,1)S(1)}, bf16[160,256]{1,0:T(8,128)(2,1)S(1)}, u32[]{:S(2)}, u32[]{:S(2)}) %collective-permute-start.8) | collective-permute-done | bytes 81952 | tf_op jit(solution)/shard_map/ppermute | solution.py:196
  64.1 5.4 %collective-permute-done.9.refs_1_.refs_2_ = bf16[160,256]{1,0:T(8,128)(2,1)S(1)} collective-permute-done((bf16[160,256]{1,0:T(8,128)(2,1)S(1)}, bf16[160,256]{1,0:T(8,128)(2,1)S(1)}, u32[]{:S(2)}, u32[]{:S(2)}) %collective-permute-start.9) | collective-permute-done | bytes 81952 | tf_op jit(solution)/shard_map/ppermute | solution.py:196
  69.5 0.0 collective-permute-done.10.refs_2_.refs_3_
  69.5 0.0 collective-permute-done.11.refs_3_.refs_4_
  69.5 5.6 %all-to-all-done.x_ref = bf16[16,40,1280]{2,1,0:T(8,128)(2,1)S(1)} async-done(((bf16[16,40,1280]{2,1,0:T(8,128)(2,1)}), bf16[16,40,1280]{2,1,0:T(8,128)(2,1)S(1)}, u32[]{:S(2)}, u32[]{:S(2)}) %all-to-all-start) | async-done | bytes 1638432 | tf_op jit(solution)/shard_map/all_to_all | solution.py:267
  75.1 1.6 %shard_map.51 = bf16[16,40,1280]{2,1,0:T(8,128)(2,1)} custom-call(bf16[16,40,1280]{2,1,0:T(8,128)(2,1)S(1)} %all-to-all-done.x_ref, bf16[160,256]{1,0:T(8,128)(2,1)S(1)} %collective-permute-done.8.refs_0_.refs_1_, bf16[160,256]{1,0:T(8,128)(2,1)S(1)} %collective-permute-done.9.refs_1_.refs_2_, bf16[160,256]{1,0:T(8,128)(2,1)S(1)} %collective-permute-done.10.refs_2_.refs_3_, ...), custom_call_target="tpu_custom_call" | custom-call | bytes 3932160 | tf_op jit(solution)/shard_map/pallas_call | solution.py:180
  76.7 6.2 %all-to-all-start.1 = ((bf16[16,40,1280]{2,1,0:T(8,128)(2,1)}), bf16[16,40,1280]{2,1,0:T(8,128)(2,1)S(1)}, u32[]{:S(2)}, u32[]{:S(2)}) async-start(bf16[16,40,1280]{2,1,0:T(8,128)(2,1)} %shard_map.51), calls=%async_computation.1 | async-start | bytes 3276800 | tf_op jit(solution)/shard_map/all_to_all | solution.py:277
  83.0 1.3 collective-permute-start.12
  84.2 2.8 %collective-permute-start.13 = (bf16[160,256]{1,0:T(8,128)(2,1)S(1)}, bf16[160,256]{1,0:T(8,128)(2,1)S(1)}, u32[]{:S(2)}, u32[]{:S(2)}) collective-permute-start(bf16[160,256]{1,0:T(8,128)(2,1)S(1)} %get-tuple-element.49), channel_id=1, source_target_pairs={{0,64},{1,65},{64,128},{65,129},{128,192},{129,193},{192,1},{193,0... | collective-permute-start | bytes 245768 | tf_op jit(solution)/shard_map/ppermute | solution.py:196
  87.1 0.4 collective-permute-start.14
  87.5 1.8 %collective-permute-done.12.refs_5_ = bf16[160,256]{1,0:T(8,128)(2,1)S(1)} collective-permute-done((bf16[160,256]{1,0:T(8,128)(2,1)S(1)}, bf16[160,256]{1,0:T(8,128)(2,1)S(1)}, u32[]{:S(2)}, u32[]{:S(2)}) %collective-permute-start.12) | collective-permute-done | bytes 81952 | tf_op jit(solution)/shard_map/ppermute | solution.py:196
  89.3 0.6 collective-permute-done.13.refs_6_
  89.9 1.6 %collective-permute-done.14.refs_7_ = bf16[160,256]{1,0:T(8,128)(2,1)S(1)} collective-permute-done((bf16[160,256]{1,0:T(8,128)(2,1)S(1)}, bf16[160,256]{1,0:T(8,128)(2,1)S(1)}, u32[]{:S(2)}, u32[]{:S(2)}) %collective-permute-start.14) | collective-permute-done | bytes 81952 | tf_op jit(solution)/shard_map/ppermute | solution.py:196
  91.5 0.1 shard_map.52.v_ref
  91.6 0.1 collective-permute-start.15
  91.7 2.1 %collective-permute-done.15._.v_far = bf16[2,4,160,256]{3,2,1,0:T(8,128)(2,1)S(1)} collective-permute-done((bf16[2,4,160,256]{3,2,1,0:T(8,128)(2,1)S(1)}, bf16[2,4,160,256]{3,2,1,0:T(8,128)(2,1)S(1)}, u32[]{:S(2)}, u32[]{:S(2)}) %collective-permute-start.15) | collective-permute-done | bytes 655392 | tf_op jit(solution)/shard_map/ppermute | solution.py:201
  93.8 9.7 %all-to-all-done.1 = bf16[16,40,1280]{2,1,0:T(8,128)(2,1)S(1)} async-done(((bf16[16,40,1280]{2,1,0:T(8,128)(2,1)}), bf16[16,40,1280]{2,1,0:T(8,128)(2,1)S(1)}, u32[]{:S(2)}, u32[]{:S(2)}) %all-to-all-start.1) | async-done | bytes 1638432 | tf_op jit(solution)/shard_map/all_to_all | solution.py:277
  103.5 0.7 shard_map.54
  104.2 0.0 copy-start.1
  104.2 3.6 %collective-permute-start.16 = (bf16[160,256]{1,0:T(8,128)(2,1)S(1)}, bf16[160,256]{1,0:T(8,128)(2,1)S(1)}, u32[]{:S(2)}, u32[]{:S(2)}) collective-permute-start(bf16[160,256]{1,0:T(8,128)(2,1)S(1)} %get-tuple-element.52), channel_id=1, source_target_pairs={{0,1},{1,0},{64,65},{65,64},{128,129},{129,128},{192,193},{193,192... | collective-permute-start | bytes 245768 | tf_op jit(solution)/shard_map/ppermute | solution.py:196
  107.8 2.4 %collective-permute-start.17 = (bf16[160,256]{1,0:T(8,128)(2,1)S(1)}, bf16[160,256]{1,0:T(8,128)(2,1)S(1)}, u32[]{:S(2)}, u32[]{:S(2)}) collective-permute-start(bf16[160,256]{1,0:T(8,128)(2,1)S(1)} %get-tuple-element.53), channel_id=1, source_target_pairs={{0,192},{1,193},{64,1},{65,0},{128,65},{129,64},{192,129},{193,128... | collective-permute-start | bytes 245768 | tf_op jit(solution)/shard_map/ppermute | solution.py:196
  110.2 0.4 collective-permute-start.18
  110.6 0.7 shard_map.55
  111.3 2.4 %collective-permute-start.19 = (bf16[160,256]{1,0:T(8,128)(2,1)S(1)}, bf16[160,256]{1,0:T(8,128)(2,1)S(1)}, u32[]{:S(2)}, u32[]{:S(2)}) collective-permute-start(bf16[160,256]{1,0:T(8,128)(2,1)S(1)} %get-tuple-element.55), channel_id=1, source_target_pairs={{0,65},{1,64},{64,129},{65,128},{128,193},{129,192},{192,0},{193,1... | collective-permute-start | bytes 245768 | tf_op jit(solution)/shard_map/ppermute | solution.py:196
  113.6 0.9 collective-permute-start.20
  114.6 0.0 collective-permute-done.16.refs_1_
  114.6 3.2 %collective-permute-start.21 = (bf16[160,256]{1,0:T(8,128)(2,1)S(1)}, bf16[160,256]{1,0:T(8,128)(2,1)S(1)}, u32[]{:S(2)}, u32[]{:S(2)}) collective-permute-start(bf16[160,256]{1,0:T(8,128)(2,1)S(1)} %get-tuple-element.57), channel_id=1, source_target_pairs={{0,129},{1,128},{64,193},{65,192},{128,0},{129,1},{192,64},{193,65... | collective-permute-start | bytes 245768 | tf_op jit(solution)/shard_map/ppermute | solution.py:196
  117.8 1.3 %collective-permute-done.17.refs_2_ = bf16[160,256]{1,0:T(8,128)(2,1)S(1)} collective-permute-done((bf16[160,256]{1,0:T(8,128)(2,1)S(1)}, bf16[160,256]{1,0:T(8,128)(2,1)S(1)}, u32[]{:S(2)}, u32[]{:S(2)}) %collective-permute-start.17) | collective-permute-done | bytes 81952 | tf_op jit(solution)/shard_map/ppermute | solution.py:196
  119.1 0.7 collective-permute-start.22
  119.8 0.0 collective-permute-done.18.refs_3_
  119.8 0.0 collective-permute-done.19.refs_4_
  119.8 0.7 collective-permute-done.20.refs_5_
  120.5 2.3 %collective-permute-done.21.refs_6_ = bf16[160,256]{1,0:T(8,128)(2,1)S(1)} collective-permute-done((bf16[160,256]{1,0:T(8,128)(2,1)S(1)}, bf16[160,256]{1,0:T(8,128)(2,1)S(1)}, u32[]{:S(2)}, u32[]{:S(2)}) %collective-permute-start.21) | collective-permute-done | bytes 81952 | tf_op jit(solution)/shard_map/ppermute | solution.py:196
  122.8 1.9 %collective-permute-done.22.refs_7_ = bf16[160,256]{1,0:T(8,128)(2,1)S(1)} collective-permute-done((bf16[160,256]{1,0:T(8,128)(2,1)S(1)}, bf16[160,256]{1,0:T(8,128)(2,1)S(1)}, u32[]{:S(2)}, u32[]{:S(2)}) %collective-permute-start.22) | collective-permute-done | bytes 81952 | tf_op jit(solution)/shard_map/ppermute | solution.py:196
  124.7 0.0 copy-done.1
  124.7 1.7 %shard_map.56 = f32[4,160,768]{2,1,0:T(8,128)} custom-call(s32[1]{0:T(128)} %bitcast.pos_ref, bf16[512,768]{1,0:T(8,128)(2,1)S(1)} %copy-done.1, bf16[160,256]{1,0:T(8,128)(2,1)S(1)} %get-tuple-element.51.refs_0_, bf16[160,256]{1,0:T(8,128)(2,1)S(1)} %collective-permute-done.16.refs_1_, bf16[160,256]{1,0:T(8,128)(2,1)S(1)} %collective-permute-done.17.refs_2_, ...), custom_call_target="tpu_custom_call" | custom-call | flops 503316480 | bytes 2883592 | tf_op jit(solution)/shard_map/pallas_call | solution.py:180
  (3 shorter events, 0.0 us)
Async XLA Ops:
  0.0 0.7 copy-start.2
  0.7 32.3 %copy-start = (bf16[768,3,512]{2,0,1:T(8,128)(2,1)S(1)}, bf16[768,3,512]{2,0,1:T(8,128)(2,1)}, u32[]{:S(2)}) copy-start(bf16[768,3,512]{2,0,1:T(8,128)(2,1)} %param.6) | copy-start | bytes 7077892
  4.5 19.3 %collective-permute-start = (bf16[320,256]{1,0:T(8,128)(2,1)S(1)}, bf16[320,256]{1,0:T(8,128)(2,1)S(1)}, u32[]{:S(2)}, u32[]{:S(2)}) collective-permute-start(bf16[320,256]{1,0:T(8,128)(2,1)S(1)} %get-tuple-element.33), channel_id=1, source_target_pairs={{0,1},{1,0},{64,65},{65,64},{128,129},{129,128},{192,193},{193,192... | collective-permute-start | bytes 491528 | tf_op jit(solution)/shard_map/ppermute | solution.py:196
  11.8 21.2 %collective-permute-start.1 = (bf16[320,256]{1,0:T(8,128)(2,1)S(1)}, bf16[320,256]{1,0:T(8,128)(2,1)S(1)}, u32[]{:S(2)}, u32[]{:S(2)}) collective-permute-start(bf16[320,256]{1,0:T(8,128)(2,1)S(1)} %get-tuple-element.34), channel_id=1, source_target_pairs={{0,192},{1,193},{64,1},{65,0},{128,65},{129,64},{192,129},{193,128... | collective-permute-start | bytes 491528 | tf_op jit(solution)/shard_map/ppermute | solution.py:196
  13.7 20.1 %collective-permute-start.2 = (bf16[320,256]{1,0:T(8,128)(2,1)S(1)}, bf16[320,256]{1,0:T(8,128)(2,1)S(1)}, u32[]{:S(2)}, u32[]{:S(2)}) collective-permute-start(bf16[320,256]{1,0:T(8,128)(2,1)S(1)} %get-tuple-element.35), channel_id=1, source_target_pairs={{0,65},{1,64},{64,129},{65,128},{128,193},{129,192},{192,0},{193,1... | collective-permute-start | bytes 491528 | tf_op jit(solution)/shard_map/ppermute | solution.py:196
  16.8 20.4 %collective-permute-start.3 = (bf16[320,256]{1,0:T(8,128)(2,1)S(1)}, bf16[320,256]{1,0:T(8,128)(2,1)S(1)}, u32[]{:S(2)}, u32[]{:S(2)}) collective-permute-start(bf16[320,256]{1,0:T(8,128)(2,1)S(1)} %get-tuple-element.36), channel_id=1, source_target_pairs={{0,128},{1,129},{64,192},{65,193},{128,1},{129,0},{192,65},{193,64... | collective-permute-start | bytes 491528 | tf_op jit(solution)/shard_map/ppermute | solution.py:196
  18.3 19.8 %collective-permute-start.4 = (bf16[320,256]{1,0:T(8,128)(2,1)S(1)}, bf16[320,256]{1,0:T(8,128)(2,1)S(1)}, u32[]{:S(2)}, u32[]{:S(2)}) collective-permute-start(bf16[320,256]{1,0:T(8,128)(2,1)S(1)} %get-tuple-element.37), channel_id=1, source_target_pairs={{0,129},{1,128},{64,193},{65,192},{128,0},{129,1},{192,64},{193,65... | collective-permute-start | bytes 491528 | tf_op jit(solution)/shard_map/ppermute | solution.py:196
  23.8 16.4 %collective-permute-start.5 = (bf16[320,256]{1,0:T(8,128)(2,1)S(1)}, bf16[320,256]{1,0:T(8,128)(2,1)S(1)}, u32[]{:S(2)}, u32[]{:S(2)}) collective-permute-start(bf16[320,256]{1,0:T(8,128)(2,1)S(1)} %get-tuple-element.38), channel_id=1, source_target_pairs={{0,64},{1,65},{64,128},{65,129},{128,192},{129,193},{192,1},{193,0... | collective-permute-start | bytes 491528 | tf_op jit(solution)/shard_map/ppermute | solution.py:196
  32.9 8.4 %collective-permute-start.6 = (bf16[320,256]{1,0:T(8,128)(2,1)S(1)}, bf16[320,256]{1,0:T(8,128)(2,1)S(1)}, u32[]{:S(2)}, u32[]{:S(2)}) collective-permute-start(bf16[320,256]{1,0:T(8,128)(2,1)S(1)} %get-tuple-element.39), channel_id=1, source_target_pairs={{0,193},{1,192},{64,0},{65,1},{128,64},{129,65},{192,128},{193,129... | collective-permute-start | bytes 491528 | tf_op jit(solution)/shard_map/ppermute | solution.py:196
  41.4 2.2 %collective-permute-start.7 = (bf16[2,4,160,256]{3,2,1,0:T(8,128)(2,1)S(1)}, bf16[2,4,160,256]{3,2,1,0:T(8,128)(2,1)S(1)}, u32[]{:S(2)}, u32[]{:S(2)}) collective-permute-start(bf16[2,4,160,256]{3,2,1,0:T(8,128)(2,1)S(1)} %shard_map.48.refs_8_), channel_id=1, source_target_pairs={{0,32},{32,0},{1,33},{33,1},{2,34},{34,2},{3,35},{35,3},{4,36},{36... | collective-permute-start | bytes 1966088 | tf_op jit(solution)/shard_map/ppermute | solution.py:201
  45.1 30.0 %all-to-all-start = ((bf16[16,40,1280]{2,1,0:T(8,128)(2,1)}), bf16[16,40,1280]{2,1,0:T(8,128)(2,1)S(1)}, u32[]{:S(2)}, u32[]{:S(2)}) async-start(bf16[16,40,1280]{2,1,0:T(8,128)(2,1)} %bitcast.2), calls=%async_computation | async-start | bytes 3276800 | tf_op jit(solution)/shard_map/all_to_all | solution.py:267
  52.5 11.6 %collective-permute-start.8 = (bf16[160,256]{1,0:T(8,128)(2,1)S(1)}, bf16[160,256]{1,0:T(8,128)(2,1)S(1)}, u32[]{:S(2)}, u32[]{:S(2)}) collective-permute-start(bf16[160,256]{1,0:T(8,128)(2,1)S(1)} %get-tuple-element.44), channel_id=1, source_target_pairs={{0,1},{1,0},{64,65},{65,64},{128,129},{129,128},{192,193},{193,192... | collective-permute-start | bytes 245768 | tf_op jit(solution)/shard_map/ppermute | solution.py:196
  56.0 13.5 %collective-permute-start.9 = (bf16[160,256]{1,0:T(8,128)(2,1)S(1)}, bf16[160,256]{1,0:T(8,128)(2,1)S(1)}, u32[]{:S(2)}, u32[]{:S(2)}) collective-permute-start(bf16[160,256]{1,0:T(8,128)(2,1)S(1)} %get-tuple-element.45), channel_id=1, source_target_pairs={{0,192},{1,193},{64,1},{65,0},{128,65},{129,64},{192,129},{193,128... | collective-permute-start | bytes 245768 | tf_op jit(solution)/shard_map/ppermute | solution.py:196
  58.4 11.1 %collective-permute-start.10 = (bf16[160,256]{1,0:T(8,128)(2,1)S(1)}, bf16[160,256]{1,0:T(8,128)(2,1)S(1)}, u32[]{:S(2)}, u32[]{:S(2)}) collective-permute-start(bf16[160,256]{1,0:T(8,128)(2,1)S(1)} %get-tuple-element.46), channel_id=1, source_target_pairs={{0,65},{1,64},{64,129},{65,128},{128,193},{129,192},{192,0},{193,1... | collective-permute-start | bytes 245768 | tf_op jit(solution)/shard_map/ppermute | solution.py:196
  61.1 8.4 %collective-permute-start.11 = (bf16[160,256]{1,0:T(8,128)(2,1)S(1)}, bf16[160,256]{1,0:T(8,128)(2,1)S(1)}, u32[]{:S(2)}, u32[]{:S(2)}) collective-permute-start(bf16[160,256]{1,0:T(8,128)(2,1)S(1)} %get-tuple-element.47), channel_id=1, source_target_pairs={{0,128},{1,129},{64,192},{65,193},{128,1},{129,0},{192,65},{193,64... | collective-permute-start | bytes 245768 | tf_op jit(solution)/shard_map/ppermute | solution.py:196
  76.7 26.7 %all-to-all-start.1 = ((bf16[16,40,1280]{2,1,0:T(8,128)(2,1)}), bf16[16,40,1280]{2,1,0:T(8,128)(2,1)S(1)}, u32[]{:S(2)}, u32[]{:S(2)}) async-start(bf16[16,40,1280]{2,1,0:T(8,128)(2,1)} %shard_map.51), calls=%async_computation.1 | async-start | bytes 3276800 | tf_op jit(solution)/shard_map/all_to_all | solution.py:277
  83.0 6.3 %collective-permute-start.12 = (bf16[160,256]{1,0:T(8,128)(2,1)S(1)}, bf16[160,256]{1,0:T(8,128)(2,1)S(1)}, u32[]{:S(2)}, u32[]{:S(2)}) collective-permute-start(bf16[160,256]{1,0:T(8,128)(2,1)S(1)} %get-tuple-element.48), channel_id=1, source_target_pairs={{0,129},{1,128},{64,193},{65,192},{128,0},{129,1},{192,64},{193,65... | collective-permute-start | bytes 245768 | tf_op jit(solution)/shard_map/ppermute | solution.py:196
  84.2 5.7 %collective-permute-start.13 = (bf16[160,256]{1,0:T(8,128)(2,1)S(1)}, bf16[160,256]{1,0:T(8,128)(2,1)S(1)}, u32[]{:S(2)}, u32[]{:S(2)}) collective-permute-start(bf16[160,256]{1,0:T(8,128)(2,1)S(1)} %get-tuple-element.49), channel_id=1, source_target_pairs={{0,64},{1,65},{64,128},{65,129},{128,192},{129,193},{192,1},{193,0... | collective-permute-start | bytes 245768 | tf_op jit(solution)/shard_map/ppermute | solution.py:196
  87.1 4.4 %collective-permute-start.14 = (bf16[160,256]{1,0:T(8,128)(2,1)S(1)}, bf16[160,256]{1,0:T(8,128)(2,1)S(1)}, u32[]{:S(2)}, u32[]{:S(2)}) collective-permute-start(bf16[160,256]{1,0:T(8,128)(2,1)S(1)} %get-tuple-element.50), channel_id=1, source_target_pairs={{0,193},{1,192},{64,0},{65,1},{128,64},{129,65},{192,128},{193,129... | collective-permute-start | bytes 245768 | tf_op jit(solution)/shard_map/ppermute | solution.py:196
  91.6 2.2 %collective-permute-start.15 = (bf16[2,4,160,256]{3,2,1,0:T(8,128)(2,1)S(1)}, bf16[2,4,160,256]{3,2,1,0:T(8,128)(2,1)S(1)}, u32[]{:S(2)}, u32[]{:S(2)}) collective-permute-start(bf16[2,4,160,256]{3,2,1,0:T(8,128)(2,1)S(1)} %shard_map.52.v_ref), channel_id=1, source_target_pairs={{0,32},{32,0},{1,33},{33,1},{2,34},{34,2},{3,35},{35,3},{4,36},{36... | collective-permute-start | bytes 1966088 | tf_op jit(solution)/shard_map/ppermute | solution.py:201
  104.2 20.6 %copy-start.1 = (bf16[512,768]{1,0:T(8,128)(2,1)S(1)}, bf16[512,768]{1,0:T(8,128)(2,1)}, u32[]{:S(2)}) copy-start(bf16[512,768]{1,0:T(8,128)(2,1)} %w_ref.1) | copy-start | bytes 2359300
  104.2 10.4 %collective-permute-start.16 = (bf16[160,256]{1,0:T(8,128)(2,1)S(1)}, bf16[160,256]{1,0:T(8,128)(2,1)S(1)}, u32[]{:S(2)}, u32[]{:S(2)}) collective-permute-start(bf16[160,256]{1,0:T(8,128)(2,1)S(1)} %get-tuple-element.52), channel_id=1, source_target_pairs={{0,1},{1,0},{64,65},{65,64},{128,129},{129,128},{192,193},{193,192... | collective-permute-start | bytes 245768 | tf_op jit(solution)/shard_map/ppermute | solution.py:196
  107.8 11.3 %collective-permute-start.17 = (bf16[160,256]{1,0:T(8,128)(2,1)S(1)}, bf16[160,256]{1,0:T(8,128)(2,1)S(1)}, u32[]{:S(2)}, u32[]{:S(2)}) collective-permute-start(bf16[160,256]{1,0:T(8,128)(2,1)S(1)} %get-tuple-element.53), channel_id=1, source_target_pairs={{0,192},{1,193},{64,1},{65,0},{128,65},{129,64},{192,129},{193,128... | collective-permute-start | bytes 245768 | tf_op jit(solution)/shard_map/ppermute | solution.py:196
  110.2 9.6 %collective-permute-start.18 = (bf16[160,256]{1,0:T(8,128)(2,1)S(1)}, bf16[160,256]{1,0:T(8,128)(2,1)S(1)}, u32[]{:S(2)}, u32[]{:S(2)}) collective-permute-start(bf16[160,256]{1,0:T(8,128)(2,1)S(1)} %get-tuple-element.54), channel_id=1, source_target_pairs={{0,193},{1,192},{64,0},{65,1},{128,64},{129,65},{192,128},{193,129... | collective-permute-start | bytes 245768 | tf_op jit(solution)/shard_map/ppermute | solution.py:196
  111.3 8.5 %collective-permute-start.19 = (bf16[160,256]{1,0:T(8,128)(2,1)S(1)}, bf16[160,256]{1,0:T(8,128)(2,1)S(1)}, u32[]{:S(2)}, u32[]{:S(2)}) collective-permute-start(bf16[160,256]{1,0:T(8,128)(2,1)S(1)} %get-tuple-element.55), channel_id=1, source_target_pairs={{0,65},{1,64},{64,129},{65,128},{128,193},{129,192},{192,0},{193,1... | collective-permute-start | bytes 245768 | tf_op jit(solution)/shard_map/ppermute | solution.py:196
  113.6 6.9 %collective-permute-start.20 = (bf16[160,256]{1,0:T(8,128)(2,1)S(1)}, bf16[160,256]{1,0:T(8,128)(2,1)S(1)}, u32[]{:S(2)}, u32[]{:S(2)}) collective-permute-start(bf16[160,256]{1,0:T(8,128)(2,1)S(1)} %get-tuple-element.56), channel_id=1, source_target_pairs={{0,128},{1,129},{64,192},{65,193},{128,1},{129,0},{192,65},{193,64... | collective-permute-start | bytes 245768 | tf_op jit(solution)/shard_map/ppermute | solution.py:196
  114.6 8.3 %collective-permute-start.21 = (bf16[160,256]{1,0:T(8,128)(2,1)S(1)}, bf16[160,256]{1,0:T(8,128)(2,1)S(1)}, u32[]{:S(2)}, u32[]{:S(2)}) collective-permute-start(bf16[160,256]{1,0:T(8,128)(2,1)S(1)} %get-tuple-element.57), channel_id=1, source_target_pairs={{0,129},{1,128},{64,193},{65,192},{128,0},{129,1},{192,64},{193,65... | collective-permute-start | bytes 245768 | tf_op jit(solution)/shard_map/ppermute | solution.py:196
  119.1 5.7 %collective-permute-start.22 = (bf16[160,256]{1,0:T(8,128)(2,1)S(1)}, bf16[160,256]{1,0:T(8,128)(2,1)S(1)}, u32[]{:S(2)}, u32[]{:S(2)}) collective-permute-start(bf16[160,256]{1,0:T(8,128)(2,1)S(1)} %get-tuple-element.58), channel_id=1, source_target_pairs={{0,64},{1,65},{64,128},{65,129},{128,192},{129,193},{192,1},{193,0... | collective-permute-start | bytes 245768 | tf_op jit(solution)/shard_map/ppermute | solution.py:196

commit v9 on v8

--- a/solution.py
+++ b/solution.py
@@ -13,7 +13,7 @@
 Z, CORE, X, Y, W = 4, 2, 4, 4, 2
 RING = Z * W
 PLANE = X * Y
-STEPS = (0, 4, 3, 5, 2, 6, 1, 7)
+STEPS = (0, 7, 1, 5, 3, 4, 6, 2)
 BF = jnp.bfloat16
 F32 = jnp.float32
 VMEM = pl.BlockSpec(memory_space=pltpu.VMEM)
@@ -53,21 +53,42 @@
     gain_copy = pltpu.make_async_copy(gain_hbm, gain_ref, gain_sem)
     for copy in (x_copies[0], gain_copy, *x_copies[1:], w_copies[1], w_copies[0]):
         copy.start()
-    gain_copy.wait()
-    gain = gain_ref[...].reshape(1, width)
-    for r in range(seqs):
-        x_copies[r].wait()
+    def norm(r):
         x = x_ref[r].astype(F32)
         mean = jnp.mean(x, axis=-1, keepdims=True)
         off = x - mean
         var = jnp.mean(off * off, axis=-1, keepdims=True)
         normed[r * length : (r + 1) * length] = (off / jnp.sqrt(var + 1e-05) * gain).astype(BF)
+
+    def project(c, r):
+        y = jnp.dot(normed[r * length : (r + 2) * length], w_ref[c], preferred_element_type=F32)
+        for h in range(mine.shape[1]):
+            columns = slice(h * HEAD_DIM, (h + 1) * HEAD_DIM)
+            block = jnp.concatenate([y[:length, columns], y[length:, columns]], axis=1)
+            mine[c, h, :, r * HEAD_DIM : (r + 2) * HEAD_DIM] = block.astype(BF)
+
+    gain_copy.wait()
+    gain = gain_ref[...].reshape(1, width)
+    for r in range(seqs // 2):
+        x_copies[r].wait()
+        norm(r)
+    for r in range(seqs // 2, seqs):
+        x_copies[r].wait()
+    w_copies[1].wait()
+    for r in range(0, seqs // 2, 2):
+        project(1, r)
+    for r in range(seqs // 2, seqs):
+        norm(r)
+    w_copies[0].wait()
+    for r in range(0, seqs // 2, 2):
+        project(0, r)
+    for r in range(seqs // 2, seqs, 2):
+        project(1, r)
+        project(0, r)
     pos = pos_ref[0]
     for c in (1, 0):
-        w_copies[c].wait()
-        blocks_by_head(jnp.dot(normed[...], w_ref[c], preferred_element_type=F32), seqs, mine)
         for i, s in enumerate(STEPS):
-            both[i][(1 - c) * length : (2 - c) * length] = mine[head_at(pos + s)]
+            both[i][(1 - c) * length : (2 - c) * length] = mine[c, head_at(pos + s)]
 
 
 def values_kernel(seqs, pos_ref, normed, w_hbm, *refs):
@@ -100,15 +121,18 @@
     length = keys.shape[2]
     half = keys.shape[1] * length
     columns = pl.ds(side * half, half)
-    total = None
-    for w in range(W):
-        term = lax.dot_general(
-            q[w].reshape(half, -1), keys[w].reshape(half, -1), (((1,), (1,)), ((), ())), preferred_element_type=F32
-        )
-        total = term if total is None else total + term
     copies = []
-    for i, rows in enumerate(cuts(half, Z)):
-        terms[rows] = total[i * length : (i + 1) * length].astype(BF)
+    for i, rows in enumerate(cuts(half, 2)):
+        total = None
+        for w in range(W):
+            term = lax.dot_general(
+                q[w, i * Z // 2 : (i + 1) * Z // 2].reshape(half // 2, -1),
+                keys[w].reshape(half, -1),
+                (((1,), (1,)), ((), ())),
+                preferred_element_type=F32,
+            )
+            total = term if total is None else total + term
+        terms[rows] = total.astype(BF)
         copies.append(pltpu.make_async_copy(terms.at[rows], out_hbm.at[rows, columns], sem.at[i]))
         copies[i].start()
     for copy in copies:
@@ -220,7 +244,7 @@
         [pair] * RING + [jax.ShapeDtypeStruct((seqs * length, width), BF)],
         [pos, ln_gain, tokens, weights],
         [
-            pltpu.VMEM((RING, length, lanes), BF),
+            pltpu.VMEM((2, RING, length, lanes), BF),
             pltpu.VMEM(ln_gain.shape, F32),
             pltpu.VMEM(tokens.shape, BF),
             pltpu.VMEM((2, width, inner), BF),
@@ -249,7 +273,7 @@
         near_kernel,
         [jax.ShapeDtypeStruct((half, full), BF), whole],
         [pos, *both, keys],
-        [pltpu.VMEM((half, half), BF), dma((Z,))],
+        [pltpu.VMEM((half, half), BF), dma((2,))],
         flops=2 * half * half * W * lanes,
         out_specs=[HBM, VMEM],
     )
@@ -257,7 +281,7 @@
         far_kernel,
         jax.ShapeDtypeStruct((half, full), BF),
         [term, query, keys_far],
-        [pltpu.VMEM((half, half), BF), dma((Z,))],
+        [pltpu.VMEM((half, half), BF), dma((2,))],
         flops=2 * half * half * W * lanes,
         hbm=(0,),
         out_specs=HBM,

time: 127 us -> 126 us (level)
  starting transfers between devices: 57.4 us -> 55.6 us
    all_to_all x1, waiting for transfers between devices: 5.58 us -> 8.44 us  [shards(): terms = lax.all_to_all(term.reshape(chunk), ('x', 'y'), 0, 0, tiled=True)]
    all_to_all x1, waiting for transfers between devices: 9.7 us -> 7.26 us  [shards(): lax.all_to_all(probs, ('x', 'y'), 0, 0, tiled=True).reshape(half, full)]
    ppermute x21, starting transfers between devices: 43.5 us -> 41.7 us  [along_ring(): got.append(lax.ppermute(part, ('z', 'w'), pairs) if s else part)]
  transfers between devices with their start and end apart: 25 -> 25, of which waited for: 19 -> 18; matrix products, arithmetic and copies ran while one was open for 0% -> 0% of each run, Pallas kernels for 2% -> 2%
where the time goes in v9:
time: 126 us; the launch traced here: 125 us
  waiting for transfers between devices  56.4 us (45%)
  starting transfers between devices  55.6 us (44%)
  Pallas kernels  12.1 us (10%)
    ppermute x21, starting transfers between devices, along_ring(): got.append(lax.ppermute(part, ('z', 'w'), pairs) if s else part)  41.7 us
    ppermute x21, waiting for transfers between devices, along_ring(): got.append(lax.ppermute(part, ('z', 'w'), pairs) if s else part)  38.1 us
    pallas_call x11, Pallas kernels, call(): pl.pallas_call(kernel, out_shape=out_shape, in_specs=specs, out_specs=out...  12.1 us
    all_to_all x1, waiting for transfers between devices, shards(): terms = lax.all_to_all(term.reshape(chunk), ('x', 'y'), 0, 0, tiled=True)  8.44 us
    all_to_all x1, starting transfers between devices, shards(): terms = lax.all_to_all(term.reshape(chunk), ('x', 'y'), 0, 0, tiled=True)  7.44 us
    all_to_all x1, waiting for transfers between devices, shards(): lax.all_to_all(probs, ('x', 'y'), 0, 0, tiled=True).reshape(half, full)  7.26 us
    all_to_all x1, starting transfers between devices, shards(): lax.all_to_all(probs, ('x', 'y'), 0, 0, tiled=True).reshape(half, full)  6.24 us
    ppermute x2, waiting for transfers between devices, other_core(): return lax.ppermute(a, 'c', [(0, 1), (1, 0)])  2.68 us
  transfers between devices with their start and end apart: 25, of which 18 were waited for; matrix products, arithmetic and copies ran while one was open for 0% of the time, Pallas kernels for 2%

profile of v9, /device:TPU:6, one launch (start us, length us, event | category | flops | bytes accessed | tf_op | source)
XLA Modules:
  0.0 125.1 jit_solution(1291307988021612498)
XLA Ops:
  0.0 0.7 copy-done.2
  0.7 3.4 %shard_map.46 = (bf16[320,256]{1,0:T(8,128)(2,1)S(1)}, bf16[320,256]{1,0:T(8,128)(2,1)S(1)}, bf16[320,256]{1,0:T(8,128)(2,1)S(1)}, bf16[320,256]{1,0:T(8,128)(2,...) custom-call(s32[1]{0:T(128)} %bitcast.pos_ref, ...), custom_call_target="tpu_custom_call" | custom-call | flops 1006632960 | bytes 6690824 | tf_op jit(solution)/shard_map/pallas_call | solution.py:204
  4.1 5.9 %collective-permute-start = (bf16[320,256]{1,0:T(8,128)(2,1)S(1)}, bf16[320,256]{1,0:T(8,128)(2,1)S(1)}, u32[]{:S(2)}, u32[]{:S(2)}) collective-permute-start(bf16[320,256]{1,0:T(8,128)(2,1)S(1)} %get-tuple-element.33), channel_id=1, source_target_pairs={{0,193},{1,192},{64,0},{65,1},{128,64},{129,65},{192,128},{193,129... | collective-permute-start | bytes 491528 | tf_op jit(solution)/shard_map/ppermute | solution.py:220
  10.1 0.0 collective-permute-start.1
  10.1 2.9 %collective-permute-start.2 = (bf16[320,256]{1,0:T(8,128)(2,1)S(1)}, bf16[320,256]{1,0:T(8,128)(2,1)S(1)}, u32[]{:S(2)}, u32[]{:S(2)}) collective-permute-start(bf16[320,256]{1,0:T(8,128)(2,1)S(1)} %get-tuple-element.35), channel_id=1, source_target_pairs={{0,65},{1,64},{64,129},{65,128},{128,193},{129,192},{192,0},{193,1... | collective-permute-start | bytes 491528 | tf_op jit(solution)/shard_map/ppermute | solution.py:220
  13.0 0.9 collective-permute-start.3
  13.9 3.4 %collective-permute-start.4 = (bf16[320,256]{1,0:T(8,128)(2,1)S(1)}, bf16[320,256]{1,0:T(8,128)(2,1)S(1)}, u32[]{:S(2)}, u32[]{:S(2)}) collective-permute-start(bf16[320,256]{1,0:T(8,128)(2,1)S(1)} %get-tuple-element.37), channel_id=1, source_target_pairs={{0,1},{1,0},{64,65},{65,64},{128,129},{129,128},{192,193},{193,192... | collective-permute-start | bytes 491528 | tf_op jit(solution)/shard_map/ppermute | solution.py:220
  17.3 0.0 collective-permute-done.refs_1_
  17.3 2.0 %collective-permute-start.5 = (bf16[320,256]{1,0:T(8,128)(2,1)S(1)}, bf16[320,256]{1,0:T(8,128)(2,1)S(1)}, u32[]{:S(2)}, u32[]{:S(2)}) collective-permute-start(bf16[320,256]{1,0:T(8,128)(2,1)S(1)} %get-tuple-element.38), channel_id=1, source_target_pairs={{0,129},{1,128},{64,193},{65,192},{128,0},{129,1},{192,64},{193,65... | collective-permute-start | bytes 491528 | tf_op jit(solution)/shard_map/ppermute | solution.py:220
  19.2 0.0 collective-permute-done.1.refs_2_
  19.2 0.9 collective-permute-start.6
  20.2 0.0 copy-done
  20.2 0.9 shard_map.47
  21.1 9.2 %collective-permute-done.2.refs_3_ = bf16[320,256]{1,0:T(8,128)(2,1)S(1)} collective-permute-done((bf16[320,256]{1,0:T(8,128)(2,1)S(1)}, bf16[320,256]{1,0:T(8,128)(2,1)S(1)}, u32[]{:S(2)}, u32[]{:S(2)}) %collective-permute-start.2) | collective-permute-done | bytes 163872 | tf_op jit(solution)/shard_map/ppermute | solution.py:220
  30.2 0.8 collective-permute-done.3.refs_4_
  31.1 7.5 %collective-permute-done.4.refs_5_ = bf16[320,256]{1,0:T(8,128)(2,1)S(1)} collective-permute-done((bf16[320,256]{1,0:T(8,128)(2,1)S(1)}, bf16[320,256]{1,0:T(8,128)(2,1)S(1)}, u32[]{:S(2)}, u32[]{:S(2)}) %collective-permute-start.4) | collective-permute-done | bytes 163872 | tf_op jit(solution)/shard_map/ppermute | solution.py:220
  38.5 0.1 collective-permute-done.5.refs_6_
  38.6 2.1 %collective-permute-done.6.refs_7_ = bf16[320,256]{1,0:T(8,128)(2,1)S(1)} collective-permute-done((bf16[320,256]{1,0:T(8,128)(2,1)S(1)}, bf16[320,256]{1,0:T(8,128)(2,1)S(1)}, u32[]{:S(2)}, u32[]{:S(2)}) %collective-permute-start.6) | collective-permute-done | bytes 163872 | tf_op jit(solution)/shard_map/ppermute | solution.py:220
  40.7 0.1 shard_map.48.refs_8_
  40.8 0.1 collective-permute-start.7
  40.9 1.5 %shard_map.49 = (bf16[640,1280]{1,0:T(8,128)(2,1)}, bf16[2,4,160,256]{3,2,1,0:T(8,128)(2,1)S(1)}) custom-call(s32[1]{0:T(128)} %bitcast.pos_ref, bf16[320,256]{1,0:T(8,128)(2,1)S(1)} %get-tuple-element.32.refs_0_, bf16[320,256]{1,0:T(8,128)(2,1)S(1)} %collective-permute-done.refs_1_, bf16[320,256]{1,0:T(8,128)(2,1)S(1)} %collective-permute-done.1.refs_2_, ...), custom_call_target="tpu_custom_call" | custom-call | flops 419430400 | bytes 3932168 | tf_op jit(solution)/shard_map/pallas_call | solution.py:204
  42.4 0.6 collective-permute-done.7.k_far
  43.0 1.5 %shard_map.50 = bf16[640,1280]{1,0:T(8,128)(2,1)} custom-call(bf16[640,1280]{1,0:T(8,128)(2,1)} %get-tuple-element.42._, bf16[2,4,160,256]{3,2,1,0:T(8,128)(2,1)S(1)} %get-tuple-element.43.q, bf16[2,4,160,256]{3,2,1,0:T(8,128)(2,1)S(1)} %collective-permute-done.7.k_far), custom_call_target="tpu_custom_call", output_to_operand_aliasing={{}: (0, {})} | custom-call | flops 419430400 | bytes 5898240 | tf_op jit(solution)/shard_map/pallas_call | solution.py:204
  44.5 7.4 %all-to-all-start = ((bf16[16,40,1280]{2,1,0:T(8,128)(2,1)}), bf16[16,40,1280]{2,1,0:T(8,128)(2,1)S(1)}, u32[]{:S(2)}, u32[]{:S(2)}) async-start(bf16[16,40,1280]{2,1,0:T(8,128)(2,1)} %bitcast.2), calls=%async_computation | async-start | bytes 3276800 | tf_op jit(solution)/shard_map/all_to_all | solution.py:291
  51.9 1.5 %collective-permute-start.8 = (bf16[160,256]{1,0:T(8,128)(2,1)S(1)}, bf16[160,256]{1,0:T(8,128)(2,1)S(1)}, u32[]{:S(2)}, u32[]{:S(2)}) collective-permute-start(bf16[160,256]{1,0:T(8,128)(2,1)S(1)} %get-tuple-element.44), channel_id=1, source_target_pairs={{0,193},{1,192},{64,0},{65,1},{128,64},{129,65},{192,128},{193,129... | collective-permute-start | bytes 245768 | tf_op jit(solution)/shard_map/ppermute | solution.py:220
  53.4 1.6 %collective-permute-start.9 = (bf16[160,256]{1,0:T(8,128)(2,1)S(1)}, bf16[160,256]{1,0:T(8,128)(2,1)S(1)}, u32[]{:S(2)}, u32[]{:S(2)}) collective-permute-start(bf16[160,256]{1,0:T(8,128)(2,1)S(1)} %get-tuple-element.45), channel_id=1, source_target_pairs={{0,64},{1,65},{64,128},{65,129},{128,192},{129,193},{192,1},{193,0... | collective-permute-start | bytes 245768 | tf_op jit(solution)/shard_map/ppermute | solution.py:220
  55.0 1.4 %collective-permute-start.10 = (bf16[160,256]{1,0:T(8,128)(2,1)S(1)}, bf16[160,256]{1,0:T(8,128)(2,1)S(1)}, u32[]{:S(2)}, u32[]{:S(2)}) collective-permute-start(bf16[160,256]{1,0:T(8,128)(2,1)S(1)} %get-tuple-element.46), channel_id=1, source_target_pairs={{0,65},{1,64},{64,129},{65,128},{128,193},{129,192},{192,0},{193,1... | collective-permute-start | bytes 245768 | tf_op jit(solution)/shard_map/ppermute | solution.py:220
  56.4 2.4 %collective-permute-start.11 = (bf16[160,256]{1,0:T(8,128)(2,1)S(1)}, bf16[160,256]{1,0:T(8,128)(2,1)S(1)}, u32[]{:S(2)}, u32[]{:S(2)}) collective-permute-start(bf16[160,256]{1,0:T(8,128)(2,1)S(1)} %get-tuple-element.47), channel_id=1, source_target_pairs={{0,192},{1,193},{64,1},{65,0},{128,65},{129,64},{192,129},{193,128... | collective-permute-start | bytes 245768 | tf_op jit(solution)/shard_map/ppermute | solution.py:220
  58.9 0.0 collective-permute-done.8.refs_0_.refs_1_
  58.9 0.2 collective-permute-done.9.refs_1_.refs_2_
  59.1 3.4 %collective-permute-done.10.refs_2_.refs_3_ = bf16[160,256]{1,0:T(8,128)(2,1)S(1)} collective-permute-done((bf16[160,256]{1,0:T(8,128)(2,1)S(1)}, bf16[160,256]{1,0:T(8,128)(2,1)S(1)}, u32[]{:S(2)}, u32[]{:S(2)}) %collective-permute-start.10) | collective-permute-done | bytes 81952 | tf_op jit(solution)/shard_map/ppermute | solution.py:220
  62.5 3.5 %collective-permute-done.11.refs_3_.refs_4_ = bf16[160,256]{1,0:T(8,128)(2,1)S(1)} collective-permute-done((bf16[160,256]{1,0:T(8,128)(2,1)S(1)}, bf16[160,256]{1,0:T(8,128)(2,1)S(1)}, u32[]{:S(2)}, u32[]{:S(2)}) %collective-permute-start.11) | collective-permute-done | bytes 81952 | tf_op jit(solution)/shard_map/ppermute | solution.py:220
  66.1 8.4 %all-to-all-done.x_ref = bf16[16,40,1280]{2,1,0:T(8,128)(2,1)S(1)} async-done(((bf16[16,40,1280]{2,1,0:T(8,128)(2,1)}), bf16[16,40,1280]{2,1,0:T(8,128)(2,1)S(1)}, u32[]{:S(2)}, u32[]{:S(2)}) %all-to-all-start) | async-done | bytes 1638432 | tf_op jit(solution)/shard_map/all_to_all | solution.py:291
  74.5 1.6 %shard_map.51 = bf16[16,40,1280]{2,1,0:T(8,128)(2,1)} custom-call(bf16[16,40,1280]{2,1,0:T(8,128)(2,1)S(1)} %all-to-all-done.x_ref, bf16[160,256]{1,0:T(8,128)(2,1)S(1)} %collective-permute-done.8.refs_0_.refs_1_, bf16[160,256]{1,0:T(8,128)(2,1)S(1)} %collective-permute-done.9.refs_1_.refs_2_, bf16[160,256]{1,0:T(8,128)(2,1)S(1)} %collective-permute-done.10.refs_2_.refs_3_, ...), custom_call_target="tpu_custom_call" | custom-call | bytes 3932160 | tf_op jit(solution)/shard_map/pallas_call | solution.py:204
  76.1 6.2 %all-to-all-start.1 = ((bf16[16,40,1280]{2,1,0:T(8,128)(2,1)}), bf16[16,40,1280]{2,1,0:T(8,128)(2,1)S(1)}, u32[]{:S(2)}, u32[]{:S(2)}) async-start(bf16[16,40,1280]{2,1,0:T(8,128)(2,1)} %shard_map.51), calls=%async_computation.1 | async-start | bytes 3276800 | tf_op jit(solution)/shard_map/all_to_all | solution.py:301
  82.4 1.9 %collective-permute-start.12 = (bf16[160,256]{1,0:T(8,128)(2,1)S(1)}, bf16[160,256]{1,0:T(8,128)(2,1)S(1)}, u32[]{:S(2)}, u32[]{:S(2)}) collective-permute-start(bf16[160,256]{1,0:T(8,128)(2,1)S(1)} %get-tuple-element.48), channel_id=1, source_target_pairs={{0,1},{1,0},{64,65},{65,64},{128,129},{129,128},{192,193},{193,192... | collective-permute-start | bytes 245768 | tf_op jit(solution)/shard_map/ppermute | solution.py:220
  84.3 1.7 %collective-permute-start.13 = (bf16[160,256]{1,0:T(8,128)(2,1)S(1)}, bf16[160,256]{1,0:T(8,128)(2,1)S(1)}, u32[]{:S(2)}, u32[]{:S(2)}) collective-permute-start(bf16[160,256]{1,0:T(8,128)(2,1)S(1)} %get-tuple-element.49), channel_id=1, source_target_pairs={{0,129},{1,128},{64,193},{65,192},{128,0},{129,1},{192,64},{193,65... | collective-permute-start | bytes 245768 | tf_op jit(solution)/shard_map/ppermute | solution.py:220
  86.0 1.2 collective-permute-start.14
  87.2 4.5 %collective-permute-done.12.refs_5_ = bf16[160,256]{1,0:T(8,128)(2,1)S(1)} collective-permute-done((bf16[160,256]{1,0:T(8,128)(2,1)S(1)}, bf16[160,256]{1,0:T(8,128)(2,1)S(1)}, u32[]{:S(2)}, u32[]{:S(2)}) %collective-permute-start.12) | collective-permute-done | bytes 81952 | tf_op jit(solution)/shard_map/ppermute | solution.py:220
  91.7 0.6 collective-permute-done.13.refs_6_
  92.2 1.1 collective-permute-done.14.refs_7_
  93.3 0.1 shard_map.52.v_ref
  93.4 0.1 collective-permute-start.15
  93.5 2.1 %collective-permute-done.15._.v_far = bf16[2,4,160,256]{3,2,1,0:T(8,128)(2,1)S(1)} collective-permute-done((bf16[2,4,160,256]{3,2,1,0:T(8,128)(2,1)S(1)}, bf16[2,4,160,256]{3,2,1,0:T(8,128)(2,1)S(1)}, u32[]{:S(2)}, u32[]{:S(2)}) %collective-permute-start.15) | collective-permute-done | bytes 655392 | tf_op jit(solution)/shard_map/ppermute | solution.py:225
  95.6 7.3 %all-to-all-done.1 = bf16[16,40,1280]{2,1,0:T(8,128)(2,1)S(1)} async-done(((bf16[16,40,1280]{2,1,0:T(8,128)(2,1)}), bf16[16,40,1280]{2,1,0:T(8,128)(2,1)S(1)}, u32[]{:S(2)}, u32[]{:S(2)}) %all-to-all-start.1) | async-done | bytes 1638432 | tf_op jit(solution)/shard_map/all_to_all | solution.py:301
  102.8 0.7 shard_map.54
  103.5 0.0 copy-start.1
  103.6 2.0 %collective-permute-start.16 = (bf16[160,256]{1,0:T(8,128)(2,1)S(1)}, bf16[160,256]{1,0:T(8,128)(2,1)S(1)}, u32[]{:S(2)}, u32[]{:S(2)}) collective-permute-start(bf16[160,256]{1,0:T(8,128)(2,1)S(1)} %get-tuple-element.52), channel_id=1, source_target_pairs={{0,1},{1,0},{64,65},{65,64},{128,129},{129,128},{192,193},{193,192... | collective-permute-start | bytes 245768 | tf_op jit(solution)/shard_map/ppermute | solution.py:220
  105.6 2.9 %collective-permute-start.17 = (bf16[160,256]{1,0:T(8,128)(2,1)S(1)}, bf16[160,256]{1,0:T(8,128)(2,1)S(1)}, u32[]{:S(2)}, u32[]{:S(2)}) collective-permute-start(bf16[160,256]{1,0:T(8,128)(2,1)S(1)} %get-tuple-element.53), channel_id=1, source_target_pairs={{0,192},{1,193},{64,1},{65,0},{128,65},{129,64},{192,129},{193,128... | collective-permute-start | bytes 245768 | tf_op jit(solution)/shard_map/ppermute | solution.py:220
  108.4 2.2 %collective-permute-start.18 = (bf16[160,256]{1,0:T(8,128)(2,1)S(1)}, bf16[160,256]{1,0:T(8,128)(2,1)S(1)}, u32[]{:S(2)}, u32[]{:S(2)}) collective-permute-start(bf16[160,256]{1,0:T(8,128)(2,1)S(1)} %get-tuple-element.54), channel_id=1, source_target_pairs={{0,193},{1,192},{64,0},{65,1},{128,64},{129,65},{192,128},{193,129... | collective-permute-start | bytes 245768 | tf_op jit(solution)/shard_map/ppermute | solution.py:220
  110.7 0.7 shard_map.55
  111.4 0.6 collective-permute-start.19
  112.0 2.9 %collective-permute-start.20 = (bf16[160,256]{1,0:T(8,128)(2,1)S(1)}, bf16[160,256]{1,0:T(8,128)(2,1)S(1)}, u32[]{:S(2)}, u32[]{:S(2)}) collective-permute-start(bf16[160,256]{1,0:T(8,128)(2,1)S(1)} %get-tuple-element.56), channel_id=1, source_target_pairs={{0,128},{1,129},{64,192},{65,193},{128,1},{129,0},{192,65},{193,64... | collective-permute-start | bytes 245768 | tf_op jit(solution)/shard_map/ppermute | solution.py:220
  114.9 0.0 collective-permute-done.16.refs_1_
  114.9 2.7 %collective-permute-start.21 = (bf16[160,256]{1,0:T(8,128)(2,1)S(1)}, bf16[160,256]{1,0:T(8,128)(2,1)S(1)}, u32[]{:S(2)}, u32[]{:S(2)}) collective-permute-start(bf16[160,256]{1,0:T(8,128)(2,1)S(1)} %get-tuple-element.57), channel_id=1, source_target_pairs={{0,129},{1,128},{64,193},{65,192},{128,0},{129,1},{192,64},{193,65... | collective-permute-start | bytes 245768 | tf_op jit(solution)/shard_map/ppermute | solution.py:220
  117.6 0.0 collective-permute-done.17.refs_2_
  117.6 0.6 collective-permute-start.22
  118.1 0.0 collective-permute-done.18.refs_3_
  118.1 2.6 %collective-permute-done.19.refs_4_ = bf16[160,256]{1,0:T(8,128)(2,1)S(1)} collective-permute-done((bf16[160,256]{1,0:T(8,128)(2,1)S(1)}, bf16[160,256]{1,0:T(8,128)(2,1)S(1)}, u32[]{:S(2)}, u32[]{:S(2)}) %collective-permute-start.19) | collective-permute-done | bytes 81952 | tf_op jit(solution)/shard_map/ppermute | solution.py:220
  120.7 0.0 collective-permute-done.20.refs_5_
  120.7 2.3 %collective-permute-done.21.refs_6_ = bf16[160,256]{1,0:T(8,128)(2,1)S(1)} collective-permute-done((bf16[160,256]{1,0:T(8,128)(2,1)S(1)}, bf16[160,256]{1,0:T(8,128)(2,1)S(1)}, u32[]{:S(2)}, u32[]{:S(2)}) %collective-permute-start.21) | collective-permute-done | bytes 81952 | tf_op jit(solution)/shard_map/ppermute | solution.py:220
  123.0 0.2 collective-permute-done.22.refs_7_
  123.2 0.0 copy-done.1
  123.2 1.7 %shard_map.56 = f32[4,160,768]{2,1,0:T(8,128)} custom-call(s32[1]{0:T(128)} %bitcast.pos_ref, bf16[512,768]{1,0:T(8,128)(2,1)S(1)} %copy-done.1, bf16[160,256]{1,0:T(8,128)(2,1)S(1)} %get-tuple-element.51.refs_0_, bf16[160,256]{1,0:T(8,128)(2,1)S(1)} %collective-permute-done.16.refs_1_, bf16[160,256]{1,0:T(8,128)(2,1)S(1)} %collective-permute-done.17.refs_2_, ...), custom_call_target="tpu_custom_call" | custom-call | flops 503316480 | bytes 2883592 | tf_op jit(solution)/shard_map/pallas_call | solution.py:204
  (3 shorter events, 0.0 us)
Async XLA Ops:
  0.0 0.7 copy-start.2
  0.7 19.5 %copy-start = (bf16[768,3,512]{2,0,1:T(8,128)(2,1)S(1)}, bf16[768,3,512]{2,0,1:T(8,128)(2,1)}, u32[]{:S(2)}) copy-start(bf16[768,3,512]{2,0,1:T(8,128)(2,1)} %param.6) | copy-start | bytes 7077892
  4.1 13.1 %collective-permute-start = (bf16[320,256]{1,0:T(8,128)(2,1)S(1)}, bf16[320,256]{1,0:T(8,128)(2,1)S(1)}, u32[]{:S(2)}, u32[]{:S(2)}) collective-permute-start(bf16[320,256]{1,0:T(8,128)(2,1)S(1)} %get-tuple-element.33), channel_id=1, source_target_pairs={{0,193},{1,192},{64,0},{65,1},{128,64},{129,65},{192,128},{193,129... | collective-permute-start | bytes 491528 | tf_op jit(solution)/shard_map/ppermute | solution.py:220
  10.1 9.2 %collective-permute-start.1 = (bf16[320,256]{1,0:T(8,128)(2,1)S(1)}, bf16[320,256]{1,0:T(8,128)(2,1)S(1)}, u32[]{:S(2)}, u32[]{:S(2)}) collective-permute-start(bf16[320,256]{1,0:T(8,128)(2,1)S(1)} %get-tuple-element.34), channel_id=1, source_target_pairs={{0,64},{1,65},{64,128},{65,129},{128,192},{129,193},{192,1},{193,0... | collective-permute-start | bytes 491528 | tf_op jit(solution)/shard_map/ppermute | solution.py:220
  10.1 20.2 %collective-permute-start.2 = (bf16[320,256]{1,0:T(8,128)(2,1)S(1)}, bf16[320,256]{1,0:T(8,128)(2,1)S(1)}, u32[]{:S(2)}, u32[]{:S(2)}) collective-permute-start(bf16[320,256]{1,0:T(8,128)(2,1)S(1)} %get-tuple-element.35), channel_id=1, source_target_pairs={{0,65},{1,64},{64,129},{65,128},{128,193},{129,192},{192,0},{193,1... | collective-permute-start | bytes 491528 | tf_op jit(solution)/shard_map/ppermute | solution.py:220
  13.0 18.1 %collective-permute-start.3 = (bf16[320,256]{1,0:T(8,128)(2,1)S(1)}, bf16[320,256]{1,0:T(8,128)(2,1)S(1)}, u32[]{:S(2)}, u32[]{:S(2)}) collective-permute-start(bf16[320,256]{1,0:T(8,128)(2,1)S(1)} %get-tuple-element.36), channel_id=1, source_target_pairs={{0,192},{1,193},{64,1},{65,0},{128,65},{129,64},{192,129},{193,128... | collective-permute-start | bytes 491528 | tf_op jit(solution)/shard_map/ppermute | solution.py:220
  13.9 24.6 %collective-permute-start.4 = (bf16[320,256]{1,0:T(8,128)(2,1)S(1)}, bf16[320,256]{1,0:T(8,128)(2,1)S(1)}, u32[]{:S(2)}, u32[]{:S(2)}) collective-permute-start(bf16[320,256]{1,0:T(8,128)(2,1)S(1)} %get-tuple-element.37), channel_id=1, source_target_pairs={{0,1},{1,0},{64,65},{65,64},{128,129},{129,128},{192,193},{193,192... | collective-permute-start | bytes 491528 | tf_op jit(solution)/shard_map/ppermute | solution.py:220
  17.3 21.3 %collective-permute-start.5 = (bf16[320,256]{1,0:T(8,128)(2,1)S(1)}, bf16[320,256]{1,0:T(8,128)(2,1)S(1)}, u32[]{:S(2)}, u32[]{:S(2)}) collective-permute-start(bf16[320,256]{1,0:T(8,128)(2,1)S(1)} %get-tuple-element.38), channel_id=1, source_target_pairs={{0,129},{1,128},{64,193},{65,192},{128,0},{129,1},{192,64},{193,65... | collective-permute-start | bytes 491528 | tf_op jit(solution)/shard_map/ppermute | solution.py:220
  19.2 21.5 %collective-permute-start.6 = (bf16[320,256]{1,0:T(8,128)(2,1)S(1)}, bf16[320,256]{1,0:T(8,128)(2,1)S(1)}, u32[]{:S(2)}, u32[]{:S(2)}) collective-permute-start(bf16[320,256]{1,0:T(8,128)(2,1)S(1)} %get-tuple-element.39), channel_id=1, source_target_pairs={{0,128},{1,129},{64,192},{65,193},{128,1},{129,0},{192,65},{193,64... | collective-permute-start | bytes 491528 | tf_op jit(solution)/shard_map/ppermute | solution.py:220
  40.8 2.2 %collective-permute-start.7 = (bf16[2,4,160,256]{3,2,1,0:T(8,128)(2,1)S(1)}, bf16[2,4,160,256]{3,2,1,0:T(8,128)(2,1)S(1)}, u32[]{:S(2)}, u32[]{:S(2)}) collective-permute-start(bf16[2,4,160,256]{3,2,1,0:T(8,128)(2,1)S(1)} %shard_map.48.refs_8_), channel_id=1, source_target_pairs={{0,32},{32,0},{1,33},{33,1},{2,34},{34,2},{3,35},{35,3},{4,36},{36... | collective-permute-start | bytes 1966088 | tf_op jit(solution)/shard_map/ppermute | solution.py:225
  44.5 30.0 %all-to-all-start = ((bf16[16,40,1280]{2,1,0:T(8,128)(2,1)}), bf16[16,40,1280]{2,1,0:T(8,128)(2,1)S(1)}, u32[]{:S(2)}, u32[]{:S(2)}) async-start(bf16[16,40,1280]{2,1,0:T(8,128)(2,1)} %bitcast.2), calls=%async_computation | async-start | bytes 3276800 | tf_op jit(solution)/shard_map/all_to_all | solution.py:291
  51.9 7.0 %collective-permute-start.8 = (bf16[160,256]{1,0:T(8,128)(2,1)S(1)}, bf16[160,256]{1,0:T(8,128)(2,1)S(1)}, u32[]{:S(2)}, u32[]{:S(2)}) collective-permute-start(bf16[160,256]{1,0:T(8,128)(2,1)S(1)} %get-tuple-element.44), channel_id=1, source_target_pairs={{0,193},{1,192},{64,0},{65,1},{128,64},{129,65},{192,128},{193,129... | collective-permute-start | bytes 245768 | tf_op jit(solution)/shard_map/ppermute | solution.py:220
  53.4 5.7 %collective-permute-start.9 = (bf16[160,256]{1,0:T(8,128)(2,1)S(1)}, bf16[160,256]{1,0:T(8,128)(2,1)S(1)}, u32[]{:S(2)}, u32[]{:S(2)}) collective-permute-start(bf16[160,256]{1,0:T(8,128)(2,1)S(1)} %get-tuple-element.45), channel_id=1, source_target_pairs={{0,64},{1,65},{64,128},{65,129},{128,192},{129,193},{192,1},{193,0... | collective-permute-start | bytes 245768 | tf_op jit(solution)/shard_map/ppermute | solution.py:220
  55.0 7.5 %collective-permute-start.10 = (bf16[160,256]{1,0:T(8,128)(2,1)S(1)}, bf16[160,256]{1,0:T(8,128)(2,1)S(1)}, u32[]{:S(2)}, u32[]{:S(2)}) collective-permute-start(bf16[160,256]{1,0:T(8,128)(2,1)S(1)} %get-tuple-element.46), channel_id=1, source_target_pairs={{0,65},{1,64},{64,129},{65,128},{128,193},{129,192},{192,0},{193,1... | collective-permute-start | bytes 245768 | tf_op jit(solution)/shard_map/ppermute | solution.py:220
  56.4 9.6 %collective-permute-start.11 = (bf16[160,256]{1,0:T(8,128)(2,1)S(1)}, bf16[160,256]{1,0:T(8,128)(2,1)S(1)}, u32[]{:S(2)}, u32[]{:S(2)}) collective-permute-start(bf16[160,256]{1,0:T(8,128)(2,1)S(1)} %get-tuple-element.47), channel_id=1, source_target_pairs={{0,192},{1,193},{64,1},{65,0},{128,65},{129,64},{192,129},{193,128... | collective-permute-start | bytes 245768 | tf_op jit(solution)/shard_map/ppermute | solution.py:220
  76.1 26.7 %all-to-all-start.1 = ((bf16[16,40,1280]{2,1,0:T(8,128)(2,1)}), bf16[16,40,1280]{2,1,0:T(8,128)(2,1)S(1)}, u32[]{:S(2)}, u32[]{:S(2)}) async-start(bf16[16,40,1280]{2,1,0:T(8,128)(2,1)} %shard_map.51), calls=%async_computation.1 | async-start | bytes 3276800 | tf_op jit(solution)/shard_map/all_to_all | solution.py:301
  82.4 9.3 %collective-permute-start.12 = (bf16[160,256]{1,0:T(8,128)(2,1)S(1)}, bf16[160,256]{1,0:T(8,128)(2,1)S(1)}, u32[]{:S(2)}, u32[]{:S(2)}) collective-permute-start(bf16[160,256]{1,0:T(8,128)(2,1)S(1)} %get-tuple-element.48), channel_id=1, source_target_pairs={{0,1},{1,0},{64,65},{65,64},{128,129},{129,128},{192,193},{193,192... | collective-permute-start | bytes 245768 | tf_op jit(solution)/shard_map/ppermute | solution.py:220
  84.3 8.0 %collective-permute-start.13 = (bf16[160,256]{1,0:T(8,128)(2,1)S(1)}, bf16[160,256]{1,0:T(8,128)(2,1)S(1)}, u32[]{:S(2)}, u32[]{:S(2)}) collective-permute-start(bf16[160,256]{1,0:T(8,128)(2,1)S(1)} %get-tuple-element.49), channel_id=1, source_target_pairs={{0,129},{1,128},{64,193},{65,192},{128,0},{129,1},{192,64},{193,65... | collective-permute-start | bytes 245768 | tf_op jit(solution)/shard_map/ppermute | solution.py:220
  86.0 7.3 %collective-permute-start.14 = (bf16[160,256]{1,0:T(8,128)(2,1)S(1)}, bf16[160,256]{1,0:T(8,128)(2,1)S(1)}, u32[]{:S(2)}, u32[]{:S(2)}) collective-permute-start(bf16[160,256]{1,0:T(8,128)(2,1)S(1)} %get-tuple-element.50), channel_id=1, source_target_pairs={{0,128},{1,129},{64,192},{65,193},{128,1},{129,0},{192,65},{193,64... | collective-permute-start | bytes 245768 | tf_op jit(solution)/shard_map/ppermute | solution.py:220
  93.4 2.2 %collective-permute-start.15 = (bf16[2,4,160,256]{3,2,1,0:T(8,128)(2,1)S(1)}, bf16[2,4,160,256]{3,2,1,0:T(8,128)(2,1)S(1)}, u32[]{:S(2)}, u32[]{:S(2)}) collective-permute-start(bf16[2,4,160,256]{3,2,1,0:T(8,128)(2,1)S(1)} %shard_map.52.v_ref), channel_id=1, source_target_pairs={{0,32},{32,0},{1,33},{33,1},{2,34},{34,2},{3,35},{35,3},{4,36},{36... | collective-permute-start | bytes 1966088 | tf_op jit(solution)/shard_map/ppermute | solution.py:225
  103.5 19.7 %copy-start.1 = (bf16[512,768]{1,0:T(8,128)(2,1)S(1)}, bf16[512,768]{1,0:T(8,128)(2,1)}, u32[]{:S(2)}) copy-start(bf16[512,768]{1,0:T(8,128)(2,1)} %w_ref.1) | copy-start | bytes 2359300
  103.6 11.3 %collective-permute-start.16 = (bf16[160,256]{1,0:T(8,128)(2,1)S(1)}, bf16[160,256]{1,0:T(8,128)(2,1)S(1)}, u32[]{:S(2)}, u32[]{:S(2)}) collective-permute-start(bf16[160,256]{1,0:T(8,128)(2,1)S(1)} %get-tuple-element.52), channel_id=1, source_target_pairs={{0,1},{1,0},{64,65},{65,64},{128,129},{129,128},{192,193},{193,192... | collective-permute-start | bytes 245768 | tf_op jit(solution)/shard_map/ppermute | solution.py:220
  105.6 12.0 %collective-permute-start.17 = (bf16[160,256]{1,0:T(8,128)(2,1)S(1)}, bf16[160,256]{1,0:T(8,128)(2,1)S(1)}, u32[]{:S(2)}, u32[]{:S(2)}) collective-permute-start(bf16[160,256]{1,0:T(8,128)(2,1)S(1)} %get-tuple-element.53), channel_id=1, source_target_pairs={{0,192},{1,193},{64,1},{65,0},{128,65},{129,64},{192,129},{193,128... | collective-permute-start | bytes 245768 | tf_op jit(solution)/shard_map/ppermute | solution.py:220
  108.4 9.7 %collective-permute-start.18 = (bf16[160,256]{1,0:T(8,128)(2,1)S(1)}, bf16[160,256]{1,0:T(8,128)(2,1)S(1)}, u32[]{:S(2)}, u32[]{:S(2)}) collective-permute-start(bf16[160,256]{1,0:T(8,128)(2,1)S(1)} %get-tuple-element.54), channel_id=1, source_target_pairs={{0,193},{1,192},{64,0},{65,1},{128,64},{129,65},{192,128},{193,129... | collective-permute-start | bytes 245768 | tf_op jit(solution)/shard_map/ppermute | solution.py:220
  111.4 9.3 %collective-permute-start.19 = (bf16[160,256]{1,0:T(8,128)(2,1)S(1)}, bf16[160,256]{1,0:T(8,128)(2,1)S(1)}, u32[]{:S(2)}, u32[]{:S(2)}) collective-permute-start(bf16[160,256]{1,0:T(8,128)(2,1)S(1)} %get-tuple-element.55), channel_id=1, source_target_pairs={{0,65},{1,64},{64,129},{65,128},{128,193},{129,192},{192,0},{193,1... | collective-permute-start | bytes 245768 | tf_op jit(solution)/shard_map/ppermute | solution.py:220
  112.0 8.7 %collective-permute-start.20 = (bf16[160,256]{1,0:T(8,128)(2,1)S(1)}, bf16[160,256]{1,0:T(8,128)(2,1)S(1)}, u32[]{:S(2)}, u32[]{:S(2)}) collective-permute-start(bf16[160,256]{1,0:T(8,128)(2,1)S(1)} %get-tuple-element.56), channel_id=1, source_target_pairs={{0,128},{1,129},{64,192},{65,193},{128,1},{129,0},{192,65},{193,64... | collective-permute-start | bytes 245768 | tf_op jit(solution)/shard_map/ppermute | solution.py:220
  114.9 8.1 %collective-permute-start.21 = (bf16[160,256]{1,0:T(8,128)(2,1)S(1)}, bf16[160,256]{1,0:T(8,128)(2,1)S(1)}, u32[]{:S(2)}, u32[]{:S(2)}) collective-permute-start(bf16[160,256]{1,0:T(8,128)(2,1)S(1)} %get-tuple-element.57), channel_id=1, source_target_pairs={{0,129},{1,128},{64,193},{65,192},{128,0},{129,1},{192,64},{193,65... | collective-permute-start | bytes 245768 | tf_op jit(solution)/shard_map/ppermute | solution.py:220
  117.6 5.7 %collective-permute-start.22 = (bf16[160,256]{1,0:T(8,128)(2,1)S(1)}, bf16[160,256]{1,0:T(8,128)(2,1)S(1)}, u32[]{:S(2)}, u32[]{:S(2)}) collective-permute-start(bf16[160,256]{1,0:T(8,128)(2,1)S(1)} %get-tuple-element.58), channel_id=1, source_target_pairs={{0,64},{1,65},{64,128},{65,129},{128,192},{129,193},{192,1},{193,0... | collective-permute-start | bytes 245768 | tf_op jit(solution)/shard_map/ppermute | solution.py:220

commit v10 on v9

--- a/solution.py
+++ b/solution.py
@@ -13,7 +13,7 @@
 Z, CORE, X, Y, W = 4, 2, 4, 4, 2
 RING = Z * W
 PLANE = X * Y
-STEPS = (0, 7, 1, 5, 3, 4, 6, 2)
+STEPS = (0, 2, 6, 3, 5, 4, 1, 7)
 BF = jnp.bfloat16
 F32 = jnp.float32
 VMEM = pl.BlockSpec(memory_space=pltpu.VMEM)
@@ -21,6 +21,7 @@
 ANY = pl.BlockSpec(memory_space=pl.ANY)
 SMEM = pl.BlockSpec(memory_space=pltpu.SMEM)
 CONTEXT_STEPS = (0, 4, 3, 7, 5, 2, 6, 1)
+FIRST_KEYS = 256
 MIB = 1024 * 1024
 
 
@@ -102,10 +103,6 @@
         outs[i][...] = mine[head_at(pos + s)]
 
 
-def cuts(rows, count):
-    return [pl.ds(i * (rows // count), rows // count) for i in range(count)]
-
-
 def put_by_sender(pos, parts, first, out):
     length = out.shape[2]
     for part, s in zip(parts, STEPS):
@@ -118,22 +115,24 @@
 
 
 def half_terms(q, keys, side, out_hbm, terms, sem):
-    length = keys.shape[2]
-    half = keys.shape[1] * length
-    columns = pl.ds(side * half, half)
+    half = keys.shape[1] * keys.shape[2]
     copies = []
-    for i, rows in enumerate(cuts(half, 2)):
+    for i, (first, count) in enumerate(((0, FIRST_KEYS), (FIRST_KEYS, half - FIRST_KEYS))):
         total = None
         for w in range(W):
             term = lax.dot_general(
-                q[w, i * Z // 2 : (i + 1) * Z // 2].reshape(half // 2, -1),
-                keys[w].reshape(half, -1),
+                q[w].reshape(half, -1),
+                keys[w].reshape(half, -1)[first : first + count],
                 (((1,), (1,)), ((), ())),
                 preferred_element_type=F32,
             )
             total = term if total is None else total + term
-        terms[rows] = total.astype(BF)
-        copies.append(pltpu.make_async_copy(terms.at[rows], out_hbm.at[rows, columns], sem.at[i]))
+        terms[:, first : first + count] = total.astype(BF)
+        copies.append(
+            pltpu.make_async_copy(
+                terms.at[:, pl.ds(first, count)], out_hbm.at[:, pl.ds(side * half + first, count)], sem.at[i]
+            )
+        )
         copies[i].start()
     for copy in copies:
         copy.wait()

time: 126 us -> 127 us (level)
  starting transfers between devices: 55.6 us -> 63.3 us
  waiting for transfers between devices: 56.4 us -> 49.8 us
    ppermute x21, starting transfers between devices: 41.7 us -> 49.4 us  [along_ring(): got.append(lax.ppermute(part, ('z', 'w'), pairs) if s else part)]
    ppermute x21, waiting for transfers between devices: 38.1 us -> 30.7 us  [along_ring(): got.append(lax.ppermute(part, ('z', 'w'), pairs) if s else part)]
  transfers between devices with their start and end apart: 25 -> 25, of which waited for: 18 -> 16; matrix products, arithmetic and copies ran while one was open for 0% -> 0% of each run, Pallas kernels for 2% -> 2%
where the time goes in v10:
time: 127 us; the launch traced here: 126 us
  starting transfers between devices  63.3 us (50%)
  waiting for transfers between devices  49.8 us (39%)
  Pallas kernels  12.1 us (10%)
    ppermute x21, starting transfers between devices, along_ring(): got.append(lax.ppermute(part, ('z', 'w'), pairs) if s else part)  49.4 us
    ppermute x21, waiting for transfers between devices, along_ring(): got.append(lax.ppermute(part, ('z', 'w'), pairs) if s else part)  30.7 us
    pallas_call x11, Pallas kernels, call(): pl.pallas_call(kernel, out_shape=out_shape, in_specs=specs, out_specs=out...  12.1 us
    all_to_all x1, waiting for transfers between devices, shards(): lax.all_to_all(probs, ('x', 'y'), 0, 0, tiled=True).reshape(half, full)  8.35 us
    all_to_all x1, waiting for transfers between devices, shards(): terms = lax.all_to_all(term.reshape(chunk), ('x', 'y'), 0, 0, tiled=True)  8.11 us
    all_to_all x1, starting transfers between devices, shards(): terms = lax.all_to_all(term.reshape(chunk), ('x', 'y'), 0, 0, tiled=True)  7.43 us
    all_to_all x1, starting transfers between devices, shards(): lax.all_to_all(probs, ('x', 'y'), 0, 0, tiled=True).reshape(half, full)  6.25 us
    ppermute x2, waiting for transfers between devices, other_core(): return lax.ppermute(a, 'c', [(0, 1), (1, 0)])  2.64 us
  transfers between devices with their start and end apart: 25, of which 16 were waited for; matrix products, arithmetic and copies ran while one was open for 0% of the time, Pallas kernels for 2%

profile of v10, /device:TPU:6, one launch (start us, length us, event | category | flops | bytes accessed | tf_op | source)
XLA Modules:
  0.0 126.2 jit_solution(2075766751832486180)
XLA Ops:
  0.0 0.7 copy-done.2
  0.7 3.4 %shard_map.46 = (bf16[320,256]{1,0:T(8,128)(2,1)S(1)}, bf16[320,256]{1,0:T(8,128)(2,1)S(1)}, bf16[320,256]{1,0:T(8,128)(2,1)S(1)}, bf16[320,256]{1,0:T(8,128)(2,...) custom-call(s32[1]{0:T(128)} %bitcast.pos_ref, ...), custom_call_target="tpu_custom_call" | custom-call | flops 1006632960 | bytes 6690824 | tf_op jit(solution)/shard_map/pallas_call | solution.py:203
  4.1 3.3 %collective-permute-start = (bf16[320,256]{1,0:T(8,128)(2,1)S(1)}, bf16[320,256]{1,0:T(8,128)(2,1)S(1)}, u32[]{:S(2)}, u32[]{:S(2)}) collective-permute-start(bf16[320,256]{1,0:T(8,128)(2,1)S(1)} %get-tuple-element.33), channel_id=1, source_target_pairs={{0,128},{1,129},{64,192},{65,193},{128,1},{129,0},{192,65},{193,64... | collective-permute-start | bytes 491528 | tf_op jit(solution)/shard_map/ppermute | solution.py:219
  7.5 3.1 %collective-permute-start.1 = (bf16[320,256]{1,0:T(8,128)(2,1)S(1)}, bf16[320,256]{1,0:T(8,128)(2,1)S(1)}, u32[]{:S(2)}, u32[]{:S(2)}) collective-permute-start(bf16[320,256]{1,0:T(8,128)(2,1)S(1)} %get-tuple-element.34), channel_id=1, source_target_pairs={{0,129},{1,128},{64,193},{65,192},{128,0},{129,1},{192,64},{193,65... | collective-permute-start | bytes 491528 | tf_op jit(solution)/shard_map/ppermute | solution.py:219
  10.6 1.8 %collective-permute-start.2 = (bf16[320,256]{1,0:T(8,128)(2,1)S(1)}, bf16[320,256]{1,0:T(8,128)(2,1)S(1)}, u32[]{:S(2)}, u32[]{:S(2)}) collective-permute-start(bf16[320,256]{1,0:T(8,128)(2,1)S(1)} %get-tuple-element.35), channel_id=1, source_target_pairs={{0,192},{1,193},{64,1},{65,0},{128,65},{129,64},{192,129},{193,128... | collective-permute-start | bytes 491528 | tf_op jit(solution)/shard_map/ppermute | solution.py:219
  12.4 3.2 %collective-permute-start.3 = (bf16[320,256]{1,0:T(8,128)(2,1)S(1)}, bf16[320,256]{1,0:T(8,128)(2,1)S(1)}, u32[]{:S(2)}, u32[]{:S(2)}) collective-permute-start(bf16[320,256]{1,0:T(8,128)(2,1)S(1)} %get-tuple-element.36), channel_id=1, source_target_pairs={{0,65},{1,64},{64,129},{65,128},{128,193},{129,192},{192,0},{193,1... | collective-permute-start | bytes 491528 | tf_op jit(solution)/shard_map/ppermute | solution.py:219
  15.6 4.9 %collective-permute-start.4 = (bf16[320,256]{1,0:T(8,128)(2,1)S(1)}, bf16[320,256]{1,0:T(8,128)(2,1)S(1)}, u32[]{:S(2)}, u32[]{:S(2)}) collective-permute-start(bf16[320,256]{1,0:T(8,128)(2,1)S(1)} %get-tuple-element.37), channel_id=1, source_target_pairs={{0,1},{1,0},{64,65},{65,64},{128,129},{129,128},{192,193},{193,192... | collective-permute-start | bytes 491528 | tf_op jit(solution)/shard_map/ppermute | solution.py:219
  20.6 0.0 collective-permute-done.refs_1_
  20.6 1.0 collective-permute-start.5
  21.6 2.3 %collective-permute-done.1.refs_2_ = bf16[320,256]{1,0:T(8,128)(2,1)S(1)} collective-permute-done((bf16[320,256]{1,0:T(8,128)(2,1)S(1)}, bf16[320,256]{1,0:T(8,128)(2,1)S(1)}, u32[]{:S(2)}, u32[]{:S(2)}) %collective-permute-start.1) | collective-permute-done | bytes 163872 | tf_op jit(solution)/shard_map/ppermute | solution.py:219
  23.9 0.0 collective-permute-start.6
  23.9 0.0 copy-done
  23.9 0.9 shard_map.47
  24.8 9.2 %collective-permute-done.2.refs_3_ = bf16[320,256]{1,0:T(8,128)(2,1)S(1)} collective-permute-done((bf16[320,256]{1,0:T(8,128)(2,1)S(1)}, bf16[320,256]{1,0:T(8,128)(2,1)S(1)}, u32[]{:S(2)}, u32[]{:S(2)}) %collective-permute-start.2) | collective-permute-done | bytes 163872 | tf_op jit(solution)/shard_map/ppermute | solution.py:219
  34.0 0.0 collective-permute-done.3.refs_4_
  34.0 0.9 collective-permute-done.4.refs_5_
  35.0 3.9 %collective-permute-done.5.refs_6_ = bf16[320,256]{1,0:T(8,128)(2,1)S(1)} collective-permute-done((bf16[320,256]{1,0:T(8,128)(2,1)S(1)}, bf16[320,256]{1,0:T(8,128)(2,1)S(1)}, u32[]{:S(2)}, u32[]{:S(2)}) %collective-permute-start.5) | collective-permute-done | bytes 163872 | tf_op jit(solution)/shard_map/ppermute | solution.py:219
  38.8 1.3 %collective-permute-done.6.refs_7_ = bf16[320,256]{1,0:T(8,128)(2,1)S(1)} collective-permute-done((bf16[320,256]{1,0:T(8,128)(2,1)S(1)}, bf16[320,256]{1,0:T(8,128)(2,1)S(1)}, u32[]{:S(2)}, u32[]{:S(2)}) %collective-permute-start.6) | collective-permute-done | bytes 163872 | tf_op jit(solution)/shard_map/ppermute | solution.py:219
  40.1 0.1 shard_map.48.refs_8_
  40.2 0.1 collective-permute-start.7
  40.3 1.5 %shard_map.49 = (bf16[640,1280]{1,0:T(8,128)(2,1)}, bf16[2,4,160,256]{3,2,1,0:T(8,128)(2,1)S(1)}) custom-call(s32[1]{0:T(128)} %bitcast.pos_ref, bf16[320,256]{1,0:T(8,128)(2,1)S(1)} %get-tuple-element.32.refs_0_, bf16[320,256]{1,0:T(8,128)(2,1)S(1)} %collective-permute-done.refs_1_, bf16[320,256]{1,0:T(8,128)(2,1)S(1)} %collective-permute-done.1.refs_2_, ...), custom_call_target="tpu_custom_call" | custom-call | flops 419430400 | bytes 3932168 | tf_op jit(solution)/shard_map/pallas_call | solution.py:203
  41.8 0.6 collective-permute-done.7.k_far
  42.4 1.5 %shard_map.50 = bf16[640,1280]{1,0:T(8,128)(2,1)} custom-call(bf16[640,1280]{1,0:T(8,128)(2,1)} %get-tuple-element.42._, bf16[2,4,160,256]{3,2,1,0:T(8,128)(2,1)S(1)} %get-tuple-element.43.q, bf16[2,4,160,256]{3,2,1,0:T(8,128)(2,1)S(1)} %collective-permute-done.7.k_far), custom_call_target="tpu_custom_call", output_to_operand_aliasing={{}: (0, {})} | custom-call | flops 419430400 | bytes 5898240 | tf_op jit(solution)/shard_map/pallas_call | solution.py:203
  43.9 7.4 %all-to-all-start = ((bf16[16,40,1280]{2,1,0:T(8,128)(2,1)}), bf16[16,40,1280]{2,1,0:T(8,128)(2,1)S(1)}, u32[]{:S(2)}, u32[]{:S(2)}) async-start(bf16[16,40,1280]{2,1,0:T(8,128)(2,1)} %bitcast.2), calls=%async_computation | async-start | bytes 3276800 | tf_op jit(solution)/shard_map/all_to_all | solution.py:290
  51.3 1.4 %collective-permute-start.8 = (bf16[160,256]{1,0:T(8,128)(2,1)S(1)}, bf16[160,256]{1,0:T(8,128)(2,1)S(1)}, u32[]{:S(2)}, u32[]{:S(2)}) collective-permute-start(bf16[160,256]{1,0:T(8,128)(2,1)S(1)} %get-tuple-element.44), channel_id=1, source_target_pairs={{0,128},{1,129},{64,192},{65,193},{128,1},{129,0},{192,65},{193,64... | collective-permute-start | bytes 245768 | tf_op jit(solution)/shard_map/ppermute | solution.py:219
  52.7 2.7 %collective-permute-start.9 = (bf16[160,256]{1,0:T(8,128)(2,1)S(1)}, bf16[160,256]{1,0:T(8,128)(2,1)S(1)}, u32[]{:S(2)}, u32[]{:S(2)}) collective-permute-start(bf16[160,256]{1,0:T(8,128)(2,1)S(1)} %get-tuple-element.45), channel_id=1, source_target_pairs={{0,129},{1,128},{64,193},{65,192},{128,0},{129,1},{192,64},{193,65... | collective-permute-start | bytes 245768 | tf_op jit(solution)/shard_map/ppermute | solution.py:219
  55.4 3.0 %collective-permute-start.10 = (bf16[160,256]{1,0:T(8,128)(2,1)S(1)}, bf16[160,256]{1,0:T(8,128)(2,1)S(1)}, u32[]{:S(2)}, u32[]{:S(2)}) collective-permute-start(bf16[160,256]{1,0:T(8,128)(2,1)S(1)} %get-tuple-element.46), channel_id=1, source_target_pairs={{0,192},{1,193},{64,1},{65,0},{128,65},{129,64},{192,129},{193,128... | collective-permute-start | bytes 245768 | tf_op jit(solution)/shard_map/ppermute | solution.py:219
  58.4 2.0 %collective-permute-start.11 = (bf16[160,256]{1,0:T(8,128)(2,1)S(1)}, bf16[160,256]{1,0:T(8,128)(2,1)S(1)}, u32[]{:S(2)}, u32[]{:S(2)}) collective-permute-start(bf16[160,256]{1,0:T(8,128)(2,1)S(1)} %get-tuple-element.47), channel_id=1, source_target_pairs={{0,65},{1,64},{64,129},{65,128},{128,193},{129,192},{192,0},{193,1... | collective-permute-start | bytes 245768 | tf_op jit(solution)/shard_map/ppermute | solution.py:219
  60.5 0.0 collective-permute-done.8.refs_0_.refs_1_
  60.5 0.0 collective-permute-done.9.refs_1_.refs_2_
  60.5 4.1 %collective-permute-done.10.refs_2_.refs_3_ = bf16[160,256]{1,0:T(8,128)(2,1)S(1)} collective-permute-done((bf16[160,256]{1,0:T(8,128)(2,1)S(1)}, bf16[160,256]{1,0:T(8,128)(2,1)S(1)}, u32[]{:S(2)}, u32[]{:S(2)}) %collective-permute-start.10) | collective-permute-done | bytes 81952 | tf_op jit(solution)/shard_map/ppermute | solution.py:219
  64.6 1.2 collective-permute-done.11.refs_3_.refs_4_
  65.8 8.1 %all-to-all-done.x_ref = bf16[16,40,1280]{2,1,0:T(8,128)(2,1)S(1)} async-done(((bf16[16,40,1280]{2,1,0:T(8,128)(2,1)}), bf16[16,40,1280]{2,1,0:T(8,128)(2,1)S(1)}, u32[]{:S(2)}, u32[]{:S(2)}) %all-to-all-start) | async-done | bytes 1638432 | tf_op jit(solution)/shard_map/all_to_all | solution.py:290
  73.9 1.6 %shard_map.51 = bf16[16,40,1280]{2,1,0:T(8,128)(2,1)} custom-call(bf16[16,40,1280]{2,1,0:T(8,128)(2,1)S(1)} %all-to-all-done.x_ref, bf16[160,256]{1,0:T(8,128)(2,1)S(1)} %collective-permute-done.8.refs_0_.refs_1_, bf16[160,256]{1,0:T(8,128)(2,1)S(1)} %collective-permute-done.9.refs_1_.refs_2_, bf16[160,256]{1,0:T(8,128)(2,1)S(1)} %collective-permute-done.10.refs_2_.refs_3_, ...), custom_call_target="tpu_custom_call" | custom-call | bytes 3932160 | tf_op jit(solution)/shard_map/pallas_call | solution.py:203
  75.5 6.2 %all-to-all-start.1 = ((bf16[16,40,1280]{2,1,0:T(8,128)(2,1)}), bf16[16,40,1280]{2,1,0:T(8,128)(2,1)S(1)}, u32[]{:S(2)}, u32[]{:S(2)}) async-start(bf16[16,40,1280]{2,1,0:T(8,128)(2,1)} %shard_map.51), calls=%async_computation.1 | async-start | bytes 3276800 | tf_op jit(solution)/shard_map/all_to_all | solution.py:300
  81.8 4.1 %collective-permute-start.12 = (bf16[160,256]{1,0:T(8,128)(2,1)S(1)}, bf16[160,256]{1,0:T(8,128)(2,1)S(1)}, u32[]{:S(2)}, u32[]{:S(2)}) collective-permute-start(bf16[160,256]{1,0:T(8,128)(2,1)S(1)} %get-tuple-element.48), channel_id=1, source_target_pairs={{0,1},{1,0},{64,65},{65,64},{128,129},{129,128},{192,193},{193,192... | collective-permute-start | bytes 245768 | tf_op jit(solution)/shard_map/ppermute | solution.py:219
  85.9 0.4 collective-permute-start.13
  86.3 2.9 %collective-permute-start.14 = (bf16[160,256]{1,0:T(8,128)(2,1)S(1)}, bf16[160,256]{1,0:T(8,128)(2,1)S(1)}, u32[]{:S(2)}, u32[]{:S(2)}) collective-permute-start(bf16[160,256]{1,0:T(8,128)(2,1)S(1)} %get-tuple-element.50), channel_id=1, source_target_pairs={{0,193},{1,192},{64,0},{65,1},{128,64},{129,65},{192,128},{193,129... | collective-permute-start | bytes 245768 | tf_op jit(solution)/shard_map/ppermute | solution.py:219
  89.1 1.1 collective-permute-done.12.refs_5_
  90.2 1.4 %collective-permute-done.13.refs_6_ = bf16[160,256]{1,0:T(8,128)(2,1)S(1)} collective-permute-done((bf16[160,256]{1,0:T(8,128)(2,1)S(1)}, bf16[160,256]{1,0:T(8,128)(2,1)S(1)}, u32[]{:S(2)}, u32[]{:S(2)}) %collective-permute-start.13) | collective-permute-done | bytes 81952 | tf_op jit(solution)/shard_map/ppermute | solution.py:219
  91.7 0.0 collective-permute-done.14.refs_7_
  91.7 0.1 shard_map.52.v_ref
  91.7 0.1 collective-permute-start.15
  91.8 2.1 %collective-permute-done.15._.v_far = bf16[2,4,160,256]{3,2,1,0:T(8,128)(2,1)S(1)} collective-permute-done((bf16[2,4,160,256]{3,2,1,0:T(8,128)(2,1)S(1)}, bf16[2,4,160,256]{3,2,1,0:T(8,128)(2,1)S(1)}, u32[]{:S(2)}, u32[]{:S(2)}) %collective-permute-start.15) | collective-permute-done | bytes 655392 | tf_op jit(solution)/shard_map/ppermute | solution.py:224
  93.9 8.4 %all-to-all-done.1 = bf16[16,40,1280]{2,1,0:T(8,128)(2,1)S(1)} async-done(((bf16[16,40,1280]{2,1,0:T(8,128)(2,1)}), bf16[16,40,1280]{2,1,0:T(8,128)(2,1)S(1)}, u32[]{:S(2)}, u32[]{:S(2)}) %all-to-all-start.1) | async-done | bytes 1638432 | tf_op jit(solution)/shard_map/all_to_all | solution.py:300
  102.3 0.7 shard_map.54
  103.0 0.0 copy-start.1
  103.0 4.2 %collective-permute-start.16 = (bf16[160,256]{1,0:T(8,128)(2,1)S(1)}, bf16[160,256]{1,0:T(8,128)(2,1)S(1)}, u32[]{:S(2)}, u32[]{:S(2)}) collective-permute-start(bf16[160,256]{1,0:T(8,128)(2,1)S(1)} %get-tuple-element.52), channel_id=1, source_target_pairs={{0,1},{1,0},{64,65},{65,64},{128,129},{129,128},{192,193},{193,192... | collective-permute-start | bytes 245768 | tf_op jit(solution)/shard_map/ppermute | solution.py:219
  107.2 1.4 %collective-permute-start.17 = (bf16[160,256]{1,0:T(8,128)(2,1)S(1)}, bf16[160,256]{1,0:T(8,128)(2,1)S(1)}, u32[]{:S(2)}, u32[]{:S(2)}) collective-permute-start(bf16[160,256]{1,0:T(8,128)(2,1)S(1)} %get-tuple-element.53), channel_id=1, source_target_pairs={{0,192},{1,193},{64,1},{65,0},{128,65},{129,64},{192,129},{193,128... | collective-permute-start | bytes 245768 | tf_op jit(solution)/shard_map/ppermute | solution.py:219
  108.6 2.2 %collective-permute-start.18 = (bf16[160,256]{1,0:T(8,128)(2,1)S(1)}, bf16[160,256]{1,0:T(8,128)(2,1)S(1)}, u32[]{:S(2)}, u32[]{:S(2)}) collective-permute-start(bf16[160,256]{1,0:T(8,128)(2,1)S(1)} %get-tuple-element.54), channel_id=1, source_target_pairs={{0,193},{1,192},{64,0},{65,1},{128,64},{129,65},{192,128},{193,129... | collective-permute-start | bytes 245768 | tf_op jit(solution)/shard_map/ppermute | solution.py:219
  110.7 0.7 shard_map.55
  111.4 3.1 %collective-permute-start.19 = (bf16[160,256]{1,0:T(8,128)(2,1)S(1)}, bf16[160,256]{1,0:T(8,128)(2,1)S(1)}, u32[]{:S(2)}, u32[]{:S(2)}) collective-permute-start(bf16[160,256]{1,0:T(8,128)(2,1)S(1)} %get-tuple-element.55), channel_id=1, source_target_pairs={{0,65},{1,64},{64,129},{65,128},{128,193},{129,192},{192,0},{193,1... | collective-permute-start | bytes 245768 | tf_op jit(solution)/shard_map/ppermute | solution.py:219
  114.5 0.3 collective-permute-start.20
  114.8 0.0 collective-permute-done.16.refs_1_
  114.8 3.9 %collective-permute-start.21 = (bf16[160,256]{1,0:T(8,128)(2,1)S(1)}, bf16[160,256]{1,0:T(8,128)(2,1)S(1)}, u32[]{:S(2)}, u32[]{:S(2)}) collective-permute-start(bf16[160,256]{1,0:T(8,128)(2,1)S(1)} %get-tuple-element.57), channel_id=1, source_target_pairs={{0,129},{1,128},{64,193},{65,192},{128,0},{129,1},{192,64},{193,65... | collective-permute-start | bytes 245768 | tf_op jit(solution)/shard_map/ppermute | solution.py:219
  118.7 0.0 collective-permute-done.17.refs_2_
  118.7 0.5 collective-permute-start.22
  119.1 0.0 collective-permute-done.18.refs_3_
  119.2 0.0 collective-permute-done.19.refs_4_
  119.2 2.3 %collective-permute-done.20.refs_5_ = bf16[160,256]{1,0:T(8,128)(2,1)S(1)} collective-permute-done((bf16[160,256]{1,0:T(8,128)(2,1)S(1)}, bf16[160,256]{1,0:T(8,128)(2,1)S(1)}, u32[]{:S(2)}, u32[]{:S(2)}) %collective-permute-start.20) | collective-permute-done | bytes 81952 | tf_op jit(solution)/shard_map/ppermute | solution.py:219
  121.5 0.3 collective-permute-done.21.refs_6_
  121.8 2.5 %collective-permute-done.22.refs_7_ = bf16[160,256]{1,0:T(8,128)(2,1)S(1)} collective-permute-done((bf16[160,256]{1,0:T(8,128)(2,1)S(1)}, bf16[160,256]{1,0:T(8,128)(2,1)S(1)}, u32[]{:S(2)}, u32[]{:S(2)}) %collective-permute-start.22) | collective-permute-done | bytes 81952 | tf_op jit(solution)/shard_map/ppermute | solution.py:219
  124.3 0.0 copy-done.1
  124.3 1.7 %shard_map.56 = f32[4,160,768]{2,1,0:T(8,128)} custom-call(s32[1]{0:T(128)} %bitcast.pos_ref, bf16[512,768]{1,0:T(8,128)(2,1)S(1)} %copy-done.1, bf16[160,256]{1,0:T(8,128)(2,1)S(1)} %get-tuple-element.51.refs_0_, bf16[160,256]{1,0:T(8,128)(2,1)S(1)} %collective-permute-done.16.refs_1_, bf16[160,256]{1,0:T(8,128)(2,1)S(1)} %collective-permute-done.17.refs_2_, ...), custom_call_target="tpu_custom_call" | custom-call | flops 503316480 | bytes 2883592 | tf_op jit(solution)/shard_map/pallas_call | solution.py:203
  (3 shorter events, 0.0 us)
Async XLA Ops:
  0.0 0.7 copy-start.2
  0.7 23.3 %copy-start = (bf16[768,3,512]{2,0,1:T(8,128)(2,1)S(1)}, bf16[768,3,512]{2,0,1:T(8,128)(2,1)}, u32[]{:S(2)}) copy-start(bf16[768,3,512]{2,0,1:T(8,128)(2,1)} %param.6) | copy-start | bytes 7077892
  4.1 16.4 %collective-permute-start = (bf16[320,256]{1,0:T(8,128)(2,1)S(1)}, bf16[320,256]{1,0:T(8,128)(2,1)S(1)}, u32[]{:S(2)}, u32[]{:S(2)}) collective-permute-start(bf16[320,256]{1,0:T(8,128)(2,1)S(1)} %get-tuple-element.33), channel_id=1, source_target_pairs={{0,128},{1,129},{64,192},{65,193},{128,1},{129,0},{192,65},{193,64... | collective-permute-start | bytes 491528 | tf_op jit(solution)/shard_map/ppermute | solution.py:219
  7.5 16.5 %collective-permute-start.1 = (bf16[320,256]{1,0:T(8,128)(2,1)S(1)}, bf16[320,256]{1,0:T(8,128)(2,1)S(1)}, u32[]{:S(2)}, u32[]{:S(2)}) collective-permute-start(bf16[320,256]{1,0:T(8,128)(2,1)S(1)} %get-tuple-element.34), channel_id=1, source_target_pairs={{0,129},{1,128},{64,193},{65,192},{128,0},{129,1},{192,64},{193,65... | collective-permute-start | bytes 491528 | tf_op jit(solution)/shard_map/ppermute | solution.py:219
  10.6 23.4 %collective-permute-start.2 = (bf16[320,256]{1,0:T(8,128)(2,1)S(1)}, bf16[320,256]{1,0:T(8,128)(2,1)S(1)}, u32[]{:S(2)}, u32[]{:S(2)}) collective-permute-start(bf16[320,256]{1,0:T(8,128)(2,1)S(1)} %get-tuple-element.35), channel_id=1, source_target_pairs={{0,192},{1,193},{64,1},{65,0},{128,65},{129,64},{192,129},{193,128... | collective-permute-start | bytes 491528 | tf_op jit(solution)/shard_map/ppermute | solution.py:219
  12.4 21.6 %collective-permute-start.3 = (bf16[320,256]{1,0:T(8,128)(2,1)S(1)}, bf16[320,256]{1,0:T(8,128)(2,1)S(1)}, u32[]{:S(2)}, u32[]{:S(2)}) collective-permute-start(bf16[320,256]{1,0:T(8,128)(2,1)S(1)} %get-tuple-element.36), channel_id=1, source_target_pairs={{0,65},{1,64},{64,129},{65,128},{128,193},{129,192},{192,0},{193,1... | collective-permute-start | bytes 491528 | tf_op jit(solution)/shard_map/ppermute | solution.py:219
  15.6 19.3 %collective-permute-start.4 = (bf16[320,256]{1,0:T(8,128)(2,1)S(1)}, bf16[320,256]{1,0:T(8,128)(2,1)S(1)}, u32[]{:S(2)}, u32[]{:S(2)}) collective-permute-start(bf16[320,256]{1,0:T(8,128)(2,1)S(1)} %get-tuple-element.37), channel_id=1, source_target_pairs={{0,1},{1,0},{64,65},{65,64},{128,129},{129,128},{192,193},{193,192... | collective-permute-start | bytes 491528 | tf_op jit(solution)/shard_map/ppermute | solution.py:219
  20.6 18.3 %collective-permute-start.5 = (bf16[320,256]{1,0:T(8,128)(2,1)S(1)}, bf16[320,256]{1,0:T(8,128)(2,1)S(1)}, u32[]{:S(2)}, u32[]{:S(2)}) collective-permute-start(bf16[320,256]{1,0:T(8,128)(2,1)S(1)} %get-tuple-element.38), channel_id=1, source_target_pairs={{0,64},{1,65},{64,128},{65,129},{128,192},{129,193},{192,1},{193,0... | collective-permute-start | bytes 491528 | tf_op jit(solution)/shard_map/ppermute | solution.py:219
  23.9 16.2 %collective-permute-start.6 = (bf16[320,256]{1,0:T(8,128)(2,1)S(1)}, bf16[320,256]{1,0:T(8,128)(2,1)S(1)}, u32[]{:S(2)}, u32[]{:S(2)}) collective-permute-start(bf16[320,256]{1,0:T(8,128)(2,1)S(1)} %get-tuple-element.39), channel_id=1, source_target_pairs={{0,193},{1,192},{64,0},{65,1},{128,64},{129,65},{192,128},{193,129... | collective-permute-start | bytes 491528 | tf_op jit(solution)/shard_map/ppermute | solution.py:219
  40.2 2.2 %collective-permute-start.7 = (bf16[2,4,160,256]{3,2,1,0:T(8,128)(2,1)S(1)}, bf16[2,4,160,256]{3,2,1,0:T(8,128)(2,1)S(1)}, u32[]{:S(2)}, u32[]{:S(2)}) collective-permute-start(bf16[2,4,160,256]{3,2,1,0:T(8,128)(2,1)S(1)} %shard_map.48.refs_8_), channel_id=1, source_target_pairs={{0,32},{32,0},{1,33},{33,1},{2,34},{34,2},{3,35},{35,3},{4,36},{36... | collective-permute-start | bytes 1966088 | tf_op jit(solution)/shard_map/ppermute | solution.py:224
  43.9 30.0 %all-to-all-start = ((bf16[16,40,1280]{2,1,0:T(8,128)(2,1)}), bf16[16,40,1280]{2,1,0:T(8,128)(2,1)S(1)}, u32[]{:S(2)}, u32[]{:S(2)}) async-start(bf16[16,40,1280]{2,1,0:T(8,128)(2,1)} %bitcast.2), calls=%async_computation | async-start | bytes 3276800 | tf_op jit(solution)/shard_map/all_to_all | solution.py:290
  51.3 9.2 %collective-permute-start.8 = (bf16[160,256]{1,0:T(8,128)(2,1)S(1)}, bf16[160,256]{1,0:T(8,128)(2,1)S(1)}, u32[]{:S(2)}, u32[]{:S(2)}) collective-permute-start(bf16[160,256]{1,0:T(8,128)(2,1)S(1)} %get-tuple-element.44), channel_id=1, source_target_pairs={{0,128},{1,129},{64,192},{65,193},{128,1},{129,0},{192,65},{193,64... | collective-permute-start | bytes 245768 | tf_op jit(solution)/shard_map/ppermute | solution.py:219
  52.7 7.8 %collective-permute-start.9 = (bf16[160,256]{1,0:T(8,128)(2,1)S(1)}, bf16[160,256]{1,0:T(8,128)(2,1)S(1)}, u32[]{:S(2)}, u32[]{:S(2)}) collective-permute-start(bf16[160,256]{1,0:T(8,128)(2,1)S(1)} %get-tuple-element.45), channel_id=1, source_target_pairs={{0,129},{1,128},{64,193},{65,192},{128,0},{129,1},{192,64},{193,65... | collective-permute-start | bytes 245768 | tf_op jit(solution)/shard_map/ppermute | solution.py:219
  55.4 9.1 %collective-permute-start.10 = (bf16[160,256]{1,0:T(8,128)(2,1)S(1)}, bf16[160,256]{1,0:T(8,128)(2,1)S(1)}, u32[]{:S(2)}, u32[]{:S(2)}) collective-permute-start(bf16[160,256]{1,0:T(8,128)(2,1)S(1)} %get-tuple-element.46), channel_id=1, source_target_pairs={{0,192},{1,193},{64,1},{65,0},{128,65},{129,64},{192,129},{193,128... | collective-permute-start | bytes 245768 | tf_op jit(solution)/shard_map/ppermute | solution.py:219
  58.4 7.4 %collective-permute-start.11 = (bf16[160,256]{1,0:T(8,128)(2,1)S(1)}, bf16[160,256]{1,0:T(8,128)(2,1)S(1)}, u32[]{:S(2)}, u32[]{:S(2)}) collective-permute-start(bf16[160,256]{1,0:T(8,128)(2,1)S(1)} %get-tuple-element.47), channel_id=1, source_target_pairs={{0,65},{1,64},{64,129},{65,128},{128,193},{129,192},{192,0},{193,1... | collective-permute-start | bytes 245768 | tf_op jit(solution)/shard_map/ppermute | solution.py:219
  75.5 26.7 %all-to-all-start.1 = ((bf16[16,40,1280]{2,1,0:T(8,128)(2,1)}), bf16[16,40,1280]{2,1,0:T(8,128)(2,1)S(1)}, u32[]{:S(2)}, u32[]{:S(2)}) async-start(bf16[16,40,1280]{2,1,0:T(8,128)(2,1)} %shard_map.51), calls=%async_computation.1 | async-start | bytes 3276800 | tf_op jit(solution)/shard_map/all_to_all | solution.py:300
  81.8 8.4 %collective-permute-start.12 = (bf16[160,256]{1,0:T(8,128)(2,1)S(1)}, bf16[160,256]{1,0:T(8,128)(2,1)S(1)}, u32[]{:S(2)}, u32[]{:S(2)}) collective-permute-start(bf16[160,256]{1,0:T(8,128)(2,1)S(1)} %get-tuple-element.48), channel_id=1, source_target_pairs={{0,1},{1,0},{64,65},{65,64},{128,129},{129,128},{192,193},{193,192... | collective-permute-start | bytes 245768 | tf_op jit(solution)/shard_map/ppermute | solution.py:219
  85.9 5.8 %collective-permute-start.13 = (bf16[160,256]{1,0:T(8,128)(2,1)S(1)}, bf16[160,256]{1,0:T(8,128)(2,1)S(1)}, u32[]{:S(2)}, u32[]{:S(2)}) collective-permute-start(bf16[160,256]{1,0:T(8,128)(2,1)S(1)} %get-tuple-element.49), channel_id=1, source_target_pairs={{0,64},{1,65},{64,128},{65,129},{128,192},{129,193},{192,1},{193,0... | collective-permute-start | bytes 245768 | tf_op jit(solution)/shard_map/ppermute | solution.py:219
  86.3 5.4 %collective-permute-start.14 = (bf16[160,256]{1,0:T(8,128)(2,1)S(1)}, bf16[160,256]{1,0:T(8,128)(2,1)S(1)}, u32[]{:S(2)}, u32[]{:S(2)}) collective-permute-start(bf16[160,256]{1,0:T(8,128)(2,1)S(1)} %get-tuple-element.50), channel_id=1, source_target_pairs={{0,193},{1,192},{64,0},{65,1},{128,64},{129,65},{192,128},{193,129... | collective-permute-start | bytes 245768 | tf_op jit(solution)/shard_map/ppermute | solution.py:219
  91.7 2.2 %collective-permute-start.15 = (bf16[2,4,160,256]{3,2,1,0:T(8,128)(2,1)S(1)}, bf16[2,4,160,256]{3,2,1,0:T(8,128)(2,1)S(1)}, u32[]{:S(2)}, u32[]{:S(2)}) collective-permute-start(bf16[2,4,160,256]{3,2,1,0:T(8,128)(2,1)S(1)} %shard_map.52.v_ref), channel_id=1, source_target_pairs={{0,32},{32,0},{1,33},{33,1},{2,34},{34,2},{3,35},{35,3},{4,36},{36... | collective-permute-start | bytes 1966088 | tf_op jit(solution)/shard_map/ppermute | solution.py:224
  103.0 21.4 %copy-start.1 = (bf16[512,768]{1,0:T(8,128)(2,1)S(1)}, bf16[512,768]{1,0:T(8,128)(2,1)}, u32[]{:S(2)}) copy-start(bf16[512,768]{1,0:T(8,128)(2,1)} %w_ref.1) | copy-start | bytes 2359300
  103.0 11.8 %collective-permute-start.16 = (bf16[160,256]{1,0:T(8,128)(2,1)S(1)}, bf16[160,256]{1,0:T(8,128)(2,1)S(1)}, u32[]{:S(2)}, u32[]{:S(2)}) collective-permute-start(bf16[160,256]{1,0:T(8,128)(2,1)S(1)} %get-tuple-element.52), channel_id=1, source_target_pairs={{0,1},{1,0},{64,65},{65,64},{128,129},{129,128},{192,193},{193,192... | collective-permute-start | bytes 245768 | tf_op jit(solution)/shard_map/ppermute | solution.py:219
  107.2 11.5 %collective-permute-start.17 = (bf16[160,256]{1,0:T(8,128)(2,1)S(1)}, bf16[160,256]{1,0:T(8,128)(2,1)S(1)}, u32[]{:S(2)}, u32[]{:S(2)}) collective-permute-start(bf16[160,256]{1,0:T(8,128)(2,1)S(1)} %get-tuple-element.53), channel_id=1, source_target_pairs={{0,192},{1,193},{64,1},{65,0},{128,65},{129,64},{192,129},{193,128... | collective-permute-start | bytes 245768 | tf_op jit(solution)/shard_map/ppermute | solution.py:219
  108.6 10.6 %collective-permute-start.18 = (bf16[160,256]{1,0:T(8,128)(2,1)S(1)}, bf16[160,256]{1,0:T(8,128)(2,1)S(1)}, u32[]{:S(2)}, u32[]{:S(2)}) collective-permute-start(bf16[160,256]{1,0:T(8,128)(2,1)S(1)} %get-tuple-element.54), channel_id=1, source_target_pairs={{0,193},{1,192},{64,0},{65,1},{128,64},{129,65},{192,128},{193,129... | collective-permute-start | bytes 245768 | tf_op jit(solution)/shard_map/ppermute | solution.py:219
  111.4 7.7 %collective-permute-start.19 = (bf16[160,256]{1,0:T(8,128)(2,1)S(1)}, bf16[160,256]{1,0:T(8,128)(2,1)S(1)}, u32[]{:S(2)}, u32[]{:S(2)}) collective-permute-start(bf16[160,256]{1,0:T(8,128)(2,1)S(1)} %get-tuple-element.55), channel_id=1, source_target_pairs={{0,65},{1,64},{64,129},{65,128},{128,193},{129,192},{192,0},{193,1... | collective-permute-start | bytes 245768 | tf_op jit(solution)/shard_map/ppermute | solution.py:219
  114.5 7.0 %collective-permute-start.20 = (bf16[160,256]{1,0:T(8,128)(2,1)S(1)}, bf16[160,256]{1,0:T(8,128)(2,1)S(1)}, u32[]{:S(2)}, u32[]{:S(2)}) collective-permute-start(bf16[160,256]{1,0:T(8,128)(2,1)S(1)} %get-tuple-element.56), channel_id=1, source_target_pairs={{0,128},{1,129},{64,192},{65,193},{128,1},{129,0},{192,65},{193,64... | collective-permute-start | bytes 245768 | tf_op jit(solution)/shard_map/ppermute | solution.py:219
  114.8 7.0 %collective-permute-start.21 = (bf16[160,256]{1,0:T(8,128)(2,1)S(1)}, bf16[160,256]{1,0:T(8,128)(2,1)S(1)}, u32[]{:S(2)}, u32[]{:S(2)}) collective-permute-start(bf16[160,256]{1,0:T(8,128)(2,1)S(1)} %get-tuple-element.57), channel_id=1, source_target_pairs={{0,129},{1,128},{64,193},{65,192},{128,0},{129,1},{192,64},{193,65... | collective-permute-start | bytes 245768 | tf_op jit(solution)/shard_map/ppermute | solution.py:219
  118.7 5.7 %collective-permute-start.22 = (bf16[160,256]{1,0:T(8,128)(2,1)S(1)}, bf16[160,256]{1,0:T(8,128)(2,1)S(1)}, u32[]{:S(2)}, u32[]{:S(2)}) collective-permute-start(bf16[160,256]{1,0:T(8,128)(2,1)S(1)} %get-tuple-element.58), channel_id=1, source_target_pairs={{0,64},{1,65},{64,128},{65,129},{128,192},{129,193},{192,1},{193,0... | collective-permute-start | bytes 245768 | tf_op jit(solution)/shard_map/ppermute | solution.py:219

commit v11 on v9

--- a/solution.py
+++ b/solution.py
@@ -13,7 +13,7 @@
 Z, CORE, X, Y, W = 4, 2, 4, 4, 2
 RING = Z * W
 PLANE = X * Y
-STEPS = (0, 7, 1, 5, 3, 4, 6, 2)
+STEPS = (0, 4, 3, 5, 2, 6, 1, 7)
 BF = jnp.bfloat16
 F32 = jnp.float32
 VMEM = pl.BlockSpec(memory_space=pltpu.VMEM)
@@ -61,11 +61,11 @@
         normed[r * length : (r + 1) * length] = (off / jnp.sqrt(var + 1e-05) * gain).astype(BF)
 
     def project(c, r):
-        y = jnp.dot(normed[r * length : (r + 2) * length], w_ref[c], preferred_element_type=F32)
+        y = jnp.dot(normed[r * length : (r + 2) * length], w_ref[c], preferred_element_type=F32).astype(BF)
         for h in range(mine.shape[1]):
             columns = slice(h * HEAD_DIM, (h + 1) * HEAD_DIM)
             block = jnp.concatenate([y[:length, columns], y[length:, columns]], axis=1)
-            mine[c, h, :, r * HEAD_DIM : (r + 2) * HEAD_DIM] = block.astype(BF)
+            mine[c, h, :, r * HEAD_DIM : (r + 2) * HEAD_DIM] = block
 
     gain_copy.wait()
     gain = gain_ref[...].reshape(1, width)
@@ -121,18 +121,15 @@
     length = keys.shape[2]
     half = keys.shape[1] * length
     columns = pl.ds(side * half, half)
+    total = None
+    for w in range(W):
+        term = lax.dot_general(
+            q[w].reshape(half, -1), keys[w].reshape(half, -1), (((1,), (1,)), ((), ())), preferred_element_type=F32
+        )
+        total = term if total is None else total + term
     copies = []
-    for i, rows in enumerate(cuts(half, 2)):
-        total = None
-        for w in range(W):
-            term = lax.dot_general(
-                q[w, i * Z // 2 : (i + 1) * Z // 2].reshape(half // 2, -1),
-                keys[w].reshape(half, -1),
-                (((1,), (1,)), ((), ())),
-                preferred_element_type=F32,
-            )
-            total = term if total is None else total + term
-        terms[rows] = total.astype(BF)
+    for i, rows in enumerate(cuts(half, Z)):
+        terms[rows] = total[i * length : (i + 1) * length].astype(BF)
         copies.append(pltpu.make_async_copy(terms.at[rows], out_hbm.at[rows, columns], sem.at[i]))
         copies[i].start()
     for copy in copies:
@@ -273,7 +270,7 @@
         near_kernel,
         [jax.ShapeDtypeStruct((half, full), BF), whole],
         [pos, *both, keys],
-        [pltpu.VMEM((half, half), BF), dma((2,))],
+        [pltpu.VMEM((half, half), BF), dma((Z,))],
         flops=2 * half * half * W * lanes,
         out_specs=[HBM, VMEM],
     )
@@ -281,7 +278,7 @@
         far_kernel,
         jax.ShapeDtypeStruct((half, full), BF),
         [term, query, keys_far],
-        [pltpu.VMEM((half, half), BF), dma((2,))],
+        [pltpu.VMEM((half, half), BF), dma((Z,))],
         flops=2 * half * half * W * lanes,
         hbm=(0,),
         out_specs=HBM,

time: 126 us -> 127 us (level)
  starting transfers between devices: 55.6 us -> 57.4 us
    all_to_all x1, waiting for transfers between devices: 8.44 us -> 5.57 us  [shards(): terms = lax.all_to_all(term.reshape(chunk), ('x', 'y'), 0, 0, tiled=True)]
    all_to_all x1, waiting for transfers between devices: 7.26 us -> 9.69 us  [shards(): lax.all_to_all(probs, ('x', 'y'), 0, 0, tiled=True).reshape(half, full)]
    ppermute x21, starting transfers between devices: 41.7 us -> 43.5 us  [along_ring(): got.append(lax.ppermute(part, ('z', 'w'), pairs) if s else part)]
  transfers between devices with their start and end apart: 25 -> 25, of which waited for: 18 -> 19; matrix products, arithmetic and copies ran while one was open for 0% -> 0% of each run, Pallas kernels for 2% -> 2%
where the time goes in v11:
time: 127 us; the launch traced here: 126 us
  starting transfers between devices  57.4 us (45%)
  waiting for transfers between devices  55.8 us (44%)
  Pallas kernels  12.1 us (10%)
    ppermute x21, starting transfers between devices, along_ring(): got.append(lax.ppermute(part, ('z', 'w'), pairs) if s else part)  43.5 us
    ppermute x21, waiting for transfers between devices, along_ring(): got.append(lax.ppermute(part, ('z', 'w'), pairs) if s else part)  37.9 us
    pallas_call x11, Pallas kernels, call(): pl.pallas_call(kernel, out_shape=out_shape, in_specs=specs, out_specs=out...  12.1 us
    all_to_all x1, waiting for transfers between devices, shards(): lax.all_to_all(probs, ('x', 'y'), 0, 0, tiled=True).reshape(half, full)  9.69 us
    all_to_all x1, starting transfers between devices, shards(): terms = lax.all_to_all(term.reshape(chunk), ('x', 'y'), 0, 0, tiled=True)  7.44 us
    all_to_all x1, starting transfers between devices, shards(): lax.all_to_all(probs, ('x', 'y'), 0, 0, tiled=True).reshape(half, full)  6.24 us
    all_to_all x1, waiting for transfers between devices, shards(): terms = lax.all_to_all(term.reshape(chunk), ('x', 'y'), 0, 0, tiled=True)  5.57 us
    ppermute x2, waiting for transfers between devices, other_core(): return lax.ppermute(a, 'c', [(0, 1), (1, 0)])  2.65 us
  transfers between devices with their start and end apart: 25, of which 19 were waited for; matrix products, arithmetic and copies ran while one was open for 0% of the time, Pallas kernels for 2%

profile of v11, /device:TPU:6, one launch (start us, length us, event | category | flops | bytes accessed | tf_op | source)
XLA Modules:
  0.0 126.2 jit_solution(5875158726366517263)
XLA Ops:
  0.0 0.7 copy-done.2
  0.7 3.4 %shard_map.46 = (bf16[320,256]{1,0:T(8,128)(2,1)S(1)}, bf16[320,256]{1,0:T(8,128)(2,1)S(1)}, bf16[320,256]{1,0:T(8,128)(2,1)S(1)}, bf16[320,256]{1,0:T(8,128)(2,...) custom-call(s32[1]{0:T(128)} %bitcast.pos_ref, ...), custom_call_target="tpu_custom_call" | custom-call | flops 1006632960 | bytes 6690824 | tf_op jit(solution)/shard_map/pallas_call | solution.py:201
  4.1 7.3 %collective-permute-start = (bf16[320,256]{1,0:T(8,128)(2,1)S(1)}, bf16[320,256]{1,0:T(8,128)(2,1)S(1)}, u32[]{:S(2)}, u32[]{:S(2)}) collective-permute-start(bf16[320,256]{1,0:T(8,128)(2,1)S(1)} %get-tuple-element.33), channel_id=1, source_target_pairs={{0,1},{1,0},{64,65},{65,64},{128,129},{129,128},{192,193},{193,192... | collective-permute-start | bytes 491528 | tf_op jit(solution)/shard_map/ppermute | solution.py:217
  11.4 1.9 %collective-permute-start.1 = (bf16[320,256]{1,0:T(8,128)(2,1)S(1)}, bf16[320,256]{1,0:T(8,128)(2,1)S(1)}, u32[]{:S(2)}, u32[]{:S(2)}) collective-permute-start(bf16[320,256]{1,0:T(8,128)(2,1)S(1)} %get-tuple-element.34), channel_id=1, source_target_pairs={{0,192},{1,193},{64,1},{65,0},{128,65},{129,64},{192,129},{193,128... | collective-permute-start | bytes 491528 | tf_op jit(solution)/shard_map/ppermute | solution.py:217
  13.3 3.1 %collective-permute-start.2 = (bf16[320,256]{1,0:T(8,128)(2,1)S(1)}, bf16[320,256]{1,0:T(8,128)(2,1)S(1)}, u32[]{:S(2)}, u32[]{:S(2)}) collective-permute-start(bf16[320,256]{1,0:T(8,128)(2,1)S(1)} %get-tuple-element.35), channel_id=1, source_target_pairs={{0,65},{1,64},{64,129},{65,128},{128,193},{129,192},{192,0},{193,1... | collective-permute-start | bytes 491528 | tf_op jit(solution)/shard_map/ppermute | solution.py:217
  16.4 1.5 %collective-permute-start.3 = (bf16[320,256]{1,0:T(8,128)(2,1)S(1)}, bf16[320,256]{1,0:T(8,128)(2,1)S(1)}, u32[]{:S(2)}, u32[]{:S(2)}) collective-permute-start(bf16[320,256]{1,0:T(8,128)(2,1)S(1)} %get-tuple-element.36), channel_id=1, source_target_pairs={{0,128},{1,129},{64,192},{65,193},{128,1},{129,0},{192,65},{193,64... | collective-permute-start | bytes 491528 | tf_op jit(solution)/shard_map/ppermute | solution.py:217
  17.9 2.7 %collective-permute-start.4 = (bf16[320,256]{1,0:T(8,128)(2,1)S(1)}, bf16[320,256]{1,0:T(8,128)(2,1)S(1)}, u32[]{:S(2)}, u32[]{:S(2)}) collective-permute-start(bf16[320,256]{1,0:T(8,128)(2,1)S(1)} %get-tuple-element.37), channel_id=1, source_target_pairs={{0,129},{1,128},{64,193},{65,192},{128,0},{129,1},{192,64},{193,65... | collective-permute-start | bytes 491528 | tf_op jit(solution)/shard_map/ppermute | solution.py:217
  20.6 2.8 %collective-permute-done.refs_1_ = bf16[320,256]{1,0:T(8,128)(2,1)S(1)} collective-permute-done((bf16[320,256]{1,0:T(8,128)(2,1)S(1)}, bf16[320,256]{1,0:T(8,128)(2,1)S(1)}, u32[]{:S(2)}, u32[]{:S(2)}) %collective-permute-start) | collective-permute-done | bytes 163872 | tf_op jit(solution)/shard_map/ppermute | solution.py:217
  23.4 0.3 collective-permute-start.5
  23.8 8.8 %collective-permute-done.1.refs_2_ = bf16[320,256]{1,0:T(8,128)(2,1)S(1)} collective-permute-done((bf16[320,256]{1,0:T(8,128)(2,1)S(1)}, bf16[320,256]{1,0:T(8,128)(2,1)S(1)}, u32[]{:S(2)}, u32[]{:S(2)}) %collective-permute-start.1) | collective-permute-done | bytes 163872 | tf_op jit(solution)/shard_map/ppermute | solution.py:217
  32.6 0.0 collective-permute-start.6
  32.6 0.0 copy-done
  32.6 0.9 shard_map.47
  33.5 0.0 collective-permute-done.2.refs_3_
  33.5 3.3 %collective-permute-done.3.refs_4_ = bf16[320,256]{1,0:T(8,128)(2,1)S(1)} collective-permute-done((bf16[320,256]{1,0:T(8,128)(2,1)S(1)}, bf16[320,256]{1,0:T(8,128)(2,1)S(1)}, u32[]{:S(2)}, u32[]{:S(2)}) %collective-permute-start.3) | collective-permute-done | bytes 163872 | tf_op jit(solution)/shard_map/ppermute | solution.py:217
  36.8 0.9 collective-permute-done.4.refs_5_
  37.7 2.2 %collective-permute-done.5.refs_6_ = bf16[320,256]{1,0:T(8,128)(2,1)S(1)} collective-permute-done((bf16[320,256]{1,0:T(8,128)(2,1)S(1)}, bf16[320,256]{1,0:T(8,128)(2,1)S(1)}, u32[]{:S(2)}, u32[]{:S(2)}) %collective-permute-start.5) | collective-permute-done | bytes 163872 | tf_op jit(solution)/shard_map/ppermute | solution.py:217
  39.9 1.1 collective-permute-done.6.refs_7_
  41.0 0.1 shard_map.48.refs_8_
  41.0 0.1 collective-permute-start.7
  41.1 1.5 %shard_map.49 = (bf16[640,1280]{1,0:T(8,128)(2,1)}, bf16[2,4,160,256]{3,2,1,0:T(8,128)(2,1)S(1)}) custom-call(s32[1]{0:T(128)} %bitcast.pos_ref, bf16[320,256]{1,0:T(8,128)(2,1)S(1)} %get-tuple-element.32.refs_0_, bf16[320,256]{1,0:T(8,128)(2,1)S(1)} %collective-permute-done.refs_1_, bf16[320,256]{1,0:T(8,128)(2,1)S(1)} %collective-permute-done.1.refs_2_, ...), custom_call_target="tpu_custom_call" | custom-call | flops 419430400 | bytes 3932168 | tf_op jit(solution)/shard_map/pallas_call | solution.py:201
  42.6 0.6 collective-permute-done.7.k_far
  43.2 1.5 %shard_map.50 = bf16[640,1280]{1,0:T(8,128)(2,1)} custom-call(bf16[640,1280]{1,0:T(8,128)(2,1)} %get-tuple-element.42._, bf16[2,4,160,256]{3,2,1,0:T(8,128)(2,1)S(1)} %get-tuple-element.43.q, bf16[2,4,160,256]{3,2,1,0:T(8,128)(2,1)S(1)} %collective-permute-done.7.k_far), custom_call_target="tpu_custom_call", output_to_operand_aliasing={{}: (0, {})} | custom-call | flops 419430400 | bytes 5898240 | tf_op jit(solution)/shard_map/pallas_call | solution.py:201
  44.7 7.4 %all-to-all-start = ((bf16[16,40,1280]{2,1,0:T(8,128)(2,1)}), bf16[16,40,1280]{2,1,0:T(8,128)(2,1)S(1)}, u32[]{:S(2)}, u32[]{:S(2)}) async-start(bf16[16,40,1280]{2,1,0:T(8,128)(2,1)} %bitcast.2), calls=%async_computation | async-start | bytes 3276800 | tf_op jit(solution)/shard_map/all_to_all | solution.py:288
  52.2 3.5 %collective-permute-start.8 = (bf16[160,256]{1,0:T(8,128)(2,1)S(1)}, bf16[160,256]{1,0:T(8,128)(2,1)S(1)}, u32[]{:S(2)}, u32[]{:S(2)}) collective-permute-start(bf16[160,256]{1,0:T(8,128)(2,1)S(1)} %get-tuple-element.44), channel_id=1, source_target_pairs={{0,1},{1,0},{64,65},{65,64},{128,129},{129,128},{192,193},{193,192... | collective-permute-start | bytes 245768 | tf_op jit(solution)/shard_map/ppermute | solution.py:217
  55.7 2.3 %collective-permute-start.9 = (bf16[160,256]{1,0:T(8,128)(2,1)S(1)}, bf16[160,256]{1,0:T(8,128)(2,1)S(1)}, u32[]{:S(2)}, u32[]{:S(2)}) collective-permute-start(bf16[160,256]{1,0:T(8,128)(2,1)S(1)} %get-tuple-element.45), channel_id=1, source_target_pairs={{0,192},{1,193},{64,1},{65,0},{128,65},{129,64},{192,129},{193,128... | collective-permute-start | bytes 245768 | tf_op jit(solution)/shard_map/ppermute | solution.py:217
  58.0 2.7 %collective-permute-start.10 = (bf16[160,256]{1,0:T(8,128)(2,1)S(1)}, bf16[160,256]{1,0:T(8,128)(2,1)S(1)}, u32[]{:S(2)}, u32[]{:S(2)}) collective-permute-start(bf16[160,256]{1,0:T(8,128)(2,1)S(1)} %get-tuple-element.46), channel_id=1, source_target_pairs={{0,65},{1,64},{64,129},{65,128},{128,193},{129,192},{192,0},{193,1... | collective-permute-start | bytes 245768 | tf_op jit(solution)/shard_map/ppermute | solution.py:217
  60.7 0.1 collective-permute-start.11
  60.8 2.9 %collective-permute-done.8.refs_0_.refs_1_ = bf16[160,256]{1,0:T(8,128)(2,1)S(1)} collective-permute-done((bf16[160,256]{1,0:T(8,128)(2,1)S(1)}, bf16[160,256]{1,0:T(8,128)(2,1)S(1)}, u32[]{:S(2)}, u32[]{:S(2)}) %collective-permute-start.8) | collective-permute-done | bytes 81952 | tf_op jit(solution)/shard_map/ppermute | solution.py:217
  63.7 5.5 %collective-permute-done.9.refs_1_.refs_2_ = bf16[160,256]{1,0:T(8,128)(2,1)S(1)} collective-permute-done((bf16[160,256]{1,0:T(8,128)(2,1)S(1)}, bf16[160,256]{1,0:T(8,128)(2,1)S(1)}, u32[]{:S(2)}, u32[]{:S(2)}) %collective-permute-start.9) | collective-permute-done | bytes 81952 | tf_op jit(solution)/shard_map/ppermute | solution.py:217
  69.2 0.0 collective-permute-done.10.refs_2_.refs_3_
  69.2 0.0 collective-permute-done.11.refs_3_.refs_4_
  69.2 5.6 %all-to-all-done.x_ref = bf16[16,40,1280]{2,1,0:T(8,128)(2,1)S(1)} async-done(((bf16[16,40,1280]{2,1,0:T(8,128)(2,1)}), bf16[16,40,1280]{2,1,0:T(8,128)(2,1)S(1)}, u32[]{:S(2)}, u32[]{:S(2)}) %all-to-all-start) | async-done | bytes 1638432 | tf_op jit(solution)/shard_map/all_to_all | solution.py:288
  74.8 1.6 %shard_map.51 = bf16[16,40,1280]{2,1,0:T(8,128)(2,1)} custom-call(bf16[16,40,1280]{2,1,0:T(8,128)(2,1)S(1)} %all-to-all-done.x_ref, bf16[160,256]{1,0:T(8,128)(2,1)S(1)} %collective-permute-done.8.refs_0_.refs_1_, bf16[160,256]{1,0:T(8,128)(2,1)S(1)} %collective-permute-done.9.refs_1_.refs_2_, bf16[160,256]{1,0:T(8,128)(2,1)S(1)} %collective-permute-done.10.refs_2_.refs_3_, ...), custom_call_target="tpu_custom_call" | custom-call | bytes 3932160 | tf_op jit(solution)/shard_map/pallas_call | solution.py:201
  76.4 6.2 %all-to-all-start.1 = ((bf16[16,40,1280]{2,1,0:T(8,128)(2,1)}), bf16[16,40,1280]{2,1,0:T(8,128)(2,1)S(1)}, u32[]{:S(2)}, u32[]{:S(2)}) async-start(bf16[16,40,1280]{2,1,0:T(8,128)(2,1)} %shard_map.51), calls=%async_computation.1 | async-start | bytes 3276800 | tf_op jit(solution)/shard_map/all_to_all | solution.py:298
  82.6 1.3 collective-permute-start.12
  83.9 2.8 %collective-permute-start.13 = (bf16[160,256]{1,0:T(8,128)(2,1)S(1)}, bf16[160,256]{1,0:T(8,128)(2,1)S(1)}, u32[]{:S(2)}, u32[]{:S(2)}) collective-permute-start(bf16[160,256]{1,0:T(8,128)(2,1)S(1)} %get-tuple-element.49), channel_id=1, source_target_pairs={{0,64},{1,65},{64,128},{65,129},{128,192},{129,193},{192,1},{193,0... | collective-permute-start | bytes 245768 | tf_op jit(solution)/shard_map/ppermute | solution.py:217
  86.7 0.4 collective-permute-start.14
  87.1 1.8 %collective-permute-done.12.refs_5_ = bf16[160,256]{1,0:T(8,128)(2,1)S(1)} collective-permute-done((bf16[160,256]{1,0:T(8,128)(2,1)S(1)}, bf16[160,256]{1,0:T(8,128)(2,1)S(1)}, u32[]{:S(2)}, u32[]{:S(2)}) %collective-permute-start.12) | collective-permute-done | bytes 81952 | tf_op jit(solution)/shard_map/ppermute | solution.py:217
  89.0 0.6 collective-permute-done.13.refs_6_
  89.5 1.6 %collective-permute-done.14.refs_7_ = bf16[160,256]{1,0:T(8,128)(2,1)S(1)} collective-permute-done((bf16[160,256]{1,0:T(8,128)(2,1)S(1)}, bf16[160,256]{1,0:T(8,128)(2,1)S(1)}, u32[]{:S(2)}, u32[]{:S(2)}) %collective-permute-start.14) | collective-permute-done | bytes 81952 | tf_op jit(solution)/shard_map/ppermute | solution.py:217
  91.2 0.1 shard_map.52.v_ref
  91.2 0.1 collective-permute-start.15
  91.3 2.1 %collective-permute-done.15._.v_far = bf16[2,4,160,256]{3,2,1,0:T(8,128)(2,1)S(1)} collective-permute-done((bf16[2,4,160,256]{3,2,1,0:T(8,128)(2,1)S(1)}, bf16[2,4,160,256]{3,2,1,0:T(8,128)(2,1)S(1)}, u32[]{:S(2)}, u32[]{:S(2)}) %collective-permute-start.15) | collective-permute-done | bytes 655392 | tf_op jit(solution)/shard_map/ppermute | solution.py:222
  93.4 9.7 %all-to-all-done.1 = bf16[16,40,1280]{2,1,0:T(8,128)(2,1)S(1)} async-done(((bf16[16,40,1280]{2,1,0:T(8,128)(2,1)}), bf16[16,40,1280]{2,1,0:T(8,128)(2,1)S(1)}, u32[]{:S(2)}, u32[]{:S(2)}) %all-to-all-start.1) | async-done | bytes 1638432 | tf_op jit(solution)/shard_map/all_to_all | solution.py:298
  103.1 0.7 shard_map.54
  103.8 0.0 copy-start.1
  103.8 3.6 %collective-permute-start.16 = (bf16[160,256]{1,0:T(8,128)(2,1)S(1)}, bf16[160,256]{1,0:T(8,128)(2,1)S(1)}, u32[]{:S(2)}, u32[]{:S(2)}) collective-permute-start(bf16[160,256]{1,0:T(8,128)(2,1)S(1)} %get-tuple-element.52), channel_id=1, source_target_pairs={{0,1},{1,0},{64,65},{65,64},{128,129},{129,128},{192,193},{193,192... | collective-permute-start | bytes 245768 | tf_op jit(solution)/shard_map/ppermute | solution.py:217
  107.4 2.4 %collective-permute-start.17 = (bf16[160,256]{1,0:T(8,128)(2,1)S(1)}, bf16[160,256]{1,0:T(8,128)(2,1)S(1)}, u32[]{:S(2)}, u32[]{:S(2)}) collective-permute-start(bf16[160,256]{1,0:T(8,128)(2,1)S(1)} %get-tuple-element.53), channel_id=1, source_target_pairs={{0,192},{1,193},{64,1},{65,0},{128,65},{129,64},{192,129},{193,128... | collective-permute-start | bytes 245768 | tf_op jit(solution)/shard_map/ppermute | solution.py:217
  109.8 0.4 collective-permute-start.18
  110.2 0.7 shard_map.55
  110.9 2.4 %collective-permute-start.19 = (bf16[160,256]{1,0:T(8,128)(2,1)S(1)}, bf16[160,256]{1,0:T(8,128)(2,1)S(1)}, u32[]{:S(2)}, u32[]{:S(2)}) collective-permute-start(bf16[160,256]{1,0:T(8,128)(2,1)S(1)} %get-tuple-element.55), channel_id=1, source_target_pairs={{0,65},{1,64},{64,129},{65,128},{128,193},{129,192},{192,0},{193,1... | collective-permute-start | bytes 245768 | tf_op jit(solution)/shard_map/ppermute | solution.py:217
  113.3 0.9 collective-permute-start.20
  114.2 0.0 collective-permute-done.16.refs_1_
  114.2 3.2 %collective-permute-start.21 = (bf16[160,256]{1,0:T(8,128)(2,1)S(1)}, bf16[160,256]{1,0:T(8,128)(2,1)S(1)}, u32[]{:S(2)}, u32[]{:S(2)}) collective-permute-start(bf16[160,256]{1,0:T(8,128)(2,1)S(1)} %get-tuple-element.57), channel_id=1, source_target_pairs={{0,129},{1,128},{64,193},{65,192},{128,0},{129,1},{192,64},{193,65... | collective-permute-start | bytes 245768 | tf_op jit(solution)/shard_map/ppermute | solution.py:217
  117.4 1.3 %collective-permute-done.17.refs_2_ = bf16[160,256]{1,0:T(8,128)(2,1)S(1)} collective-permute-done((bf16[160,256]{1,0:T(8,128)(2,1)S(1)}, bf16[160,256]{1,0:T(8,128)(2,1)S(1)}, u32[]{:S(2)}, u32[]{:S(2)}) %collective-permute-start.17) | collective-permute-done | bytes 81952 | tf_op jit(solution)/shard_map/ppermute | solution.py:217
  118.7 0.7 collective-permute-start.22
  119.4 0.0 collective-permute-done.18.refs_3_
  119.4 0.0 collective-permute-done.19.refs_4_
  119.4 0.7 collective-permute-done.20.refs_5_
  120.2 2.3 %collective-permute-done.21.refs_6_ = bf16[160,256]{1,0:T(8,128)(2,1)S(1)} collective-permute-done((bf16[160,256]{1,0:T(8,128)(2,1)S(1)}, bf16[160,256]{1,0:T(8,128)(2,1)S(1)}, u32[]{:S(2)}, u32[]{:S(2)}) %collective-permute-start.21) | collective-permute-done | bytes 81952 | tf_op jit(solution)/shard_map/ppermute | solution.py:217
  122.5 1.9 %collective-permute-done.22.refs_7_ = bf16[160,256]{1,0:T(8,128)(2,1)S(1)} collective-permute-done((bf16[160,256]{1,0:T(8,128)(2,1)S(1)}, bf16[160,256]{1,0:T(8,128)(2,1)S(1)}, u32[]{:S(2)}, u32[]{:S(2)}) %collective-permute-start.22) | collective-permute-done | bytes 81952 | tf_op jit(solution)/shard_map/ppermute | solution.py:217
  124.4 0.0 copy-done.1
  124.4 1.7 %shard_map.56 = f32[4,160,768]{2,1,0:T(8,128)} custom-call(s32[1]{0:T(128)} %bitcast.pos_ref, bf16[512,768]{1,0:T(8,128)(2,1)S(1)} %copy-done.1, bf16[160,256]{1,0:T(8,128)(2,1)S(1)} %get-tuple-element.51.refs_0_, bf16[160,256]{1,0:T(8,128)(2,1)S(1)} %collective-permute-done.16.refs_1_, bf16[160,256]{1,0:T(8,128)(2,1)S(1)} %collective-permute-done.17.refs_2_, ...), custom_call_target="tpu_custom_call" | custom-call | flops 503316480 | bytes 2883592 | tf_op jit(solution)/shard_map/pallas_call | solution.py:201
  (3 shorter events, 0.0 us)
Async XLA Ops:
  0.0 0.7 copy-start.2
  0.7 31.9 %copy-start = (bf16[768,3,512]{2,0,1:T(8,128)(2,1)S(1)}, bf16[768,3,512]{2,0,1:T(8,128)(2,1)}, u32[]{:S(2)}) copy-start(bf16[768,3,512]{2,0,1:T(8,128)(2,1)} %param.6) | copy-start | bytes 7077892
  4.1 19.3 %collective-permute-start = (bf16[320,256]{1,0:T(8,128)(2,1)S(1)}, bf16[320,256]{1,0:T(8,128)(2,1)S(1)}, u32[]{:S(2)}, u32[]{:S(2)}) collective-permute-start(bf16[320,256]{1,0:T(8,128)(2,1)S(1)} %get-tuple-element.33), channel_id=1, source_target_pairs={{0,1},{1,0},{64,65},{65,64},{128,129},{129,128},{192,193},{193,192... | collective-permute-start | bytes 491528 | tf_op jit(solution)/shard_map/ppermute | solution.py:217
  11.4 21.2 %collective-permute-start.1 = (bf16[320,256]{1,0:T(8,128)(2,1)S(1)}, bf16[320,256]{1,0:T(8,128)(2,1)S(1)}, u32[]{:S(2)}, u32[]{:S(2)}) collective-permute-start(bf16[320,256]{1,0:T(8,128)(2,1)S(1)} %get-tuple-element.34), channel_id=1, source_target_pairs={{0,192},{1,193},{64,1},{65,0},{128,65},{129,64},{192,129},{193,128... | collective-permute-start | bytes 491528 | tf_op jit(solution)/shard_map/ppermute | solution.py:217
  13.3 20.2 %collective-permute-start.2 = (bf16[320,256]{1,0:T(8,128)(2,1)S(1)}, bf16[320,256]{1,0:T(8,128)(2,1)S(1)}, u32[]{:S(2)}, u32[]{:S(2)}) collective-permute-start(bf16[320,256]{1,0:T(8,128)(2,1)S(1)} %get-tuple-element.35), channel_id=1, source_target_pairs={{0,65},{1,64},{64,129},{65,128},{128,193},{129,192},{192,0},{193,1... | collective-permute-start | bytes 491528 | tf_op jit(solution)/shard_map/ppermute | solution.py:217
  16.4 20.4 %collective-permute-start.3 = (bf16[320,256]{1,0:T(8,128)(2,1)S(1)}, bf16[320,256]{1,0:T(8,128)(2,1)S(1)}, u32[]{:S(2)}, u32[]{:S(2)}) collective-permute-start(bf16[320,256]{1,0:T(8,128)(2,1)S(1)} %get-tuple-element.36), channel_id=1, source_target_pairs={{0,128},{1,129},{64,192},{65,193},{128,1},{129,0},{192,65},{193,64... | collective-permute-start | bytes 491528 | tf_op jit(solution)/shard_map/ppermute | solution.py:217
  17.9 19.8 %collective-permute-start.4 = (bf16[320,256]{1,0:T(8,128)(2,1)S(1)}, bf16[320,256]{1,0:T(8,128)(2,1)S(1)}, u32[]{:S(2)}, u32[]{:S(2)}) collective-permute-start(bf16[320,256]{1,0:T(8,128)(2,1)S(1)} %get-tuple-element.37), channel_id=1, source_target_pairs={{0,129},{1,128},{64,193},{65,192},{128,0},{129,1},{192,64},{193,65... | collective-permute-start | bytes 491528 | tf_op jit(solution)/shard_map/ppermute | solution.py:217
  23.4 16.4 %collective-permute-start.5 = (bf16[320,256]{1,0:T(8,128)(2,1)S(1)}, bf16[320,256]{1,0:T(8,128)(2,1)S(1)}, u32[]{:S(2)}, u32[]{:S(2)}) collective-permute-start(bf16[320,256]{1,0:T(8,128)(2,1)S(1)} %get-tuple-element.38), channel_id=1, source_target_pairs={{0,64},{1,65},{64,128},{65,129},{128,192},{129,193},{192,1},{193,0... | collective-permute-start | bytes 491528 | tf_op jit(solution)/shard_map/ppermute | solution.py:217
  32.6 8.3 %collective-permute-start.6 = (bf16[320,256]{1,0:T(8,128)(2,1)S(1)}, bf16[320,256]{1,0:T(8,128)(2,1)S(1)}, u32[]{:S(2)}, u32[]{:S(2)}) collective-permute-start(bf16[320,256]{1,0:T(8,128)(2,1)S(1)} %get-tuple-element.39), channel_id=1, source_target_pairs={{0,193},{1,192},{64,0},{65,1},{128,64},{129,65},{192,128},{193,129... | collective-permute-start | bytes 491528 | tf_op jit(solution)/shard_map/ppermute | solution.py:217
  41.0 2.2 %collective-permute-start.7 = (bf16[2,4,160,256]{3,2,1,0:T(8,128)(2,1)S(1)}, bf16[2,4,160,256]{3,2,1,0:T(8,128)(2,1)S(1)}, u32[]{:S(2)}, u32[]{:S(2)}) collective-permute-start(bf16[2,4,160,256]{3,2,1,0:T(8,128)(2,1)S(1)} %shard_map.48.refs_8_), channel_id=1, source_target_pairs={{0,32},{32,0},{1,33},{33,1},{2,34},{34,2},{3,35},{35,3},{4,36},{36... | collective-permute-start | bytes 1966088 | tf_op jit(solution)/shard_map/ppermute | solution.py:222
  44.7 30.1 %all-to-all-start = ((bf16[16,40,1280]{2,1,0:T(8,128)(2,1)}), bf16[16,40,1280]{2,1,0:T(8,128)(2,1)S(1)}, u32[]{:S(2)}, u32[]{:S(2)}) async-start(bf16[16,40,1280]{2,1,0:T(8,128)(2,1)} %bitcast.2), calls=%async_computation | async-start | bytes 3276800 | tf_op jit(solution)/shard_map/all_to_all | solution.py:288
  52.2 11.6 %collective-permute-start.8 = (bf16[160,256]{1,0:T(8,128)(2,1)S(1)}, bf16[160,256]{1,0:T(8,128)(2,1)S(1)}, u32[]{:S(2)}, u32[]{:S(2)}) collective-permute-start(bf16[160,256]{1,0:T(8,128)(2,1)S(1)} %get-tuple-element.44), channel_id=1, source_target_pairs={{0,1},{1,0},{64,65},{65,64},{128,129},{129,128},{192,193},{193,192... | collective-permute-start | bytes 245768 | tf_op jit(solution)/shard_map/ppermute | solution.py:217
  55.7 13.5 %collective-permute-start.9 = (bf16[160,256]{1,0:T(8,128)(2,1)S(1)}, bf16[160,256]{1,0:T(8,128)(2,1)S(1)}, u32[]{:S(2)}, u32[]{:S(2)}) collective-permute-start(bf16[160,256]{1,0:T(8,128)(2,1)S(1)} %get-tuple-element.45), channel_id=1, source_target_pairs={{0,192},{1,193},{64,1},{65,0},{128,65},{129,64},{192,129},{193,128... | collective-permute-start | bytes 245768 | tf_op jit(solution)/shard_map/ppermute | solution.py:217
  58.0 11.1 %collective-permute-start.10 = (bf16[160,256]{1,0:T(8,128)(2,1)S(1)}, bf16[160,256]{1,0:T(8,128)(2,1)S(1)}, u32[]{:S(2)}, u32[]{:S(2)}) collective-permute-start(bf16[160,256]{1,0:T(8,128)(2,1)S(1)} %get-tuple-element.46), channel_id=1, source_target_pairs={{0,65},{1,64},{64,129},{65,128},{128,193},{129,192},{192,0},{193,1... | collective-permute-start | bytes 245768 | tf_op jit(solution)/shard_map/ppermute | solution.py:217
  60.7 8.5 %collective-permute-start.11 = (bf16[160,256]{1,0:T(8,128)(2,1)S(1)}, bf16[160,256]{1,0:T(8,128)(2,1)S(1)}, u32[]{:S(2)}, u32[]{:S(2)}) collective-permute-start(bf16[160,256]{1,0:T(8,128)(2,1)S(1)} %get-tuple-element.47), channel_id=1, source_target_pairs={{0,128},{1,129},{64,192},{65,193},{128,1},{129,0},{192,65},{193,64... | collective-permute-start | bytes 245768 | tf_op jit(solution)/shard_map/ppermute | solution.py:217
  76.4 26.7 %all-to-all-start.1 = ((bf16[16,40,1280]{2,1,0:T(8,128)(2,1)}), bf16[16,40,1280]{2,1,0:T(8,128)(2,1)S(1)}, u32[]{:S(2)}, u32[]{:S(2)}) async-start(bf16[16,40,1280]{2,1,0:T(8,128)(2,1)} %shard_map.51), calls=%async_computation.1 | async-start | bytes 3276800 | tf_op jit(solution)/shard_map/all_to_all | solution.py:298
  82.6 6.3 %collective-permute-start.12 = (bf16[160,256]{1,0:T(8,128)(2,1)S(1)}, bf16[160,256]{1,0:T(8,128)(2,1)S(1)}, u32[]{:S(2)}, u32[]{:S(2)}) collective-permute-start(bf16[160,256]{1,0:T(8,128)(2,1)S(1)} %get-tuple-element.48), channel_id=1, source_target_pairs={{0,129},{1,128},{64,193},{65,192},{128,0},{129,1},{192,64},{193,65... | collective-permute-start | bytes 245768 | tf_op jit(solution)/shard_map/ppermute | solution.py:217
  83.9 5.7 %collective-permute-start.13 = (bf16[160,256]{1,0:T(8,128)(2,1)S(1)}, bf16[160,256]{1,0:T(8,128)(2,1)S(1)}, u32[]{:S(2)}, u32[]{:S(2)}) collective-permute-start(bf16[160,256]{1,0:T(8,128)(2,1)S(1)} %get-tuple-element.49), channel_id=1, source_target_pairs={{0,64},{1,65},{64,128},{65,129},{128,192},{129,193},{192,1},{193,0... | collective-permute-start | bytes 245768 | tf_op jit(solution)/shard_map/ppermute | solution.py:217
  86.7 4.4 %collective-permute-start.14 = (bf16[160,256]{1,0:T(8,128)(2,1)S(1)}, bf16[160,256]{1,0:T(8,128)(2,1)S(1)}, u32[]{:S(2)}, u32[]{:S(2)}) collective-permute-start(bf16[160,256]{1,0:T(8,128)(2,1)S(1)} %get-tuple-element.50), channel_id=1, source_target_pairs={{0,193},{1,192},{64,0},{65,1},{128,64},{129,65},{192,128},{193,129... | collective-permute-start | bytes 245768 | tf_op jit(solution)/shard_map/ppermute | solution.py:217
  91.2 2.2 %collective-permute-start.15 = (bf16[2,4,160,256]{3,2,1,0:T(8,128)(2,1)S(1)}, bf16[2,4,160,256]{3,2,1,0:T(8,128)(2,1)S(1)}, u32[]{:S(2)}, u32[]{:S(2)}) collective-permute-start(bf16[2,4,160,256]{3,2,1,0:T(8,128)(2,1)S(1)} %shard_map.52.v_ref), channel_id=1, source_target_pairs={{0,32},{32,0},{1,33},{33,1},{2,34},{34,2},{3,35},{35,3},{4,36},{36... | collective-permute-start | bytes 1966088 | tf_op jit(solution)/shard_map/ppermute | solution.py:222
  103.8 20.6 %copy-start.1 = (bf16[512,768]{1,0:T(8,128)(2,1)S(1)}, bf16[512,768]{1,0:T(8,128)(2,1)}, u32[]{:S(2)}) copy-start(bf16[512,768]{1,0:T(8,128)(2,1)} %w_ref.1) | copy-start | bytes 2359300
  103.8 10.4 %collective-permute-start.16 = (bf16[160,256]{1,0:T(8,128)(2,1)S(1)}, bf16[160,256]{1,0:T(8,128)(2,1)S(1)}, u32[]{:S(2)}, u32[]{:S(2)}) collective-permute-start(bf16[160,256]{1,0:T(8,128)(2,1)S(1)} %get-tuple-element.52), channel_id=1, source_target_pairs={{0,1},{1,0},{64,65},{65,64},{128,129},{129,128},{192,193},{193,192... | collective-permute-start | bytes 245768 | tf_op jit(solution)/shard_map/ppermute | solution.py:217
  107.4 11.3 %collective-permute-start.17 = (bf16[160,256]{1,0:T(8,128)(2,1)S(1)}, bf16[160,256]{1,0:T(8,128)(2,1)S(1)}, u32[]{:S(2)}, u32[]{:S(2)}) collective-permute-start(bf16[160,256]{1,0:T(8,128)(2,1)S(1)} %get-tuple-element.53), channel_id=1, source_target_pairs={{0,192},{1,193},{64,1},{65,0},{128,65},{129,64},{192,129},{193,128... | collective-permute-start | bytes 245768 | tf_op jit(solution)/shard_map/ppermute | solution.py:217
  109.8 9.6 %collective-permute-start.18 = (bf16[160,256]{1,0:T(8,128)(2,1)S(1)}, bf16[160,256]{1,0:T(8,128)(2,1)S(1)}, u32[]{:S(2)}, u32[]{:S(2)}) collective-permute-start(bf16[160,256]{1,0:T(8,128)(2,1)S(1)} %get-tuple-element.54), channel_id=1, source_target_pairs={{0,193},{1,192},{64,0},{65,1},{128,64},{129,65},{192,128},{193,129... | collective-permute-start | bytes 245768 | tf_op jit(solution)/shard_map/ppermute | solution.py:217
  110.9 8.5 %collective-permute-start.19 = (bf16[160,256]{1,0:T(8,128)(2,1)S(1)}, bf16[160,256]{1,0:T(8,128)(2,1)S(1)}, u32[]{:S(2)}, u32[]{:S(2)}) collective-permute-start(bf16[160,256]{1,0:T(8,128)(2,1)S(1)} %get-tuple-element.55), channel_id=1, source_target_pairs={{0,65},{1,64},{64,129},{65,128},{128,193},{129,192},{192,0},{193,1... | collective-permute-start | bytes 245768 | tf_op jit(solution)/shard_map/ppermute | solution.py:217
  113.3 6.9 %collective-permute-start.20 = (bf16[160,256]{1,0:T(8,128)(2,1)S(1)}, bf16[160,256]{1,0:T(8,128)(2,1)S(1)}, u32[]{:S(2)}, u32[]{:S(2)}) collective-permute-start(bf16[160,256]{1,0:T(8,128)(2,1)S(1)} %get-tuple-element.56), channel_id=1, source_target_pairs={{0,128},{1,129},{64,192},{65,193},{128,1},{129,0},{192,65},{193,64... | collective-permute-start | bytes 245768 | tf_op jit(solution)/shard_map/ppermute | solution.py:217
  114.2 8.3 %collective-permute-start.21 = (bf16[160,256]{1,0:T(8,128)(2,1)S(1)}, bf16[160,256]{1,0:T(8,128)(2,1)S(1)}, u32[]{:S(2)}, u32[]{:S(2)}) collective-permute-start(bf16[160,256]{1,0:T(8,128)(2,1)S(1)} %get-tuple-element.57), channel_id=1, source_target_pairs={{0,129},{1,128},{64,193},{65,192},{128,0},{129,1},{192,64},{193,65... | collective-permute-start | bytes 245768 | tf_op jit(solution)/shard_map/ppermute | solution.py:217
  118.7 5.7 %collective-permute-start.22 = (bf16[160,256]{1,0:T(8,128)(2,1)S(1)}, bf16[160,256]{1,0:T(8,128)(2,1)S(1)}, u32[]{:S(2)}, u32[]{:S(2)}) collective-permute-start(bf16[160,256]{1,0:T(8,128)(2,1)S(1)} %get-tuple-element.58), channel_id=1, source_target_pairs={{0,64},{1,65},{64,128},{65,129},{128,192},{129,193},{192,1},{193,0... | collective-permute-start | bytes 245768 | tf_op jit(solution)/shard_map/ppermute | solution.py:217

commit v12 on v11

--- a/solution.py
+++ b/solution.py
@@ -51,7 +51,7 @@
     x_copies = [pltpu.make_async_copy(x_hbm.at[r], x_ref.at[r], x_sem.at[r]) for r in range(seqs)]
     w_copies = [pltpu.make_async_copy(w_hbm.at[c], w_ref.at[c], w_sem.at[c]) for c in range(2)]
     gain_copy = pltpu.make_async_copy(gain_hbm, gain_ref, gain_sem)
-    for copy in (x_copies[0], gain_copy, *x_copies[1:], w_copies[1], w_copies[0]):
+    for copy in (x_copies[0], gain_copy, *x_copies[1:]):
         copy.start()
     def norm(r):
         x = x_ref[r].astype(F32)
@@ -71,6 +71,9 @@
     gain = gain_ref[...].reshape(1, width)
     for r in range(seqs // 2):
         x_copies[r].wait()
+    for c in (1, 0):
+        w_copies[c].start()
+    for r in range(seqs // 2):
         norm(r)
     for r in range(seqs // 2, seqs):
         x_copies[r].wait()

time: 127 us -> 127 us (level)
  no operation moved by 1% of the time
where the time goes in v12:
time: 127 us
  starting transfers between devices  57.4 us (45%)
  waiting for transfers between devices  55.7 us (44%)
  Pallas kernels  12.8 us (10%)
    ppermute x21, starting transfers between devices, along_ring(): got.append(lax.ppermute(part, ('z', 'w'), pairs) if s else part)  43.5 us
    ppermute x21, waiting for transfers between devices, along_ring(): got.append(lax.ppermute(part, ('z', 'w'), pairs) if s else part)  37.8 us
    pallas_call x11, Pallas kernels, call(): pl.pallas_call(kernel, out_shape=out_shape, in_specs=specs, out_specs=out...  12.8 us
    all_to_all x1, waiting for transfers between devices, shards(): lax.all_to_all(probs, ('x', 'y'), 0, 0, tiled=True).reshape(half, full)  9.7 us
    all_to_all x1, starting transfers between devices, shards(): terms = lax.all_to_all(term.reshape(chunk), ('x', 'y'), 0, 0, tiled=True)  7.43 us
    all_to_all x1, starting transfers between devices, shards(): lax.all_to_all(probs, ('x', 'y'), 0, 0, tiled=True).reshape(half, full)  6.25 us
    all_to_all x1, waiting for transfers between devices, shards(): terms = lax.all_to_all(term.reshape(chunk), ('x', 'y'), 0, 0, tiled=True)  5.57 us
    ppermute x2, waiting for transfers between devices, other_core(): return lax.ppermute(a, 'c', [(0, 1), (1, 0)])  2.65 us
  transfers between devices with their start and end apart: 25, of which 19 were waited for; matrix products, arithmetic and copies ran while one was open for 0% of the time, Pallas kernels for 2%

profile of v12, /device:TPU:6, one launch (start us, length us, event | category | flops | bytes accessed | tf_op | source)
XLA Modules:
  0.0 126.9 jit_solution(14591366688755276)
XLA Ops:
  0.0 0.7 copy-done.2
  0.7 4.1 %shard_map.46 = (bf16[320,256]{1,0:T(8,128)(2,1)S(1)}, bf16[320,256]{1,0:T(8,128)(2,1)S(1)}, bf16[320,256]{1,0:T(8,128)(2,1)S(1)}, bf16[320,256]{1,0:T(8,128)(2,...) custom-call(s32[1]{0:T(128)} %bitcast.pos_ref, ...), custom_call_target="tpu_custom_call" | custom-call | flops 1006632960 | bytes 6690824 | tf_op jit(solution)/shard_map/pallas_call | solution.py:204
  4.8 7.3 %collective-permute-start = (bf16[320,256]{1,0:T(8,128)(2,1)S(1)}, bf16[320,256]{1,0:T(8,128)(2,1)S(1)}, u32[]{:S(2)}, u32[]{:S(2)}) collective-permute-start(bf16[320,256]{1,0:T(8,128)(2,1)S(1)} %get-tuple-element.33), channel_id=1, source_target_pairs={{0,1},{1,0},{64,65},{65,64},{128,129},{129,128},{192,193},{193,192... | collective-permute-start | bytes 491528 | tf_op jit(solution)/shard_map/ppermute | solution.py:220
  12.1 1.9 %collective-permute-start.1 = (bf16[320,256]{1,0:T(8,128)(2,1)S(1)}, bf16[320,256]{1,0:T(8,128)(2,1)S(1)}, u32[]{:S(2)}, u32[]{:S(2)}) collective-permute-start(bf16[320,256]{1,0:T(8,128)(2,1)S(1)} %get-tuple-element.34), channel_id=1, source_target_pairs={{0,192},{1,193},{64,1},{65,0},{128,65},{129,64},{192,129},{193,128... | collective-permute-start | bytes 491528 | tf_op jit(solution)/shard_map/ppermute | solution.py:220
  14.0 3.1 %collective-permute-start.2 = (bf16[320,256]{1,0:T(8,128)(2,1)S(1)}, bf16[320,256]{1,0:T(8,128)(2,1)S(1)}, u32[]{:S(2)}, u32[]{:S(2)}) collective-permute-start(bf16[320,256]{1,0:T(8,128)(2,1)S(1)} %get-tuple-element.35), channel_id=1, source_target_pairs={{0,65},{1,64},{64,129},{65,128},{128,193},{129,192},{192,0},{193,1... | collective-permute-start | bytes 491528 | tf_op jit(solution)/shard_map/ppermute | solution.py:220
  17.1 1.5 %collective-permute-start.3 = (bf16[320,256]{1,0:T(8,128)(2,1)S(1)}, bf16[320,256]{1,0:T(8,128)(2,1)S(1)}, u32[]{:S(2)}, u32[]{:S(2)}) collective-permute-start(bf16[320,256]{1,0:T(8,128)(2,1)S(1)} %get-tuple-element.36), channel_id=1, source_target_pairs={{0,128},{1,129},{64,192},{65,193},{128,1},{129,0},{192,65},{193,64... | collective-permute-start | bytes 491528 | tf_op jit(solution)/shard_map/ppermute | solution.py:220
  18.6 2.7 %collective-permute-start.4 = (bf16[320,256]{1,0:T(8,128)(2,1)S(1)}, bf16[320,256]{1,0:T(8,128)(2,1)S(1)}, u32[]{:S(2)}, u32[]{:S(2)}) collective-permute-start(bf16[320,256]{1,0:T(8,128)(2,1)S(1)} %get-tuple-element.37), channel_id=1, source_target_pairs={{0,129},{1,128},{64,193},{65,192},{128,0},{129,1},{192,64},{193,65... | collective-permute-start | bytes 491528 | tf_op jit(solution)/shard_map/ppermute | solution.py:220
  21.3 2.8 %collective-permute-done.refs_1_ = bf16[320,256]{1,0:T(8,128)(2,1)S(1)} collective-permute-done((bf16[320,256]{1,0:T(8,128)(2,1)S(1)}, bf16[320,256]{1,0:T(8,128)(2,1)S(1)}, u32[]{:S(2)}, u32[]{:S(2)}) %collective-permute-start) | collective-permute-done | bytes 163872 | tf_op jit(solution)/shard_map/ppermute | solution.py:220
  24.1 0.4 collective-permute-start.5
  24.5 8.8 %collective-permute-done.1.refs_2_ = bf16[320,256]{1,0:T(8,128)(2,1)S(1)} collective-permute-done((bf16[320,256]{1,0:T(8,128)(2,1)S(1)}, bf16[320,256]{1,0:T(8,128)(2,1)S(1)}, u32[]{:S(2)}, u32[]{:S(2)}) %collective-permute-start.1) | collective-permute-done | bytes 163872 | tf_op jit(solution)/shard_map/ppermute | solution.py:220
  33.3 0.0 collective-permute-start.6
  33.3 0.0 copy-done
  33.3 0.9 shard_map.47
  34.2 0.0 collective-permute-done.2.refs_3_
  34.2 3.3 %collective-permute-done.3.refs_4_ = bf16[320,256]{1,0:T(8,128)(2,1)S(1)} collective-permute-done((bf16[320,256]{1,0:T(8,128)(2,1)S(1)}, bf16[320,256]{1,0:T(8,128)(2,1)S(1)}, u32[]{:S(2)}, u32[]{:S(2)}) %collective-permute-start.3) | collective-permute-done | bytes 163872 | tf_op jit(solution)/shard_map/ppermute | solution.py:220
  37.5 0.9 collective-permute-done.4.refs_5_
  38.4 2.2 %collective-permute-done.5.refs_6_ = bf16[320,256]{1,0:T(8,128)(2,1)S(1)} collective-permute-done((bf16[320,256]{1,0:T(8,128)(2,1)S(1)}, bf16[320,256]{1,0:T(8,128)(2,1)S(1)}, u32[]{:S(2)}, u32[]{:S(2)}) %collective-permute-start.5) | collective-permute-done | bytes 163872 | tf_op jit(solution)/shard_map/ppermute | solution.py:220
  40.5 1.1 collective-permute-done.6.refs_7_
  41.7 0.1 shard_map.48.refs_8_
  41.7 0.1 collective-permute-start.7
  41.8 1.5 %shard_map.49 = (bf16[640,1280]{1,0:T(8,128)(2,1)}, bf16[2,4,160,256]{3,2,1,0:T(8,128)(2,1)S(1)}) custom-call(s32[1]{0:T(128)} %bitcast.pos_ref, bf16[320,256]{1,0:T(8,128)(2,1)S(1)} %get-tuple-element.32.refs_0_, bf16[320,256]{1,0:T(8,128)(2,1)S(1)} %collective-permute-done.refs_1_, bf16[320,256]{1,0:T(8,128)(2,1)S(1)} %collective-permute-done.1.refs_2_, ...), custom_call_target="tpu_custom_call" | custom-call | flops 419430400 | bytes 3932168 | tf_op jit(solution)/shard_map/pallas_call | solution.py:204
  43.4 0.6 collective-permute-done.7.k_far
  43.9 1.5 %shard_map.50 = bf16[640,1280]{1,0:T(8,128)(2,1)} custom-call(bf16[640,1280]{1,0:T(8,128)(2,1)} %get-tuple-element.42._, bf16[2,4,160,256]{3,2,1,0:T(8,128)(2,1)S(1)} %get-tuple-element.43.q, bf16[2,4,160,256]{3,2,1,0:T(8,128)(2,1)S(1)} %collective-permute-done.7.k_far), custom_call_target="tpu_custom_call", output_to_operand_aliasing={{}: (0, {})} | custom-call | flops 419430400 | bytes 5898240 | tf_op jit(solution)/shard_map/pallas_call | solution.py:204
  45.4 7.4 %all-to-all-start = ((bf16[16,40,1280]{2,1,0:T(8,128)(2,1)}), bf16[16,40,1280]{2,1,0:T(8,128)(2,1)S(1)}, u32[]{:S(2)}, u32[]{:S(2)}) async-start(bf16[16,40,1280]{2,1,0:T(8,128)(2,1)} %bitcast.2), calls=%async_computation | async-start | bytes 3276800 | tf_op jit(solution)/shard_map/all_to_all | solution.py:291
  52.8 3.5 %collective-permute-start.8 = (bf16[160,256]{1,0:T(8,128)(2,1)S(1)}, bf16[160,256]{1,0:T(8,128)(2,1)S(1)}, u32[]{:S(2)}, u32[]{:S(2)}) collective-permute-start(bf16[160,256]{1,0:T(8,128)(2,1)S(1)} %get-tuple-element.44), channel_id=1, source_target_pairs={{0,1},{1,0},{64,65},{65,64},{128,129},{129,128},{192,193},{193,192... | collective-permute-start | bytes 245768 | tf_op jit(solution)/shard_map/ppermute | solution.py:220
  56.4 2.3 %collective-permute-start.9 = (bf16[160,256]{1,0:T(8,128)(2,1)S(1)}, bf16[160,256]{1,0:T(8,128)(2,1)S(1)}, u32[]{:S(2)}, u32[]{:S(2)}) collective-permute-start(bf16[160,256]{1,0:T(8,128)(2,1)S(1)} %get-tuple-element.45), channel_id=1, source_target_pairs={{0,192},{1,193},{64,1},{65,0},{128,65},{129,64},{192,129},{193,128... | collective-permute-start | bytes 245768 | tf_op jit(solution)/shard_map/ppermute | solution.py:220
  58.7 2.7 %collective-permute-start.10 = (bf16[160,256]{1,0:T(8,128)(2,1)S(1)}, bf16[160,256]{1,0:T(8,128)(2,1)S(1)}, u32[]{:S(2)}, u32[]{:S(2)}) collective-permute-start(bf16[160,256]{1,0:T(8,128)(2,1)S(1)} %get-tuple-element.46), channel_id=1, source_target_pairs={{0,65},{1,64},{64,129},{65,128},{128,193},{129,192},{192,0},{193,1... | collective-permute-start | bytes 245768 | tf_op jit(solution)/shard_map/ppermute | solution.py:220
  61.4 0.1 collective-permute-start.11
  61.5 2.9 %collective-permute-done.8.refs_0_.refs_1_ = bf16[160,256]{1,0:T(8,128)(2,1)S(1)} collective-permute-done((bf16[160,256]{1,0:T(8,128)(2,1)S(1)}, bf16[160,256]{1,0:T(8,128)(2,1)S(1)}, u32[]{:S(2)}, u32[]{:S(2)}) %collective-permute-start.8) | collective-permute-done | bytes 81952 | tf_op jit(solution)/shard_map/ppermute | solution.py:220
  64.4 5.5 %collective-permute-done.9.refs_1_.refs_2_ = bf16[160,256]{1,0:T(8,128)(2,1)S(1)} collective-permute-done((bf16[160,256]{1,0:T(8,128)(2,1)S(1)}, bf16[160,256]{1,0:T(8,128)(2,1)S(1)}, u32[]{:S(2)}, u32[]{:S(2)}) %collective-permute-start.9) | collective-permute-done | bytes 81952 | tf_op jit(solution)/shard_map/ppermute | solution.py:220
  69.9 0.0 collective-permute-done.10.refs_2_.refs_3_
  69.9 0.0 collective-permute-done.11.refs_3_.refs_4_
  69.9 5.6 %all-to-all-done.x_ref = bf16[16,40,1280]{2,1,0:T(8,128)(2,1)S(1)} async-done(((bf16[16,40,1280]{2,1,0:T(8,128)(2,1)}), bf16[16,40,1280]{2,1,0:T(8,128)(2,1)S(1)}, u32[]{:S(2)}, u32[]{:S(2)}) %all-to-all-start) | async-done | bytes 1638432 | tf_op jit(solution)/shard_map/all_to_all | solution.py:291
  75.5 1.6 %shard_map.51 = bf16[16,40,1280]{2,1,0:T(8,128)(2,1)} custom-call(bf16[16,40,1280]{2,1,0:T(8,128)(2,1)S(1)} %all-to-all-done.x_ref, bf16[160,256]{1,0:T(8,128)(2,1)S(1)} %collective-permute-done.8.refs_0_.refs_1_, bf16[160,256]{1,0:T(8,128)(2,1)S(1)} %collective-permute-done.9.refs_1_.refs_2_, bf16[160,256]{1,0:T(8,128)(2,1)S(1)} %collective-permute-done.10.refs_2_.refs_3_, ...), custom_call_target="tpu_custom_call" | custom-call | bytes 3932160 | tf_op jit(solution)/shard_map/pallas_call | solution.py:204
  77.1 6.2 %all-to-all-start.1 = ((bf16[16,40,1280]{2,1,0:T(8,128)(2,1)}), bf16[16,40,1280]{2,1,0:T(8,128)(2,1)S(1)}, u32[]{:S(2)}, u32[]{:S(2)}) async-start(bf16[16,40,1280]{2,1,0:T(8,128)(2,1)} %shard_map.51), calls=%async_computation.1 | async-start | bytes 3276800 | tf_op jit(solution)/shard_map/all_to_all | solution.py:301
  83.3 1.2 collective-permute-start.12
  84.6 2.8 %collective-permute-start.13 = (bf16[160,256]{1,0:T(8,128)(2,1)S(1)}, bf16[160,256]{1,0:T(8,128)(2,1)S(1)}, u32[]{:S(2)}, u32[]{:S(2)}) collective-permute-start(bf16[160,256]{1,0:T(8,128)(2,1)S(1)} %get-tuple-element.49), channel_id=1, source_target_pairs={{0,64},{1,65},{64,128},{65,129},{128,192},{129,193},{192,1},{193,0... | collective-permute-start | bytes 245768 | tf_op jit(solution)/shard_map/ppermute | solution.py:220
  87.4 0.4 collective-permute-start.14
  87.8 1.8 %collective-permute-done.12.refs_5_ = bf16[160,256]{1,0:T(8,128)(2,1)S(1)} collective-permute-done((bf16[160,256]{1,0:T(8,128)(2,1)S(1)}, bf16[160,256]{1,0:T(8,128)(2,1)S(1)}, u32[]{:S(2)}, u32[]{:S(2)}) %collective-permute-start.12) | collective-permute-done | bytes 81952 | tf_op jit(solution)/shard_map/ppermute | solution.py:220
  89.7 0.6 collective-permute-done.13.refs_6_
  90.2 1.6 %collective-permute-done.14.refs_7_ = bf16[160,256]{1,0:T(8,128)(2,1)S(1)} collective-permute-done((bf16[160,256]{1,0:T(8,128)(2,1)S(1)}, bf16[160,256]{1,0:T(8,128)(2,1)S(1)}, u32[]{:S(2)}, u32[]{:S(2)}) %collective-permute-start.14) | collective-permute-done | bytes 81952 | tf_op jit(solution)/shard_map/ppermute | solution.py:220
  91.9 0.1 shard_map.52.v_ref
  91.9 0.1 collective-permute-start.15
  92.0 2.1 %collective-permute-done.15._.v_far = bf16[2,4,160,256]{3,2,1,0:T(8,128)(2,1)S(1)} collective-permute-done((bf16[2,4,160,256]{3,2,1,0:T(8,128)(2,1)S(1)}, bf16[2,4,160,256]{3,2,1,0:T(8,128)(2,1)S(1)}, u32[]{:S(2)}, u32[]{:S(2)}) %collective-permute-start.15) | collective-permute-done | bytes 655392 | tf_op jit(solution)/shard_map/ppermute | solution.py:225
  94.1 9.7 %all-to-all-done.1 = bf16[16,40,1280]{2,1,0:T(8,128)(2,1)S(1)} async-done(((bf16[16,40,1280]{2,1,0:T(8,128)(2,1)}), bf16[16,40,1280]{2,1,0:T(8,128)(2,1)S(1)}, u32[]{:S(2)}, u32[]{:S(2)}) %all-to-all-start.1) | async-done | bytes 1638432 | tf_op jit(solution)/shard_map/all_to_all | solution.py:301
  103.8 0.7 shard_map.54
  104.5 0.0 copy-start.1
  104.5 3.6 %collective-permute-start.16 = (bf16[160,256]{1,0:T(8,128)(2,1)S(1)}, bf16[160,256]{1,0:T(8,128)(2,1)S(1)}, u32[]{:S(2)}, u32[]{:S(2)}) collective-permute-start(bf16[160,256]{1,0:T(8,128)(2,1)S(1)} %get-tuple-element.52), channel_id=1, source_target_pairs={{0,1},{1,0},{64,65},{65,64},{128,129},{129,128},{192,193},{193,192... | collective-permute-start | bytes 245768 | tf_op jit(solution)/shard_map/ppermute | solution.py:220
  108.2 2.4 %collective-permute-start.17 = (bf16[160,256]{1,0:T(8,128)(2,1)S(1)}, bf16[160,256]{1,0:T(8,128)(2,1)S(1)}, u32[]{:S(2)}, u32[]{:S(2)}) collective-permute-start(bf16[160,256]{1,0:T(8,128)(2,1)S(1)} %get-tuple-element.53), channel_id=1, source_target_pairs={{0,192},{1,193},{64,1},{65,0},{128,65},{129,64},{192,129},{193,128... | collective-permute-start | bytes 245768 | tf_op jit(solution)/shard_map/ppermute | solution.py:220
  110.5 0.4 collective-permute-start.18
  110.9 0.7 shard_map.55
  111.6 2.4 %collective-permute-start.19 = (bf16[160,256]{1,0:T(8,128)(2,1)S(1)}, bf16[160,256]{1,0:T(8,128)(2,1)S(1)}, u32[]{:S(2)}, u32[]{:S(2)}) collective-permute-start(bf16[160,256]{1,0:T(8,128)(2,1)S(1)} %get-tuple-element.55), channel_id=1, source_target_pairs={{0,65},{1,64},{64,129},{65,128},{128,193},{129,192},{192,0},{193,1... | collective-permute-start | bytes 245768 | tf_op jit(solution)/shard_map/ppermute | solution.py:220
  114.0 0.9 collective-permute-start.20
  114.9 0.0 collective-permute-done.16.refs_1_
  114.9 3.2 %collective-permute-start.21 = (bf16[160,256]{1,0:T(8,128)(2,1)S(1)}, bf16[160,256]{1,0:T(8,128)(2,1)S(1)}, u32[]{:S(2)}, u32[]{:S(2)}) collective-permute-start(bf16[160,256]{1,0:T(8,128)(2,1)S(1)} %get-tuple-element.57), channel_id=1, source_target_pairs={{0,129},{1,128},{64,193},{65,192},{128,0},{129,1},{192,64},{193,65... | collective-permute-start | bytes 245768 | tf_op jit(solution)/shard_map/ppermute | solution.py:220
  118.1 1.3 %collective-permute-done.17.refs_2_ = bf16[160,256]{1,0:T(8,128)(2,1)S(1)} collective-permute-done((bf16[160,256]{1,0:T(8,128)(2,1)S(1)}, bf16[160,256]{1,0:T(8,128)(2,1)S(1)}, u32[]{:S(2)}, u32[]{:S(2)}) %collective-permute-start.17) | collective-permute-done | bytes 81952 | tf_op jit(solution)/shard_map/ppermute | solution.py:220
  119.4 0.7 collective-permute-start.22
  120.1 0.0 collective-permute-done.18.refs_3_
  120.1 0.0 collective-permute-done.19.refs_4_
  120.2 0.7 collective-permute-done.20.refs_5_
  120.9 2.3 %collective-permute-done.21.refs_6_ = bf16[160,256]{1,0:T(8,128)(2,1)S(1)} collective-permute-done((bf16[160,256]{1,0:T(8,128)(2,1)S(1)}, bf16[160,256]{1,0:T(8,128)(2,1)S(1)}, u32[]{:S(2)}, u32[]{:S(2)}) %collective-permute-start.21) | collective-permute-done | bytes 81952 | tf_op jit(solution)/shard_map/ppermute | solution.py:220
  123.2 1.9 %collective-permute-done.22.refs_7_ = bf16[160,256]{1,0:T(8,128)(2,1)S(1)} collective-permute-done((bf16[160,256]{1,0:T(8,128)(2,1)S(1)}, bf16[160,256]{1,0:T(8,128)(2,1)S(1)}, u32[]{:S(2)}, u32[]{:S(2)}) %collective-permute-start.22) | collective-permute-done | bytes 81952 | tf_op jit(solution)/shard_map/ppermute | solution.py:220
  125.1 0.0 copy-done.1
  125.1 1.7 %shard_map.56 = f32[4,160,768]{2,1,0:T(8,128)} custom-call(s32[1]{0:T(128)} %bitcast.pos_ref, bf16[512,768]{1,0:T(8,128)(2,1)S(1)} %copy-done.1, bf16[160,256]{1,0:T(8,128)(2,1)S(1)} %get-tuple-element.51.refs_0_, bf16[160,256]{1,0:T(8,128)(2,1)S(1)} %collective-permute-done.16.refs_1_, bf16[160,256]{1,0:T(8,128)(2,1)S(1)} %collective-permute-done.17.refs_2_, ...), custom_call_target="tpu_custom_call" | custom-call | flops 503316480 | bytes 2883592 | tf_op jit(solution)/shard_map/pallas_call | solution.py:204
  (3 shorter events, 0.0 us)
Async XLA Ops:
  0.0 0.7 copy-start.2
  0.7 32.6 %copy-start = (bf16[768,3,512]{2,0,1:T(8,128)(2,1)S(1)}, bf16[768,3,512]{2,0,1:T(8,128)(2,1)}, u32[]{:S(2)}) copy-start(bf16[768,3,512]{2,0,1:T(8,128)(2,1)} %param.6) | copy-start | bytes 7077892
  4.8 19.3 %collective-permute-start = (bf16[320,256]{1,0:T(8,128)(2,1)S(1)}, bf16[320,256]{1,0:T(8,128)(2,1)S(1)}, u32[]{:S(2)}, u32[]{:S(2)}) collective-permute-start(bf16[320,256]{1,0:T(8,128)(2,1)S(1)} %get-tuple-element.33), channel_id=1, source_target_pairs={{0,1},{1,0},{64,65},{65,64},{128,129},{129,128},{192,193},{193,192... | collective-permute-start | bytes 491528 | tf_op jit(solution)/shard_map/ppermute | solution.py:220
  12.1 21.2 %collective-permute-start.1 = (bf16[320,256]{1,0:T(8,128)(2,1)S(1)}, bf16[320,256]{1,0:T(8,128)(2,1)S(1)}, u32[]{:S(2)}, u32[]{:S(2)}) collective-permute-start(bf16[320,256]{1,0:T(8,128)(2,1)S(1)} %get-tuple-element.34), channel_id=1, source_target_pairs={{0,192},{1,193},{64,1},{65,0},{128,65},{129,64},{192,129},{193,128... | collective-permute-start | bytes 491528 | tf_op jit(solution)/shard_map/ppermute | solution.py:220
  14.0 20.2 %collective-permute-start.2 = (bf16[320,256]{1,0:T(8,128)(2,1)S(1)}, bf16[320,256]{1,0:T(8,128)(2,1)S(1)}, u32[]{:S(2)}, u32[]{:S(2)}) collective-permute-start(bf16[320,256]{1,0:T(8,128)(2,1)S(1)} %get-tuple-element.35), channel_id=1, source_target_pairs={{0,65},{1,64},{64,129},{65,128},{128,193},{129,192},{192,0},{193,1... | collective-permute-start | bytes 491528 | tf_op jit(solution)/shard_map/ppermute | solution.py:220
  17.1 20.3 %collective-permute-start.3 = (bf16[320,256]{1,0:T(8,128)(2,1)S(1)}, bf16[320,256]{1,0:T(8,128)(2,1)S(1)}, u32[]{:S(2)}, u32[]{:S(2)}) collective-permute-start(bf16[320,256]{1,0:T(8,128)(2,1)S(1)} %get-tuple-element.36), channel_id=1, source_target_pairs={{0,128},{1,129},{64,192},{65,193},{128,1},{129,0},{192,65},{193,64... | collective-permute-start | bytes 491528 | tf_op jit(solution)/shard_map/ppermute | solution.py:220
  18.6 19.8 %collective-permute-start.4 = (bf16[320,256]{1,0:T(8,128)(2,1)S(1)}, bf16[320,256]{1,0:T(8,128)(2,1)S(1)}, u32[]{:S(2)}, u32[]{:S(2)}) collective-permute-start(bf16[320,256]{1,0:T(8,128)(2,1)S(1)} %get-tuple-element.37), channel_id=1, source_target_pairs={{0,129},{1,128},{64,193},{65,192},{128,0},{129,1},{192,64},{193,65... | collective-permute-start | bytes 491528 | tf_op jit(solution)/shard_map/ppermute | solution.py:220
  24.1 16.4 %collective-permute-start.5 = (bf16[320,256]{1,0:T(8,128)(2,1)S(1)}, bf16[320,256]{1,0:T(8,128)(2,1)S(1)}, u32[]{:S(2)}, u32[]{:S(2)}) collective-permute-start(bf16[320,256]{1,0:T(8,128)(2,1)S(1)} %get-tuple-element.38), channel_id=1, source_target_pairs={{0,64},{1,65},{64,128},{65,129},{128,192},{129,193},{192,1},{193,0... | collective-permute-start | bytes 491528 | tf_op jit(solution)/shard_map/ppermute | solution.py:220
  33.3 8.4 %collective-permute-start.6 = (bf16[320,256]{1,0:T(8,128)(2,1)S(1)}, bf16[320,256]{1,0:T(8,128)(2,1)S(1)}, u32[]{:S(2)}, u32[]{:S(2)}) collective-permute-start(bf16[320,256]{1,0:T(8,128)(2,1)S(1)} %get-tuple-element.39), channel_id=1, source_target_pairs={{0,193},{1,192},{64,0},{65,1},{128,64},{129,65},{192,128},{193,129... | collective-permute-start | bytes 491528 | tf_op jit(solution)/shard_map/ppermute | solution.py:220
  41.7 2.2 %collective-permute-start.7 = (bf16[2,4,160,256]{3,2,1,0:T(8,128)(2,1)S(1)}, bf16[2,4,160,256]{3,2,1,0:T(8,128)(2,1)S(1)}, u32[]{:S(2)}, u32[]{:S(2)}) collective-permute-start(bf16[2,4,160,256]{3,2,1,0:T(8,128)(2,1)S(1)} %shard_map.48.refs_8_), channel_id=1, source_target_pairs={{0,32},{32,0},{1,33},{33,1},{2,34},{34,2},{3,35},{35,3},{4,36},{36... | collective-permute-start | bytes 1966088 | tf_op jit(solution)/shard_map/ppermute | solution.py:225
  45.4 30.0 %all-to-all-start = ((bf16[16,40,1280]{2,1,0:T(8,128)(2,1)}), bf16[16,40,1280]{2,1,0:T(8,128)(2,1)S(1)}, u32[]{:S(2)}, u32[]{:S(2)}) async-start(bf16[16,40,1280]{2,1,0:T(8,128)(2,1)} %bitcast.2), calls=%async_computation | async-start | bytes 3276800 | tf_op jit(solution)/shard_map/all_to_all | solution.py:291
  52.8 11.6 %collective-permute-start.8 = (bf16[160,256]{1,0:T(8,128)(2,1)S(1)}, bf16[160,256]{1,0:T(8,128)(2,1)S(1)}, u32[]{:S(2)}, u32[]{:S(2)}) collective-permute-start(bf16[160,256]{1,0:T(8,128)(2,1)S(1)} %get-tuple-element.44), channel_id=1, source_target_pairs={{0,1},{1,0},{64,65},{65,64},{128,129},{129,128},{192,193},{193,192... | collective-permute-start | bytes 245768 | tf_op jit(solution)/shard_map/ppermute | solution.py:220
  56.4 13.5 %collective-permute-start.9 = (bf16[160,256]{1,0:T(8,128)(2,1)S(1)}, bf16[160,256]{1,0:T(8,128)(2,1)S(1)}, u32[]{:S(2)}, u32[]{:S(2)}) collective-permute-start(bf16[160,256]{1,0:T(8,128)(2,1)S(1)} %get-tuple-element.45), channel_id=1, source_target_pairs={{0,192},{1,193},{64,1},{65,0},{128,65},{129,64},{192,129},{193,128... | collective-permute-start | bytes 245768 | tf_op jit(solution)/shard_map/ppermute | solution.py:220
  58.7 11.2 %collective-permute-start.10 = (bf16[160,256]{1,0:T(8,128)(2,1)S(1)}, bf16[160,256]{1,0:T(8,128)(2,1)S(1)}, u32[]{:S(2)}, u32[]{:S(2)}) collective-permute-start(bf16[160,256]{1,0:T(8,128)(2,1)S(1)} %get-tuple-element.46), channel_id=1, source_target_pairs={{0,65},{1,64},{64,129},{65,128},{128,193},{129,192},{192,0},{193,1... | collective-permute-start | bytes 245768 | tf_op jit(solution)/shard_map/ppermute | solution.py:220
  61.4 8.5 %collective-permute-start.11 = (bf16[160,256]{1,0:T(8,128)(2,1)S(1)}, bf16[160,256]{1,0:T(8,128)(2,1)S(1)}, u32[]{:S(2)}, u32[]{:S(2)}) collective-permute-start(bf16[160,256]{1,0:T(8,128)(2,1)S(1)} %get-tuple-element.47), channel_id=1, source_target_pairs={{0,128},{1,129},{64,192},{65,193},{128,1},{129,0},{192,65},{193,64... | collective-permute-start | bytes 245768 | tf_op jit(solution)/shard_map/ppermute | solution.py:220
  77.1 26.7 %all-to-all-start.1 = ((bf16[16,40,1280]{2,1,0:T(8,128)(2,1)}), bf16[16,40,1280]{2,1,0:T(8,128)(2,1)S(1)}, u32[]{:S(2)}, u32[]{:S(2)}) async-start(bf16[16,40,1280]{2,1,0:T(8,128)(2,1)} %shard_map.51), calls=%async_computation.1 | async-start | bytes 3276800 | tf_op jit(solution)/shard_map/all_to_all | solution.py:301
  83.3 6.3 %collective-permute-start.12 = (bf16[160,256]{1,0:T(8,128)(2,1)S(1)}, bf16[160,256]{1,0:T(8,128)(2,1)S(1)}, u32[]{:S(2)}, u32[]{:S(2)}) collective-permute-start(bf16[160,256]{1,0:T(8,128)(2,1)S(1)} %get-tuple-element.48), channel_id=1, source_target_pairs={{0,129},{1,128},{64,193},{65,192},{128,0},{129,1},{192,64},{193,65... | collective-permute-start | bytes 245768 | tf_op jit(solution)/shard_map/ppermute | solution.py:220
  84.6 5.7 %collective-permute-start.13 = (bf16[160,256]{1,0:T(8,128)(2,1)S(1)}, bf16[160,256]{1,0:T(8,128)(2,1)S(1)}, u32[]{:S(2)}, u32[]{:S(2)}) collective-permute-start(bf16[160,256]{1,0:T(8,128)(2,1)S(1)} %get-tuple-element.49), channel_id=1, source_target_pairs={{0,64},{1,65},{64,128},{65,129},{128,192},{129,193},{192,1},{193,0... | collective-permute-start | bytes 245768 | tf_op jit(solution)/shard_map/ppermute | solution.py:220
  87.4 4.4 %collective-permute-start.14 = (bf16[160,256]{1,0:T(8,128)(2,1)S(1)}, bf16[160,256]{1,0:T(8,128)(2,1)S(1)}, u32[]{:S(2)}, u32[]{:S(2)}) collective-permute-start(bf16[160,256]{1,0:T(8,128)(2,1)S(1)} %get-tuple-element.50), channel_id=1, source_target_pairs={{0,193},{1,192},{64,0},{65,1},{128,64},{129,65},{192,128},{193,129... | collective-permute-start | bytes 245768 | tf_op jit(solution)/shard_map/ppermute | solution.py:220
  91.9 2.2 %collective-permute-start.15 = (bf16[2,4,160,256]{3,2,1,0:T(8,128)(2,1)S(1)}, bf16[2,4,160,256]{3,2,1,0:T(8,128)(2,1)S(1)}, u32[]{:S(2)}, u32[]{:S(2)}) collective-permute-start(bf16[2,4,160,256]{3,2,1,0:T(8,128)(2,1)S(1)} %shard_map.52.v_ref), channel_id=1, source_target_pairs={{0,32},{32,0},{1,33},{33,1},{2,34},{34,2},{3,35},{35,3},{4,36},{36... | collective-permute-start | bytes 1966088 | tf_op jit(solution)/shard_map/ppermute | solution.py:225
  104.5 20.5 %copy-start.1 = (bf16[512,768]{1,0:T(8,128)(2,1)S(1)}, bf16[512,768]{1,0:T(8,128)(2,1)}, u32[]{:S(2)}) copy-start(bf16[512,768]{1,0:T(8,128)(2,1)} %w_ref.1) | copy-start | bytes 2359300
  104.5 10.4 %collective-permute-start.16 = (bf16[160,256]{1,0:T(8,128)(2,1)S(1)}, bf16[160,256]{1,0:T(8,128)(2,1)S(1)}, u32[]{:S(2)}, u32[]{:S(2)}) collective-permute-start(bf16[160,256]{1,0:T(8,128)(2,1)S(1)} %get-tuple-element.52), channel_id=1, source_target_pairs={{0,1},{1,0},{64,65},{65,64},{128,129},{129,128},{192,193},{193,192... | collective-permute-start | bytes 245768 | tf_op jit(solution)/shard_map/ppermute | solution.py:220
  108.2 11.3 %collective-permute-start.17 = (bf16[160,256]{1,0:T(8,128)(2,1)S(1)}, bf16[160,256]{1,0:T(8,128)(2,1)S(1)}, u32[]{:S(2)}, u32[]{:S(2)}) collective-permute-start(bf16[160,256]{1,0:T(8,128)(2,1)S(1)} %get-tuple-element.53), channel_id=1, source_target_pairs={{0,192},{1,193},{64,1},{65,0},{128,65},{129,64},{192,129},{193,128... | collective-permute-start | bytes 245768 | tf_op jit(solution)/shard_map/ppermute | solution.py:220
  110.5 9.6 %collective-permute-start.18 = (bf16[160,256]{1,0:T(8,128)(2,1)S(1)}, bf16[160,256]{1,0:T(8,128)(2,1)S(1)}, u32[]{:S(2)}, u32[]{:S(2)}) collective-permute-start(bf16[160,256]{1,0:T(8,128)(2,1)S(1)} %get-tuple-element.54), channel_id=1, source_target_pairs={{0,193},{1,192},{64,0},{65,1},{128,64},{129,65},{192,128},{193,129... | collective-permute-start | bytes 245768 | tf_op jit(solution)/shard_map/ppermute | solution.py:220
  111.6 8.6 %collective-permute-start.19 = (bf16[160,256]{1,0:T(8,128)(2,1)S(1)}, bf16[160,256]{1,0:T(8,128)(2,1)S(1)}, u32[]{:S(2)}, u32[]{:S(2)}) collective-permute-start(bf16[160,256]{1,0:T(8,128)(2,1)S(1)} %get-tuple-element.55), channel_id=1, source_target_pairs={{0,65},{1,64},{64,129},{65,128},{128,193},{129,192},{192,0},{193,1... | collective-permute-start | bytes 245768 | tf_op jit(solution)/shard_map/ppermute | solution.py:220
  114.0 6.9 %collective-permute-start.20 = (bf16[160,256]{1,0:T(8,128)(2,1)S(1)}, bf16[160,256]{1,0:T(8,128)(2,1)S(1)}, u32[]{:S(2)}, u32[]{:S(2)}) collective-permute-start(bf16[160,256]{1,0:T(8,128)(2,1)S(1)} %get-tuple-element.56), channel_id=1, source_target_pairs={{0,128},{1,129},{64,192},{65,193},{128,1},{129,0},{192,65},{193,64... | collective-permute-start | bytes 245768 | tf_op jit(solution)/shard_map/ppermute | solution.py:220
  114.9 8.3 %collective-permute-start.21 = (bf16[160,256]{1,0:T(8,128)(2,1)S(1)}, bf16[160,256]{1,0:T(8,128)(2,1)S(1)}, u32[]{:S(2)}, u32[]{:S(2)}) collective-permute-start(bf16[160,256]{1,0:T(8,128)(2,1)S(1)} %get-tuple-element.57), channel_id=1, source_target_pairs={{0,129},{1,128},{64,193},{65,192},{128,0},{129,1},{192,64},{193,65... | collective-permute-start | bytes 245768 | tf_op jit(solution)/shard_map/ppermute | solution.py:220
  119.4 5.7 %collective-permute-start.22 = (bf16[160,256]{1,0:T(8,128)(2,1)S(1)}, bf16[160,256]{1,0:T(8,128)(2,1)S(1)}, u32[]{:S(2)}, u32[]{:S(2)}) collective-permute-start(bf16[160,256]{1,0:T(8,128)(2,1)S(1)} %get-tuple-element.58), channel_id=1, source_target_pairs={{0,64},{1,65},{64,128},{65,129},{128,192},{129,193},{192,1},{193,0... | collective-permute-start | bytes 245768 | tf_op jit(solution)/shard_map/ppermute | solution.py:220

commit v13 on v11

--- a/solution.py
+++ b/solution.py
@@ -51,7 +51,7 @@
     x_copies = [pltpu.make_async_copy(x_hbm.at[r], x_ref.at[r], x_sem.at[r]) for r in range(seqs)]
     w_copies = [pltpu.make_async_copy(w_hbm.at[c], w_ref.at[c], w_sem.at[c]) for c in range(2)]
     gain_copy = pltpu.make_async_copy(gain_hbm, gain_ref, gain_sem)
-    for copy in (x_copies[0], gain_copy, *x_copies[1:], w_copies[1], w_copies[0]):
+    for copy in (x_copies[0], w_copies[1], gain_copy, *x_copies[1:], w_copies[0]):
         copy.start()
     def norm(r):
         x = x_ref[r].astype(F32)
@@ -79,11 +79,10 @@
         project(1, r)
     for r in range(seqs // 2, seqs):
         norm(r)
-    w_copies[0].wait()
-    for r in range(0, seqs // 2, 2):
-        project(0, r)
     for r in range(seqs // 2, seqs, 2):
         project(1, r)
+    w_copies[0].wait()
+    for r in range(0, seqs, 2):
         project(0, r)
     pos = pos_ref[0]
     for c in (1, 0):

time: 127 us -> 127 us (level)
  no operation moved by 1% of the time
where the time goes in v13:
time: 127 us; the launch traced here: 126 us
  starting transfers between devices  57.4 us (45%)
  waiting for transfers between devices  55.7 us (44%)
  Pallas kernels  12.1 us (10%)
    ppermute x21, starting transfers between devices, along_ring(): got.append(lax.ppermute(part, ('z', 'w'), pairs) if s else part)  43.5 us
    ppermute x21, waiting for transfers between devices, along_ring(): got.append(lax.ppermute(part, ('z', 'w'), pairs) if s else part)  37.8 us
    pallas_call x11, Pallas kernels, call(): pl.pallas_call(kernel, out_shape=out_shape, in_specs=specs, out_specs=out...  12.1 us
    all_to_all x1, waiting for transfers between devices, shards(): lax.all_to_all(probs, ('x', 'y'), 0, 0, tiled=True).reshape(half, full)  9.68 us
    all_to_all x1, starting transfers between devices, shards(): terms = lax.all_to_all(term.reshape(chunk), ('x', 'y'), 0, 0, tiled=True)  7.44 us
    all_to_all x1, starting transfers between devices, shards(): lax.all_to_all(probs, ('x', 'y'), 0, 0, tiled=True).reshape(half, full)  6.25 us
    all_to_all x1, waiting for transfers between devices, shards(): terms = lax.all_to_all(term.reshape(chunk), ('x', 'y'), 0, 0, tiled=True)  5.58 us
    ppermute x2, waiting for transfers between devices, other_core(): return lax.ppermute(a, 'c', [(0, 1), (1, 0)])  2.65 us
  transfers between devices with their start and end apart: 25, of which 19 were waited for; matrix products, arithmetic and copies ran while one was open for 0% of the time, Pallas kernels for 2%

profile of v13, /device:TPU:6, one launch (start us, length us, event | category | flops | bytes accessed | tf_op | source)
XLA Modules:
  0.0 126.2 jit_solution(10407775972842905179)
XLA Ops:
  0.0 0.7 copy-done.2
  0.7 3.4 %shard_map.46 = (bf16[320,256]{1,0:T(8,128)(2,1)S(1)}, bf16[320,256]{1,0:T(8,128)(2,1)S(1)}, bf16[320,256]{1,0:T(8,128)(2,1)S(1)}, bf16[320,256]{1,0:T(8,128)(2,...) custom-call(s32[1]{0:T(128)} %bitcast.pos_ref, ...), custom_call_target="tpu_custom_call" | custom-call | flops 1006632960 | bytes 6690824 | tf_op jit(solution)/shard_map/pallas_call | solution.py:200
  4.1 7.3 %collective-permute-start = (bf16[320,256]{1,0:T(8,128)(2,1)S(1)}, bf16[320,256]{1,0:T(8,128)(2,1)S(1)}, u32[]{:S(2)}, u32[]{:S(2)}) collective-permute-start(bf16[320,256]{1,0:T(8,128)(2,1)S(1)} %get-tuple-element.33), channel_id=1, source_target_pairs={{0,1},{1,0},{64,65},{65,64},{128,129},{129,128},{192,193},{193,192... | collective-permute-start | bytes 491528 | tf_op jit(solution)/shard_map/ppermute | solution.py:216
  11.4 1.9 %collective-permute-start.1 = (bf16[320,256]{1,0:T(8,128)(2,1)S(1)}, bf16[320,256]{1,0:T(8,128)(2,1)S(1)}, u32[]{:S(2)}, u32[]{:S(2)}) collective-permute-start(bf16[320,256]{1,0:T(8,128)(2,1)S(1)} %get-tuple-element.34), channel_id=1, source_target_pairs={{0,192},{1,193},{64,1},{65,0},{128,65},{129,64},{192,129},{193,128... | collective-permute-start | bytes 491528 | tf_op jit(solution)/shard_map/ppermute | solution.py:216
  13.3 3.1 %collective-permute-start.2 = (bf16[320,256]{1,0:T(8,128)(2,1)S(1)}, bf16[320,256]{1,0:T(8,128)(2,1)S(1)}, u32[]{:S(2)}, u32[]{:S(2)}) collective-permute-start(bf16[320,256]{1,0:T(8,128)(2,1)S(1)} %get-tuple-element.35), channel_id=1, source_target_pairs={{0,65},{1,64},{64,129},{65,128},{128,193},{129,192},{192,0},{193,1... | collective-permute-start | bytes 491528 | tf_op jit(solution)/shard_map/ppermute | solution.py:216
  16.4 1.5 %collective-permute-start.3 = (bf16[320,256]{1,0:T(8,128)(2,1)S(1)}, bf16[320,256]{1,0:T(8,128)(2,1)S(1)}, u32[]{:S(2)}, u32[]{:S(2)}) collective-permute-start(bf16[320,256]{1,0:T(8,128)(2,1)S(1)} %get-tuple-element.36), channel_id=1, source_target_pairs={{0,128},{1,129},{64,192},{65,193},{128,1},{129,0},{192,65},{193,64... | collective-permute-start | bytes 491528 | tf_op jit(solution)/shard_map/ppermute | solution.py:216
  17.9 2.7 %collective-permute-start.4 = (bf16[320,256]{1,0:T(8,128)(2,1)S(1)}, bf16[320,256]{1,0:T(8,128)(2,1)S(1)}, u32[]{:S(2)}, u32[]{:S(2)}) collective-permute-start(bf16[320,256]{1,0:T(8,128)(2,1)S(1)} %get-tuple-element.37), channel_id=1, source_target_pairs={{0,129},{1,128},{64,193},{65,192},{128,0},{129,1},{192,64},{193,65... | collective-permute-start | bytes 491528 | tf_op jit(solution)/shard_map/ppermute | solution.py:216
  20.6 2.8 %collective-permute-done.refs_1_ = bf16[320,256]{1,0:T(8,128)(2,1)S(1)} collective-permute-done((bf16[320,256]{1,0:T(8,128)(2,1)S(1)}, bf16[320,256]{1,0:T(8,128)(2,1)S(1)}, u32[]{:S(2)}, u32[]{:S(2)}) %collective-permute-start) | collective-permute-done | bytes 163872 | tf_op jit(solution)/shard_map/ppermute | solution.py:216
  23.4 0.4 collective-permute-start.5
  23.7 8.8 %collective-permute-done.1.refs_2_ = bf16[320,256]{1,0:T(8,128)(2,1)S(1)} collective-permute-done((bf16[320,256]{1,0:T(8,128)(2,1)S(1)}, bf16[320,256]{1,0:T(8,128)(2,1)S(1)}, u32[]{:S(2)}, u32[]{:S(2)}) %collective-permute-start.1) | collective-permute-done | bytes 163872 | tf_op jit(solution)/shard_map/ppermute | solution.py:216
  32.6 0.0 collective-permute-start.6
  32.6 0.0 copy-done
  32.6 0.9 shard_map.47
  33.5 0.0 collective-permute-done.2.refs_3_
  33.5 3.3 %collective-permute-done.3.refs_4_ = bf16[320,256]{1,0:T(8,128)(2,1)S(1)} collective-permute-done((bf16[320,256]{1,0:T(8,128)(2,1)S(1)}, bf16[320,256]{1,0:T(8,128)(2,1)S(1)}, u32[]{:S(2)}, u32[]{:S(2)}) %collective-permute-start.3) | collective-permute-done | bytes 163872 | tf_op jit(solution)/shard_map/ppermute | solution.py:216
  36.8 0.9 collective-permute-done.4.refs_5_
  37.7 2.2 %collective-permute-done.5.refs_6_ = bf16[320,256]{1,0:T(8,128)(2,1)S(1)} collective-permute-done((bf16[320,256]{1,0:T(8,128)(2,1)S(1)}, bf16[320,256]{1,0:T(8,128)(2,1)S(1)}, u32[]{:S(2)}, u32[]{:S(2)}) %collective-permute-start.5) | collective-permute-done | bytes 163872 | tf_op jit(solution)/shard_map/ppermute | solution.py:216
  39.8 1.1 collective-permute-done.6.refs_7_
  40.9 0.1 shard_map.48.refs_8_
  41.0 0.1 collective-permute-start.7
  41.1 1.5 %shard_map.49 = (bf16[640,1280]{1,0:T(8,128)(2,1)}, bf16[2,4,160,256]{3,2,1,0:T(8,128)(2,1)S(1)}) custom-call(s32[1]{0:T(128)} %bitcast.pos_ref, bf16[320,256]{1,0:T(8,128)(2,1)S(1)} %get-tuple-element.32.refs_0_, bf16[320,256]{1,0:T(8,128)(2,1)S(1)} %collective-permute-done.refs_1_, bf16[320,256]{1,0:T(8,128)(2,1)S(1)} %collective-permute-done.1.refs_2_, ...), custom_call_target="tpu_custom_call" | custom-call | flops 419430400 | bytes 3932168 | tf_op jit(solution)/shard_map/pallas_call | solution.py:200
  42.6 0.6 collective-permute-done.7.k_far
  43.2 1.5 %shard_map.50 = bf16[640,1280]{1,0:T(8,128)(2,1)} custom-call(bf16[640,1280]{1,0:T(8,128)(2,1)} %get-tuple-element.42._, bf16[2,4,160,256]{3,2,1,0:T(8,128)(2,1)S(1)} %get-tuple-element.43.q, bf16[2,4,160,256]{3,2,1,0:T(8,128)(2,1)S(1)} %collective-permute-done.7.k_far), custom_call_target="tpu_custom_call", output_to_operand_aliasing={{}: (0, {})} | custom-call | flops 419430400 | bytes 5898240 | tf_op jit(solution)/shard_map/pallas_call | solution.py:200
  44.7 7.4 %all-to-all-start = ((bf16[16,40,1280]{2,1,0:T(8,128)(2,1)}), bf16[16,40,1280]{2,1,0:T(8,128)(2,1)S(1)}, u32[]{:S(2)}, u32[]{:S(2)}) async-start(bf16[16,40,1280]{2,1,0:T(8,128)(2,1)} %bitcast.2), calls=%async_computation | async-start | bytes 3276800 | tf_op jit(solution)/shard_map/all_to_all | solution.py:287
  52.1 3.5 %collective-permute-start.8 = (bf16[160,256]{1,0:T(8,128)(2,1)S(1)}, bf16[160,256]{1,0:T(8,128)(2,1)S(1)}, u32[]{:S(2)}, u32[]{:S(2)}) collective-permute-start(bf16[160,256]{1,0:T(8,128)(2,1)S(1)} %get-tuple-element.44), channel_id=1, source_target_pairs={{0,1},{1,0},{64,65},{65,64},{128,129},{129,128},{192,193},{193,192... | collective-permute-start | bytes 245768 | tf_op jit(solution)/shard_map/ppermute | solution.py:216
  55.7 2.3 %collective-permute-start.9 = (bf16[160,256]{1,0:T(8,128)(2,1)S(1)}, bf16[160,256]{1,0:T(8,128)(2,1)S(1)}, u32[]{:S(2)}, u32[]{:S(2)}) collective-permute-start(bf16[160,256]{1,0:T(8,128)(2,1)S(1)} %get-tuple-element.45), channel_id=1, source_target_pairs={{0,192},{1,193},{64,1},{65,0},{128,65},{129,64},{192,129},{193,128... | collective-permute-start | bytes 245768 | tf_op jit(solution)/shard_map/ppermute | solution.py:216
  58.0 2.7 %collective-permute-start.10 = (bf16[160,256]{1,0:T(8,128)(2,1)S(1)}, bf16[160,256]{1,0:T(8,128)(2,1)S(1)}, u32[]{:S(2)}, u32[]{:S(2)}) collective-permute-start(bf16[160,256]{1,0:T(8,128)(2,1)S(1)} %get-tuple-element.46), channel_id=1, source_target_pairs={{0,65},{1,64},{64,129},{65,128},{128,193},{129,192},{192,0},{193,1... | collective-permute-start | bytes 245768 | tf_op jit(solution)/shard_map/ppermute | solution.py:216
  60.7 0.1 collective-permute-start.11
  60.8 2.9 %collective-permute-done.8.refs_0_.refs_1_ = bf16[160,256]{1,0:T(8,128)(2,1)S(1)} collective-permute-done((bf16[160,256]{1,0:T(8,128)(2,1)S(1)}, bf16[160,256]{1,0:T(8,128)(2,1)S(1)}, u32[]{:S(2)}, u32[]{:S(2)}) %collective-permute-start.8) | collective-permute-done | bytes 81952 | tf_op jit(solution)/shard_map/ppermute | solution.py:216
  63.7 5.5 %collective-permute-done.9.refs_1_.refs_2_ = bf16[160,256]{1,0:T(8,128)(2,1)S(1)} collective-permute-done((bf16[160,256]{1,0:T(8,128)(2,1)S(1)}, bf16[160,256]{1,0:T(8,128)(2,1)S(1)}, u32[]{:S(2)}, u32[]{:S(2)}) %collective-permute-start.9) | collective-permute-done | bytes 81952 | tf_op jit(solution)/shard_map/ppermute | solution.py:216
  69.2 0.0 collective-permute-done.10.refs_2_.refs_3_
  69.2 0.0 collective-permute-done.11.refs_3_.refs_4_
  69.2 5.6 %all-to-all-done.x_ref = bf16[16,40,1280]{2,1,0:T(8,128)(2,1)S(1)} async-done(((bf16[16,40,1280]{2,1,0:T(8,128)(2,1)}), bf16[16,40,1280]{2,1,0:T(8,128)(2,1)S(1)}, u32[]{:S(2)}, u32[]{:S(2)}) %all-to-all-start) | async-done | bytes 1638432 | tf_op jit(solution)/shard_map/all_to_all | solution.py:287
  74.7 1.6 %shard_map.51 = bf16[16,40,1280]{2,1,0:T(8,128)(2,1)} custom-call(bf16[16,40,1280]{2,1,0:T(8,128)(2,1)S(1)} %all-to-all-done.x_ref, bf16[160,256]{1,0:T(8,128)(2,1)S(1)} %collective-permute-done.8.refs_0_.refs_1_, bf16[160,256]{1,0:T(8,128)(2,1)S(1)} %collective-permute-done.9.refs_1_.refs_2_, bf16[160,256]{1,0:T(8,128)(2,1)S(1)} %collective-permute-done.10.refs_2_.refs_3_, ...), custom_call_target="tpu_custom_call" | custom-call | bytes 3932160 | tf_op jit(solution)/shard_map/pallas_call | solution.py:200
  76.4 6.2 %all-to-all-start.1 = ((bf16[16,40,1280]{2,1,0:T(8,128)(2,1)}), bf16[16,40,1280]{2,1,0:T(8,128)(2,1)S(1)}, u32[]{:S(2)}, u32[]{:S(2)}) async-start(bf16[16,40,1280]{2,1,0:T(8,128)(2,1)} %shard_map.51), calls=%async_computation.1 | async-start | bytes 3276800 | tf_op jit(solution)/shard_map/all_to_all | solution.py:297
  82.6 1.2 collective-permute-start.12
  83.9 2.8 %collective-permute-start.13 = (bf16[160,256]{1,0:T(8,128)(2,1)S(1)}, bf16[160,256]{1,0:T(8,128)(2,1)S(1)}, u32[]{:S(2)}, u32[]{:S(2)}) collective-permute-start(bf16[160,256]{1,0:T(8,128)(2,1)S(1)} %get-tuple-element.49), channel_id=1, source_target_pairs={{0,64},{1,65},{64,128},{65,129},{128,192},{129,193},{192,1},{193,0... | collective-permute-start | bytes 245768 | tf_op jit(solution)/shard_map/ppermute | solution.py:216
  86.7 0.4 collective-permute-start.14
  87.1 1.8 %collective-permute-done.12.refs_5_ = bf16[160,256]{1,0:T(8,128)(2,1)S(1)} collective-permute-done((bf16[160,256]{1,0:T(8,128)(2,1)S(1)}, bf16[160,256]{1,0:T(8,128)(2,1)S(1)}, u32[]{:S(2)}, u32[]{:S(2)}) %collective-permute-start.12) | collective-permute-done | bytes 81952 | tf_op jit(solution)/shard_map/ppermute | solution.py:216
  88.9 0.6 collective-permute-done.13.refs_6_
  89.5 1.6 %collective-permute-done.14.refs_7_ = bf16[160,256]{1,0:T(8,128)(2,1)S(1)} collective-permute-done((bf16[160,256]{1,0:T(8,128)(2,1)S(1)}, bf16[160,256]{1,0:T(8,128)(2,1)S(1)}, u32[]{:S(2)}, u32[]{:S(2)}) %collective-permute-start.14) | collective-permute-done | bytes 81952 | tf_op jit(solution)/shard_map/ppermute | solution.py:216
  91.1 0.1 shard_map.52.v_ref
  91.2 0.1 collective-permute-start.15
  91.3 2.1 %collective-permute-done.15._.v_far = bf16[2,4,160,256]{3,2,1,0:T(8,128)(2,1)S(1)} collective-permute-done((bf16[2,4,160,256]{3,2,1,0:T(8,128)(2,1)S(1)}, bf16[2,4,160,256]{3,2,1,0:T(8,128)(2,1)S(1)}, u32[]{:S(2)}, u32[]{:S(2)}) %collective-permute-start.15) | collective-permute-done | bytes 655392 | tf_op jit(solution)/shard_map/ppermute | solution.py:221
  93.4 9.7 %all-to-all-done.1 = bf16[16,40,1280]{2,1,0:T(8,128)(2,1)S(1)} async-done(((bf16[16,40,1280]{2,1,0:T(8,128)(2,1)}), bf16[16,40,1280]{2,1,0:T(8,128)(2,1)S(1)}, u32[]{:S(2)}, u32[]{:S(2)}) %all-to-all-start.1) | async-done | bytes 1638432 | tf_op jit(solution)/shard_map/all_to_all | solution.py:297
  103.1 0.7 shard_map.54
  103.8 0.0 copy-start.1
  103.8 3.6 %collective-permute-start.16 = (bf16[160,256]{1,0:T(8,128)(2,1)S(1)}, bf16[160,256]{1,0:T(8,128)(2,1)S(1)}, u32[]{:S(2)}, u32[]{:S(2)}) collective-permute-start(bf16[160,256]{1,0:T(8,128)(2,1)S(1)} %get-tuple-element.52), channel_id=1, source_target_pairs={{0,1},{1,0},{64,65},{65,64},{128,129},{129,128},{192,193},{193,192... | collective-permute-start | bytes 245768 | tf_op jit(solution)/shard_map/ppermute | solution.py:216
  107.4 2.3 %collective-permute-start.17 = (bf16[160,256]{1,0:T(8,128)(2,1)S(1)}, bf16[160,256]{1,0:T(8,128)(2,1)S(1)}, u32[]{:S(2)}, u32[]{:S(2)}) collective-permute-start(bf16[160,256]{1,0:T(8,128)(2,1)S(1)} %get-tuple-element.53), channel_id=1, source_target_pairs={{0,192},{1,193},{64,1},{65,0},{128,65},{129,64},{192,129},{193,128... | collective-permute-start | bytes 245768 | tf_op jit(solution)/shard_map/ppermute | solution.py:216
  109.8 0.4 collective-permute-start.18
  110.2 0.7 shard_map.55
  110.9 2.4 %collective-permute-start.19 = (bf16[160,256]{1,0:T(8,128)(2,1)S(1)}, bf16[160,256]{1,0:T(8,128)(2,1)S(1)}, u32[]{:S(2)}, u32[]{:S(2)}) collective-permute-start(bf16[160,256]{1,0:T(8,128)(2,1)S(1)} %get-tuple-element.55), channel_id=1, source_target_pairs={{0,65},{1,64},{64,129},{65,128},{128,193},{129,192},{192,0},{193,1... | collective-permute-start | bytes 245768 | tf_op jit(solution)/shard_map/ppermute | solution.py:216
  113.2 0.9 collective-permute-start.20
  114.2 0.0 collective-permute-done.16.refs_1_
  114.2 3.2 %collective-permute-start.21 = (bf16[160,256]{1,0:T(8,128)(2,1)S(1)}, bf16[160,256]{1,0:T(8,128)(2,1)S(1)}, u32[]{:S(2)}, u32[]{:S(2)}) collective-permute-start(bf16[160,256]{1,0:T(8,128)(2,1)S(1)} %get-tuple-element.57), channel_id=1, source_target_pairs={{0,129},{1,128},{64,193},{65,192},{128,0},{129,1},{192,64},{193,65... | collective-permute-start | bytes 245768 | tf_op jit(solution)/shard_map/ppermute | solution.py:216
  117.4 1.3 %collective-permute-done.17.refs_2_ = bf16[160,256]{1,0:T(8,128)(2,1)S(1)} collective-permute-done((bf16[160,256]{1,0:T(8,128)(2,1)S(1)}, bf16[160,256]{1,0:T(8,128)(2,1)S(1)}, u32[]{:S(2)}, u32[]{:S(2)}) %collective-permute-start.17) | collective-permute-done | bytes 81952 | tf_op jit(solution)/shard_map/ppermute | solution.py:216
  118.7 0.7 collective-permute-start.22
  119.4 0.0 collective-permute-done.18.refs_3_
  119.4 0.0 collective-permute-done.19.refs_4_
  119.4 0.7 collective-permute-done.20.refs_5_
  120.2 2.3 %collective-permute-done.21.refs_6_ = bf16[160,256]{1,0:T(8,128)(2,1)S(1)} collective-permute-done((bf16[160,256]{1,0:T(8,128)(2,1)S(1)}, bf16[160,256]{1,0:T(8,128)(2,1)S(1)}, u32[]{:S(2)}, u32[]{:S(2)}) %collective-permute-start.21) | collective-permute-done | bytes 81952 | tf_op jit(solution)/shard_map/ppermute | solution.py:216
  122.4 1.9 %collective-permute-done.22.refs_7_ = bf16[160,256]{1,0:T(8,128)(2,1)S(1)} collective-permute-done((bf16[160,256]{1,0:T(8,128)(2,1)S(1)}, bf16[160,256]{1,0:T(8,128)(2,1)S(1)}, u32[]{:S(2)}, u32[]{:S(2)}) %collective-permute-start.22) | collective-permute-done | bytes 81952 | tf_op jit(solution)/shard_map/ppermute | solution.py:216
  124.4 0.0 copy-done.1
  124.4 1.7 %shard_map.56 = f32[4,160,768]{2,1,0:T(8,128)} custom-call(s32[1]{0:T(128)} %bitcast.pos_ref, bf16[512,768]{1,0:T(8,128)(2,1)S(1)} %copy-done.1, bf16[160,256]{1,0:T(8,128)(2,1)S(1)} %get-tuple-element.51.refs_0_, bf16[160,256]{1,0:T(8,128)(2,1)S(1)} %collective-permute-done.16.refs_1_, bf16[160,256]{1,0:T(8,128)(2,1)S(1)} %collective-permute-done.17.refs_2_, ...), custom_call_target="tpu_custom_call" | custom-call | flops 503316480 | bytes 2883592 | tf_op jit(solution)/shard_map/pallas_call | solution.py:200
  (3 shorter events, 0.0 us)
Async XLA Ops:
  0.0 0.7 copy-start.2
  0.7 31.9 %copy-start = (bf16[768,3,512]{2,0,1:T(8,128)(2,1)S(1)}, bf16[768,3,512]{2,0,1:T(8,128)(2,1)}, u32[]{:S(2)}) copy-start(bf16[768,3,512]{2,0,1:T(8,128)(2,1)} %param.6) | copy-start | bytes 7077892
  4.1 19.3 %collective-permute-start = (bf16[320,256]{1,0:T(8,128)(2,1)S(1)}, bf16[320,256]{1,0:T(8,128)(2,1)S(1)}, u32[]{:S(2)}, u32[]{:S(2)}) collective-permute-start(bf16[320,256]{1,0:T(8,128)(2,1)S(1)} %get-tuple-element.33), channel_id=1, source_target_pairs={{0,1},{1,0},{64,65},{65,64},{128,129},{129,128},{192,193},{193,192... | collective-permute-start | bytes 491528 | tf_op jit(solution)/shard_map/ppermute | solution.py:216
  11.4 21.2 %collective-permute-start.1 = (bf16[320,256]{1,0:T(8,128)(2,1)S(1)}, bf16[320,256]{1,0:T(8,128)(2,1)S(1)}, u32[]{:S(2)}, u32[]{:S(2)}) collective-permute-start(bf16[320,256]{1,0:T(8,128)(2,1)S(1)} %get-tuple-element.34), channel_id=1, source_target_pairs={{0,192},{1,193},{64,1},{65,0},{128,65},{129,64},{192,129},{193,128... | collective-permute-start | bytes 491528 | tf_op jit(solution)/shard_map/ppermute | solution.py:216
  13.3 20.2 %collective-permute-start.2 = (bf16[320,256]{1,0:T(8,128)(2,1)S(1)}, bf16[320,256]{1,0:T(8,128)(2,1)S(1)}, u32[]{:S(2)}, u32[]{:S(2)}) collective-permute-start(bf16[320,256]{1,0:T(8,128)(2,1)S(1)} %get-tuple-element.35), channel_id=1, source_target_pairs={{0,65},{1,64},{64,129},{65,128},{128,193},{129,192},{192,0},{193,1... | collective-permute-start | bytes 491528 | tf_op jit(solution)/shard_map/ppermute | solution.py:216
  16.4 20.4 %collective-permute-start.3 = (bf16[320,256]{1,0:T(8,128)(2,1)S(1)}, bf16[320,256]{1,0:T(8,128)(2,1)S(1)}, u32[]{:S(2)}, u32[]{:S(2)}) collective-permute-start(bf16[320,256]{1,0:T(8,128)(2,1)S(1)} %get-tuple-element.36), channel_id=1, source_target_pairs={{0,128},{1,129},{64,192},{65,193},{128,1},{129,0},{192,65},{193,64... | collective-permute-start | bytes 491528 | tf_op jit(solution)/shard_map/ppermute | solution.py:216
  17.9 19.8 %collective-permute-start.4 = (bf16[320,256]{1,0:T(8,128)(2,1)S(1)}, bf16[320,256]{1,0:T(8,128)(2,1)S(1)}, u32[]{:S(2)}, u32[]{:S(2)}) collective-permute-start(bf16[320,256]{1,0:T(8,128)(2,1)S(1)} %get-tuple-element.37), channel_id=1, source_target_pairs={{0,129},{1,128},{64,193},{65,192},{128,0},{129,1},{192,64},{193,65... | collective-permute-start | bytes 491528 | tf_op jit(solution)/shard_map/ppermute | solution.py:216
  23.4 16.5 %collective-permute-start.5 = (bf16[320,256]{1,0:T(8,128)(2,1)S(1)}, bf16[320,256]{1,0:T(8,128)(2,1)S(1)}, u32[]{:S(2)}, u32[]{:S(2)}) collective-permute-start(bf16[320,256]{1,0:T(8,128)(2,1)S(1)} %get-tuple-element.38), channel_id=1, source_target_pairs={{0,64},{1,65},{64,128},{65,129},{128,192},{129,193},{192,1},{193,0... | collective-permute-start | bytes 491528 | tf_op jit(solution)/shard_map/ppermute | solution.py:216
  32.6 8.4 %collective-permute-start.6 = (bf16[320,256]{1,0:T(8,128)(2,1)S(1)}, bf16[320,256]{1,0:T(8,128)(2,1)S(1)}, u32[]{:S(2)}, u32[]{:S(2)}) collective-permute-start(bf16[320,256]{1,0:T(8,128)(2,1)S(1)} %get-tuple-element.39), channel_id=1, source_target_pairs={{0,193},{1,192},{64,0},{65,1},{128,64},{129,65},{192,128},{193,129... | collective-permute-start | bytes 491528 | tf_op jit(solution)/shard_map/ppermute | solution.py:216
  41.0 2.2 %collective-permute-start.7 = (bf16[2,4,160,256]{3,2,1,0:T(8,128)(2,1)S(1)}, bf16[2,4,160,256]{3,2,1,0:T(8,128)(2,1)S(1)}, u32[]{:S(2)}, u32[]{:S(2)}) collective-permute-start(bf16[2,4,160,256]{3,2,1,0:T(8,128)(2,1)S(1)} %shard_map.48.refs_8_), channel_id=1, source_target_pairs={{0,32},{32,0},{1,33},{33,1},{2,34},{34,2},{3,35},{35,3},{4,36},{36... | collective-permute-start | bytes 1966088 | tf_op jit(solution)/shard_map/ppermute | solution.py:221
  44.7 30.0 %all-to-all-start = ((bf16[16,40,1280]{2,1,0:T(8,128)(2,1)}), bf16[16,40,1280]{2,1,0:T(8,128)(2,1)S(1)}, u32[]{:S(2)}, u32[]{:S(2)}) async-start(bf16[16,40,1280]{2,1,0:T(8,128)(2,1)} %bitcast.2), calls=%async_computation | async-start | bytes 3276800 | tf_op jit(solution)/shard_map/all_to_all | solution.py:287
  52.1 11.6 %collective-permute-start.8 = (bf16[160,256]{1,0:T(8,128)(2,1)S(1)}, bf16[160,256]{1,0:T(8,128)(2,1)S(1)}, u32[]{:S(2)}, u32[]{:S(2)}) collective-permute-start(bf16[160,256]{1,0:T(8,128)(2,1)S(1)} %get-tuple-element.44), channel_id=1, source_target_pairs={{0,1},{1,0},{64,65},{65,64},{128,129},{129,128},{192,193},{193,192... | collective-permute-start | bytes 245768 | tf_op jit(solution)/shard_map/ppermute | solution.py:216
  55.7 13.5 %collective-permute-start.9 = (bf16[160,256]{1,0:T(8,128)(2,1)S(1)}, bf16[160,256]{1,0:T(8,128)(2,1)S(1)}, u32[]{:S(2)}, u32[]{:S(2)}) collective-permute-start(bf16[160,256]{1,0:T(8,128)(2,1)S(1)} %get-tuple-element.45), channel_id=1, source_target_pairs={{0,192},{1,193},{64,1},{65,0},{128,65},{129,64},{192,129},{193,128... | collective-permute-start | bytes 245768 | tf_op jit(solution)/shard_map/ppermute | solution.py:216
  58.0 11.1 %collective-permute-start.10 = (bf16[160,256]{1,0:T(8,128)(2,1)S(1)}, bf16[160,256]{1,0:T(8,128)(2,1)S(1)}, u32[]{:S(2)}, u32[]{:S(2)}) collective-permute-start(bf16[160,256]{1,0:T(8,128)(2,1)S(1)} %get-tuple-element.46), channel_id=1, source_target_pairs={{0,65},{1,64},{64,129},{65,128},{128,193},{129,192},{192,0},{193,1... | collective-permute-start | bytes 245768 | tf_op jit(solution)/shard_map/ppermute | solution.py:216
  60.7 8.4 %collective-permute-start.11 = (bf16[160,256]{1,0:T(8,128)(2,1)S(1)}, bf16[160,256]{1,0:T(8,128)(2,1)S(1)}, u32[]{:S(2)}, u32[]{:S(2)}) collective-permute-start(bf16[160,256]{1,0:T(8,128)(2,1)S(1)} %get-tuple-element.47), channel_id=1, source_target_pairs={{0,128},{1,129},{64,192},{65,193},{128,1},{129,0},{192,65},{193,64... | collective-permute-start | bytes 245768 | tf_op jit(solution)/shard_map/ppermute | solution.py:216
  76.4 26.7 %all-to-all-start.1 = ((bf16[16,40,1280]{2,1,0:T(8,128)(2,1)}), bf16[16,40,1280]{2,1,0:T(8,128)(2,1)S(1)}, u32[]{:S(2)}, u32[]{:S(2)}) async-start(bf16[16,40,1280]{2,1,0:T(8,128)(2,1)} %shard_map.51), calls=%async_computation.1 | async-start | bytes 3276800 | tf_op jit(solution)/shard_map/all_to_all | solution.py:297
  82.6 6.3 %collective-permute-start.12 = (bf16[160,256]{1,0:T(8,128)(2,1)S(1)}, bf16[160,256]{1,0:T(8,128)(2,1)S(1)}, u32[]{:S(2)}, u32[]{:S(2)}) collective-permute-start(bf16[160,256]{1,0:T(8,128)(2,1)S(1)} %get-tuple-element.48), channel_id=1, source_target_pairs={{0,129},{1,128},{64,193},{65,192},{128,0},{129,1},{192,64},{193,65... | collective-permute-start | bytes 245768 | tf_op jit(solution)/shard_map/ppermute | solution.py:216
  83.9 5.7 %collective-permute-start.13 = (bf16[160,256]{1,0:T(8,128)(2,1)S(1)}, bf16[160,256]{1,0:T(8,128)(2,1)S(1)}, u32[]{:S(2)}, u32[]{:S(2)}) collective-permute-start(bf16[160,256]{1,0:T(8,128)(2,1)S(1)} %get-tuple-element.49), channel_id=1, source_target_pairs={{0,64},{1,65},{64,128},{65,129},{128,192},{129,193},{192,1},{193,0... | collective-permute-start | bytes 245768 | tf_op jit(solution)/shard_map/ppermute | solution.py:216
  86.7 4.4 %collective-permute-start.14 = (bf16[160,256]{1,0:T(8,128)(2,1)S(1)}, bf16[160,256]{1,0:T(8,128)(2,1)S(1)}, u32[]{:S(2)}, u32[]{:S(2)}) collective-permute-start(bf16[160,256]{1,0:T(8,128)(2,1)S(1)} %get-tuple-element.50), channel_id=1, source_target_pairs={{0,193},{1,192},{64,0},{65,1},{128,64},{129,65},{192,128},{193,129... | collective-permute-start | bytes 245768 | tf_op jit(solution)/shard_map/ppermute | solution.py:216
  91.2 2.2 %collective-permute-start.15 = (bf16[2,4,160,256]{3,2,1,0:T(8,128)(2,1)S(1)}, bf16[2,4,160,256]{3,2,1,0:T(8,128)(2,1)S(1)}, u32[]{:S(2)}, u32[]{:S(2)}) collective-permute-start(bf16[2,4,160,256]{3,2,1,0:T(8,128)(2,1)S(1)} %shard_map.52.v_ref), channel_id=1, source_target_pairs={{0,32},{32,0},{1,33},{33,1},{2,34},{34,2},{3,35},{35,3},{4,36},{36... | collective-permute-start | bytes 1966088 | tf_op jit(solution)/shard_map/ppermute | solution.py:221
  103.8 20.6 %copy-start.1 = (bf16[512,768]{1,0:T(8,128)(2,1)S(1)}, bf16[512,768]{1,0:T(8,128)(2,1)}, u32[]{:S(2)}) copy-start(bf16[512,768]{1,0:T(8,128)(2,1)} %w_ref.1) | copy-start | bytes 2359300
  103.8 10.4 %collective-permute-start.16 = (bf16[160,256]{1,0:T(8,128)(2,1)S(1)}, bf16[160,256]{1,0:T(8,128)(2,1)S(1)}, u32[]{:S(2)}, u32[]{:S(2)}) collective-permute-start(bf16[160,256]{1,0:T(8,128)(2,1)S(1)} %get-tuple-element.52), channel_id=1, source_target_pairs={{0,1},{1,0},{64,65},{65,64},{128,129},{129,128},{192,193},{193,192... | collective-permute-start | bytes 245768 | tf_op jit(solution)/shard_map/ppermute | solution.py:216
  107.4 11.3 %collective-permute-start.17 = (bf16[160,256]{1,0:T(8,128)(2,1)S(1)}, bf16[160,256]{1,0:T(8,128)(2,1)S(1)}, u32[]{:S(2)}, u32[]{:S(2)}) collective-permute-start(bf16[160,256]{1,0:T(8,128)(2,1)S(1)} %get-tuple-element.53), channel_id=1, source_target_pairs={{0,192},{1,193},{64,1},{65,0},{128,65},{129,64},{192,129},{193,128... | collective-permute-start | bytes 245768 | tf_op jit(solution)/shard_map/ppermute | solution.py:216
  109.8 9.6 %collective-permute-start.18 = (bf16[160,256]{1,0:T(8,128)(2,1)S(1)}, bf16[160,256]{1,0:T(8,128)(2,1)S(1)}, u32[]{:S(2)}, u32[]{:S(2)}) collective-permute-start(bf16[160,256]{1,0:T(8,128)(2,1)S(1)} %get-tuple-element.54), channel_id=1, source_target_pairs={{0,193},{1,192},{64,0},{65,1},{128,64},{129,65},{192,128},{193,129... | collective-permute-start | bytes 245768 | tf_op jit(solution)/shard_map/ppermute | solution.py:216
  110.9 8.5 %collective-permute-start.19 = (bf16[160,256]{1,0:T(8,128)(2,1)S(1)}, bf16[160,256]{1,0:T(8,128)(2,1)S(1)}, u32[]{:S(2)}, u32[]{:S(2)}) collective-permute-start(bf16[160,256]{1,0:T(8,128)(2,1)S(1)} %get-tuple-element.55), channel_id=1, source_target_pairs={{0,65},{1,64},{64,129},{65,128},{128,193},{129,192},{192,0},{193,1... | collective-permute-start | bytes 245768 | tf_op jit(solution)/shard_map/ppermute | solution.py:216
  113.2 6.9 %collective-permute-start.20 = (bf16[160,256]{1,0:T(8,128)(2,1)S(1)}, bf16[160,256]{1,0:T(8,128)(2,1)S(1)}, u32[]{:S(2)}, u32[]{:S(2)}) collective-permute-start(bf16[160,256]{1,0:T(8,128)(2,1)S(1)} %get-tuple-element.56), channel_id=1, source_target_pairs={{0,128},{1,129},{64,192},{65,193},{128,1},{129,0},{192,65},{193,64... | collective-permute-start | bytes 245768 | tf_op jit(solution)/shard_map/ppermute | solution.py:216
  114.2 8.3 %collective-permute-start.21 = (bf16[160,256]{1,0:T(8,128)(2,1)S(1)}, bf16[160,256]{1,0:T(8,128)(2,1)S(1)}, u32[]{:S(2)}, u32[]{:S(2)}) collective-permute-start(bf16[160,256]{1,0:T(8,128)(2,1)S(1)} %get-tuple-element.57), channel_id=1, source_target_pairs={{0,129},{1,128},{64,193},{65,192},{128,0},{129,1},{192,64},{193,65... | collective-permute-start | bytes 245768 | tf_op jit(solution)/shard_map/ppermute | solution.py:216
  118.7 5.7 %collective-permute-start.22 = (bf16[160,256]{1,0:T(8,128)(2,1)S(1)}, bf16[160,256]{1,0:T(8,128)(2,1)S(1)}, u32[]{:S(2)}, u32[]{:S(2)}) collective-permute-start(bf16[160,256]{1,0:T(8,128)(2,1)S(1)} %get-tuple-element.58), channel_id=1, source_target_pairs={{0,64},{1,65},{64,128},{65,129},{128,192},{129,193},{192,1},{193,0... | collective-permute-start | bytes 245768 | tf_op jit(solution)/shard_map/ppermute | solution.py:216

commit v14 on v11

--- a/solution.py
+++ b/solution.py
@@ -20,7 +20,7 @@
 HBM = pl.BlockSpec(memory_space=pltpu.HBM)
 ANY = pl.BlockSpec(memory_space=pl.ANY)
 SMEM = pl.BlockSpec(memory_space=pltpu.SMEM)
-CONTEXT_STEPS = (0, 4, 3, 7, 5, 2, 6, 1)
+CONTEXT_STEPS = (0, 4, 2, 6, 3, 5, 1, 7)
 MIB = 1024 * 1024
 
 
@@ -300,7 +300,7 @@
     values_far = other_core(values)
     seen = call(seen_kernel, jax.ShapeDtypeStruct((8, 128), F32), [values_far], unread=(0,))
     context = []
-    for blocks in ((0, 3), (1, 2)):
+    for blocks in ((0, 2), (1, 3)):
         steps = [s for s in CONTEXT_STEPS if s % Z in blocks]
         parts = call(
             functools.partial(context_kernel, blocks, steps),

time: 127 us -> 126 us (level)
  waiting for transfers between devices: 55.8 us -> 51.9 us
  starting transfers between devices: 57.4 us -> 59.9 us
    ppermute x21, waiting for transfers between devices: 37.9 us -> 34 us  [along_ring(): got.append(lax.ppermute(part, ('z', 'w'), pairs) if s else part)]
    ppermute x21, starting transfers between devices: 43.5 us -> 46 us  [along_ring(): got.append(lax.ppermute(part, ('z', 'w'), pairs) if s else part)]
  transfers between devices with their start and end apart: 25 -> 25, of which waited for: 19 -> 17; matrix products, arithmetic and copies ran while one was open for 0% -> 0% of each run, Pallas kernels for 2% -> 3%
where the time goes in v14:
time: 126 us; the launch traced here: 125 us
  starting transfers between devices  59.9 us (48%)
  waiting for transfers between devices  51.9 us (41%)
  Pallas kernels  12.1 us (10%)
    ppermute x21, starting transfers between devices, along_ring(): got.append(lax.ppermute(part, ('z', 'w'), pairs) if s else part)  46 us
    ppermute x21, waiting for transfers between devices, along_ring(): got.append(lax.ppermute(part, ('z', 'w'), pairs) if s else part)  34 us
    pallas_call x11, Pallas kernels, call(): pl.pallas_call(kernel, out_shape=out_shape, in_specs=specs, out_specs=out...  12.1 us
    all_to_all x1, waiting for transfers between devices, shards(): lax.all_to_all(probs, ('x', 'y'), 0, 0, tiled=True).reshape(half, full)  9.69 us
    all_to_all x1, starting transfers between devices, shards(): terms = lax.all_to_all(term.reshape(chunk), ('x', 'y'), 0, 0, tiled=True)  7.44 us
    all_to_all x1, starting transfers between devices, shards(): lax.all_to_all(probs, ('x', 'y'), 0, 0, tiled=True).reshape(half, full)  6.24 us
    all_to_all x1, waiting for transfers between devices, shards(): terms = lax.all_to_all(term.reshape(chunk), ('x', 'y'), 0, 0, tiled=True)  5.57 us
    ppermute x2, waiting for transfers between devices, other_core(): return lax.ppermute(a, 'c', [(0, 1), (1, 0)])  2.65 us
  transfers between devices with their start and end apart: 25, of which 17 were waited for; matrix products, arithmetic and copies ran while one was open for 0% of the time, Pallas kernels for 3%

profile of v14, /device:TPU:6, one launch (start us, length us, event | category | flops | bytes accessed | tf_op | source)
XLA Modules:
  0.0 124.9 jit_solution(7582619832811885717)
XLA Ops:
  0.0 0.7 copy-done.2
  0.7 3.4 %shard_map.46 = (bf16[320,256]{1,0:T(8,128)(2,1)S(1)}, bf16[320,256]{1,0:T(8,128)(2,1)S(1)}, bf16[320,256]{1,0:T(8,128)(2,1)S(1)}, bf16[320,256]{1,0:T(8,128)(2,...) custom-call(s32[1]{0:T(128)} %bitcast.pos_ref, ...), custom_call_target="tpu_custom_call" | custom-call | flops 1006632960 | bytes 6690824 | tf_op jit(solution)/shard_map/pallas_call | solution.py:201
  4.1 7.3 %collective-permute-start = (bf16[320,256]{1,0:T(8,128)(2,1)S(1)}, bf16[320,256]{1,0:T(8,128)(2,1)S(1)}, u32[]{:S(2)}, u32[]{:S(2)}) collective-permute-start(bf16[320,256]{1,0:T(8,128)(2,1)S(1)} %get-tuple-element.33), channel_id=1, source_target_pairs={{0,1},{1,0},{64,65},{65,64},{128,129},{129,128},{192,193},{193,192... | collective-permute-start | bytes 491528 | tf_op jit(solution)/shard_map/ppermute | solution.py:217
  11.4 1.9 %collective-permute-start.1 = (bf16[320,256]{1,0:T(8,128)(2,1)S(1)}, bf16[320,256]{1,0:T(8,128)(2,1)S(1)}, u32[]{:S(2)}, u32[]{:S(2)}) collective-permute-start(bf16[320,256]{1,0:T(8,128)(2,1)S(1)} %get-tuple-element.34), channel_id=1, source_target_pairs={{0,192},{1,193},{64,1},{65,0},{128,65},{129,64},{192,129},{193,128... | collective-permute-start | bytes 491528 | tf_op jit(solution)/shard_map/ppermute | solution.py:217
  13.3 3.1 %collective-permute-start.2 = (bf16[320,256]{1,0:T(8,128)(2,1)S(1)}, bf16[320,256]{1,0:T(8,128)(2,1)S(1)}, u32[]{:S(2)}, u32[]{:S(2)}) collective-permute-start(bf16[320,256]{1,0:T(8,128)(2,1)S(1)} %get-tuple-element.35), channel_id=1, source_target_pairs={{0,65},{1,64},{64,129},{65,128},{128,193},{129,192},{192,0},{193,1... | collective-permute-start | bytes 491528 | tf_op jit(solution)/shard_map/ppermute | solution.py:217
  16.4 1.5 %collective-permute-start.3 = (bf16[320,256]{1,0:T(8,128)(2,1)S(1)}, bf16[320,256]{1,0:T(8,128)(2,1)S(1)}, u32[]{:S(2)}, u32[]{:S(2)}) collective-permute-start(bf16[320,256]{1,0:T(8,128)(2,1)S(1)} %get-tuple-element.36), channel_id=1, source_target_pairs={{0,128},{1,129},{64,192},{65,193},{128,1},{129,0},{192,65},{193,64... | collective-permute-start | bytes 491528 | tf_op jit(solution)/shard_map/ppermute | solution.py:217
  17.9 2.7 %collective-permute-start.4 = (bf16[320,256]{1,0:T(8,128)(2,1)S(1)}, bf16[320,256]{1,0:T(8,128)(2,1)S(1)}, u32[]{:S(2)}, u32[]{:S(2)}) collective-permute-start(bf16[320,256]{1,0:T(8,128)(2,1)S(1)} %get-tuple-element.37), channel_id=1, source_target_pairs={{0,129},{1,128},{64,193},{65,192},{128,0},{129,1},{192,64},{193,65... | collective-permute-start | bytes 491528 | tf_op jit(solution)/shard_map/ppermute | solution.py:217
  20.6 2.8 %collective-permute-done.refs_1_ = bf16[320,256]{1,0:T(8,128)(2,1)S(1)} collective-permute-done((bf16[320,256]{1,0:T(8,128)(2,1)S(1)}, bf16[320,256]{1,0:T(8,128)(2,1)S(1)}, u32[]{:S(2)}, u32[]{:S(2)}) %collective-permute-start) | collective-permute-done | bytes 163872 | tf_op jit(solution)/shard_map/ppermute | solution.py:217
  23.4 0.3 collective-permute-start.5
  23.8 8.8 %collective-permute-done.1.refs_2_ = bf16[320,256]{1,0:T(8,128)(2,1)S(1)} collective-permute-done((bf16[320,256]{1,0:T(8,128)(2,1)S(1)}, bf16[320,256]{1,0:T(8,128)(2,1)S(1)}, u32[]{:S(2)}, u32[]{:S(2)}) %collective-permute-start.1) | collective-permute-done | bytes 163872 | tf_op jit(solution)/shard_map/ppermute | solution.py:217
  32.6 0.0 collective-permute-start.6
  32.6 0.0 copy-done
  32.6 0.9 shard_map.47
  33.5 0.0 collective-permute-done.2.refs_3_
  33.5 3.3 %collective-permute-done.3.refs_4_ = bf16[320,256]{1,0:T(8,128)(2,1)S(1)} collective-permute-done((bf16[320,256]{1,0:T(8,128)(2,1)S(1)}, bf16[320,256]{1,0:T(8,128)(2,1)S(1)}, u32[]{:S(2)}, u32[]{:S(2)}) %collective-permute-start.3) | collective-permute-done | bytes 163872 | tf_op jit(solution)/shard_map/ppermute | solution.py:217
  36.8 0.9 collective-permute-done.4.refs_5_
  37.7 2.2 %collective-permute-done.5.refs_6_ = bf16[320,256]{1,0:T(8,128)(2,1)S(1)} collective-permute-done((bf16[320,256]{1,0:T(8,128)(2,1)S(1)}, bf16[320,256]{1,0:T(8,128)(2,1)S(1)}, u32[]{:S(2)}, u32[]{:S(2)}) %collective-permute-start.5) | collective-permute-done | bytes 163872 | tf_op jit(solution)/shard_map/ppermute | solution.py:217
  39.9 1.1 collective-permute-done.6.refs_7_
  41.0 0.1 shard_map.48.refs_8_
  41.0 0.1 collective-permute-start.7
  41.1 1.5 %shard_map.49 = (bf16[640,1280]{1,0:T(8,128)(2,1)}, bf16[2,4,160,256]{3,2,1,0:T(8,128)(2,1)S(1)}) custom-call(s32[1]{0:T(128)} %bitcast.pos_ref, bf16[320,256]{1,0:T(8,128)(2,1)S(1)} %get-tuple-element.32.refs_0_, bf16[320,256]{1,0:T(8,128)(2,1)S(1)} %collective-permute-done.refs_1_, bf16[320,256]{1,0:T(8,128)(2,1)S(1)} %collective-permute-done.1.refs_2_, ...), custom_call_target="tpu_custom_call" | custom-call | flops 419430400 | bytes 3932168 | tf_op jit(solution)/shard_map/pallas_call | solution.py:201
  42.6 0.6 collective-permute-done.7.k_far
  43.2 1.5 %shard_map.50 = bf16[640,1280]{1,0:T(8,128)(2,1)} custom-call(bf16[640,1280]{1,0:T(8,128)(2,1)} %get-tuple-element.42._, bf16[2,4,160,256]{3,2,1,0:T(8,128)(2,1)S(1)} %get-tuple-element.43.q, bf16[2,4,160,256]{3,2,1,0:T(8,128)(2,1)S(1)} %collective-permute-done.7.k_far), custom_call_target="tpu_custom_call", output_to_operand_aliasing={{}: (0, {})} | custom-call | flops 419430400 | bytes 5898240 | tf_op jit(solution)/shard_map/pallas_call | solution.py:201
  44.7 7.4 %all-to-all-start = ((bf16[16,40,1280]{2,1,0:T(8,128)(2,1)}), bf16[16,40,1280]{2,1,0:T(8,128)(2,1)S(1)}, u32[]{:S(2)}, u32[]{:S(2)}) async-start(bf16[16,40,1280]{2,1,0:T(8,128)(2,1)} %bitcast.2), calls=%async_computation | async-start | bytes 3276800 | tf_op jit(solution)/shard_map/all_to_all | solution.py:288
  52.2 3.5 %collective-permute-start.8 = (bf16[160,256]{1,0:T(8,128)(2,1)S(1)}, bf16[160,256]{1,0:T(8,128)(2,1)S(1)}, u32[]{:S(2)}, u32[]{:S(2)}) collective-permute-start(bf16[160,256]{1,0:T(8,128)(2,1)S(1)} %get-tuple-element.44), channel_id=1, source_target_pairs={{0,1},{1,0},{64,65},{65,64},{128,129},{129,128},{192,193},{193,192... | collective-permute-start | bytes 245768 | tf_op jit(solution)/shard_map/ppermute | solution.py:217
  55.7 2.3 %collective-permute-start.9 = (bf16[160,256]{1,0:T(8,128)(2,1)S(1)}, bf16[160,256]{1,0:T(8,128)(2,1)S(1)}, u32[]{:S(2)}, u32[]{:S(2)}) collective-permute-start(bf16[160,256]{1,0:T(8,128)(2,1)S(1)} %get-tuple-element.45), channel_id=1, source_target_pairs={{0,192},{1,193},{64,1},{65,0},{128,65},{129,64},{192,129},{193,128... | collective-permute-start | bytes 245768 | tf_op jit(solution)/shard_map/ppermute | solution.py:217
  58.0 2.7 %collective-permute-start.10 = (bf16[160,256]{1,0:T(8,128)(2,1)S(1)}, bf16[160,256]{1,0:T(8,128)(2,1)S(1)}, u32[]{:S(2)}, u32[]{:S(2)}) collective-permute-start(bf16[160,256]{1,0:T(8,128)(2,1)S(1)} %get-tuple-element.46), channel_id=1, source_target_pairs={{0,65},{1,64},{64,129},{65,128},{128,193},{129,192},{192,0},{193,1... | collective-permute-start | bytes 245768 | tf_op jit(solution)/shard_map/ppermute | solution.py:217
  60.7 0.1 collective-permute-start.11
  60.8 2.9 %collective-permute-done.8.refs_0_.refs_1_ = bf16[160,256]{1,0:T(8,128)(2,1)S(1)} collective-permute-done((bf16[160,256]{1,0:T(8,128)(2,1)S(1)}, bf16[160,256]{1,0:T(8,128)(2,1)S(1)}, u32[]{:S(2)}, u32[]{:S(2)}) %collective-permute-start.8) | collective-permute-done | bytes 81952 | tf_op jit(solution)/shard_map/ppermute | solution.py:217
  63.7 5.5 %collective-permute-done.9.refs_1_.refs_2_ = bf16[160,256]{1,0:T(8,128)(2,1)S(1)} collective-permute-done((bf16[160,256]{1,0:T(8,128)(2,1)S(1)}, bf16[160,256]{1,0:T(8,128)(2,1)S(1)}, u32[]{:S(2)}, u32[]{:S(2)}) %collective-permute-start.9) | collective-permute-done | bytes 81952 | tf_op jit(solution)/shard_map/ppermute | solution.py:217
  69.2 0.0 collective-permute-done.10.refs_2_.refs_3_
  69.2 0.0 collective-permute-done.11.refs_3_.refs_4_
  69.2 5.6 %all-to-all-done.x_ref = bf16[16,40,1280]{2,1,0:T(8,128)(2,1)S(1)} async-done(((bf16[16,40,1280]{2,1,0:T(8,128)(2,1)}), bf16[16,40,1280]{2,1,0:T(8,128)(2,1)S(1)}, u32[]{:S(2)}, u32[]{:S(2)}) %all-to-all-start) | async-done | bytes 1638432 | tf_op jit(solution)/shard_map/all_to_all | solution.py:288
  74.8 1.6 %shard_map.51 = bf16[16,40,1280]{2,1,0:T(8,128)(2,1)} custom-call(bf16[16,40,1280]{2,1,0:T(8,128)(2,1)S(1)} %all-to-all-done.x_ref, bf16[160,256]{1,0:T(8,128)(2,1)S(1)} %collective-permute-done.8.refs_0_.refs_1_, bf16[160,256]{1,0:T(8,128)(2,1)S(1)} %collective-permute-done.9.refs_1_.refs_2_, bf16[160,256]{1,0:T(8,128)(2,1)S(1)} %collective-permute-done.10.refs_2_.refs_3_, ...), custom_call_target="tpu_custom_call" | custom-call | bytes 3932160 | tf_op jit(solution)/shard_map/pallas_call | solution.py:201
  76.4 6.2 %all-to-all-start.1 = ((bf16[16,40,1280]{2,1,0:T(8,128)(2,1)}), bf16[16,40,1280]{2,1,0:T(8,128)(2,1)S(1)}, u32[]{:S(2)}, u32[]{:S(2)}) async-start(bf16[16,40,1280]{2,1,0:T(8,128)(2,1)} %shard_map.51), calls=%async_computation.1 | async-start | bytes 3276800 | tf_op jit(solution)/shard_map/all_to_all | solution.py:298
  82.6 1.3 %collective-permute-start.12 = (bf16[160,256]{1,0:T(8,128)(2,1)S(1)}, bf16[160,256]{1,0:T(8,128)(2,1)S(1)}, u32[]{:S(2)}, u32[]{:S(2)}) collective-permute-start(bf16[160,256]{1,0:T(8,128)(2,1)S(1)} %get-tuple-element.48), channel_id=1, source_target_pairs={{0,129},{1,128},{64,193},{65,192},{128,0},{129,1},{192,64},{193,65... | collective-permute-start | bytes 245768 | tf_op jit(solution)/shard_map/ppermute | solution.py:217
  83.9 2.8 %collective-permute-start.13 = (bf16[160,256]{1,0:T(8,128)(2,1)S(1)}, bf16[160,256]{1,0:T(8,128)(2,1)S(1)}, u32[]{:S(2)}, u32[]{:S(2)}) collective-permute-start(bf16[160,256]{1,0:T(8,128)(2,1)S(1)} %get-tuple-element.49), channel_id=1, source_target_pairs={{0,64},{1,65},{64,128},{65,129},{128,192},{129,193},{192,1},{193,0... | collective-permute-start | bytes 245768 | tf_op jit(solution)/shard_map/ppermute | solution.py:217
  86.7 0.4 collective-permute-start.14
  87.1 1.8 %collective-permute-done.12.refs_5_ = bf16[160,256]{1,0:T(8,128)(2,1)S(1)} collective-permute-done((bf16[160,256]{1,0:T(8,128)(2,1)S(1)}, bf16[160,256]{1,0:T(8,128)(2,1)S(1)}, u32[]{:S(2)}, u32[]{:S(2)}) %collective-permute-start.12) | collective-permute-done | bytes 81952 | tf_op jit(solution)/shard_map/ppermute | solution.py:217
  89.0 0.6 collective-permute-done.13.refs_6_
  89.5 1.6 %collective-permute-done.14.refs_7_ = bf16[160,256]{1,0:T(8,128)(2,1)S(1)} collective-permute-done((bf16[160,256]{1,0:T(8,128)(2,1)S(1)}, bf16[160,256]{1,0:T(8,128)(2,1)S(1)}, u32[]{:S(2)}, u32[]{:S(2)}) %collective-permute-start.14) | collective-permute-done | bytes 81952 | tf_op jit(solution)/shard_map/ppermute | solution.py:217
  91.2 0.1 shard_map.52.v_ref
  91.2 0.1 collective-permute-start.15
  91.3 2.1 %collective-permute-done.15._.v_far = bf16[2,4,160,256]{3,2,1,0:T(8,128)(2,1)S(1)} collective-permute-done((bf16[2,4,160,256]{3,2,1,0:T(8,128)(2,1)S(1)}, bf16[2,4,160,256]{3,2,1,0:T(8,128)(2,1)S(1)}, u32[]{:S(2)}, u32[]{:S(2)}) %collective-permute-start.15) | collective-permute-done | bytes 655392 | tf_op jit(solution)/shard_map/ppermute | solution.py:222
  93.4 9.7 %all-to-all-done.1 = bf16[16,40,1280]{2,1,0:T(8,128)(2,1)S(1)} async-done(((bf16[16,40,1280]{2,1,0:T(8,128)(2,1)}), bf16[16,40,1280]{2,1,0:T(8,128)(2,1)S(1)}, u32[]{:S(2)}, u32[]{:S(2)}) %all-to-all-start.1) | async-done | bytes 1638432 | tf_op jit(solution)/shard_map/all_to_all | solution.py:298
  103.1 0.7 shard_map.54
  103.8 0.0 copy-start.1
  103.8 3.6 %collective-permute-start.16 = (bf16[160,256]{1,0:T(8,128)(2,1)S(1)}, bf16[160,256]{1,0:T(8,128)(2,1)S(1)}, u32[]{:S(2)}, u32[]{:S(2)}) collective-permute-start(bf16[160,256]{1,0:T(8,128)(2,1)S(1)} %get-tuple-element.52), channel_id=1, source_target_pairs={{0,1},{1,0},{64,65},{65,64},{128,129},{129,128},{192,193},{193,192... | collective-permute-start | bytes 245768 | tf_op jit(solution)/shard_map/ppermute | solution.py:217
  107.4 0.1 collective-permute-start.17
  107.5 4.1 %collective-permute-start.18 = (bf16[160,256]{1,0:T(8,128)(2,1)S(1)}, bf16[160,256]{1,0:T(8,128)(2,1)S(1)}, u32[]{:S(2)}, u32[]{:S(2)}) collective-permute-start(bf16[160,256]{1,0:T(8,128)(2,1)S(1)} %get-tuple-element.54), channel_id=1, source_target_pairs={{0,129},{1,128},{64,193},{65,192},{128,0},{129,1},{192,64},{193,65... | collective-permute-start | bytes 245768 | tf_op jit(solution)/shard_map/ppermute | solution.py:217
  111.6 0.7 shard_map.55
  112.3 1.2 collective-permute-start.19
  113.5 3.9 %collective-permute-start.20 = (bf16[160,256]{1,0:T(8,128)(2,1)S(1)}, bf16[160,256]{1,0:T(8,128)(2,1)S(1)}, u32[]{:S(2)}, u32[]{:S(2)}) collective-permute-start(bf16[160,256]{1,0:T(8,128)(2,1)S(1)} %get-tuple-element.56), channel_id=1, source_target_pairs={{0,65},{1,64},{64,129},{65,128},{128,193},{129,192},{192,0},{193,1... | collective-permute-start | bytes 245768 | tf_op jit(solution)/shard_map/ppermute | solution.py:217
  117.4 0.0 collective-permute-done.16.refs_1_
  117.4 0.0 collective-permute-start.21
  117.4 0.0 collective-permute-done.17.refs_2_
  117.4 3.2 %collective-permute-start.22 = (bf16[160,256]{1,0:T(8,128)(2,1)S(1)}, bf16[160,256]{1,0:T(8,128)(2,1)S(1)}, u32[]{:S(2)}, u32[]{:S(2)}) collective-permute-start(bf16[160,256]{1,0:T(8,128)(2,1)S(1)} %get-tuple-element.58), channel_id=1, source_target_pairs={{0,193},{1,192},{64,0},{65,1},{128,64},{129,65},{192,128},{193,129... | collective-permute-start | bytes 245768 | tf_op jit(solution)/shard_map/ppermute | solution.py:217
  120.6 0.0 collective-permute-done.18.refs_3_
  120.6 0.4 collective-permute-done.19.refs_4_
  121.0 0.0 collective-permute-done.20.refs_5_
  121.0 2.0 %collective-permute-done.21.refs_6_ = bf16[160,256]{1,0:T(8,128)(2,1)S(1)} collective-permute-done((bf16[160,256]{1,0:T(8,128)(2,1)S(1)}, bf16[160,256]{1,0:T(8,128)(2,1)S(1)}, u32[]{:S(2)}, u32[]{:S(2)}) %collective-permute-start.21) | collective-permute-done | bytes 81952 | tf_op jit(solution)/shard_map/ppermute | solution.py:217
  123.0 0.0 collective-permute-done.22.refs_7_
  123.1 0.0 copy-done.1
  123.1 1.7 %shard_map.56 = f32[4,160,768]{2,1,0:T(8,128)} custom-call(s32[1]{0:T(128)} %bitcast.pos_ref, bf16[512,768]{1,0:T(8,128)(2,1)S(1)} %copy-done.1, bf16[160,256]{1,0:T(8,128)(2,1)S(1)} %get-tuple-element.51.refs_0_, bf16[160,256]{1,0:T(8,128)(2,1)S(1)} %collective-permute-done.16.refs_1_, bf16[160,256]{1,0:T(8,128)(2,1)S(1)} %collective-permute-done.17.refs_2_, ...), custom_call_target="tpu_custom_call" | custom-call | flops 503316480 | bytes 2883592 | tf_op jit(solution)/shard_map/pallas_call | solution.py:201
  (3 shorter events, 0.0 us)
Async XLA Ops:
  0.0 0.7 copy-start.2
  0.7 31.9 %copy-start = (bf16[768,3,512]{2,0,1:T(8,128)(2,1)S(1)}, bf16[768,3,512]{2,0,1:T(8,128)(2,1)}, u32[]{:S(2)}) copy-start(bf16[768,3,512]{2,0,1:T(8,128)(2,1)} %param.6) | copy-start | bytes 7077892
  4.1 19.3 %collective-permute-start = (bf16[320,256]{1,0:T(8,128)(2,1)S(1)}, bf16[320,256]{1,0:T(8,128)(2,1)S(1)}, u32[]{:S(2)}, u32[]{:S(2)}) collective-permute-start(bf16[320,256]{1,0:T(8,128)(2,1)S(1)} %get-tuple-element.33), channel_id=1, source_target_pairs={{0,1},{1,0},{64,65},{65,64},{128,129},{129,128},{192,193},{193,192... | collective-permute-start | bytes 491528 | tf_op jit(solution)/shard_map/ppermute | solution.py:217
  11.4 21.2 %collective-permute-start.1 = (bf16[320,256]{1,0:T(8,128)(2,1)S(1)}, bf16[320,256]{1,0:T(8,128)(2,1)S(1)}, u32[]{:S(2)}, u32[]{:S(2)}) collective-permute-start(bf16[320,256]{1,0:T(8,128)(2,1)S(1)} %get-tuple-element.34), channel_id=1, source_target_pairs={{0,192},{1,193},{64,1},{65,0},{128,65},{129,64},{192,129},{193,128... | collective-permute-start | bytes 491528 | tf_op jit(solution)/shard_map/ppermute | solution.py:217
  13.3 20.2 %collective-permute-start.2 = (bf16[320,256]{1,0:T(8,128)(2,1)S(1)}, bf16[320,256]{1,0:T(8,128)(2,1)S(1)}, u32[]{:S(2)}, u32[]{:S(2)}) collective-permute-start(bf16[320,256]{1,0:T(8,128)(2,1)S(1)} %get-tuple-element.35), channel_id=1, source_target_pairs={{0,65},{1,64},{64,129},{65,128},{128,193},{129,192},{192,0},{193,1... | collective-permute-start | bytes 491528 | tf_op jit(solution)/shard_map/ppermute | solution.py:217
  16.4 20.4 %collective-permute-start.3 = (bf16[320,256]{1,0:T(8,128)(2,1)S(1)}, bf16[320,256]{1,0:T(8,128)(2,1)S(1)}, u32[]{:S(2)}, u32[]{:S(2)}) collective-permute-start(bf16[320,256]{1,0:T(8,128)(2,1)S(1)} %get-tuple-element.36), channel_id=1, source_target_pairs={{0,128},{1,129},{64,192},{65,193},{128,1},{129,0},{192,65},{193,64... | collective-permute-start | bytes 491528 | tf_op jit(solution)/shard_map/ppermute | solution.py:217
  17.9 19.8 %collective-permute-start.4 = (bf16[320,256]{1,0:T(8,128)(2,1)S(1)}, bf16[320,256]{1,0:T(8,128)(2,1)S(1)}, u32[]{:S(2)}, u32[]{:S(2)}) collective-permute-start(bf16[320,256]{1,0:T(8,128)(2,1)S(1)} %get-tuple-element.37), channel_id=1, source_target_pairs={{0,129},{1,128},{64,193},{65,192},{128,0},{129,1},{192,64},{193,65... | collective-permute-start | bytes 491528 | tf_op jit(solution)/shard_map/ppermute | solution.py:217
  23.4 16.4 %collective-permute-start.5 = (bf16[320,256]{1,0:T(8,128)(2,1)S(1)}, bf16[320,256]{1,0:T(8,128)(2,1)S(1)}, u32[]{:S(2)}, u32[]{:S(2)}) collective-permute-start(bf16[320,256]{1,0:T(8,128)(2,1)S(1)} %get-tuple-element.38), channel_id=1, source_target_pairs={{0,64},{1,65},{64,128},{65,129},{128,192},{129,193},{192,1},{193,0... | collective-permute-start | bytes 491528 | tf_op jit(solution)/shard_map/ppermute | solution.py:217
  32.6 8.3 %collective-permute-start.6 = (bf16[320,256]{1,0:T(8,128)(2,1)S(1)}, bf16[320,256]{1,0:T(8,128)(2,1)S(1)}, u32[]{:S(2)}, u32[]{:S(2)}) collective-permute-start(bf16[320,256]{1,0:T(8,128)(2,1)S(1)} %get-tuple-element.39), channel_id=1, source_target_pairs={{0,193},{1,192},{64,0},{65,1},{128,64},{129,65},{192,128},{193,129... | collective-permute-start | bytes 491528 | tf_op jit(solution)/shard_map/ppermute | solution.py:217
  41.0 2.2 %collective-permute-start.7 = (bf16[2,4,160,256]{3,2,1,0:T(8,128)(2,1)S(1)}, bf16[2,4,160,256]{3,2,1,0:T(8,128)(2,1)S(1)}, u32[]{:S(2)}, u32[]{:S(2)}) collective-permute-start(bf16[2,4,160,256]{3,2,1,0:T(8,128)(2,1)S(1)} %shard_map.48.refs_8_), channel_id=1, source_target_pairs={{0,32},{32,0},{1,33},{33,1},{2,34},{34,2},{3,35},{35,3},{4,36},{36... | collective-permute-start | bytes 1966088 | tf_op jit(solution)/shard_map/ppermute | solution.py:222
  44.7 30.1 %all-to-all-start = ((bf16[16,40,1280]{2,1,0:T(8,128)(2,1)}), bf16[16,40,1280]{2,1,0:T(8,128)(2,1)S(1)}, u32[]{:S(2)}, u32[]{:S(2)}) async-start(bf16[16,40,1280]{2,1,0:T(8,128)(2,1)} %bitcast.2), calls=%async_computation | async-start | bytes 3276800 | tf_op jit(solution)/shard_map/all_to_all | solution.py:288
  52.2 11.6 %collective-permute-start.8 = (bf16[160,256]{1,0:T(8,128)(2,1)S(1)}, bf16[160,256]{1,0:T(8,128)(2,1)S(1)}, u32[]{:S(2)}, u32[]{:S(2)}) collective-permute-start(bf16[160,256]{1,0:T(8,128)(2,1)S(1)} %get-tuple-element.44), channel_id=1, source_target_pairs={{0,1},{1,0},{64,65},{65,64},{128,129},{129,128},{192,193},{193,192... | collective-permute-start | bytes 245768 | tf_op jit(solution)/shard_map/ppermute | solution.py:217
  55.7 13.5 %collective-permute-start.9 = (bf16[160,256]{1,0:T(8,128)(2,1)S(1)}, bf16[160,256]{1,0:T(8,128)(2,1)S(1)}, u32[]{:S(2)}, u32[]{:S(2)}) collective-permute-start(bf16[160,256]{1,0:T(8,128)(2,1)S(1)} %get-tuple-element.45), channel_id=1, source_target_pairs={{0,192},{1,193},{64,1},{65,0},{128,65},{129,64},{192,129},{193,128... | collective-permute-start | bytes 245768 | tf_op jit(solution)/shard_map/ppermute | solution.py:217
  58.0 11.1 %collective-permute-start.10 = (bf16[160,256]{1,0:T(8,128)(2,1)S(1)}, bf16[160,256]{1,0:T(8,128)(2,1)S(1)}, u32[]{:S(2)}, u32[]{:S(2)}) collective-permute-start(bf16[160,256]{1,0:T(8,128)(2,1)S(1)} %get-tuple-element.46), channel_id=1, source_target_pairs={{0,65},{1,64},{64,129},{65,128},{128,193},{129,192},{192,0},{193,1... | collective-permute-start | bytes 245768 | tf_op jit(solution)/shard_map/ppermute | solution.py:217
  60.7 8.5 %collective-permute-start.11 = (bf16[160,256]{1,0:T(8,128)(2,1)S(1)}, bf16[160,256]{1,0:T(8,128)(2,1)S(1)}, u32[]{:S(2)}, u32[]{:S(2)}) collective-permute-start(bf16[160,256]{1,0:T(8,128)(2,1)S(1)} %get-tuple-element.47), channel_id=1, source_target_pairs={{0,128},{1,129},{64,192},{65,193},{128,1},{129,0},{192,65},{193,64... | collective-permute-start | bytes 245768 | tf_op jit(solution)/shard_map/ppermute | solution.py:217
  76.4 26.7 %all-to-all-start.1 = ((bf16[16,40,1280]{2,1,0:T(8,128)(2,1)}), bf16[16,40,1280]{2,1,0:T(8,128)(2,1)S(1)}, u32[]{:S(2)}, u32[]{:S(2)}) async-start(bf16[16,40,1280]{2,1,0:T(8,128)(2,1)} %shard_map.51), calls=%async_computation.1 | async-start | bytes 3276800 | tf_op jit(solution)/shard_map/all_to_all | solution.py:298
  82.6 6.3 %collective-permute-start.12 = (bf16[160,256]{1,0:T(8,128)(2,1)S(1)}, bf16[160,256]{1,0:T(8,128)(2,1)S(1)}, u32[]{:S(2)}, u32[]{:S(2)}) collective-permute-start(bf16[160,256]{1,0:T(8,128)(2,1)S(1)} %get-tuple-element.48), channel_id=1, source_target_pairs={{0,129},{1,128},{64,193},{65,192},{128,0},{129,1},{192,64},{193,65... | collective-permute-start | bytes 245768 | tf_op jit(solution)/shard_map/ppermute | solution.py:217
  83.9 5.7 %collective-permute-start.13 = (bf16[160,256]{1,0:T(8,128)(2,1)S(1)}, bf16[160,256]{1,0:T(8,128)(2,1)S(1)}, u32[]{:S(2)}, u32[]{:S(2)}) collective-permute-start(bf16[160,256]{1,0:T(8,128)(2,1)S(1)} %get-tuple-element.49), channel_id=1, source_target_pairs={{0,64},{1,65},{64,128},{65,129},{128,192},{129,193},{192,1},{193,0... | collective-permute-start | bytes 245768 | tf_op jit(solution)/shard_map/ppermute | solution.py:217
  86.7 4.4 %collective-permute-start.14 = (bf16[160,256]{1,0:T(8,128)(2,1)S(1)}, bf16[160,256]{1,0:T(8,128)(2,1)S(1)}, u32[]{:S(2)}, u32[]{:S(2)}) collective-permute-start(bf16[160,256]{1,0:T(8,128)(2,1)S(1)} %get-tuple-element.50), channel_id=1, source_target_pairs={{0,193},{1,192},{64,0},{65,1},{128,64},{129,65},{192,128},{193,129... | collective-permute-start | bytes 245768 | tf_op jit(solution)/shard_map/ppermute | solution.py:217
  91.2 2.2 %collective-permute-start.15 = (bf16[2,4,160,256]{3,2,1,0:T(8,128)(2,1)S(1)}, bf16[2,4,160,256]{3,2,1,0:T(8,128)(2,1)S(1)}, u32[]{:S(2)}, u32[]{:S(2)}) collective-permute-start(bf16[2,4,160,256]{3,2,1,0:T(8,128)(2,1)S(1)} %shard_map.52.v_ref), channel_id=1, source_target_pairs={{0,32},{32,0},{1,33},{33,1},{2,34},{34,2},{3,35},{35,3},{4,36},{36... | collective-permute-start | bytes 1966088 | tf_op jit(solution)/shard_map/ppermute | solution.py:222
  103.8 19.2 %copy-start.1 = (bf16[512,768]{1,0:T(8,128)(2,1)S(1)}, bf16[512,768]{1,0:T(8,128)(2,1)}, u32[]{:S(2)}) copy-start(bf16[512,768]{1,0:T(8,128)(2,1)} %w_ref.1) | copy-start | bytes 2359300
  103.8 13.6 %collective-permute-start.16 = (bf16[160,256]{1,0:T(8,128)(2,1)S(1)}, bf16[160,256]{1,0:T(8,128)(2,1)S(1)}, u32[]{:S(2)}, u32[]{:S(2)}) collective-permute-start(bf16[160,256]{1,0:T(8,128)(2,1)S(1)} %get-tuple-element.52), channel_id=1, source_target_pairs={{0,1},{1,0},{64,65},{65,64},{128,129},{129,128},{192,193},{193,192... | collective-permute-start | bytes 245768 | tf_op jit(solution)/shard_map/ppermute | solution.py:217
  107.4 10.0 %collective-permute-start.17 = (bf16[160,256]{1,0:T(8,128)(2,1)S(1)}, bf16[160,256]{1,0:T(8,128)(2,1)S(1)}, u32[]{:S(2)}, u32[]{:S(2)}) collective-permute-start(bf16[160,256]{1,0:T(8,128)(2,1)S(1)} %get-tuple-element.53), channel_id=1, source_target_pairs={{0,128},{1,129},{64,192},{65,193},{128,1},{129,0},{192,65},{193,64... | collective-permute-start | bytes 245768 | tf_op jit(solution)/shard_map/ppermute | solution.py:217
  107.5 13.1 %collective-permute-start.18 = (bf16[160,256]{1,0:T(8,128)(2,1)S(1)}, bf16[160,256]{1,0:T(8,128)(2,1)S(1)}, u32[]{:S(2)}, u32[]{:S(2)}) collective-permute-start(bf16[160,256]{1,0:T(8,128)(2,1)S(1)} %get-tuple-element.54), channel_id=1, source_target_pairs={{0,129},{1,128},{64,193},{65,192},{128,0},{129,1},{192,64},{193,65... | collective-permute-start | bytes 245768 | tf_op jit(solution)/shard_map/ppermute | solution.py:217
  112.3 8.7 %collective-permute-start.19 = (bf16[160,256]{1,0:T(8,128)(2,1)S(1)}, bf16[160,256]{1,0:T(8,128)(2,1)S(1)}, u32[]{:S(2)}, u32[]{:S(2)}) collective-permute-start(bf16[160,256]{1,0:T(8,128)(2,1)S(1)} %get-tuple-element.55), channel_id=1, source_target_pairs={{0,192},{1,193},{64,1},{65,0},{128,65},{129,64},{192,129},{193,128... | collective-permute-start | bytes 245768 | tf_op jit(solution)/shard_map/ppermute | solution.py:217
  113.5 7.5 %collective-permute-start.20 = (bf16[160,256]{1,0:T(8,128)(2,1)S(1)}, bf16[160,256]{1,0:T(8,128)(2,1)S(1)}, u32[]{:S(2)}, u32[]{:S(2)}) collective-permute-start(bf16[160,256]{1,0:T(8,128)(2,1)S(1)} %get-tuple-element.56), channel_id=1, source_target_pairs={{0,65},{1,64},{64,129},{65,128},{128,193},{129,192},{192,0},{193,1... | collective-permute-start | bytes 245768 | tf_op jit(solution)/shard_map/ppermute | solution.py:217
  117.4 5.7 %collective-permute-start.21 = (bf16[160,256]{1,0:T(8,128)(2,1)S(1)}, bf16[160,256]{1,0:T(8,128)(2,1)S(1)}, u32[]{:S(2)}, u32[]{:S(2)}) collective-permute-start(bf16[160,256]{1,0:T(8,128)(2,1)S(1)} %get-tuple-element.57), channel_id=1, source_target_pairs={{0,64},{1,65},{64,128},{65,129},{128,192},{129,193},{192,1},{193,0... | collective-permute-start | bytes 245768 | tf_op jit(solution)/shard_map/ppermute | solution.py:217
  117.4 5.6 %collective-permute-start.22 = (bf16[160,256]{1,0:T(8,128)(2,1)S(1)}, bf16[160,256]{1,0:T(8,128)(2,1)S(1)}, u32[]{:S(2)}, u32[]{:S(2)}) collective-permute-start(bf16[160,256]{1,0:T(8,128)(2,1)S(1)} %get-tuple-element.58), channel_id=1, source_target_pairs={{0,193},{1,192},{64,0},{65,1},{128,64},{129,65},{192,128},{193,129... | collective-permute-start | bytes 245768 | tf_op jit(solution)/shard_map/ppermute | solution.py:217

commit v15 on v14

--- a/solution.py
+++ b/solution.py
@@ -20,7 +20,7 @@
 HBM = pl.BlockSpec(memory_space=pltpu.HBM)
 ANY = pl.BlockSpec(memory_space=pl.ANY)
 SMEM = pl.BlockSpec(memory_space=pltpu.SMEM)
-CONTEXT_STEPS = (0, 4, 2, 6, 3, 5, 1, 7)
+CONTEXT_STEPS = (0, 4, 3, 5, 2, 6, 1, 7)
 MIB = 1024 * 1024
 
 
@@ -300,7 +300,7 @@
     values_far = other_core(values)
     seen = call(seen_kernel, jax.ShapeDtypeStruct((8, 128), F32), [values_far], unread=(0,))
     context = []
-    for blocks in ((0, 2), (1, 3)):
+    for blocks in ((0,), (1, 2, 3)):
         steps = [s for s in CONTEXT_STEPS if s % Z in blocks]
         parts = call(
             functools.partial(context_kernel, blocks, steps),

time: 126 us -> 126 us (level)
  waiting for transfers between devices: 51.9 us -> 54.6 us
  starting transfers between devices: 59.9 us -> 58 us
    ppermute x21, waiting for transfers between devices: 34 us -> 36.7 us  [along_ring(): got.append(lax.ppermute(part, ('z', 'w'), pairs) if s else part)]
    ppermute x21, starting transfers between devices: 46 us -> 44.1 us  [along_ring(): got.append(lax.ppermute(part, ('z', 'w'), pairs) if s else part)]
  transfers between devices with their start and end apart: 25 -> 25, of which waited for: 17 -> 19; matrix products, arithmetic and copies ran while one was open for 0% -> 0% of each run, Pallas kernels for 3% -> 3%
where the time goes in v15:
time: 126 us
  starting transfers between devices  58 us (46%)
  waiting for transfers between devices  54.6 us (43%)
  Pallas kernels  12.1 us (10%)
    ppermute x21, starting transfers between devices, along_ring(): got.append(lax.ppermute(part, ('z', 'w'), pairs) if s else part)  44.1 us
    ppermute x21, waiting for transfers between devices, along_ring(): got.append(lax.ppermute(part, ('z', 'w'), pairs) if s else part)  36.7 us
    pallas_call x11, Pallas kernels, call(): pl.pallas_call(kernel, out_shape=out_shape, in_specs=specs, out_specs=out...  12.1 us
    all_to_all x1, waiting for transfers between devices, shards(): lax.all_to_all(probs, ('x', 'y'), 0, 0, tiled=True).reshape(half, full)  9.69 us
    all_to_all x1, starting transfers between devices, shards(): terms = lax.all_to_all(term.reshape(chunk), ('x', 'y'), 0, 0, tiled=True)  7.44 us
    all_to_all x1, starting transfers between devices, shards(): lax.all_to_all(probs, ('x', 'y'), 0, 0, tiled=True).reshape(half, full)  6.24 us
    all_to_all x1, waiting for transfers between devices, shards(): terms = lax.all_to_all(term.reshape(chunk), ('x', 'y'), 0, 0, tiled=True)  5.57 us
    ppermute x2, waiting for transfers between devices, other_core(): return lax.ppermute(a, 'c', [(0, 1), (1, 0)])  2.65 us
  transfers between devices with their start and end apart: 25, of which 19 were waited for; matrix products, arithmetic and copies ran while one was open for 0% of the time, Pallas kernels for 3%

profile of v15, /device:TPU:6, one launch (start us, length us, event | category | flops | bytes accessed | tf_op | source)
XLA Modules:
  0.0 125.6 jit_solution(10418605220603398327)
XLA Ops:
  0.0 0.7 copy-done.2
  0.7 3.4 %shard_map.46 = (bf16[320,256]{1,0:T(8,128)(2,1)S(1)}, bf16[320,256]{1,0:T(8,128)(2,1)S(1)}, bf16[320,256]{1,0:T(8,128)(2,1)S(1)}, bf16[320,256]{1,0:T(8,128)(2,...) custom-call(s32[1]{0:T(128)} %bitcast.pos_ref, ...), custom_call_target="tpu_custom_call" | custom-call | flops 1006632960 | bytes 6690824 | tf_op jit(solution)/shard_map/pallas_call | solution.py:201
  4.1 7.3 %collective-permute-start = (bf16[320,256]{1,0:T(8,128)(2,1)S(1)}, bf16[320,256]{1,0:T(8,128)(2,1)S(1)}, u32[]{:S(2)}, u32[]{:S(2)}) collective-permute-start(bf16[320,256]{1,0:T(8,128)(2,1)S(1)} %get-tuple-element.33), channel_id=1, source_target_pairs={{0,1},{1,0},{64,65},{65,64},{128,129},{129,128},{192,193},{193,192... | collective-permute-start | bytes 491528 | tf_op jit(solution)/shard_map/ppermute | solution.py:217
  11.4 1.9 %collective-permute-start.1 = (bf16[320,256]{1,0:T(8,128)(2,1)S(1)}, bf16[320,256]{1,0:T(8,128)(2,1)S(1)}, u32[]{:S(2)}, u32[]{:S(2)}) collective-permute-start(bf16[320,256]{1,0:T(8,128)(2,1)S(1)} %get-tuple-element.34), channel_id=1, source_target_pairs={{0,192},{1,193},{64,1},{65,0},{128,65},{129,64},{192,129},{193,128... | collective-permute-start | bytes 491528 | tf_op jit(solution)/shard_map/ppermute | solution.py:217
  13.3 3.1 %collective-permute-start.2 = (bf16[320,256]{1,0:T(8,128)(2,1)S(1)}, bf16[320,256]{1,0:T(8,128)(2,1)S(1)}, u32[]{:S(2)}, u32[]{:S(2)}) collective-permute-start(bf16[320,256]{1,0:T(8,128)(2,1)S(1)} %get-tuple-element.35), channel_id=1, source_target_pairs={{0,65},{1,64},{64,129},{65,128},{128,193},{129,192},{192,0},{193,1... | collective-permute-start | bytes 491528 | tf_op jit(solution)/shard_map/ppermute | solution.py:217
  16.4 1.5 %collective-permute-start.3 = (bf16[320,256]{1,0:T(8,128)(2,1)S(1)}, bf16[320,256]{1,0:T(8,128)(2,1)S(1)}, u32[]{:S(2)}, u32[]{:S(2)}) collective-permute-start(bf16[320,256]{1,0:T(8,128)(2,1)S(1)} %get-tuple-element.36), channel_id=1, source_target_pairs={{0,128},{1,129},{64,192},{65,193},{128,1},{129,0},{192,65},{193,64... | collective-permute-start | bytes 491528 | tf_op jit(solution)/shard_map/ppermute | solution.py:217
  17.9 2.7 %collective-permute-start.4 = (bf16[320,256]{1,0:T(8,128)(2,1)S(1)}, bf16[320,256]{1,0:T(8,128)(2,1)S(1)}, u32[]{:S(2)}, u32[]{:S(2)}) collective-permute-start(bf16[320,256]{1,0:T(8,128)(2,1)S(1)} %get-tuple-element.37), channel_id=1, source_target_pairs={{0,129},{1,128},{64,193},{65,192},{128,0},{129,1},{192,64},{193,65... | collective-permute-start | bytes 491528 | tf_op jit(solution)/shard_map/ppermute | solution.py:217
  20.6 2.8 %collective-permute-done.refs_1_ = bf16[320,256]{1,0:T(8,128)(2,1)S(1)} collective-permute-done((bf16[320,256]{1,0:T(8,128)(2,1)S(1)}, bf16[320,256]{1,0:T(8,128)(2,1)S(1)}, u32[]{:S(2)}, u32[]{:S(2)}) %collective-permute-start) | collective-permute-done | bytes 163872 | tf_op jit(solution)/shard_map/ppermute | solution.py:217
  23.4 0.3 collective-permute-start.5
  23.8 8.8 %collective-permute-done.1.refs_2_ = bf16[320,256]{1,0:T(8,128)(2,1)S(1)} collective-permute-done((bf16[320,256]{1,0:T(8,128)(2,1)S(1)}, bf16[320,256]{1,0:T(8,128)(2,1)S(1)}, u32[]{:S(2)}, u32[]{:S(2)}) %collective-permute-start.1) | collective-permute-done | bytes 163872 | tf_op jit(solution)/shard_map/ppermute | solution.py:217
  32.6 0.0 collective-permute-start.6
  32.6 0.0 copy-done
  32.6 0.9 shard_map.47
  33.5 0.0 collective-permute-done.2.refs_3_
  33.5 3.3 %collective-permute-done.3.refs_4_ = bf16[320,256]{1,0:T(8,128)(2,1)S(1)} collective-permute-done((bf16[320,256]{1,0:T(8,128)(2,1)S(1)}, bf16[320,256]{1,0:T(8,128)(2,1)S(1)}, u32[]{:S(2)}, u32[]{:S(2)}) %collective-permute-start.3) | collective-permute-done | bytes 163872 | tf_op jit(solution)/shard_map/ppermute | solution.py:217
  36.8 0.9 collective-permute-done.4.refs_5_
  37.7 2.2 %collective-permute-done.5.refs_6_ = bf16[320,256]{1,0:T(8,128)(2,1)S(1)} collective-permute-done((bf16[320,256]{1,0:T(8,128)(2,1)S(1)}, bf16[320,256]{1,0:T(8,128)(2,1)S(1)}, u32[]{:S(2)}, u32[]{:S(2)}) %collective-permute-start.5) | collective-permute-done | bytes 163872 | tf_op jit(solution)/shard_map/ppermute | solution.py:217
  39.9 1.1 collective-permute-done.6.refs_7_
  41.0 0.1 shard_map.48.refs_8_
  41.0 0.1 collective-permute-start.7
  41.1 1.5 %shard_map.49 = (bf16[640,1280]{1,0:T(8,128)(2,1)}, bf16[2,4,160,256]{3,2,1,0:T(8,128)(2,1)S(1)}) custom-call(s32[1]{0:T(128)} %bitcast.pos_ref, bf16[320,256]{1,0:T(8,128)(2,1)S(1)} %get-tuple-element.32.refs_0_, bf16[320,256]{1,0:T(8,128)(2,1)S(1)} %collective-permute-done.refs_1_, bf16[320,256]{1,0:T(8,128)(2,1)S(1)} %collective-permute-done.1.refs_2_, ...), custom_call_target="tpu_custom_call" | custom-call | flops 419430400 | bytes 3932168 | tf_op jit(solution)/shard_map/pallas_call | solution.py:201
  42.6 0.6 collective-permute-done.7.k_far
  43.2 1.5 %shard_map.50 = bf16[640,1280]{1,0:T(8,128)(2,1)} custom-call(bf16[640,1280]{1,0:T(8,128)(2,1)} %get-tuple-element.42._, bf16[2,4,160,256]{3,2,1,0:T(8,128)(2,1)S(1)} %get-tuple-element.43.q, bf16[2,4,160,256]{3,2,1,0:T(8,128)(2,1)S(1)} %collective-permute-done.7.k_far), custom_call_target="tpu_custom_call", output_to_operand_aliasing={{}: (0, {})} | custom-call | flops 419430400 | bytes 5898240 | tf_op jit(solution)/shard_map/pallas_call | solution.py:201
  44.7 7.4 %all-to-all-start = ((bf16[16,40,1280]{2,1,0:T(8,128)(2,1)}), bf16[16,40,1280]{2,1,0:T(8,128)(2,1)S(1)}, u32[]{:S(2)}, u32[]{:S(2)}) async-start(bf16[16,40,1280]{2,1,0:T(8,128)(2,1)} %bitcast.2), calls=%async_computation | async-start | bytes 3276800 | tf_op jit(solution)/shard_map/all_to_all | solution.py:288
  52.2 3.5 %collective-permute-start.8 = (bf16[160,256]{1,0:T(8,128)(2,1)S(1)}, bf16[160,256]{1,0:T(8,128)(2,1)S(1)}, u32[]{:S(2)}, u32[]{:S(2)}) collective-permute-start(bf16[160,256]{1,0:T(8,128)(2,1)S(1)} %get-tuple-element.44), channel_id=1, source_target_pairs={{0,1},{1,0},{64,65},{65,64},{128,129},{129,128},{192,193},{193,192... | collective-permute-start | bytes 245768 | tf_op jit(solution)/shard_map/ppermute | solution.py:217
  55.7 2.3 %collective-permute-start.9 = (bf16[160,256]{1,0:T(8,128)(2,1)S(1)}, bf16[160,256]{1,0:T(8,128)(2,1)S(1)}, u32[]{:S(2)}, u32[]{:S(2)}) collective-permute-start(bf16[160,256]{1,0:T(8,128)(2,1)S(1)} %get-tuple-element.45), channel_id=1, source_target_pairs={{0,192},{1,193},{64,1},{65,0},{128,65},{129,64},{192,129},{193,128... | collective-permute-start | bytes 245768 | tf_op jit(solution)/shard_map/ppermute | solution.py:217
  58.0 2.7 %collective-permute-start.10 = (bf16[160,256]{1,0:T(8,128)(2,1)S(1)}, bf16[160,256]{1,0:T(8,128)(2,1)S(1)}, u32[]{:S(2)}, u32[]{:S(2)}) collective-permute-start(bf16[160,256]{1,0:T(8,128)(2,1)S(1)} %get-tuple-element.46), channel_id=1, source_target_pairs={{0,65},{1,64},{64,129},{65,128},{128,193},{129,192},{192,0},{193,1... | collective-permute-start | bytes 245768 | tf_op jit(solution)/shard_map/ppermute | solution.py:217
  60.7 0.1 collective-permute-start.11
  60.8 2.9 %collective-permute-done.8.refs_0_.refs_1_ = bf16[160,256]{1,0:T(8,128)(2,1)S(1)} collective-permute-done((bf16[160,256]{1,0:T(8,128)(2,1)S(1)}, bf16[160,256]{1,0:T(8,128)(2,1)S(1)}, u32[]{:S(2)}, u32[]{:S(2)}) %collective-permute-start.8) | collective-permute-done | bytes 81952 | tf_op jit(solution)/shard_map/ppermute | solution.py:217
  63.7 5.5 %collective-permute-done.9.refs_1_.refs_2_ = bf16[160,256]{1,0:T(8,128)(2,1)S(1)} collective-permute-done((bf16[160,256]{1,0:T(8,128)(2,1)S(1)}, bf16[160,256]{1,0:T(8,128)(2,1)S(1)}, u32[]{:S(2)}, u32[]{:S(2)}) %collective-permute-start.9) | collective-permute-done | bytes 81952 | tf_op jit(solution)/shard_map/ppermute | solution.py:217
  69.2 0.0 collective-permute-done.10.refs_2_.refs_3_
  69.2 0.0 collective-permute-done.11.refs_3_.refs_4_
  69.2 5.6 %all-to-all-done.x_ref = bf16[16,40,1280]{2,1,0:T(8,128)(2,1)S(1)} async-done(((bf16[16,40,1280]{2,1,0:T(8,128)(2,1)}), bf16[16,40,1280]{2,1,0:T(8,128)(2,1)S(1)}, u32[]{:S(2)}, u32[]{:S(2)}) %all-to-all-start) | async-done | bytes 1638432 | tf_op jit(solution)/shard_map/all_to_all | solution.py:288
  74.8 1.6 %shard_map.51 = bf16[16,40,1280]{2,1,0:T(8,128)(2,1)} custom-call(bf16[16,40,1280]{2,1,0:T(8,128)(2,1)S(1)} %all-to-all-done.x_ref, bf16[160,256]{1,0:T(8,128)(2,1)S(1)} %collective-permute-done.8.refs_0_.refs_1_, bf16[160,256]{1,0:T(8,128)(2,1)S(1)} %collective-permute-done.9.refs_1_.refs_2_, bf16[160,256]{1,0:T(8,128)(2,1)S(1)} %collective-permute-done.10.refs_2_.refs_3_, ...), custom_call_target="tpu_custom_call" | custom-call | bytes 3932160 | tf_op jit(solution)/shard_map/pallas_call | solution.py:201
  76.4 6.2 %all-to-all-start.1 = ((bf16[16,40,1280]{2,1,0:T(8,128)(2,1)}), bf16[16,40,1280]{2,1,0:T(8,128)(2,1)S(1)}, u32[]{:S(2)}, u32[]{:S(2)}) async-start(bf16[16,40,1280]{2,1,0:T(8,128)(2,1)} %shard_map.51), calls=%async_computation.1 | async-start | bytes 3276800 | tf_op jit(solution)/shard_map/all_to_all | solution.py:298
  82.6 1.3 collective-permute-start.12
  83.9 2.8 %collective-permute-start.13 = (bf16[160,256]{1,0:T(8,128)(2,1)S(1)}, bf16[160,256]{1,0:T(8,128)(2,1)S(1)}, u32[]{:S(2)}, u32[]{:S(2)}) collective-permute-start(bf16[160,256]{1,0:T(8,128)(2,1)S(1)} %get-tuple-element.49), channel_id=1, source_target_pairs={{0,64},{1,65},{64,128},{65,129},{128,192},{129,193},{192,1},{193,0... | collective-permute-start | bytes 245768 | tf_op jit(solution)/shard_map/ppermute | solution.py:217
  86.7 0.4 collective-permute-start.14
  87.1 1.8 %collective-permute-done.12.refs_5_ = bf16[160,256]{1,0:T(8,128)(2,1)S(1)} collective-permute-done((bf16[160,256]{1,0:T(8,128)(2,1)S(1)}, bf16[160,256]{1,0:T(8,128)(2,1)S(1)}, u32[]{:S(2)}, u32[]{:S(2)}) %collective-permute-start.12) | collective-permute-done | bytes 81952 | tf_op jit(solution)/shard_map/ppermute | solution.py:217
  89.0 0.6 collective-permute-done.13.refs_6_
  89.5 1.6 %collective-permute-done.14.refs_7_ = bf16[160,256]{1,0:T(8,128)(2,1)S(1)} collective-permute-done((bf16[160,256]{1,0:T(8,128)(2,1)S(1)}, bf16[160,256]{1,0:T(8,128)(2,1)S(1)}, u32[]{:S(2)}, u32[]{:S(2)}) %collective-permute-start.14) | collective-permute-done | bytes 81952 | tf_op jit(solution)/shard_map/ppermute | solution.py:217
  91.2 0.1 shard_map.52.v_ref
  91.2 0.1 collective-permute-start.15
  91.3 2.1 %collective-permute-done.15._.v_far = bf16[2,4,160,256]{3,2,1,0:T(8,128)(2,1)S(1)} collective-permute-done((bf16[2,4,160,256]{3,2,1,0:T(8,128)(2,1)S(1)}, bf16[2,4,160,256]{3,2,1,0:T(8,128)(2,1)S(1)}, u32[]{:S(2)}, u32[]{:S(2)}) %collective-permute-start.15) | collective-permute-done | bytes 655392 | tf_op jit(solution)/shard_map/ppermute | solution.py:222
  93.4 9.7 %all-to-all-done.1 = bf16[16,40,1280]{2,1,0:T(8,128)(2,1)S(1)} async-done(((bf16[16,40,1280]{2,1,0:T(8,128)(2,1)}), bf16[16,40,1280]{2,1,0:T(8,128)(2,1)S(1)}, u32[]{:S(2)}, u32[]{:S(2)}) %all-to-all-start.1) | async-done | bytes 1638432 | tf_op jit(solution)/shard_map/all_to_all | solution.py:298
  103.1 0.4 shard_map.54
  103.6 0.0 copy-start.1
  103.6 3.6 %collective-permute-start.16 = (bf16[160,256]{1,0:T(8,128)(2,1)S(1)}, bf16[160,256]{1,0:T(8,128)(2,1)S(1)}, u32[]{:S(2)}, u32[]{:S(2)}) collective-permute-start(bf16[160,256]{1,0:T(8,128)(2,1)S(1)} %get-tuple-element.52), channel_id=1, source_target_pairs={{0,1},{1,0},{64,65},{65,64},{128,129},{129,128},{192,193},{193,192... | collective-permute-start | bytes 245768 | tf_op jit(solution)/shard_map/ppermute | solution.py:217
  107.2 1.0 shard_map.55
  108.1 2.4 %collective-permute-start.17 = (bf16[160,256]{1,0:T(8,128)(2,1)S(1)}, bf16[160,256]{1,0:T(8,128)(2,1)S(1)}, u32[]{:S(2)}, u32[]{:S(2)}) collective-permute-start(bf16[160,256]{1,0:T(8,128)(2,1)S(1)} %get-tuple-element.53), channel_id=1, source_target_pairs={{0,192},{1,193},{64,1},{65,0},{128,65},{129,64},{192,129},{193,128... | collective-permute-start | bytes 245768 | tf_op jit(solution)/shard_map/ppermute | solution.py:217
  110.6 2.7 %collective-permute-start.18 = (bf16[160,256]{1,0:T(8,128)(2,1)S(1)}, bf16[160,256]{1,0:T(8,128)(2,1)S(1)}, u32[]{:S(2)}, u32[]{:S(2)}) collective-permute-start(bf16[160,256]{1,0:T(8,128)(2,1)S(1)} %get-tuple-element.54), channel_id=1, source_target_pairs={{0,65},{1,64},{64,129},{65,128},{128,193},{129,192},{192,0},{193,1... | collective-permute-start | bytes 245768 | tf_op jit(solution)/shard_map/ppermute | solution.py:217
  113.3 0.1 collective-permute-start.19
  113.3 4.1 %collective-permute-start.20 = (bf16[160,256]{1,0:T(8,128)(2,1)S(1)}, bf16[160,256]{1,0:T(8,128)(2,1)S(1)}, u32[]{:S(2)}, u32[]{:S(2)}) collective-permute-start(bf16[160,256]{1,0:T(8,128)(2,1)S(1)} %get-tuple-element.56), channel_id=1, source_target_pairs={{0,129},{1,128},{64,193},{65,192},{128,0},{129,1},{192,64},{193,65... | collective-permute-start | bytes 245768 | tf_op jit(solution)/shard_map/ppermute | solution.py:217
  117.4 0.0 collective-permute-done.16.refs_1_
  117.4 0.0 collective-permute-start.21
  117.4 2.0 %collective-permute-done.17.refs_2_ = bf16[160,256]{1,0:T(8,128)(2,1)S(1)} collective-permute-done((bf16[160,256]{1,0:T(8,128)(2,1)S(1)}, bf16[160,256]{1,0:T(8,128)(2,1)S(1)}, u32[]{:S(2)}, u32[]{:S(2)}) %collective-permute-start.17) | collective-permute-done | bytes 81952 | tf_op jit(solution)/shard_map/ppermute | solution.py:217
  119.4 1.3 %collective-permute-start.22 = (bf16[160,256]{1,0:T(8,128)(2,1)S(1)}, bf16[160,256]{1,0:T(8,128)(2,1)S(1)}, u32[]{:S(2)}, u32[]{:S(2)}) collective-permute-start(bf16[160,256]{1,0:T(8,128)(2,1)S(1)} %get-tuple-element.58), channel_id=1, source_target_pairs={{0,193},{1,192},{64,0},{65,1},{128,64},{129,65},{192,128},{193,129... | collective-permute-start | bytes 245768 | tf_op jit(solution)/shard_map/ppermute | solution.py:217
  120.6 0.0 collective-permute-done.18.refs_3_
  120.6 0.0 collective-permute-done.19.refs_4_
  120.6 1.3 %collective-permute-done.20.refs_5_ = bf16[160,256]{1,0:T(8,128)(2,1)S(1)} collective-permute-done((bf16[160,256]{1,0:T(8,128)(2,1)S(1)}, bf16[160,256]{1,0:T(8,128)(2,1)S(1)}, u32[]{:S(2)}, u32[]{:S(2)}) %collective-permute-start.20) | collective-permute-done | bytes 81952 | tf_op jit(solution)/shard_map/ppermute | solution.py:217
  121.9 1.1 collective-permute-done.21.refs_6_
  123.1 0.7 collective-permute-done.22.refs_7_
  123.8 0.0 copy-done.1
  123.8 1.7 %shard_map.56 = f32[4,160,768]{2,1,0:T(8,128)} custom-call(s32[1]{0:T(128)} %bitcast.pos_ref, bf16[512,768]{1,0:T(8,128)(2,1)S(1)} %copy-done.1, bf16[160,256]{1,0:T(8,128)(2,1)S(1)} %get-tuple-element.51.refs_0_, bf16[160,256]{1,0:T(8,128)(2,1)S(1)} %collective-permute-done.16.refs_1_, bf16[160,256]{1,0:T(8,128)(2,1)S(1)} %collective-permute-done.17.refs_2_, ...), custom_call_target="tpu_custom_call" | custom-call | flops 503316480 | bytes 2883592 | tf_op jit(solution)/shard_map/pallas_call | solution.py:201
  (3 shorter events, 0.0 us)
Async XLA Ops:
  0.0 0.7 copy-start.2
  0.7 31.9 %copy-start = (bf16[768,3,512]{2,0,1:T(8,128)(2,1)S(1)}, bf16[768,3,512]{2,0,1:T(8,128)(2,1)}, u32[]{:S(2)}) copy-start(bf16[768,3,512]{2,0,1:T(8,128)(2,1)} %param.6) | copy-start | bytes 7077892
  4.1 19.3 %collective-permute-start = (bf16[320,256]{1,0:T(8,128)(2,1)S(1)}, bf16[320,256]{1,0:T(8,128)(2,1)S(1)}, u32[]{:S(2)}, u32[]{:S(2)}) collective-permute-start(bf16[320,256]{1,0:T(8,128)(2,1)S(1)} %get-tuple-element.33), channel_id=1, source_target_pairs={{0,1},{1,0},{64,65},{65,64},{128,129},{129,128},{192,193},{193,192... | collective-permute-start | bytes 491528 | tf_op jit(solution)/shard_map/ppermute | solution.py:217
  11.4 21.2 %collective-permute-start.1 = (bf16[320,256]{1,0:T(8,128)(2,1)S(1)}, bf16[320,256]{1,0:T(8,128)(2,1)S(1)}, u32[]{:S(2)}, u32[]{:S(2)}) collective-permute-start(bf16[320,256]{1,0:T(8,128)(2,1)S(1)} %get-tuple-element.34), channel_id=1, source_target_pairs={{0,192},{1,193},{64,1},{65,0},{128,65},{129,64},{192,129},{193,128... | collective-permute-start | bytes 491528 | tf_op jit(solution)/shard_map/ppermute | solution.py:217
  13.3 20.2 %collective-permute-start.2 = (bf16[320,256]{1,0:T(8,128)(2,1)S(1)}, bf16[320,256]{1,0:T(8,128)(2,1)S(1)}, u32[]{:S(2)}, u32[]{:S(2)}) collective-permute-start(bf16[320,256]{1,0:T(8,128)(2,1)S(1)} %get-tuple-element.35), channel_id=1, source_target_pairs={{0,65},{1,64},{64,129},{65,128},{128,193},{129,192},{192,0},{193,1... | collective-permute-start | bytes 491528 | tf_op jit(solution)/shard_map/ppermute | solution.py:217
  16.4 20.4 %collective-permute-start.3 = (bf16[320,256]{1,0:T(8,128)(2,1)S(1)}, bf16[320,256]{1,0:T(8,128)(2,1)S(1)}, u32[]{:S(2)}, u32[]{:S(2)}) collective-permute-start(bf16[320,256]{1,0:T(8,128)(2,1)S(1)} %get-tuple-element.36), channel_id=1, source_target_pairs={{0,128},{1,129},{64,192},{65,193},{128,1},{129,0},{192,65},{193,64... | collective-permute-start | bytes 491528 | tf_op jit(solution)/shard_map/ppermute | solution.py:217
  17.9 19.8 %collective-permute-start.4 = (bf16[320,256]{1,0:T(8,128)(2,1)S(1)}, bf16[320,256]{1,0:T(8,128)(2,1)S(1)}, u32[]{:S(2)}, u32[]{:S(2)}) collective-permute-start(bf16[320,256]{1,0:T(8,128)(2,1)S(1)} %get-tuple-element.37), channel_id=1, source_target_pairs={{0,129},{1,128},{64,193},{65,192},{128,0},{129,1},{192,64},{193,65... | collective-permute-start | bytes 491528 | tf_op jit(solution)/shard_map/ppermute | solution.py:217
  23.4 16.4 %collective-permute-start.5 = (bf16[320,256]{1,0:T(8,128)(2,1)S(1)}, bf16[320,256]{1,0:T(8,128)(2,1)S(1)}, u32[]{:S(2)}, u32[]{:S(2)}) collective-permute-start(bf16[320,256]{1,0:T(8,128)(2,1)S(1)} %get-tuple-element.38), channel_id=1, source_target_pairs={{0,64},{1,65},{64,128},{65,129},{128,192},{129,193},{192,1},{193,0... | collective-permute-start | bytes 491528 | tf_op jit(solution)/shard_map/ppermute | solution.py:217
  32.6 8.3 %collective-permute-start.6 = (bf16[320,256]{1,0:T(8,128)(2,1)S(1)}, bf16[320,256]{1,0:T(8,128)(2,1)S(1)}, u32[]{:S(2)}, u32[]{:S(2)}) collective-permute-start(bf16[320,256]{1,0:T(8,128)(2,1)S(1)} %get-tuple-element.39), channel_id=1, source_target_pairs={{0,193},{1,192},{64,0},{65,1},{128,64},{129,65},{192,128},{193,129... | collective-permute-start | bytes 491528 | tf_op jit(solution)/shard_map/ppermute | solution.py:217
  41.0 2.2 %collective-permute-start.7 = (bf16[2,4,160,256]{3,2,1,0:T(8,128)(2,1)S(1)}, bf16[2,4,160,256]{3,2,1,0:T(8,128)(2,1)S(1)}, u32[]{:S(2)}, u32[]{:S(2)}) collective-permute-start(bf16[2,4,160,256]{3,2,1,0:T(8,128)(2,1)S(1)} %shard_map.48.refs_8_), channel_id=1, source_target_pairs={{0,32},{32,0},{1,33},{33,1},{2,34},{34,2},{3,35},{35,3},{4,36},{36... | collective-permute-start | bytes 1966088 | tf_op jit(solution)/shard_map/ppermute | solution.py:222
  44.7 30.1 %all-to-all-start = ((bf16[16,40,1280]{2,1,0:T(8,128)(2,1)}), bf16[16,40,1280]{2,1,0:T(8,128)(2,1)S(1)}, u32[]{:S(2)}, u32[]{:S(2)}) async-start(bf16[16,40,1280]{2,1,0:T(8,128)(2,1)} %bitcast.2), calls=%async_computation | async-start | bytes 3276800 | tf_op jit(solution)/shard_map/all_to_all | solution.py:288
  52.2 11.6 %collective-permute-start.8 = (bf16[160,256]{1,0:T(8,128)(2,1)S(1)}, bf16[160,256]{1,0:T(8,128)(2,1)S(1)}, u32[]{:S(2)}, u32[]{:S(2)}) collective-permute-start(bf16[160,256]{1,0:T(8,128)(2,1)S(1)} %get-tuple-element.44), channel_id=1, source_target_pairs={{0,1},{1,0},{64,65},{65,64},{128,129},{129,128},{192,193},{193,192... | collective-permute-start | bytes 245768 | tf_op jit(solution)/shard_map/ppermute | solution.py:217
  55.7 13.5 %collective-permute-start.9 = (bf16[160,256]{1,0:T(8,128)(2,1)S(1)}, bf16[160,256]{1,0:T(8,128)(2,1)S(1)}, u32[]{:S(2)}, u32[]{:S(2)}) collective-permute-start(bf16[160,256]{1,0:T(8,128)(2,1)S(1)} %get-tuple-element.45), channel_id=1, source_target_pairs={{0,192},{1,193},{64,1},{65,0},{128,65},{129,64},{192,129},{193,128... | collective-permute-start | bytes 245768 | tf_op jit(solution)/shard_map/ppermute | solution.py:217
  58.0 11.1 %collective-permute-start.10 = (bf16[160,256]{1,0:T(8,128)(2,1)S(1)}, bf16[160,256]{1,0:T(8,128)(2,1)S(1)}, u32[]{:S(2)}, u32[]{:S(2)}) collective-permute-start(bf16[160,256]{1,0:T(8,128)(2,1)S(1)} %get-tuple-element.46), channel_id=1, source_target_pairs={{0,65},{1,64},{64,129},{65,128},{128,193},{129,192},{192,0},{193,1... | collective-permute-start | bytes 245768 | tf_op jit(solution)/shard_map/ppermute | solution.py:217
  60.7 8.5 %collective-permute-start.11 = (bf16[160,256]{1,0:T(8,128)(2,1)S(1)}, bf16[160,256]{1,0:T(8,128)(2,1)S(1)}, u32[]{:S(2)}, u32[]{:S(2)}) collective-permute-start(bf16[160,256]{1,0:T(8,128)(2,1)S(1)} %get-tuple-element.47), channel_id=1, source_target_pairs={{0,128},{1,129},{64,192},{65,193},{128,1},{129,0},{192,65},{193,64... | collective-permute-start | bytes 245768 | tf_op jit(solution)/shard_map/ppermute | solution.py:217
  76.4 26.7 %all-to-all-start.1 = ((bf16[16,40,1280]{2,1,0:T(8,128)(2,1)}), bf16[16,40,1280]{2,1,0:T(8,128)(2,1)S(1)}, u32[]{:S(2)}, u32[]{:S(2)}) async-start(bf16[16,40,1280]{2,1,0:T(8,128)(2,1)} %shard_map.51), calls=%async_computation.1 | async-start | bytes 3276800 | tf_op jit(solution)/shard_map/all_to_all | solution.py:298
  82.6 6.3 %collective-permute-start.12 = (bf16[160,256]{1,0:T(8,128)(2,1)S(1)}, bf16[160,256]{1,0:T(8,128)(2,1)S(1)}, u32[]{:S(2)}, u32[]{:S(2)}) collective-permute-start(bf16[160,256]{1,0:T(8,128)(2,1)S(1)} %get-tuple-element.48), channel_id=1, source_target_pairs={{0,129},{1,128},{64,193},{65,192},{128,0},{129,1},{192,64},{193,65... | collective-permute-start | bytes 245768 | tf_op jit(solution)/shard_map/ppermute | solution.py:217
  83.9 5.7 %collective-permute-start.13 = (bf16[160,256]{1,0:T(8,128)(2,1)S(1)}, bf16[160,256]{1,0:T(8,128)(2,1)S(1)}, u32[]{:S(2)}, u32[]{:S(2)}) collective-permute-start(bf16[160,256]{1,0:T(8,128)(2,1)S(1)} %get-tuple-element.49), channel_id=1, source_target_pairs={{0,64},{1,65},{64,128},{65,129},{128,192},{129,193},{192,1},{193,0... | collective-permute-start | bytes 245768 | tf_op jit(solution)/shard_map/ppermute | solution.py:217
  86.7 4.4 %collective-permute-start.14 = (bf16[160,256]{1,0:T(8,128)(2,1)S(1)}, bf16[160,256]{1,0:T(8,128)(2,1)S(1)}, u32[]{:S(2)}, u32[]{:S(2)}) collective-permute-start(bf16[160,256]{1,0:T(8,128)(2,1)S(1)} %get-tuple-element.50), channel_id=1, source_target_pairs={{0,193},{1,192},{64,0},{65,1},{128,64},{129,65},{192,128},{193,129... | collective-permute-start | bytes 245768 | tf_op jit(solution)/shard_map/ppermute | solution.py:217
  91.2 2.2 %collective-permute-start.15 = (bf16[2,4,160,256]{3,2,1,0:T(8,128)(2,1)S(1)}, bf16[2,4,160,256]{3,2,1,0:T(8,128)(2,1)S(1)}, u32[]{:S(2)}, u32[]{:S(2)}) collective-permute-start(bf16[2,4,160,256]{3,2,1,0:T(8,128)(2,1)S(1)} %shard_map.52.v_ref), channel_id=1, source_target_pairs={{0,32},{32,0},{1,33},{33,1},{2,34},{34,2},{3,35},{35,3},{4,36},{36... | collective-permute-start | bytes 1966088 | tf_op jit(solution)/shard_map/ppermute | solution.py:222
  103.6 20.2 %copy-start.1 = (bf16[512,768]{1,0:T(8,128)(2,1)S(1)}, bf16[512,768]{1,0:T(8,128)(2,1)}, u32[]{:S(2)}) copy-start(bf16[512,768]{1,0:T(8,128)(2,1)} %w_ref.1) | copy-start | bytes 2359300
  103.6 13.8 %collective-permute-start.16 = (bf16[160,256]{1,0:T(8,128)(2,1)S(1)}, bf16[160,256]{1,0:T(8,128)(2,1)S(1)}, u32[]{:S(2)}, u32[]{:S(2)}) collective-permute-start(bf16[160,256]{1,0:T(8,128)(2,1)S(1)} %get-tuple-element.52), channel_id=1, source_target_pairs={{0,1},{1,0},{64,65},{65,64},{128,129},{129,128},{192,193},{193,192... | collective-permute-start | bytes 245768 | tf_op jit(solution)/shard_map/ppermute | solution.py:217
  108.1 11.2 %collective-permute-start.17 = (bf16[160,256]{1,0:T(8,128)(2,1)S(1)}, bf16[160,256]{1,0:T(8,128)(2,1)S(1)}, u32[]{:S(2)}, u32[]{:S(2)}) collective-permute-start(bf16[160,256]{1,0:T(8,128)(2,1)S(1)} %get-tuple-element.53), channel_id=1, source_target_pairs={{0,192},{1,193},{64,1},{65,0},{128,65},{129,64},{192,129},{193,128... | collective-permute-start | bytes 245768 | tf_op jit(solution)/shard_map/ppermute | solution.py:217
  110.6 10.1 %collective-permute-start.18 = (bf16[160,256]{1,0:T(8,128)(2,1)S(1)}, bf16[160,256]{1,0:T(8,128)(2,1)S(1)}, u32[]{:S(2)}, u32[]{:S(2)}) collective-permute-start(bf16[160,256]{1,0:T(8,128)(2,1)S(1)} %get-tuple-element.54), channel_id=1, source_target_pairs={{0,65},{1,64},{64,129},{65,128},{128,193},{129,192},{192,0},{193,1... | collective-permute-start | bytes 245768 | tf_op jit(solution)/shard_map/ppermute | solution.py:217
  113.3 7.4 %collective-permute-start.19 = (bf16[160,256]{1,0:T(8,128)(2,1)S(1)}, bf16[160,256]{1,0:T(8,128)(2,1)S(1)}, u32[]{:S(2)}, u32[]{:S(2)}) collective-permute-start(bf16[160,256]{1,0:T(8,128)(2,1)S(1)} %get-tuple-element.55), channel_id=1, source_target_pairs={{0,128},{1,129},{64,192},{65,193},{128,1},{129,0},{192,65},{193,64... | collective-permute-start | bytes 245768 | tf_op jit(solution)/shard_map/ppermute | solution.py:217
  113.3 8.6 %collective-permute-start.20 = (bf16[160,256]{1,0:T(8,128)(2,1)S(1)}, bf16[160,256]{1,0:T(8,128)(2,1)S(1)}, u32[]{:S(2)}, u32[]{:S(2)}) collective-permute-start(bf16[160,256]{1,0:T(8,128)(2,1)S(1)} %get-tuple-element.56), channel_id=1, source_target_pairs={{0,129},{1,128},{64,193},{65,192},{128,0},{129,1},{192,64},{193,65... | collective-permute-start | bytes 245768 | tf_op jit(solution)/shard_map/ppermute | solution.py:217
  117.4 5.7 %collective-permute-start.21 = (bf16[160,256]{1,0:T(8,128)(2,1)S(1)}, bf16[160,256]{1,0:T(8,128)(2,1)S(1)}, u32[]{:S(2)}, u32[]{:S(2)}) collective-permute-start(bf16[160,256]{1,0:T(8,128)(2,1)S(1)} %get-tuple-element.57), channel_id=1, source_target_pairs={{0,64},{1,65},{64,128},{65,129},{128,192},{129,193},{192,1},{193,0... | collective-permute-start | bytes 245768 | tf_op jit(solution)/shard_map/ppermute | solution.py:217
  119.4 4.4 %collective-permute-start.22 = (bf16[160,256]{1,0:T(8,128)(2,1)S(1)}, bf16[160,256]{1,0:T(8,128)(2,1)S(1)}, u32[]{:S(2)}, u32[]{:S(2)}) collective-permute-start(bf16[160,256]{1,0:T(8,128)(2,1)S(1)} %get-tuple-element.58), channel_id=1, source_target_pairs={{0,193},{1,192},{64,0},{65,1},{128,64},{129,65},{192,128},{193,129... | collective-permute-start | bytes 245768 | tf_op jit(solution)/shard_map/ppermute | solution.py:217
